TPU v7x, 128 devices: a whole 4x4x4 slice. The times are simulated.
128 devices in a mesh: ptg: 8 (over y_lo, z), img: 16 (over y_hi, x, core).
Axes of the slice: x: 4, y: 4 (y_hi: 2, y_lo: 2; y = y_hi * 2 + y_lo), z: 4, core: 2. Of those that a mesh axis runs over, the one named last changes fastest.
Arguments:
- image: bfloat16 [2048, 8192], P(None, 'img'), may hold values from -6 to 6
- beam: float32 [8, 2048, 2048], P('ptg', 'img'), may hold values from 0.2 to 1
- counts: int32 [8, 2048, 2048], P('ptg', None, 'img'), may hold values from 0 to 15
- offsets: int32 [8], P('ptg'), may hold values from 0 to 6144, as said below
Outputs:
- hessian_image: float32 [2048, 8192], P('ptg', 'img')
Inputs may be any that keep to these rules, and one draw needn't show every extreme that they name: offsets rise with the pointing; the first is 0 and the last is 6144.
All inputs are finite; a program needn't handle non-finite values.
Results may differ from a plain program's by a relative error of at most 0.0095.
Values may be sent and summed in bfloat16 or wider, within the bound.
No kernel may reach another device: no remote copies, remote signals or barrier semaphores. Data moves between devices by JAX's collectives and lax.ppermute only.
A program may use at most 64 MiB of HBM per device.

v0:
```python
import math

import jax
import jax.numpy as jnp
from jax import lax
from jax.sharding import PartitionSpec as P


def tables(points):
    index_row = jnp.arange(points, dtype=jnp.int32)
    phase = index_row[:, None] * index_row[None, :] % points
    angle = phase.astype(jnp.float32) * (2.0 * math.pi / points)
    return (jnp.cos(angle).astype(jnp.bfloat16), (-jnp.sin(angle)).astype(jnp.bfloat16))


def shards(image, beam, counts, offsets):
    points = counts.shape[1]
    start = offsets[0]
    cosine, sine_table = tables(points)
    strip = lax.all_to_all(image, "img", split_axis=0, concat_axis=1, tiled=True)
    window = lax.dynamic_slice_in_dim(strip, start, points, 1)
    beamed = (beam[0] * window.astype(jnp.float32)).astype(jnp.bfloat16)
    row_real = jnp.dot(beamed, cosine, preferred_element_type=jnp.float32).astype(jnp.bfloat16)
    row_imag = jnp.dot(beamed, sine_table, preferred_element_type=jnp.float32).astype(jnp.bfloat16)
    col_real, col_imag = (
        lax.all_to_all(row_real, "img", split_axis=1, concat_axis=0, tiled=True),
        lax.all_to_all(row_imag, "img", split_axis=1, concat_axis=0, tiled=True),
    )
    spec_real = jnp.dot(cosine, col_real, preferred_element_type=jnp.float32) - jnp.dot(
        sine_table, col_imag, preferred_element_type=jnp.float32
    )
    spec_imag = jnp.dot(sine_table, col_real, preferred_element_type=jnp.float32) + jnp.dot(
        cosine, col_imag, preferred_element_type=jnp.float32
    )
    weight = counts[0].astype(jnp.float32) / float(points * points)
    weighted_real = (weight * spec_real).astype(jnp.bfloat16)
    weighted_imag = (weight * spec_imag).astype(jnp.bfloat16)
    back_real = (
        jnp.dot(cosine, weighted_real, preferred_element_type=jnp.float32)
        + jnp.dot(sine_table, weighted_imag, preferred_element_type=jnp.float32)
    ).astype(jnp.bfloat16)
    back_imag = (
        jnp.dot(cosine, weighted_imag, preferred_element_type=jnp.float32)
        - jnp.dot(sine_table, weighted_real, preferred_element_type=jnp.float32)
    ).astype(jnp.bfloat16)
    rows_real, rows_imag = (
        lax.all_to_all(back_real, "img", split_axis=0, concat_axis=1, tiled=True),
        lax.all_to_all(back_imag, "img", split_axis=0, concat_axis=1, tiled=True),
    )
    image_real = jnp.dot(rows_real, cosine, preferred_element_type=jnp.float32) + jnp.dot(
        rows_imag, sine_table, preferred_element_type=jnp.float32
    )
    contribution = (beam[0] * image_real).astype(jnp.bfloat16)
    placed = lax.dynamic_update_slice_in_dim(
        jnp.zeros((contribution.shape[0], strip.shape[1]), jnp.bfloat16), contribution, start, 1
    )
    tile_terms = lax.all_to_all(placed, "img", split_axis=1, concat_axis=0, tiled=True).astype(
        jnp.float32
    )
    summed = lax.psum(tile_terms.astype(jnp.bfloat16), "ptg").astype(jnp.float32)
    share_rows = summed.shape[0] // lax.axis_size("ptg")
    return lax.dynamic_slice_in_dim(summed, lax.axis_index("ptg") * share_rows, share_rows, 0)


def solution(mesh):
    return jax.shard_map(
        shards,
        mesh=mesh,
        in_specs=(P(None, "img"), P("ptg", "img", None), P("ptg", None, "img"), P("ptg")),
        out_specs=P("ptg", "img"),
        check_vma=False,
    )
```

profile of v0, /device:TPU:14, one launch (start us, length us, event | category | flops | bytes accessed | tf_op | source)
XLA Modules:
  0.0 1022.3 jit_solution(5209906066337299994)
XLA Ops:
  6.5 6.5 all-to-all-start
  13.7 25.6 %all-to-all-done = bf16[16,128,512]{2,1,0:T(8,128)(2,1)S(1)} async-done(((bf16[16,128,512]{2,1,0:T(8,128)(2,1)}), bf16[16,128,512]{2,1,0:T(8,128)(2,1)S(1)}, u32[]{:S(2)}, u32[]{:S(2)}) %all-to-all-start) | async-done | bytes 2097184 | tf_op jit(solution)/shard_map/all_to_all | solution.py:20
  39.5 1.0 copy-done
  40.5 0.2 fusion.35
  40.8 63.3 %fusion.34 = bf16[16,16,8,128]{3,2,1,0:T(8,128)(2,1)S(1)} fusion(bf16[128,2048]{1,0:T(8,128)(2,1)S(1)} %fusion.35), kind=kOutput, calls=%fused_computation.39 | convolution fusion | flops 1141112832 | bytes 1048576 | tf_op jit(solution)/shard_map/dot_general | solution.py:24
  104.1 0.9 copy.31
  105.0 8.2 all-to-all-start.2
  113.2 62.3 %fusion.33 = bf16[16,16,8,128]{3,2,1,0:T(8,128)(2,1)S(1)} fusion(bf16[128,2048]{1,0:T(8,128)(2,1)S(1)} %fusion.35), kind=kOutput, calls=%fused_computation.38 | convolution fusion | flops 1136918528 | bytes 1048576 | tf_op jit(solution)/shard_map/dot_general | solution.py:23
  175.5 0.9 copy.32
  176.4 7.6 all-to-all-start.1
  184.0 70.0 %fusion.8 = f32[2048,128]{1,0:T(8,128)S(1)} fusion(bf16[2048,128]{1,0:T(8,128)(2,1)S(1)} %bitcast.75), kind=kOutput, calls=%fused_computation.13 | convolution fusion | flops 1136656384 | bytes 1572864 | tf_op jit(solution)/shard_map/dot_general | solution.py:32
  254.0 70.0 %fusion.10 = f32[2048,128]{1,0:T(8,128)S(1)} fusion(bf16[2048,128]{1,0:T(8,128)(2,1)S(1)} %bitcast.79), kind=kOutput, calls=%fused_computation.15 | convolution fusion | flops 1136656384 | bytes 1572864 | tf_op jit(solution)/shard_map/dot_general | solution.py:29
  324.0 71.3 %fusion.27 = bf16[2048,128]{1,0:T(8,128)(2,1)S(1)} fusion(f32[2048,128]{1,0:T(8,128)S(1)} %fusion.8, bf16[2048,128]{1,0:T(8,128)(2,1)S(1)} %bitcast.80, s32[1,2048,128]{2,1,0:T(8,128)S(1)} %copy-done.2), kind=kOutput, calls=%fused_computation.32 | convolution fusion | flops 1142161408 | bytes 3145728 | tf_op jit(solution)/shard_map/dot_general | solution.py:32
  395.3 70.0 %fusion.6 = f32[2048,128]{1,0:T(8,128)S(1)} fusion(bf16[2048,128]{1,0:T(8,128)(2,1)S(1)} %fusion.27), kind=kOutput, calls=%fused_computation.11 | convolution fusion | flops 1136656384 | bytes 1572864 | tf_op jit(solution)/shard_map/dot_general | solution.py:43
  465.2 71.3 %fusion.26 = bf16[2048,128]{1,0:T(8,128)(2,1)S(1)} fusion(f32[2048,128]{1,0:T(8,128)S(1)} %fusion.10, bf16[2048,128]{1,0:T(8,128)(2,1)S(1)} %bitcast.76, s32[1,2048,128]{2,1,0:T(8,128)S(1)} %copy-done.2), kind=kOutput, calls=%fused_computation.31 | convolution fusion | flops 1142161408 | bytes 3145728 | tf_op jit(solution)/shard_map/dot_general | solution.py:29
  536.5 70.0 %fusion.9 = f32[2048,128]{1,0:T(8,128)S(1)} fusion(bf16[2048,128]{1,0:T(8,128)(2,1)S(1)} %fusion.26), kind=kOutput, calls=%fused_computation.14 | convolution fusion | flops 1136656384 | bytes 1572864 | tf_op jit(solution)/shard_map/dot_general | solution.py:39
  606.5 71.2 %fusion.30 = bf16[2048,128]{1,0:T(8,128)(2,1)S(1)} fusion(f32[2048,128]{1,0:T(8,128)S(1)} %fusion.9, bf16[2048,128]{1,0:T(8,128)(2,1)S(1)} %fusion.27), kind=kOutput, calls=%fused_computation.35 | convolution fusion | flops 1141374976 | bytes 2097152 | tf_op jit(solution)/shard_map/dot_general | solution.py:40
  677.7 1.0 copy.22
  678.7 7.2 all-to-all-start.3
  686.0 71.2 %fusion.29 = bf16[2048,128]{1,0:T(8,128)(2,1)S(1)} fusion(f32[2048,128]{1,0:T(8,128)S(1)} %fusion.6, bf16[2048,128]{1,0:T(8,128)(2,1)S(1)} %fusion.26), kind=kOutput, calls=%fused_computation.34 | convolution fusion | flops 1141374976 | bytes 2097152 | tf_op jit(solution)/shard_map/dot_general | solution.py:44
  757.1 1.0 copy.23
  758.2 7.2 all-to-all-start.4
  765.4 0.5 all-reduce.2.cloned.1.call-start
  765.9 62.4 %fusion.7 = f32[128,2048]{1,0:T(8,128)S(1)} fusion(bf16[128,2048]{0,1:T(8,128)(2,1)S(1)} %bitcast.77), kind=kOutput, calls=%fused_computation.12 | convolution fusion | flops 1136656384 | bytes 1572864 | tf_op jit(solution)/shard_map/dot_general | solution.py:50
  828.3 63.5 %fusion.28 = bf16[128,2048]{1,0:T(8,128)(2,1)S(1)} fusion(f32[128,2048]{1,0:T(8,128)S(1)} %fusion.7, bf16[128,2048]{0,1:T(8,128)(2,1)S(1)} %bitcast.78, f32[1,128,2048]{2,1,0:T(8,128)S(1)} %copy-done.1), kind=kOutput, calls=%fused_computation.33 | convolution fusion | flops 1141637120 | bytes 3145728 | tf_op jit(solution)/shard_map/dot_general | solution.py:50
  891.9 0.3 copy.24
  892.1 0.3 broadcast_in_dim.2
  892.4 1.1 dynamic_update_slice.3
  893.6 33.5 %all_to_all.114 = bf16[128,16,512]{0,2,1:T(8,128)(2,1)} all-to-all(bf16[128,16,512]{0,2,1:T(8,128)(2,1)S(1)} %bitcast.71), channel_id=1, replica_groups=mesh['ptg'=8,'img'=16] {'img'}, dimensions={1} | all-to-all | bytes 4194304 | tf_op jit(solution)/shard_map/all_to_all | solution.py:57
  927.1 3.9 copy.25
  931.0 82.5 %all-reduce.2.cloned.1.call-done = bf16[2048,512]{1,0:T(8,128)(2,1)} async-done(((bf16[2048,512]{1,0:T(8,128)(2,1)}), bf16[2048,512]{1,0:T(8,128)(2,1)}) %all-reduce.2.cloned.1.call-update) | async-done | bytes 2097168 | tf_op jit(solution)/shard_map/psum | solution.py:60
  1013.5 1.8 dynamic-slice_convert_fusion
  (11 shorter events, 0.3 us)
Async XLA Ops:
  6.5 32.7 %all-to-all-start = ((bf16[16,128,512]{2,1,0:T(8,128)(2,1)}), bf16[16,128,512]{2,1,0:T(8,128)(2,1)S(1)}, u32[]{:S(2)}, u32[]{:S(2)}) async-start(bf16[16,128,512]{2,1,0:T(8,128)(2,1)} %bitcast.74), calls=%async_computation | async-start | bytes 4194304 | tf_op jit(solution)/shard_map/all_to_all | solution.py:20
  39.3 1.2 copy-start
  105.0 71.4 %all-to-all-start.2 = ((bf16[128,16,128]{2,0,1:T(8,128)(2,1)}), bf16[128,16,128]{2,0,1:T(8,128)(2,1)S(1)}, u32[]{:S(2)}, u32[]{:S(2)}) async-start(bf16[128,16,128]{2,0,1:T(8,128)(2,1)} %bitcast.64), calls=%async_computation.2 | async-start | bytes 1048576 | tf_op jit(solution)/shard_map/all_to_all | solution.py:27
  176.4 77.6 %all-to-all-start.1 = ((bf16[128,16,128]{2,0,1:T(8,128)(2,1)}), bf16[128,16,128]{2,0,1:T(8,128)(2,1)S(1)}, u32[]{:S(2)}, u32[]{:S(2)}) async-start(bf16[128,16,128]{2,0,1:T(8,128)(2,1)} %bitcast.65), calls=%async_computation.1 | async-start | bytes 1048576 | tf_op jit(solution)/shard_map/all_to_all | solution.py:26
  254.0 70.0 %copy-start.2 = (s32[1,2048,128]{2,1,0:T(8,128)S(1)}, s32[1,2048,128]{2,1,0:T(8,128)}, u32[]{:S(2)}) copy-start(s32[1,2048,128]{2,1,0:T(8,128)} %param.6) | copy-start | bytes 3145732
  678.7 79.4 %all-to-all-start.3 = ((bf16[16,128,128]{1,2,0:T(8,128)(2,1)}), bf16[16,128,128]{1,2,0:T(8,128)(2,1)S(1)}, u32[]{:S(2)}, u32[]{:S(2)}) async-start(bf16[16,128,128]{1,2,0:T(8,128)(2,1)} %copy.22), calls=%async_computation.3 | async-start | bytes 1048576 | tf_op jit(solution)/shard_map/all_to_all | solution.py:47
  758.2 70.1 %all-to-all-start.4 = ((bf16[16,128,128]{1,2,0:T(8,128)(2,1)}), bf16[16,128,128]{1,2,0:T(8,128)(2,1)S(1)}, u32[]{:S(2)}, u32[]{:S(2)}) async-start(bf16[16,128,128]{1,2,0:T(8,128)(2,1)} %copy.23), calls=%async_computation.4 | async-start | bytes 1048576 | tf_op jit(solution)/shard_map/all_to_all | solution.py:48
  765.4 248.1 %all-reduce.2.cloned.1.call-start = ((), (), s32[]{:S(2)}) async-start(), calls=%async_computation.6 | async-start | bytes 4194304 | tf_op jit(solution)/shard_map/psum | solution.py:60
  765.9 62.4 %copy-start.1 = (f32[1,128,2048]{2,1,0:T(8,128)S(1)}, f32[1,128,2048]{2,1,0:T(8,128)}, u32[]{:S(2)}) copy-start(f32[1,128,2048]{2,1,0:T(8,128)} %param.5) | copy-start | bytes 3145732
Sparse Core Ops, SparseCore 0:
  931.1 82.3 all-reduce.1
where the time goes:
time: 1030 us; the launch traced here: 1020 us
  matrix products  816 us (79%)
  waiting for transfers between devices  108 us (10%)
  starting transfers between devices  37.2 us (4%)
  blocking collectives  33.5 us (3%)
  between operations  14.4 us (1%)
  local copies, waits for them, and re-layouts  10.7 us (1%)
    psum x1, waiting for transfers between devices, shards(): lax.psum(tile_terms.astype(jnp.bfloat16), 'ptg').astype(jnp.float32)  82.5 us
    dot_general x1, matrix products, shards(): jnp.dot(sine_table, col_real, preferred_element_type=jnp.float32)  71.3 us
    dot_general x1, matrix products, shards(): jnp.dot(sine_table, col_imag, preferred_element_type=jnp.float32)  71.3 us
    dot_general x1, matrix products, shards(): jnp.dot(sine_table, weighted_imag, preferred_element_type=jnp.float32)  71.2 us
    dot_general x1, matrix products, shards(): jnp.dot(sine_table, weighted_real, preferred_element_type=jnp.float32)  71.2 us
    dot_general x1, matrix products, shards(): jnp.dot(cosine, col_imag, preferred_element_type=jnp.float32)  70 us
    dot_general x1, matrix products, shards(): jnp.dot(cosine, col_real, preferred_element_type=jnp.float32)  70 us
    dot_general x1, matrix products, shards(): jnp.dot(cosine, weighted_real, preferred_element_type=jnp.float32)  70 us
  transfers between devices with their start and end apart: 6, of which 2 were waited for; matrix products, arithmetic and copies ran while one was open for 26% of the time, Pallas kernels for 0%

commit v1 on v0

v1 whole, which is shorter than its diff:
```python
import numpy as np

import jax
import jax.numpy as jnp
from jax import lax
from jax.sharding import PartitionSpec as P


def first_frequency(device, devices, points):
    half = points // devices // 2
    low = device < devices // 2
    return np.where(low, 2 * half * device, 2 * half * (devices - 1 - device) + half)


def tables(points, devices):
    index = np.arange(points)
    angle = 2.0 * np.pi / points * np.arange(points)
    cos_of, sin_of = np.cos(angle), -np.sin(angle)
    phase = index[:, None] * index[None, :] % points
    half = points // devices // 2
    device = np.arange(devices)
    freq = first_frequency(device, devices, points)[:, None] + np.arange(half)[None, :]
    row_phase = index[:, None, None] * freq[None] % points
    row_imag = sin_of[row_phase]
    row_imag[:, 0, 0] = cos_of[index * (points // 2) % points]
    row = np.concatenate([cos_of[row_phase], row_imag], axis=2).reshape(points, points)
    as_bf16 = lambda t: jnp.asarray(t.astype(np.float32)).astype(jnp.bfloat16)
    return as_bf16(cos_of[phase]), as_bf16(sin_of[phase]), as_bf16(row)


def dot(a, b, dims=((1,), (0,))):
    return lax.dot_general(a, b, (dims, ((), ())), preferred_element_type=jnp.float32)


def paired_weights(counts, devices):
    points = counts.shape[0]
    me = lax.axis_index("img")
    low = me < devices // 2
    held = counts.astype(jnp.bfloat16)
    half = held.shape[1] // 2
    lower, upper = held[:, :half], held[:, half:]
    other = lax.ppermute(upper, "img", [(i, devices - 1 - i) for i in range(devices)])
    edge = lax.ppermute(
        held[:, 0].reshape(points // 128, 128),
        "img",
        [(i, (devices - i) % (devices // 2)) for i in range(devices // 2, devices)],
    ).reshape(points, 1)
    direct = jnp.where(low, lower, other).astype(jnp.float32)
    mirror = jnp.where(low, other, lower)
    first = jnp.where(low, jnp.where(me == 0, held[:, :1], edge), upper[:, :1])
    mirror = jnp.concatenate([first, jnp.flip(mirror, 1)[:, : half - 1], edge], 1)
    mirror = jnp.concatenate([mirror[:1], jnp.flip(mirror[1:], 0)], 0).astype(jnp.float32)
    nyquist = 0.5 * (edge.astype(jnp.float32) + mirror[:, half:])
    weight = direct + mirror[:, :half]
    zero = me == 0
    left = jnp.where(zero, 0.5, 1.0) * weight[:, :1]
    right = jnp.where(zero, nyquist, weight[:, :1])
    return jnp.concatenate([left, weight[:, 1:], right, weight[:, 1:]], 1)


def shards(image, beam, counts, offsets):
    points = counts.shape[1]
    devices = lax.axis_size("img")
    pointings = lax.axis_size("ptg")
    rows = points // devices
    start = offsets[0]
    me = lax.axis_index("img")
    ptg = lax.axis_index("ptg")
    cosine, sine_table, row_table = tables(points, devices)
    starts = lax.all_gather(offsets, "ptg", axis=0, tiled=True)
    strip = lax.all_to_all(image, "img", split_axis=0, concat_axis=1, tiled=True)
    weight = paired_weights(counts[0], devices) * (1.0 / float(points * points))
    window = lax.dynamic_slice_in_dim(strip, start, points, 1)
    beamed = (beam[0] * window.astype(jnp.float32)).astype(jnp.bfloat16)
    row = dot(beamed, row_table).astype(jnp.bfloat16)
    col = lax.all_to_all(row, "img", split_axis=1, concat_axis=0, tiled=True)
    by_cos, by_sin = dot(cosine, col), dot(sine_table, col)
    half = col.shape[1] // 2
    sign = jnp.where(jnp.arange(2 * half) < half, -1.0, 1.0)
    packed = (me == 0) & (jnp.arange(2 * half) % half == 0)
    swap = lambda t: jnp.concatenate([t[:, half:], t[:, :half]], 1)
    upper = weight * (by_cos + jnp.where(packed, 0.0, sign * swap(by_sin)))
    lower = jnp.where(packed, weight * by_sin, -sign * swap(upper))
    back = (
        dot(cosine, upper.astype(jnp.bfloat16)) + dot(sine_table, lower.astype(jnp.bfloat16))
    ).astype(jnp.bfloat16)
    spectrum_rows = lax.all_to_all(back, "img", split_axis=0, concat_axis=1, tiled=True)
    pixels = dot(spectrum_rows, row_table, ((1,), (1,)))
    contribution = (beam[0] * pixels).astype(jnp.bfloat16)
    twice = jnp.concatenate([contribution, contribution], 1)
    by_class = lax.dynamic_slice_in_dim(twice, (points - start % points) % points, points, 1)
    share = points // pointings
    terms = lax.all_to_all(by_class, "ptg", split_axis=1, concat_axis=0, tiled=True)
    terms = terms.reshape(pointings, rows, share).astype(jnp.float32)
    laps = strip.shape[1] // points
    column = jnp.arange(laps)[:, None] * points + ptg * share + jnp.arange(share)[None, :]
    sums = 0.0
    for p in range(pointings):
        inside = (column >= starts[p]) & (column < starts[p] + points)
        sums = sums + jnp.where(inside[:, None, :], terms[p][None], 0.0)
    sums = sums.astype(jnp.bfloat16).reshape(2, laps // 2, rows, share)
    core = me % 2
    mine = lax.dynamic_index_in_dim(sums, core, 0, keepdims=False)
    theirs = lax.dynamic_index_in_dim(sums, 1 - core, 0, keepdims=False)
    got = lax.ppermute(theirs, "img", [(i, i ^ 1) for i in range(devices)])
    both = jnp.where(
        core == 0, jnp.concatenate([mine, got], 1), jnp.concatenate([got, mine], 1)
    )
    tile = strip.shape[1] // devices
    per_lap = points // tile
    halves = tile // share
    received = []
    for turn in range(2):
        pairs = []
        for q in range(pointings):
            for i in range(devices):
                lap = 2 * (i % 2) + (turn ^ (q % 2))
                pairs.append((q * devices + i, (i // 2) * devices + per_lap * lap + q // halves))
        block = lax.dynamic_index_in_dim(both, turn ^ (ptg % 2), 0, keepdims=False)
        received.append(lax.ppermute(block, ("ptg", "img"), pairs))
    odd = (me // per_lap) % 2 == 1
    out = jnp.where(
        odd,
        jnp.concatenate([received[1], received[0]], 1),
        jnp.concatenate([received[0], received[1]], 1),
    )
    return out.astype(jnp.float32)


def solution(mesh):
    return jax.shard_map(
        shards,
        mesh=mesh,
        in_specs=(P(None, "img"), P("ptg", "img", None), P("ptg", None, "img"), P("ptg")),
        out_specs=P("ptg", "img"),
        check_vma=False,
    )
```

time: 1030 us -> 179 us (0.17)
  matrix products: 816 us -> 29.7 us
  waiting for transfers between devices: 108 us -> 50.2 us
  blocking collectives: 33.5 us -> 13.3 us
  local copies, waits for them, and re-layouts: 10.7 us -> 26.2 us
  other arithmetic: 2.05 us -> 12.8 us
    dot_general x12 -> x6, matrix products: 816 us -> 29.7 us  [dot(): lax.dot_general(a, b, (dims, ((), ())), preferred_element_type=jnp.float32)]
    psum x1 -> x0, waiting for transfers between devices: 82.5 us -> none  [shards(): lax.psum(tile_terms.astype(jnp.bfloat16), 'ptg').astype(jnp.float32)]
    all_to_all x1 -> x0, blocking collectives: 33.5 us -> none  [shards(): lax.all_to_all(placed, 'img', split_axis=1, concat_axis=0, tiled=True)]
    ppermute x0 -> x5, waiting for transfers between devices: none -> 31.3 us  [the longest x1 17.1 us: paired_weights(): lax.ppermute(held[:, 0].reshape(points // 128, 128), 'img', [(i, (devices...]
    all_to_all x1, waiting for transfers between devices: 25.6 us -> 0.01 us  [shards(): lax.all_to_all(image, 'img', split_axis=0, concat_axis=1, tiled=True)]
    all_to_all x4 -> x3, waiting for transfers between devices: 0.01 us -> 18.9 us  [the longest x1 9.53 us: shards(): lax.all_to_all(back, 'img', split_axis=0, concat_axis=1, tiled=True)]
    unnamed x6 -> x29, local copies, waits for them, and re-layouts: 1.01 us -> 14.6 us
    unnamed x0 -> x1, blocking collectives: none -> 13.3 us
  transfers between devices with their start and end apart: 6 -> 9, of which waited for: 2 -> 7; matrix products, arithmetic and copies ran while one was open for 26% -> 18% of each run, Pallas kernels for 0% -> 0%
where the time goes in v1:
time: 179 us; the launch traced here: 176 us
  waiting for transfers between devices  50.2 us (28%)
  starting transfers between devices  37.3 us (21%)
  matrix products  29.7 us (17%)
  local copies, waits for them, and re-layouts  26.2 us (15%)
  blocking collectives  13.3 us (7%)
  other arithmetic  12.8 us (7%)
  between operations  6.11 us (3%)
    dot_general x6, matrix products, dot(): lax.dot_general(a, b, (dims, ((), ())), preferred_element_type=jnp.float32)  29.7 us
    ppermute x1, waiting for transfers between devices, paired_weights(): lax.ppermute(held[:, 0].reshape(points // 128, 128), 'img', [(i, (devices...  17.1 us
    unnamed x29, local copies, waits for them, and re-layouts  14.6 us
    unnamed x1, blocking collectives  13.3 us
    ppermute x2, waiting for transfers between devices, shards(): received.append(lax.ppermute(block, ('ptg', 'img'), pairs))  10.9 us
    all_to_all x1, waiting for transfers between devices, shards(): lax.all_to_all(back, 'img', split_axis=0, concat_axis=1, tiled=True)  9.53 us
    all_to_all x1, waiting for transfers between devices, shards(): col = lax.all_to_all(row, 'img', split_axis=1, concat_axis=0, tiled=True)  9.32 us
    all_to_all x1, starting transfers between devices, shards(): lax.all_to_all(by_class, 'ptg', split_axis=1, concat_axis=0, tiled=True)  6.79 us
  transfers between devices with their start and end apart: 9, of which 7 were waited for; matrix products, arithmetic and copies ran while one was open for 18% of the time, Pallas kernels for 0%

profile of v1, /device:TPU:14, one launch (start us, length us, event | category | flops | bytes accessed | tf_op | source)
XLA Modules:
  0.0 175.6 jit_solution(2476705663585144167)
XLA Ops:
  0.0 6.7 %all-to-all-start = ((bf16[16,128,512]{2,1,0:T(8,128)(2,1)}), bf16[16,128,512]{2,1,0:T(8,128)(2,1)S(1)}, u32[]{:S(2)}, u32[]{:S(2)}) async-start(bf16[16,128,512]{2,1,0:T(8,128)(2,1)} %bitcast.99), calls=%async_computation | async-start | bytes 4194304 | tf_op jit(solution)/shard_map/all_to_all | solution.py:71
  6.7 2.5 %copy.17 = s32[1,2048,128]{1,2,0:T(8,128)} copy(s32[1,2048,128]{2,1,0:T(8,128)} %param.9) | data formatting | bytes 2097152 | tf_op args[2]
  9.2 1.3 convert_bitcast_fusion.1
  10.5 1.3 collective-permute-start.1
  12.7 5.7 %collective-permute-start = (bf16[2048,64]{0,1:T(8,128)(2,1)}, bf16[2048,64]{0,1:T(8,128)(2,1)S(1)}, u32[]{:S(2)}, u32[]{:S(2)}) collective-permute-start(bf16[2048,64]{0,1:T(8,128)(2,1)} %get-tuple-element.19), channel_id=1, source_target_pairs={{0,15},{1,14},{2,13},{3,12},{4,11},{5,10},{6,9},{7,8},{8,7},{9,6},... | collective-permute-start | bytes 786440 | tf_op jit(solution)/shard_map/ppermute | solution.py:42
  19.1 17.1 %collective-permute-done.1 = bf16[16,128]{1,0:T(8,128)(2,1)S(1)} collective-permute-done((bf16[16,128]{1,0:T(8,128)(2,1)S(1)}, bf16[16,128]{1,0:T(8,128)(2,1)S(1)}, u32[]{:S(2)}, u32[]{:S(2)}) %collective-permute-start.1) | collective-permute-done | bytes 4128 | tf_op jit(solution)/shard_map/ppermute | solution.py:43
  37.0 2.1 %collective-permute-done = bf16[2048,64]{0,1:T(8,128)(2,1)S(1)} collective-permute-done((bf16[2048,64]{0,1:T(8,128)(2,1)}, bf16[2048,64]{0,1:T(8,128)(2,1)S(1)}, u32[]{:S(2)}, u32[]{:S(2)}) %collective-permute-start) | collective-permute-done | bytes 262176 | tf_op jit(solution)/shard_map/ppermute | solution.py:42
  39.8 1.8 %slice_select_fusion = bf16[2048,63]{0,1:T(8,128)(2,1)} fusion(bf16[2048,64]{0,1:T(8,128)(2,1)} %get-tuple-element.20, bf16[2048,64]{0,1:T(8,128)(2,1)S(1)} %collective-permute-done, pred[]{:T(512)S(6)} %lt.150), kind=kLoop, calls=%fused_computation.42 | loop fusion | flops 129024 | bytes 774145 | tf_op jit(solution)/shard_map/jit(_where)/select_n | solution.py:49
  41.5 6.1 %slice.114 = bf16[2048,63]{0,1:T(8,128)(2,1)S(1)} reverse(bf16[2048,63]{0,1:T(8,128)(2,1)} %slice_select_fusion), dimensions={1} | reverse | bytes 516096 | tf_op jit(solution)/shard_map/slice | solution.py:51
  48.5 8.4 %reverse.1 = bf16[2048,65]{0,1:T(8,128)(2,1)} reverse(bf16[2048,65]{0,1:T(8,128)(2,1)} %bitcast.101), dimensions={0} | reverse | bytes 532480
  56.9 1.1 slice.184
  58.0 1.0 fusion.24
  59.2 4.8 %fusion.4 = bf16[16,16,8,128]{3,2,1,0:T(8,128)(2,1)S(1)} fusion(bf16[2048,2048]{1,0:T(8,128)(2,1)} %constant.125, f32[1,128,2048]{2,1,0:T(8,128)S(1)} %copy-done, bf16[128,8192]{1,0:T(8,128)(2,1)S(1)} %bitcast.95, s32[]{:T(128)S(6)} %select_n.175), kind=kOutput, calls=%fused_computation.8 | convolution fusion | flops 1074790400 | bytes 10485764 | tf_op jit(solution)/shard_map/dot_general | solution.py:32
  64.0 0.9 copy.36
  64.9 6.5 %all-to-all-start.1 = ((bf16[128,16,128]{2,0,1:T(8,128)(2,1)}), bf16[128,16,128]{2,0,1:T(8,128)(2,1)S(1)}, u32[]{:S(2)}, u32[]{:S(2)}) async-start(bf16[128,16,128]{2,0,1:T(8,128)(2,1)} %bitcast.83), calls=%async_computation.1 | async-start | bytes 1048576 | tf_op jit(solution)/shard_map/all_to_all | solution.py:76
  71.7 9.3 %all-to-all-done.1 = bf16[128,16,128]{2,0,1:T(8,128)(2,1)S(1)} async-done(((bf16[128,16,128]{2,0,1:T(8,128)(2,1)}), bf16[128,16,128]{2,0,1:T(8,128)(2,1)S(1)}, u32[]{:S(2)}, u32[]{:S(2)}) %all-to-all-start.1) | async-done | bytes 524320 | tf_op jit(solution)/shard_map/all_to_all | solution.py:76
  81.3 6.3 %fusion.35 = f32[2048,128]{0,1:T(8,128)S(1)} fusion(bf16[2048,2048]{1,0:T(8,128)(2,1)} %constant.132, bf16[2048,128]{1,0:T(8,128)(2,1)S(1)} %bitcast.97), kind=kOutput, calls=%fused_computation.87 | convolution fusion | flops 1073741824 | bytes 9961472 | tf_op jit(solution)/shard_map/dot_general | solution.py:32
  87.8 6.5 %fusion = f32[2048,128]{0,1:T(8,128)S(1)} fusion(bf16[2048,2048]{1,0:T(8,128)(2,1)} %constant.129, bf16[2048,128]{1,0:T(8,128)(2,1)S(1)} %bitcast.98, f32[2048,64]{0,1:T(8,128)S(1)} %get-tuple-element.16, f32[2048,64]{0,1:T(8,128)S(1)} %get-tuple-element.15, f32[2048,63]{0,1:T(8,128)S(1)} %slice.148, f32[2048,1]{0,1:T(1,128)S(1)} %get-tuple-element.18, ...), kind=kOutput, calls=%fused_computation.3 | convolution fusion | flops 1076101120 | bytes 11543168 | tf_op jit(solution)/shard_map/dot_general | solution.py:32
  94.7 2.9 %fusion.19 = f32[128,2048]{1,0:T(8,128)S(1)} fusion(bf16[2048,2048]{1,0:T(8,128)(2,1)S(1)} %bitcast.91, f32[2048,128]{0,1:T(8,128)S(1)} %fusion), kind=kOutput, calls=%fused_computation.34 | convolution fusion | flops 1074003968 | bytes 10485760 | tf_op jit(solution)/shard_map/dot_general | solution.py:32
  97.7 3.0 %fusion.3 = bf16[16,16,8,128]{3,2,1,0:T(8,128)(2,1)S(1)} fusion(f32[128,2048]{1,0:T(8,128)S(1)} %fusion.19, bf16[2048,2048]{1,0:T(8,128)(2,1)S(1)} %bitcast.93, f32[2048,64]{0,1:T(8,128)S(1)} %get-tuple-element.14, f32[2048,64]{0,1:T(8,128)S(1)} %get-tuple-element.13, f32[2048,128]{0,1:T(8,128)S(1)} %fusion.35, f32[2048,63]{0,1:T(8,128)S(1)} %slice.148, ...), kind=kOutput, calls=%fused_computation.7 | convolution fusion | flops 1076625408 | bytes 12591744 | tf_op jit(solution)/shard_map/dot_general | solution.py:32
  100.6 0.9 copy.35
  101.6 6.3 %all-to-all-start.2 = ((bf16[16,128,128]{1,2,0:T(8,128)(2,1)}), bf16[16,128,128]{1,2,0:T(8,128)(2,1)S(1)}, u32[]{:S(2)}, u32[]{:S(2)}) async-start(bf16[16,128,128]{1,2,0:T(8,128)(2,1)} %bitcast.82), calls=%async_computation.2 | async-start | bytes 1048576 | tf_op jit(solution)/shard_map/all_to_all | solution.py:87
  107.9 9.5 %all-to-all-done.2 = bf16[16,128,128]{1,2,0:T(8,128)(2,1)S(1)} async-done(((bf16[16,128,128]{1,2,0:T(8,128)(2,1)}), bf16[16,128,128]{1,2,0:T(8,128)(2,1)S(1)}, u32[]{:S(2)}, u32[]{:S(2)}) %all-to-all-start.2) | async-done | bytes 524320 | tf_op jit(solution)/shard_map/all_to_all | solution.py:87
  117.4 6.3 %fusion.2 = bf16[128,2048]{1,0:T(8,128)(2,1)S(1)} fusion(bf16[128,2048]{0,1:T(8,128)(2,1)S(1)} %bitcast.96, bf16[2048,2048]{1,0:T(8,128)(2,1)} %constant.125, f32[1,128,2048]{2,1,0:T(8,128)S(1)} %copy-done), kind=kOutput, calls=%fused_computation.6 | convolution fusion | flops 1074266112 | bytes 10485760 | tf_op jit(solution)/shard_map/dot_general | solution.py:32
  124.5 1.0 copy.23
  125.5 6.8 %all-to-all-start.3 = ((bf16[128,8,256]{2,0,1:T(8,128)(2,1)}), bf16[128,8,256]{2,0,1:T(8,128)(2,1)S(1)}, u32[]{:S(2)}, u32[]{:S(2)}) async-start(bf16[128,8,256]{2,0,1:T(8,128)(2,1)} %copy.23), calls=%async_computation.3 | async-start | bytes 1048576 | tf_op jit(solution)/shard_map/all_to_all | solution.py:93
  133.7 13.3 %all-reduce = s32[8]{0:T(128)S(1)} all-reduce(s32[8]{0:T(128)S(1)} %dynamic-update-slice), channel_id=1, replica_groups=mesh['ptg'=8,'img'=16] {'ptg'}, use_global_device_ids=true, to_apply=%add | all-reduce | flops 8 | bytes 64
  152.7 5.1 %compare_and_fusion.7 = (pred[2,2,256]{2,1,0:T(4,128)(4,1)S(1)}, pred[2,2,256]{2,1,0:T(4,128)(4,1)S(1)}, pred[2,2,256]{2,1,0:T(4,128)(4,1)S(1)}, pred[2,2,256]{2...) fusion(s32[]{:T(128)S(6)} %add.168, s32[]{:T(128)} %bitcast.1, ...), kind=kLoop, calls=%fused_computation.71 | loop fusion | flops 25600 | bytes 8272 | tf_op jit(solution)/shard_map/and | solution.py:99
  158.5 1.3 collective-permute-done.2
  159.9 3.8 %collective-permute-start.4 = (bf16[256,256]{1,0:T(8,128)(2,1)S(1)}, bf16[256,256]{1,0:T(8,128)(2,1)S(1)}, u32[]{:S(2)}, u32[]{:S(2)}) collective-permute-start(bf16[256,256]{1,0:T(8,128)(2,1)S(1)} %get-tuple-element.22), channel_id=1, source_target_pairs={{0,0},{1,8},{2,16},{3,24},{4,32},{5,40},{6,48},{7,56},{8,64},{9,72... | collective-permute-start | bytes 393224 | tf_op jit(solution)/shard_map/ppermute | solution.py:120
  163.8 8.0 %collective-permute-done.4 = bf16[256,256]{1,0:T(8,128)(2,1)S(1)} collective-permute-done((bf16[256,256]{1,0:T(8,128)(2,1)S(1)}, bf16[256,256]{1,0:T(8,128)(2,1)S(1)}, u32[]{:S(2)}, u32[]{:S(2)}) %collective-permute-start.4) | collective-permute-done | bytes 131104 | tf_op jit(solution)/shard_map/ppermute | solution.py:120
  171.8 2.9 %collective-permute-done.3 = bf16[256,256]{1,0:T(8,128)(2,1)S(1)} collective-permute-done((bf16[256,256]{1,0:T(8,128)(2,1)S(1)}, bf16[256,256]{1,0:T(8,128)(2,1)S(1)}, u32[]{:S(2)}, u32[]{:S(2)}) %collective-permute-start.3) | collective-permute-done | bytes 131104 | tf_op jit(solution)/shard_map/ppermute | solution.py:120
  (57 shorter events, 9.2 us)
Async XLA Ops:
  0.0 59.1 %copy-start = (f32[1,128,2048]{2,1,0:T(8,128)S(1)}, f32[1,128,2048]{2,1,0:T(8,128)}, u32[]{:S(2)}) copy-start(f32[1,128,2048]{2,1,0:T(8,128)} %param.8) | copy-start | bytes 3145732
  0.0 58.9 %all-to-all-start = ((bf16[16,128,512]{2,1,0:T(8,128)(2,1)}), bf16[16,128,512]{2,1,0:T(8,128)(2,1)S(1)}, u32[]{:S(2)}, u32[]{:S(2)}) async-start(bf16[16,128,512]{2,1,0:T(8,128)(2,1)} %bitcast.99), calls=%async_computation | async-start | bytes 4194304 | tf_op jit(solution)/shard_map/all_to_all | solution.py:71
  10.5 1.3 copy-start.1
  10.5 25.6 %collective-permute-start.1 = (bf16[16,128]{1,0:T(8,128)(2,1)S(1)}, bf16[16,128]{1,0:T(8,128)(2,1)S(1)}, u32[]{:S(2)}, u32[]{:S(2)}) collective-permute-start(bf16[16,128]{1,0:T(8,128)(2,1)S(1)} %bitcast.107), channel_id=1, source_target_pairs={{8,0},{9,7},{10,6},{11,5},{12,4},{13,3},{14,2},{15,1},{24,16},{25,... | collective-permute-start | bytes 12296 | tf_op jit(solution)/shard_map/ppermute | solution.py:43
  12.7 26.4 %collective-permute-start = (bf16[2048,64]{0,1:T(8,128)(2,1)}, bf16[2048,64]{0,1:T(8,128)(2,1)S(1)}, u32[]{:S(2)}, u32[]{:S(2)}) collective-permute-start(bf16[2048,64]{0,1:T(8,128)(2,1)} %get-tuple-element.19), channel_id=1, source_target_pairs={{0,15},{1,14},{2,13},{3,12},{4,11},{5,10},{6,9},{7,8},{8,7},{9,6},... | collective-permute-start | bytes 786440 | tf_op jit(solution)/shard_map/ppermute | solution.py:42
  39.0 0.7 copy-start.4
  59.2 12.3 %copy-start.2 = (bf16[2048,128]{0,1:T(8,128)(2,1)S(1)}, bf16[2048,128]{0,1:T(8,128)(2,1)}, u32[]{:S(2)}) copy-start(bf16[2048,128]{0,1:T(8,128)(2,1)} %copy-done.1) | copy-start | bytes 1572868
  59.2 12.3 %copy-start.3 = (f32[2048,65]{0,1:T(8,128)S(1)}, f32[2048,65]{0,1:T(8,128)}, u32[]{:S(2)}) copy-start(f32[2048,65]{0,1:T(8,128)} %fusion.24) | copy-start | bytes 1597444
  59.2 12.3 %copy-start.5 = (bf16[2048,64]{0,1:T(8,128)(2,1)S(1)}, bf16[2048,64]{0,1:T(8,128)(2,1)}, u32[]{:S(2)}) copy-start(bf16[2048,64]{0,1:T(8,128)(2,1)} %copy-done.4) | copy-start | bytes 786436
  64.9 16.1 %all-to-all-start.1 = ((bf16[128,16,128]{2,0,1:T(8,128)(2,1)}), bf16[128,16,128]{2,0,1:T(8,128)(2,1)S(1)}, u32[]{:S(2)}, u32[]{:S(2)}) async-start(bf16[128,16,128]{2,0,1:T(8,128)(2,1)} %bitcast.83), calls=%async_computation.1 | async-start | bytes 1048576 | tf_op jit(solution)/shard_map/all_to_all | solution.py:76
  87.6 6.7 %slice-start = ((s8[8388608]{0:T(1024)(128)(4,1)}), s8[4194304]{0:T(1024)(128)(4,1)S(1)}, s32[]{:S(2)}) async-start(s8[8388608]{0:T(1024)(128)(4,1)} %bitcast.90), calls=%async_computation.4 | async-start | bytes 8388608
  87.6 10.0 %slice-start.2 = ((s8[8388608]{0:T(1024)(128)(4,1)}), s8[4194304]{0:T(1024)(128)(4,1)S(1)}, s32[]{:S(2)}) async-start(s8[8388608]{0:T(1024)(128)(4,1)} %bitcast.92), calls=%async_computation.6 | async-start | bytes 8388608
  87.8 7.0 %slice-start.1 = ((s8[8388608]{0:T(1024)(128)(4,1)}), s8[4194304]{0:T(1024)(128)(4,1)S(1)}, s32[]{:S(2)}) async-start(s8[8388608]{0:T(1024)(128)(4,1)} %bitcast.90), calls=%async_computation.5 | async-start | bytes 8388608
  87.8 9.9 %slice-start.3 = ((s8[8388608]{0:T(1024)(128)(4,1)}), s8[4194304]{0:T(1024)(128)(4,1)S(1)}, s32[]{:S(2)}) async-start(s8[8388608]{0:T(1024)(128)(4,1)} %bitcast.92), calls=%async_computation.7 | async-start | bytes 8388608
  100.6 31.7 %copy-start.6 = (u32[128]{0:T(128)S(1)}, u32[128]{0:T(128)}, u32[]{:S(2)}) copy-start(u32[128]{0:T(128)} %constant.135) | copy-start | bytes 1540
  101.6 15.9 %all-to-all-start.2 = ((bf16[16,128,128]{1,2,0:T(8,128)(2,1)}), bf16[16,128,128]{1,2,0:T(8,128)(2,1)S(1)}, u32[]{:S(2)}, u32[]{:S(2)}) async-start(bf16[16,128,128]{1,2,0:T(8,128)(2,1)} %bitcast.82), calls=%async_computation.2 | async-start | bytes 1048576 | tf_op jit(solution)/shard_map/all_to_all | solution.py:87
  125.5 32.3 %all-to-all-start.3 = ((bf16[128,8,256]{2,0,1:T(8,128)(2,1)}), bf16[128,8,256]{2,0,1:T(8,128)(2,1)S(1)}, u32[]{:S(2)}, u32[]{:S(2)}) async-start(bf16[128,8,256]{2,0,1:T(8,128)(2,1)} %copy.23), calls=%async_computation.3 | async-start | bytes 1048576 | tf_op jit(solution)/shard_map/all_to_all | solution.py:93
  158.4 1.4 collective-permute-start.2
  159.9 11.9 %collective-permute-start.4 = (bf16[256,256]{1,0:T(8,128)(2,1)S(1)}, bf16[256,256]{1,0:T(8,128)(2,1)S(1)}, u32[]{:S(2)}, u32[]{:S(2)}) collective-permute-start(bf16[256,256]{1,0:T(8,128)(2,1)S(1)} %get-tuple-element.22), channel_id=1, source_target_pairs={{0,0},{1,8},{2,16},{3,24},{4,32},{5,40},{6,48},{7,56},{8,64},{9,72... | collective-permute-start | bytes 393224 | tf_op jit(solution)/shard_map/ppermute | solution.py:120
  163.7 11.0 %collective-permute-start.3 = (bf16[256,256]{1,0:T(8,128)(2,1)S(1)}, bf16[256,256]{1,0:T(8,128)(2,1)S(1)}, u32[]{:S(2)}, u32[]{:S(2)}) collective-permute-start(bf16[256,256]{1,0:T(8,128)(2,1)S(1)} %get-tuple-element.21), channel_id=1, source_target_pairs={{0,4},{1,12},{2,20},{3,28},{4,36},{5,44},{6,52},{7,60},{8,68},{9,7... | collective-permute-start | bytes 393224 | tf_op jit(solution)/shard_map/ppermute | solution.py:120

commit v2 on v0

v2 whole, which is shorter than its diff:
```python
import functools

import numpy as np

import jax
import jax.numpy as jnp
from jax import lax
from jax.experimental import pallas as pl
from jax.experimental.pallas import tpu as pltpu
from jax.sharding import PartitionSpec as P

F32, BF16 = jnp.float32, jnp.bfloat16
NT = (((1,), (1,)), ((), ()))
NN = (((1,), (0,)), ((), ()))
VMEM = pl.BlockSpec(memory_space=pltpu.VMEM)
SMEM = pl.BlockSpec(memory_space=pltpu.SMEM)


def dot(a, b, dims=NN):
    return lax.dot_general(a, b, dims, preferred_element_type=F32)


def row_tables(points, devices):
    half, lanes = points // 2, points // devices
    index = np.arange(half)
    turn = 2.0 * np.pi / points * np.arange(points)
    cos_of, sin_of = np.cos(turn), -np.sin(turn)
    made = []
    for odd in (0, 1):
        blocks = np.arange(devices // 2)
        if odd:
            blocks = blocks[::-1]
        freq = lanes * blocks[:, None] + 2 * np.arange(lanes // 2)[None, :] + odd
        phase = index[:, None, None] * freq[None] % points
        imag = sin_of[phase]
        if not odd:
            imag[:, 0, 0] = cos_of[index * half % points]
        made.append(np.concatenate([cos_of[phase], imag], axis=2).reshape(half, half))
    return np.stack(made)


def column_tables(points):
    half = points // 2
    index = np.arange(half)
    turn = 2.0 * np.pi / points * np.arange(points)
    cos_of, sin_of = np.cos(turn), -np.sin(turn)
    even = index[:, None] * (2 * index[None, :]) % points
    odd = index[:, None] * (2 * index[None, :] + 1) % points
    return [
        cos_of[even].T,
        sin_of[even].T,
        cos_of[odd].T,
        sin_of[odd].T,
        cos_of[odd],
        sin_of[odd],
    ]


def bf16(table):
    return jnp.asarray(np.asarray(table, np.float32).astype(jnp.bfloat16))


def lane_choice(lanes):
    half = lanes // 2
    k = np.arange(half)
    chosen = np.zeros((2, lanes, 2, 2, half), np.float32)
    for copy in (0, 1):
        chosen[0, 2 * k, 0, copy, k] = 1
        chosen[0, 2 * k + 1, 1, copy, k] = 1
        chosen[1, lanes - 1 - 2 * k, 0, copy, k] = 1
        chosen[1, lanes - 2 * k[1:], 1, copy, k[1:]] = 1
    return chosen.reshape(2, lanes, 4 * half)


def row_choice():
    k = np.arange(128)
    direct, negated = np.zeros((256, 256), np.float32), np.zeros((256, 256), np.float32)
    direct[k, 2 * k] = 1
    direct[128 + k, 2 * k + 1] = 1
    negated[k[1:], 256 - 2 * k[1:]] = 1
    negated[128 + k, 255 - 2 * k] = 1
    return direct, negated


def choose_kernel(counts_ref, choice_ref, first_ref, own_ref, send_ref, edge_ref):
    points = counts_ref.shape[0]
    lane = lax.broadcasted_iota(jnp.int32, (256, 128), 1)
    for b in range(points // 512):
        low = counts_ref[pl.ds(256 * b, 256)].astype(F32).astype(BF16)
        high = counts_ref[pl.ds(256 * b + points // 2, 256)].astype(F32).astype(BF16)
        got_low, got_high = dot(low, choice_ref[...]), dot(high, choice_ref[...])
        own_ref[pl.ds(256 * b, 256)] = got_low[:, :128].astype(BF16)
        own_ref[pl.ds(256 * b + points // 2, 256)] = got_high[:, :128].astype(BF16)
        send_ref[pl.ds(256 * b, 256)] = jnp.where(
            lane < 64, got_low[:, 128:], got_high[:, 128:]
        ).astype(BF16)
    edges = []
    for b in range(points // 128):
        block = counts_ref[pl.ds(128 * b, 128)].astype(F32).astype(BF16)
        edges.append(dot(first_ref[...], block, NT)[:1])
    edge_ref[...] = jnp.concatenate(edges, 0).astype(BF16)


def weight_kernel(me_ref, own_ref, got_ref, edge_ref, eye_ref, direct_ref, negated_ref, out_ref, plus, minus):
    points = own_ref.shape[0]
    me = me_ref[0]
    low, zero = me < 8, me == 0
    edge = dot(eye_ref[...], edge_ref[...], NT)
    lane = lax.broadcasted_iota(jnp.int32, (128, 128), 1)
    for b in range(points // 128):
        rows = pl.ds(128 * b, 128)
        own = own_ref[rows].astype(F32)
        packed = got_ref[pl.ds(128 * b % (points // 2), 128)].astype(F32)
        moved = pltpu.roll(packed, 64, 1)
        in_left = 128 * b < points // 2
        got = jnp.where((lane < 64) == in_left, packed, moved)
        column = jnp.broadcast_to(edge[:, b : b + 1], (128, 128))
        straight = jnp.where(low, own, got)
        mirrored = jnp.where(low, got, own)
        first = jnp.where(zero, jnp.where(lane == 0, own, column), column)
        mirrored = jnp.where(low & (lane % 64 == 0), first, mirrored)
        straight = jnp.where(zero & (lane == 64), column, straight)
        plus[rows] = straight.astype(BF16)
        minus[rows] = mirrored
    blocks = points // 256
    row = lax.broadcasted_iota(jnp.int32, (256, 128), 0)
    wide = lax.broadcasted_iota(jnp.int32, (256, 128), 1)
    scale = jnp.where(zero & (wide % 64 == 0), 0.5, 1.0)
    for b in range(blocks):
        taken = dot(direct_ref[...], plus[pl.ds(256 * b, 256)])
        taken += dot(negated_ref[...], minus[pl.ds(256 * (blocks - 1 - b), 256)].astype(BF16))
        wrapped = minus[pl.ds(256 * ((blocks - b) % blocks), 1)]
        taken = scale * (taken + jnp.where(row == 0, wrapped, 0.0))
        out_ref[pl.ds(128 * b, 128)] = taken[:128].astype(BF16)
        out_ref[pl.ds(points // 2 + 128 * b, 128)] = taken[128:].astype(BF16)


def row_kernel(start_ref, tiles_ref, beam_ref, table_ref, out_ref):
    tiles, rows, wide = tiles_ref.shape
    points = beam_ref.shape[1]
    start = start_ref[0]
    per_lap = points // wide
    lane = lax.broadcasted_iota(jnp.int32, (rows, wide), 1)
    beamed = []
    for block in range(per_lap):
        window = jnp.zeros((rows, wide), F32)
        for lap in range(tiles // per_lap):
            column = lane + (lap * points + block * wide)
            inside = (column >= start) & (column < start + points)
            window = jnp.where(inside, tiles_ref[lap * per_lap + block].astype(F32), window)
        beamed.append(window * beam_ref[:, pl.ds(block * wide, wide)])
    left = jnp.concatenate(beamed[: per_lap // 2], 1)
    right = jnp.concatenate(beamed[per_lap // 2 :], 1)
    blocks = out_ref.shape[0] // 2
    for odd in (0, 1):
        folded = (left - right if odd else left + right).astype(BF16)
        for part in range(blocks // 2):
            spectrum = dot(folded, table_ref[odd, :, pl.ds(256 * part, 256)]).astype(BF16)
            out_ref[odd * blocks + 2 * part] = spectrum[:, :128]
            out_ref[odd * blocks + 2 * part + 1] = spectrum[:, 128:]


def column_kernel(me_ref, x_ref, weight_ref, c0, s0, c1, s1, c1t, s1t, out_ref, upper, lower):
    points = x_ref.shape[0]
    half = points // 2
    scale = 1.0 / float(points * points)
    lane = lax.broadcasted_iota(jnp.int32, (256, 128), 1)
    sign = jnp.where(lane < 64, -1.0, 1.0)
    packed = (me_ref[0] == 0) & (lane % 64 == 0)
    first, second = x_ref[:half].astype(F32), x_ref[half:].astype(F32)
    for odd in (0, 1):
        folded = (first - second if odd else first + second).astype(BF16)
        for m in range(half // 256):
            rows = pl.ds(256 * m, 256)
            by_cos = dot((c1 if odd else c0)[rows], folded)
            by_sin = dot((s1 if odd else s0)[rows], folded)
            weight = weight_ref[pl.ds(odd * half + 256 * m, 256)].astype(F32) * scale
            up = weight * (by_cos + jnp.where(packed, 0.0, sign * pltpu.roll(by_sin, 64, 1)))
            down = jnp.where(packed, weight * by_sin, -sign * pltpu.roll(up, 64, 1))
            upper[odd, rows] = up.astype(BF16)
            lower[odd, rows] = down.astype(BF16)
    for m in range(half // 256):
        rows = pl.ds(256 * m, 256)
        even = dot(c0[rows], upper[0]) + dot(s0[rows], lower[0])
        odd = dot(c1t[rows], upper[1]) + dot(s1t[rows], lower[1])
        out_ref[rows] = (even + odd).astype(BF16)
        out_ref[pl.ds(half + 256 * m, 256)] = (even - odd).astype(BF16)


def pixel_kernel(x_ref, beam_ref, table_ref, out_ref):
    blocks, rows, _ = x_ref.shape
    half = beam_ref.shape[1] // 2
    share = out_ref.shape[2]
    even = jnp.concatenate([x_ref[b] for b in range(blocks // 2)], 1)
    odd = jnp.concatenate([x_ref[b] for b in range(blocks // 2, blocks)], 1)
    for part in range(half // share):
        lanes = pl.ds(share * part, share)
        by_even = dot(even, table_ref[0, lanes, :], NT)
        by_odd = dot(odd, table_ref[1, lanes, :], NT)
        out_ref[part] = (beam_ref[:, lanes] * (by_even + by_odd)).astype(BF16)
        late = pl.ds(half + share * part, share)
        out_ref[part + half // share] = (beam_ref[:, late] * (by_even - by_odd)).astype(BF16)


def sum_kernel(points, me_ref, starts_ref, terms_ref, mine_ref, theirs_ref):
    pointings, rows, share = terms_ref.shape
    ptg, core = me_ref[0], me_ref[1]
    lane = lax.broadcasted_iota(jnp.int32, (rows, share), 1)
    for ref, side in ((mine_ref, core), (theirs_ref, 1 - core)):
        for turn in range(2):
            lap = 2 * side + jnp.where(ptg % 2 == turn, 0, 1)
            column = lane + (lap * points + ptg * share)
            total = jnp.zeros((rows, share), F32)
            for p in range(pointings):
                inside = (column >= starts_ref[p]) & (column < starts_ref[p] + points)
                total += jnp.where(inside, terms_ref[p].astype(F32), 0.0)
            ref[turn] = total.astype(BF16)


def call(kernel, outs, specs, *args, scratch=(), flops=0, moved=4 << 20, limit=48):
    return pl.pallas_call(
        kernel,
        out_shape=outs,
        in_specs=specs,
        out_specs=jax.tree.map(lambda _: VMEM, outs),
        scratch_shapes=list(scratch),
        compiler_params=pltpu.CompilerParams(vmem_limit_bytes=limit << 20),
        cost_estimate=pl.CostEstimate(flops=flops, bytes_accessed=moved, transcendentals=0),
    )(*args)


def shape(*dims, dtype=BF16):
    return jax.ShapeDtypeStruct(dims, dtype)


def shards(image, beam, counts, offsets):
    points = counts.shape[1]
    devices = lax.axis_size("img")
    pointings = lax.axis_size("ptg")
    rows = points // devices
    tile = image.shape[1]
    me = lax.axis_index("img").astype(jnp.int32)
    ptg = lax.axis_index("ptg").astype(jnp.int32)
    start = offsets[0]
    place = me.reshape(1)

    tiles = lax.all_to_all(image, "img", split_axis=0, concat_axis=0, tiled=True)
    tiles = tiles.reshape(devices, rows, tile)

    starts = jnp.where(jnp.arange(pointings) == ptg, start, 0)
    for bit in (1, 2, 4):
        starts = starts + lax.ppermute(starts, "ptg", [(p, p ^ bit) for p in range(pointings)])

    choice = bf16(lane_choice(counts.shape[2]))
    choice = jnp.where(me < devices // 2, choice[0], choice[1])
    first_lane = np.zeros((16, 128), np.float32)
    first_lane[0, 0] = 1
    own, send, edge = call(
        choose_kernel,
        (shape(points, 128), shape(points // 2, 128), shape(points // 128, 128)),
        [VMEM] * 3,
        counts[0],
        choice,
        bf16(first_lane),
        flops=points * 128 * 512,
    )
    got = lax.ppermute(send, "img", [(i, devices - 1 - i) for i in range(devices)])
    edge = lax.ppermute(
        edge,
        "img",
        [(i, (devices - i) % (devices // 2)) for i in range(devices // 2, devices)],
    )
    direct, negated = row_choice()
    weight = call(
        weight_kernel,
        shape(points, 128),
        [SMEM] + [VMEM] * 6,
        place,
        own,
        got,
        edge,
        bf16(np.eye(128)),
        bf16(direct),
        bf16(negated),
        scratch=[pltpu.VMEM((points, 128), BF16), pltpu.VMEM((points, 128), F32)],
        flops=points * 128 * 1024,
    )

    twice = jnp.concatenate([beam[0], beam[0]], 1)
    turned = lax.dynamic_slice_in_dim(twice, (points - start % points) % points, points, 1)
    row_table = bf16(row_tables(points, devices))
    spectrum = call(
        row_kernel,
        shape(devices, rows, 128),
        [SMEM] + [VMEM] * 3,
        start.reshape(1),
        tiles,
        turned,
        row_table,
        flops=rows * points * points,
    )
    col = lax.all_to_all(spectrum, "img", split_axis=0, concat_axis=0, tiled=True)
    back = call(
        column_kernel,
        shape(points, 128),
        [SMEM] + [VMEM] * 8,
        place,
        col.reshape(points, 128),
        weight,
        *[bf16(t) for t in column_tables(points)],
        scratch=[pltpu.VMEM((2, points // 2, 128), BF16)] * 2,
        flops=8 * points * points * 128 // 2,
        moved=16 << 20,
    )
    lines = lax.all_to_all(
        back.reshape(devices, rows, 128), "img", split_axis=0, concat_axis=0, tiled=True
    )
    share = points // pointings
    contribution = call(
        pixel_kernel,
        shape(pointings, rows, share),
        [VMEM] * 3,
        lines,
        turned,
        row_table,
        flops=rows * points * points,
    )
    terms = lax.all_to_all(contribution, "ptg", split_axis=0, concat_axis=0, tiled=True)
    mine, theirs = call(
        functools.partial(sum_kernel, points),
        (shape(2, rows, share), shape(2, rows, share)),
        [SMEM, SMEM, VMEM],
        jnp.stack([ptg, me % 2]),
        starts,
        terms,
        moved=1 << 20,
    )
    other = lax.ppermute(theirs, "img", [(i, i ^ 1) for i in range(devices)])
    per_lap = points // tile
    halves = tile // share
    received = []
    for turn in range(2):
        pairs = []
        for q in range(pointings):
            for i in range(devices):
                lap = 2 * (i % 2) + (turn ^ (q % 2))
                pairs.append((q * devices + i, (i // 2) * devices + per_lap * lap + q // halves))
        block = jnp.concatenate([mine[turn], other[turn]], 0)
        received.append(lax.ppermute(block, ("ptg", "img"), pairs))
    lap = me // per_lap
    out = jnp.where(
        lap % 2 == 1,
        jnp.concatenate([received[1], received[0]], 1),
        jnp.concatenate([received[0], received[1]], 1),
    ).astype(F32)
    flipped = jnp.concatenate([out[rows:], out[:rows]], 0)
    return jnp.where(lap >= 2, flipped, out)


def solution(mesh):
    return jax.shard_map(
        shards,
        mesh=mesh,
        in_specs=(P(None, "img"), P("ptg", "img", None), P("ptg", None, "img"), P("ptg")),
        out_specs=P("ptg", "img"),
        check_vma=False,
    )
```

time: 1030 us -> 134 us (0.13)
  matrix products: 816 us -> 0 us
  waiting for transfers between devices: 108 us -> 60.6 us
  blocking collectives: 33.5 us -> 0 us
  Pallas kernels: 0 us -> 19.5 us
  between operations: 14.4 us -> 0.92 us
    dot_general x12 -> x0, matrix products: 816 us -> none  [the longest x1 71.3 us: shards(): jnp.dot(sine_table, col_real, preferred_element_type=jnp.float32)]
    psum x1 -> x0, waiting for transfers between devices: 82.5 us -> none  [shards(): lax.psum(tile_terms.astype(jnp.bfloat16), 'ptg').astype(jnp.float32)]
    all_to_all x1 -> x0, blocking collectives: 33.5 us -> none  [shards(): lax.all_to_all(placed, 'img', split_axis=1, concat_axis=0, tiled=True)]
    ppermute x0 -> x8, waiting for transfers between devices: none -> 29.4 us  [the longest x3 9.67 us: shards(): lax.ppermute(starts, 'ptg', [(p, p ^ bit) for p in range(pointings)])]
    pallas_call x0 -> x6, Pallas kernels: none -> 19.5 us  [call(): pl.pallas_call(kernel, out_shape=outs, in_specs=specs, out_specs=jax.tree...]
    ppermute x0 -> x8, starting transfers between devices: none -> 16.8 us  [the longest x2 7.16 us: shards(): received.append(lax.ppermute(block, ('ptg', 'img'), pairs))]
    all_to_all x5 -> x4, starting transfers between devices: 36.7 us -> 27.6 us  [the longest x1 8 us: shards(): lax.all_to_all(spectrum, 'img', split_axis=0, concat_axis=0, tiled=True)]
    all_to_all x5 -> x4, waiting for transfers between devices: 25.6 us -> 31.2 us  [the longest x1 23.7 us: shards(): lax.all_to_all(image, 'img', split_axis=0, concat_axis=0, tiled=True)]
  transfers between devices with their start and end apart: 6 -> 12, of which waited for: 2 -> 9; matrix products, arithmetic and copies ran while one was open for 26% -> 1% of each run, Pallas kernels for 0% -> 5%
where the time goes in v2:
time: 134 us
  waiting for transfers between devices  60.6 us (45%)
  starting transfers between devices  44.4 us (33%)
  Pallas kernels  19.5 us (15%)
  local copies, waits for them, and re-layouts  5.27 us (4%)
  other arithmetic  2.95 us (2%)
    all_to_all x1, waiting for transfers between devices, shards(): lax.all_to_all(image, 'img', split_axis=0, concat_axis=0, tiled=True)  23.7 us
    pallas_call x6, Pallas kernels, call(): pl.pallas_call(kernel, out_shape=outs, in_specs=specs, out_specs=jax.tree...  19.5 us
    ppermute x3, waiting for transfers between devices, shards(): lax.ppermute(starts, 'ptg', [(p, p ^ bit) for p in range(pointings)])  9.67 us
    ppermute x2, waiting for transfers between devices, shards(): received.append(lax.ppermute(block, ('ptg', 'img'), pairs))  9.13 us
    ppermute x1, waiting for transfers between devices, shards(): lax.ppermute(edge, 'img', [(i, (devices - i) % (devices // 2)) for i in r...  8.26 us
    all_to_all x1, starting transfers between devices, shards(): lax.all_to_all(spectrum, 'img', split_axis=0, concat_axis=0, tiled=True)  8 us
    all_to_all x1, waiting for transfers between devices, shards(): lax.all_to_all(back.reshape(devices, rows, 128), 'img', split_axis=0, con...  7.53 us
    ppermute x2, starting transfers between devices, shards(): received.append(lax.ppermute(block, ('ptg', 'img'), pairs))  7.16 us
  transfers between devices with their start and end apart: 12, of which 9 were waited for; matrix products, arithmetic and copies ran while one was open for 1% of the time, Pallas kernels for 5%

profile of v2, /device:TPU:14, one launch (start us, length us, event | category | flops | bytes accessed | tf_op | source)
XLA Modules:
  0.0 133.6 jit_solution(8890972603138207342)
XLA Ops:
  0.0 6.5 %all-to-all-start = ((bf16[16,128,512]{2,1,0:T(8,128)(2,1)}), bf16[16,128,512]{2,1,0:T(8,128)(2,1)S(1)}, u32[]{:S(2)}, u32[]{:S(2)}) async-start(bf16[16,128,512]{2,1,0:T(8,128)(2,1)} %bitcast.27), calls=%async_computation | async-start | bytes 4194304 | tf_op jit(solution)/shard_map/all_to_all | solution.py:247
  7.2 1.8 %fusion.beam_ref = f32[128,2048]{1,0:T(8,128)S(1)} fusion(s32[]{:T(128)S(6)} %select_n.64, f32[128,2048]{1,0:T(8,128)} %bitcast.28), kind=kLoop, calls=%fused_computation.2 | loop fusion | flops 262144 | bytes 2097156 | tf_op jit(solution)/shard_map/concatenate | solution.py:289
  9.1 23.7 %all-to-all-done.tiles_ref = bf16[16,128,512]{2,1,0:T(8,128)(2,1)S(1)} async-done(((bf16[16,128,512]{2,1,0:T(8,128)(2,1)}), bf16[16,128,512]{2,1,0:T(8,128)(2,1)S(1)}, u32[]{:S(2)}, u32[]{:S(2)}) %all-to-all-start) | async-done | bytes 2097184 | tf_op jit(solution)/shard_map/all_to_all | solution.py:247
  32.7 3.2 %shard_map.154 = bf16[16,128,128]{2,1,0:T(8,128)(2,1)S(1)} custom-call(s32[1]{0:T(128)} %copy.17.start_ref, bf16[16,128,512]{2,1,0:T(8,128)(2,1)S(1)} %all-to-all-done.tiles_ref, f32[128,2048]{1,0:T(8,128)S(1)} %fusion.beam_ref, bf16[2,1024,1024]{2,1,0:T(8,128)(2,1)} %constant.88.clone.table_ref), custom_call_target="tpu_custom_call" | custom-call | flops 536870912 | bytes 4194304 | tf_op jit(solution)/shard_map/pallas_call | solution.py:221
  35.9 0.8 copy-done
  36.7 8.0 %all-to-all-start.1 = ((bf16[16,128,128]{2,1,0:T(8,128)(2,1)}), bf16[16,128,128]{2,1,0:T(8,128)(2,1)S(1)}, u32[]{:S(2)}, u32[]{:S(2)}) async-start(bf16[16,128,128]{2,1,0:T(8,128)(2,1)} %copy-done), calls=%async_computation.1 | async-start | bytes 1048576 | tf_op jit(solution)/shard_map/all_to_all | solution.py:302
  44.8 1.2 copy-done.3
  46.0 0.6 shard_map.155
  46.6 2.7 %collective-permute-start.3 = (bf16[1024,128]{1,0:T(8,128)(2,1)S(1)}, bf16[1024,128]{1,0:T(8,128)(2,1)S(1)}, u32[]{:S(2)}, u32[]{:S(2)}) collective-permute-start(bf16[1024,128]{1,0:T(8,128)(2,1)S(1)} %get-tuple-element.11), channel_id=1, source_target_pairs={{0,15},{1,14},{2,13},{3,12},{4,11},{5,10},{6,9},{7,8},{8,7},{9,6},... | collective-permute-start | bytes 786440 | tf_op jit(solution)/shard_map/ppermute | solution.py:267
  49.4 1.3 collective-permute-start.4
  50.7 8.3 %collective-permute-done.4.edge_ref = bf16[16,128]{1,0:T(8,128)(2,1)S(1)} collective-permute-done((bf16[16,128]{1,0:T(8,128)(2,1)S(1)}, bf16[16,128]{1,0:T(8,128)(2,1)S(1)}, u32[]{:S(2)}, u32[]{:S(2)}) %collective-permute-start.4) | collective-permute-done | bytes 4128 | tf_op jit(solution)/shard_map/ppermute | solution.py:268
  58.9 1.1 collective-permute-done.3.got_ref
  60.0 1.4 %shard_map.156.weight_ref = bf16[2048,128]{1,0:T(8,128)(2,1)S(1)} custom-call(s32[1]{0:T(128)} %bitcast.3.me_ref, bf16[2048,128]{1,0:T(8,128)(2,1)S(1)} %get-tuple-element.10.own_ref, bf16[1024,128]{1,0:T(8,128)(2,1)S(1)} %collective-permute-done.3.got_ref, bf16[16,128]{1,0:T(8,128)(2,1)S(1)} %collective-permute-done.4.edge_ref, ...), custom_call_target="tpu_custom_call" | custom-call | flops 268435456 | bytes 4194304 | tf_op jit(solution)/shard_map/pallas_call | solution.py:221
  61.4 1.6 %copy-done.1 = bf16[1024,1024]{1,0:T(8,128)(2,1)S(1)} copy-done((bf16[1024,1024]{1,0:T(8,128)(2,1)S(1)}, bf16[1024,1024]{1,0:T(8,128)(2,1)}, u32[]{:S(2)}) %copy-start.1) | copy-done | bytes 2097176
  63.0 1.6 %copy-done.2 = bf16[1024,1024]{1,0:T(8,128)(2,1)S(1)} copy-done((bf16[1024,1024]{1,0:T(8,128)(2,1)S(1)}, bf16[1024,1024]{1,0:T(8,128)(2,1)}, u32[]{:S(2)}) %copy-start.2) | copy-done | bytes 2097176
  64.6 8.8 %shard_map.157 = bf16[2048,128]{1,0:T(8,128)(2,1)} custom-call(s32[1]{0:T(128)} %bitcast.3.me_ref, bf16[2048,128]{1,0:T(8,128)(2,1)S(1)} %bitcast.25, bf16[2048,128]{1,0:T(8,128)(2,1)S(1)} %shard_map.156.weight_ref, bf16[1024,1024]{1,0:T(8,128)(2,1)S(1)} %copy-done.1, bf16[1024,1024]{1,0:T(8,128)(2,1)S(1)} %copy-done.2, ...), custom_call_target="tpu_custom_call" | custom-call | flops 2147483648 | bytes 16777216 | tf_op jit(solution)/shard_map/pallas_call | solution.py:221
  73.4 6.3 %all-to-all-start.2 = ((bf16[16,128,128]{2,1,0:T(8,128)(2,1)}), bf16[16,128,128]{2,1,0:T(8,128)(2,1)S(1)}, u32[]{:S(2)}, u32[]{:S(2)}) async-start(bf16[16,128,128]{2,1,0:T(8,128)(2,1)} %bitcast.9), calls=%async_computation.2 | async-start | bytes 1048576 | tf_op jit(solution)/shard_map/all_to_all | solution.py:315
  79.7 2.0 %collective-permute-start = (s32[8]{0:T(128)S(1)}, s32[8]{0:T(128)S(1)}, u32[]{:S(2)}, u32[]{:S(2)}) collective-permute-start(s32[8]{0:T(128)S(1)} %compare_select_fusion), channel_id=1, source_target_pairs={{0,16},{16,0},{32,48},{48,32},{64,80},{80,64},{96,112},{112,96},{1... | collective-permute-start | bytes 104 | tf_op jit(solution)/shard_map/ppermute | solution.py:252
  81.7 7.5 %all-to-all-done.2.x_ref = bf16[16,128,128]{2,1,0:T(8,128)(2,1)S(1)} async-done(((bf16[16,128,128]{2,1,0:T(8,128)(2,1)}), bf16[16,128,128]{2,1,0:T(8,128)(2,1)S(1)}, u32[]{:S(2)}, u32[]{:S(2)}) %all-to-all-start.2) | async-done | bytes 524320 | tf_op jit(solution)/shard_map/all_to_all | solution.py:315
  89.2 4.5 %shard_map.158 = bf16[8,128,256]{2,1,0:T(8,128)(2,1)} custom-call(bf16[16,128,128]{2,1,0:T(8,128)(2,1)S(1)} %all-to-all-done.2.x_ref, f32[128,2048]{1,0:T(8,128)S(1)} %fusion.beam_ref, bf16[2,1024,1024]{2,1,0:T(8,128)(2,1)} %constant.88.clone.table_ref), custom_call_target="tpu_custom_call" | custom-call | flops 536870912 | bytes 4194304 | tf_op jit(solution)/shard_map/pallas_call | solution.py:221
  93.7 6.8 %all-to-all-start.3 = ((bf16[8,128,256]{2,1,0:T(8,128)(2,1)}), bf16[8,128,256]{2,1,0:T(8,128)(2,1)S(1)}, u32[]{:S(2)}, u32[]{:S(2)}) async-start(bf16[8,128,256]{2,1,0:T(8,128)(2,1)} %shard_map.158), calls=%async_computation.3 | async-start | bytes 1048576 | tf_op jit(solution)/shard_map/all_to_all | solution.py:328
  100.6 3.0 %collective-permute-start.1 = (s32[8]{0:T(128)S(1)}, s32[8]{0:T(128)S(1)}, u32[]{:S(2)}, u32[]{:S(2)}) collective-permute-start(s32[8]{0:T(128)S(1)} %fusion.3), channel_id=1, source_target_pairs={{0,32},{16,48},{32,0},{48,16},{64,96},{80,112},{96,64},{112,80},{1... | collective-permute-start | bytes 104 | tf_op jit(solution)/shard_map/ppermute | solution.py:252
  103.6 6.6 %collective-permute-done.1 = s32[8]{0:T(128)S(1)} collective-permute-done((s32[8]{0:T(128)S(1)}, s32[8]{0:T(128)S(1)}, u32[]{:S(2)}, u32[]{:S(2)}) %collective-permute-start.1) | collective-permute-done | bytes 64 | tf_op jit(solution)/shard_map/ppermute | solution.py:252
  110.2 0.5 collective-permute-start.2
  110.7 3.1 %collective-permute-done.2 = s32[8]{0:T(128)S(1)} collective-permute-done((s32[8]{0:T(128)S(1)}, s32[8]{0:T(128)S(1)}, u32[]{:S(2)}, u32[]{:S(2)}) %collective-permute-start.2) | collective-permute-done | bytes 64 | tf_op jit(solution)/shard_map/ppermute | solution.py:252
  113.8 1.0 shard_map.159
  114.9 1.3 collective-permute-done.5
  116.2 1.3 collective-permute-start.6
  117.6 5.8 %collective-permute-start.7 = (bf16[256,256]{1,0:T(8,128)(2,1)S(1)}, bf16[256,256]{1,0:T(8,128)(2,1)S(1)}, u32[]{:S(2)}, u32[]{:S(2)}) collective-permute-start(bf16[256,256]{1,0:T(8,128)(2,1)S(1)} %pad_maximum_fusion.1), channel_id=1, source_target_pairs={{0,0},{1,8},{2,16},{3,24},{4,32},{5,40},{6,48},{7,56},{8,64},{9,72... | collective-permute-start | bytes 393224 | tf_op jit(solution)/shard_map/ppermute | solution.py:349
  123.5 3.1 %collective-permute-done.6 = bf16[256,256]{1,0:T(8,128)(2,1)S(1)} collective-permute-done((bf16[256,256]{1,0:T(8,128)(2,1)S(1)}, bf16[256,256]{1,0:T(8,128)(2,1)S(1)}, u32[]{:S(2)}, u32[]{:S(2)}) %collective-permute-start.6) | collective-permute-done | bytes 131104 | tf_op jit(solution)/shard_map/ppermute | solution.py:349
  126.6 6.0 %collective-permute-done.7 = bf16[256,256]{1,0:T(8,128)(2,1)S(1)} collective-permute-done((bf16[256,256]{1,0:T(8,128)(2,1)S(1)}, bf16[256,256]{1,0:T(8,128)(2,1)S(1)}, u32[]{:S(2)}, u32[]{:S(2)}) %collective-permute-start.7) | collective-permute-done | bytes 131104 | tf_op jit(solution)/shard_map/ppermute | solution.py:349
  132.8 0.9 maximum_select_fusion
  (32 shorter events, 0.4 us)
Async XLA Ops:
  0.0 32.7 %all-to-all-start = ((bf16[16,128,512]{2,1,0:T(8,128)(2,1)}), bf16[16,128,512]{2,1,0:T(8,128)(2,1)S(1)}, u32[]{:S(2)}, u32[]{:S(2)}) async-start(bf16[16,128,512]{2,1,0:T(8,128)(2,1)} %bitcast.27), calls=%async_computation | async-start | bytes 4194304 | tf_op jit(solution)/shard_map/all_to_all | solution.py:247
  9.0 35.7 %copy-start.8 = (bf16[1,128,256]{2,1,0:T(8,128)(2,1)S(1)}, bf16[1,128,256]{2,1,0:T(8,128)(2,1)}, u32[]{:S(2)}) copy-start(bf16[1,128,256]{2,1,0:T(8,128)(2,1)} %constant.98) | copy-start | bytes 196612
  9.1 35.7 %copy-start.9 = (bf16[1,128,256]{2,1,0:T(8,128)(2,1)S(1)}, bf16[1,128,256]{2,1,0:T(8,128)(2,1)}, u32[]{:S(2)}) copy-start(bf16[1,128,256]{2,1,0:T(8,128)(2,1)} %constant.99) | copy-start | bytes 196612
  9.1 35.7 %copy-start.7 = (bf16[16,128]{1,0:T(8,128)(2,1)S(1)}, bf16[16,128]{1,0:T(8,128)(2,1)}, u32[]{:S(2)}) copy-start(bf16[16,128]{1,0:T(8,128)(2,1)} %constant.84.clone.first_ref) | copy-start | bytes 12292
  35.9 0.8 copy-start
  36.7 23.3 %copy-start.4 = (bf16[256,256]{1,0:T(8,128)(2,1)S(1)}, bf16[256,256]{1,0:T(8,128)(2,1)}, u32[]{:S(2)}) copy-start(bf16[256,256]{1,0:T(8,128)(2,1)} %constant.86.clone.direct_ref) | copy-start | bytes 393220
  36.7 23.3 %copy-start.5 = (bf16[256,256]{1,0:T(8,128)(2,1)S(1)}, bf16[256,256]{1,0:T(8,128)(2,1)}, u32[]{:S(2)}) copy-start(bf16[256,256]{1,0:T(8,128)(2,1)} %constant.87.clone.negated_ref) | copy-start | bytes 393220
  36.7 23.3 %copy-start.6 = (bf16[128,128]{1,0:T(8,128)(2,1)S(1)}, bf16[128,128]{1,0:T(8,128)(2,1)}, u32[]{:S(2)}) copy-start(bf16[128,128]{1,0:T(8,128)(2,1)} %constant.85.clone.eye_ref) | copy-start | bytes 98308
  36.7 24.6 %all-to-all-start.1 = ((bf16[16,128,128]{2,1,0:T(8,128)(2,1)}), bf16[16,128,128]{2,1,0:T(8,128)(2,1)S(1)}, u32[]{:S(2)}, u32[]{:S(2)}) async-start(bf16[16,128,128]{2,1,0:T(8,128)(2,1)} %copy-done), calls=%async_computation.1 | async-start | bytes 1048576 | tf_op jit(solution)/shard_map/all_to_all | solution.py:302
  44.8 1.2 copy-start.3
  46.6 13.4 %collective-permute-start.3 = (bf16[1024,128]{1,0:T(8,128)(2,1)S(1)}, bf16[1024,128]{1,0:T(8,128)(2,1)S(1)}, u32[]{:S(2)}, u32[]{:S(2)}) collective-permute-start(bf16[1024,128]{1,0:T(8,128)(2,1)S(1)} %get-tuple-element.11), channel_id=1, source_target_pairs={{0,15},{1,14},{2,13},{3,12},{4,11},{5,10},{6,9},{7,8},{8,7},{9,6},... | collective-permute-start | bytes 786440 | tf_op jit(solution)/shard_map/ppermute | solution.py:267
  49.4 9.5 %collective-permute-start.4 = (bf16[16,128]{1,0:T(8,128)(2,1)S(1)}, bf16[16,128]{1,0:T(8,128)(2,1)S(1)}, u32[]{:S(2)}, u32[]{:S(2)}) collective-permute-start(bf16[16,128]{1,0:T(8,128)(2,1)S(1)} %get-tuple-element.12), channel_id=1, source_target_pairs={{8,0},{9,7},{10,6},{11,5},{12,4},{13,3},{14,2},{15,1},{24,16},{25,... | collective-permute-start | bytes 12296 | tf_op jit(solution)/shard_map/ppermute | solution.py:268
  61.4 1.6 %copy-start.1 = (bf16[1024,1024]{1,0:T(8,128)(2,1)S(1)}, bf16[1024,1024]{1,0:T(8,128)(2,1)}, u32[]{:S(2)}) copy-start(bf16[1024,1024]{1,0:T(8,128)(2,1)} %constant.89.clone.c0) | copy-start | bytes 6291460
  63.0 1.6 %copy-start.2 = (bf16[1024,1024]{1,0:T(8,128)(2,1)S(1)}, bf16[1024,1024]{1,0:T(8,128)(2,1)}, u32[]{:S(2)}) copy-start(bf16[1024,1024]{1,0:T(8,128)(2,1)} %constant.90.clone.s0) | copy-start | bytes 6291460
  73.4 15.8 %all-to-all-start.2 = ((bf16[16,128,128]{2,1,0:T(8,128)(2,1)}), bf16[16,128,128]{2,1,0:T(8,128)(2,1)S(1)}, u32[]{:S(2)}, u32[]{:S(2)}) async-start(bf16[16,128,128]{2,1,0:T(8,128)(2,1)} %bitcast.9), calls=%async_computation.2 | async-start | bytes 1048576 | tf_op jit(solution)/shard_map/all_to_all | solution.py:315
  79.7 20.9 %collective-permute-start = (s32[8]{0:T(128)S(1)}, s32[8]{0:T(128)S(1)}, u32[]{:S(2)}, u32[]{:S(2)}) collective-permute-start(s32[8]{0:T(128)S(1)} %compare_select_fusion), channel_id=1, source_target_pairs={{0,16},{16,0},{32,48},{48,32},{64,80},{80,64},{96,112},{112,96},{1... | collective-permute-start | bytes 104 | tf_op jit(solution)/shard_map/ppermute | solution.py:252
  93.7 20.0 %all-to-all-start.3 = ((bf16[8,128,256]{2,1,0:T(8,128)(2,1)}), bf16[8,128,256]{2,1,0:T(8,128)(2,1)S(1)}, u32[]{:S(2)}, u32[]{:S(2)}) async-start(bf16[8,128,256]{2,1,0:T(8,128)(2,1)} %shard_map.158), calls=%async_computation.3 | async-start | bytes 1048576 | tf_op jit(solution)/shard_map/all_to_all | solution.py:328
  100.6 9.6 %collective-permute-start.1 = (s32[8]{0:T(128)S(1)}, s32[8]{0:T(128)S(1)}, u32[]{:S(2)}, u32[]{:S(2)}) collective-permute-start(s32[8]{0:T(128)S(1)} %fusion.3), channel_id=1, source_target_pairs={{0,32},{16,48},{32,0},{48,16},{64,96},{80,112},{96,64},{112,80},{1... | collective-permute-start | bytes 104 | tf_op jit(solution)/shard_map/ppermute | solution.py:252
  110.2 3.5 %collective-permute-start.2 = (s32[8]{0:T(128)S(1)}, s32[8]{0:T(128)S(1)}, u32[]{:S(2)}, u32[]{:S(2)}) collective-permute-start(s32[8]{0:T(128)S(1)} %fusion.4), channel_id=1, source_target_pairs={{0,64},{16,80},{32,96},{48,112},{64,0},{80,16},{96,32},{112,48},{1... | collective-permute-start | bytes 104 | tf_op jit(solution)/shard_map/ppermute | solution.py:252
  114.8 1.4 %collective-permute-start.5 = (bf16[2,128,256]{2,1,0:T(8,128)(2,1)S(1)}, bf16[2,128,256]{2,1,0:T(8,128)(2,1)S(1)}, u32[]{:S(2)}, u32[]{:S(2)}) collective-permute-start(bf16[2,128,256]{2,1,0:T(8,128)(2,1)S(1)} %get-tuple-element.14), channel_id=1, source_target_pairs={{0,1},{1,0},{2,3},{3,2},{4,5},{5,4},{6,7},{7,6},{8,9},{9,8},{10,11... | collective-permute-start | bytes 393224 | tf_op jit(solution)/shard_map/ppermute | solution.py:338
  116.2 10.4 %collective-permute-start.6 = (bf16[256,256]{1,0:T(8,128)(2,1)S(1)}, bf16[256,256]{1,0:T(8,128)(2,1)S(1)}, u32[]{:S(2)}, u32[]{:S(2)}) collective-permute-start(bf16[256,256]{1,0:T(8,128)(2,1)S(1)} %pad_maximum_fusion), channel_id=1, source_target_pairs={{0,4},{1,12},{2,20},{3,28},{4,36},{5,44},{6,52},{7,60},{8,68},{9,7... | collective-permute-start | bytes 393224 | tf_op jit(solution)/shard_map/ppermute | solution.py:349
  117.6 15.0 %collective-permute-start.7 = (bf16[256,256]{1,0:T(8,128)(2,1)S(1)}, bf16[256,256]{1,0:T(8,128)(2,1)S(1)}, u32[]{:S(2)}, u32[]{:S(2)}) collective-permute-start(bf16[256,256]{1,0:T(8,128)(2,1)S(1)} %pad_maximum_fusion.1), channel_id=1, source_target_pairs={{0,0},{1,8},{2,16},{3,24},{4,32},{5,40},{6,48},{7,56},{8,64},{9,72... | collective-permute-start | bytes 393224 | tf_op jit(solution)/shard_map/ppermute | solution.py:349

commit v3 on v2

--- a/solution.py
+++ b/solution.py
@@ -217,7 +217,7 @@
             ref[turn] = total.astype(BF16)
 
 
-def call(kernel, outs, specs, *args, scratch=(), flops=0, moved=4 << 20, limit=48):
+def call(kernel, outs, specs, *args, scratch=(), flops=0, moved=4 << 20, limit=16):
     return pl.pallas_call(
         kernel,
         out_shape=outs,
@@ -289,6 +289,7 @@
     twice = jnp.concatenate([beam[0], beam[0]], 1)
     turned = lax.dynamic_slice_in_dim(twice, (points - start % points) % points, points, 1)
     row_table = bf16(row_tables(points, devices))
+    tiles, weight, starts = lax.optimization_barrier((tiles, weight, starts))
     spectrum = call(
         row_kernel,
         shape(devices, rows, 128),
@@ -311,6 +312,7 @@
         scratch=[pltpu.VMEM((2, points // 2, 128), BF16)] * 2,
         flops=8 * points * points * 128 // 2,
         moved=16 << 20,
+        limit=24,
     )
     lines = lax.all_to_all(
         back.reshape(devices, rows, 128), "img", split_axis=0, concat_axis=0, tiled=True

time: 134 us -> 124 us (0.925)
  blocking collectives: 0 us -> 31.1 us
  waiting for transfers between devices: 60.6 us -> 36.2 us
  starting transfers between devices: 44.4 us -> 31.6 us
  Pallas kernels: 19.5 us -> 11.5 us
  local copies, waits for them, and re-layouts: 5.27 us -> 8.72 us
    all_to_all x0 -> x2, blocking collectives: none -> 31.1 us  [the longest x1 16.2 us: shards(): lax.all_to_all(spectrum, 'img', split_axis=0, concat_axis=0, tiled=True)]
    all_to_all x1, waiting for transfers between devices: 23.7 us -> 0.01 us  [shards(): lax.all_to_all(image, 'img', split_axis=0, concat_axis=0, tiled=True)]
    all_to_all x2 -> x0, starting transfers between devices: 14.3 us -> none  [the longest x1 8 us: shards(): lax.all_to_all(spectrum, 'img', split_axis=0, concat_axis=0, tiled=True)]
    all_to_all x1, waiting for transfers between devices: 0.01 us -> 9.35 us  [shards(): lax.all_to_all(contribution, 'ptg', split_axis=0, concat_axis=0, tiled=True)]
    pallas_call x6, Pallas kernels: 19.5 us -> 11.5 us  [call(): pl.pallas_call(kernel, out_shape=outs, in_specs=specs, out_specs=jax.tree...]
    all_to_all x2 -> x0, waiting for transfers between devices: 7.53 us -> none  [the longest x1 7.53 us: shards(): lax.all_to_all(back.reshape(devices, rows, 128), 'img', split_axis=0, con...]
    ppermute x3, waiting for transfers between devices: 9.67 us -> 3.73 us  [shards(): lax.ppermute(starts, 'ptg', [(p, p ^ bit) for p in range(pointings)])]
    unnamed x20 -> x38, local copies, waits for them, and re-layouts: 5.22 us -> 8.66 us
  transfers between devices with their start and end apart: 12 -> 10, of which waited for: 9 -> 8; matrix products, arithmetic and copies ran while one was open for 1% -> 2% of each run, Pallas kernels for 5% -> 2%
where the time goes in v3:
time: 124 us
  waiting for transfers between devices  36.2 us (29%)
  starting transfers between devices  31.6 us (25%)
  blocking collectives  31.1 us (25%)
  Pallas kernels  11.5 us (9%)
  local copies, waits for them, and re-layouts  8.72 us (7%)
  other arithmetic  3.58 us (3%)
    all_to_all x1, blocking collectives, shards(): lax.all_to_all(spectrum, 'img', split_axis=0, concat_axis=0, tiled=True)  16.2 us
    all_to_all x1, blocking collectives, shards(): lax.all_to_all(back.reshape(devices, rows, 128), 'img', split_axis=0, con...  15 us
    pallas_call x6, Pallas kernels, call(): pl.pallas_call(kernel, out_shape=outs, in_specs=specs, out_specs=jax.tree...  11.5 us
    ppermute x1, waiting for transfers between devices, shards(): lax.ppermute(edge, 'img', [(i, (devices - i) % (devices // 2)) for i in r...  9.85 us
    all_to_all x1, waiting for transfers between devices, shards(): lax.all_to_all(contribution, 'ptg', split_axis=0, concat_axis=0, tiled=True)  9.35 us
    ppermute x2, waiting for transfers between devices, shards(): received.append(lax.ppermute(block, ('ptg', 'img'), pairs))  9.13 us
    unnamed x38, local copies, waits for them, and re-layouts  8.66 us
    ppermute x2, starting transfers between devices, shards(): received.append(lax.ppermute(block, ('ptg', 'img'), pairs))  7.37 us
  transfers between devices with their start and end apart: 10, of which 8 were waited for; matrix products, arithmetic and copies ran while one was open for 2% of the time, Pallas kernels for 2%

profile of v3, /device:TPU:14, one launch (start us, length us, event | category | flops | bytes accessed | tf_op | source)
XLA Modules:
  0.0 123.6 jit_solution(7390626198962325200)
XLA Ops:
  0.0 6.7 %all-to-all-start = ((bf16[16,128,512]{2,1,0:T(8,128)(2,1)}), bf16[16,128,512]{2,1,0:T(8,128)(2,1)S(1)}, u32[]{:S(2)}, u32[]{:S(2)}) async-start(bf16[16,128,512]{2,1,0:T(8,128)(2,1)} %bitcast.28), calls=%async_computation | async-start | bytes 4194304 | tf_op jit(solution)/shard_map/all_to_all | solution.py:247
  8.0 1.9 %collective-permute-start.2 = (s32[8]{0:T(128)}, s32[8]{0:T(128)S(1)}, u32[]{:S(2)}, u32[]{:S(2)}) collective-permute-start(s32[8]{0:T(128)} %compare_select_fusion), channel_id=1, source_target_pairs={{0,16},{16,0},{32,48},{48,32},{64,80},{80,64},{96,112},{112,96},{1... | collective-permute-start | bytes 104 | tf_op jit(solution)/shard_map/ppermute | solution.py:252
  9.9 1.2 shard_map.154
  11.1 0.8 copy-done.11
  11.9 2.4 %collective-permute-start = (bf16[1024,128]{1,0:T(8,128)(2,1)}, bf16[1024,128]{1,0:T(8,128)(2,1)S(1)}, u32[]{:S(2)}, u32[]{:S(2)}) collective-permute-start(bf16[1024,128]{1,0:T(8,128)(2,1)} %get-tuple-element.14), channel_id=1, source_target_pairs={{0,15},{1,14},{2,13},{3,12},{4,11},{5,10},{6,9},{7,8},{8,7},{9,6},... | collective-permute-start | bytes 786440 | tf_op jit(solution)/shard_map/ppermute | solution.py:267
  14.4 1.3 %collective-permute-start.1 = (bf16[16,128]{1,0:T(8,128)(2,1)S(1)}, bf16[16,128]{1,0:T(8,128)(2,1)S(1)}, u32[]{:S(2)}, u32[]{:S(2)}) collective-permute-start(bf16[16,128]{1,0:T(8,128)(2,1)S(1)} %get-tuple-element.15), channel_id=1, source_target_pairs={{8,0},{9,7},{10,6},{11,5},{12,4},{13,3},{14,2},{15,1},{24,16},{25,... | collective-permute-start | bytes 12296 | tf_op jit(solution)/shard_map/ppermute | solution.py:268
  15.7 1.9 %fusion.beam_ref = f32[128,2048]{1,0:T(8,128)S(1)} fusion(s32[]{:T(128)S(6)} %select_n.67, f32[128,2048]{1,0:T(8,128)} %bitcast.29), kind=kLoop, calls=%fused_computation.2 | loop fusion | flops 262144 | bytes 2097156 | tf_op jit(solution)/shard_map/concatenate | solution.py:289
  17.6 3.7 %collective-permute-start.3 = (s32[8]{0:T(128)S(1)}, s32[8]{0:T(128)S(1)}, u32[]{:S(2)}, u32[]{:S(2)}) collective-permute-start(s32[8]{0:T(128)S(1)} %fusion.3), channel_id=1, source_target_pairs={{0,32},{16,48},{32,0},{48,16},{64,96},{80,112},{96,64},{112,80},{1... | collective-permute-start | bytes 104 | tf_op jit(solution)/shard_map/ppermute | solution.py:252
  21.3 1.5 %collective-permute-done.3 = s32[8]{0:T(128)S(1)} collective-permute-done((s32[8]{0:T(128)S(1)}, s32[8]{0:T(128)S(1)}, u32[]{:S(2)}, u32[]{:S(2)}) %collective-permute-start.3) | collective-permute-done | bytes 64 | tf_op jit(solution)/shard_map/ppermute | solution.py:252
  22.8 1.3 %collective-permute-start.4 = (s32[8]{0:T(128)S(1)}, s32[8]{0:T(128)S(1)}, u32[]{:S(2)}, u32[]{:S(2)}) collective-permute-start(s32[8]{0:T(128)S(1)} %fusion.4), channel_id=1, source_target_pairs={{0,64},{16,80},{32,96},{48,112},{64,0},{80,16},{96,32},{112,48},{1... | collective-permute-start | bytes 104 | tf_op jit(solution)/shard_map/ppermute | solution.py:252
  24.2 2.2 %collective-permute-done.4 = s32[8]{0:T(128)S(1)} collective-permute-done((s32[8]{0:T(128)S(1)}, s32[8]{0:T(128)S(1)}, u32[]{:S(2)}, u32[]{:S(2)}) %collective-permute-start.4) | collective-permute-done | bytes 64 | tf_op jit(solution)/shard_map/ppermute | solution.py:252
  26.4 9.8 %collective-permute-done.1.edge_ref = bf16[16,128]{1,0:T(8,128)(2,1)S(1)} collective-permute-done((bf16[16,128]{1,0:T(8,128)(2,1)S(1)}, bf16[16,128]{1,0:T(8,128)(2,1)S(1)}, u32[]{:S(2)}, u32[]{:S(2)}) %collective-permute-start.1) | collective-permute-done | bytes 4128 | tf_op jit(solution)/shard_map/ppermute | solution.py:268
  36.2 2.8 %collective-permute-done.got_ref = bf16[1024,128]{1,0:T(8,128)(2,1)S(1)} collective-permute-done((bf16[1024,128]{1,0:T(8,128)(2,1)}, bf16[1024,128]{1,0:T(8,128)(2,1)S(1)}, u32[]{:S(2)}, u32[]{:S(2)}) %collective-permute-start) | collective-permute-done | bytes 262176 | tf_op jit(solution)/shard_map/ppermute | solution.py:267
  39.0 0.9 copy-done.14
  40.7 1.4 %shard_map.155.weight_ref = bf16[2048,128]{1,0:T(8,128)(2,1)S(1)} custom-call(s32[1]{0:T(128)} %bitcast.3.me_ref, bf16[2048,128]{1,0:T(8,128)(2,1)S(1)} %copy-done.12, bf16[1024,128]{1,0:T(8,128)(2,1)S(1)} %collective-permute-done.got_ref, bf16[16,128]{1,0:T(8,128)(2,1)S(1)} %collective-permute-done.1.edge_ref, bf16[128,128]{1,0:T(8,128)(2,1)S(1)} %copy-done.15, ...), custom_call_target="tpu_custom_call" | custom-call | flops 268435456 | bytes 4194304 | tf_op jit(solution)/shard_map/pallas_call | solution.py:221
  42.8 2.2 %copy-done = bf16[2,1024,1024]{2,1,0:T(8,128)(2,1)S(1)} copy-done((bf16[2,1024,1024]{2,1,0:T(8,128)(2,1)S(1)}, bf16[2,1024,1024]{2,1,0:T(8,128)(2,1)}, u32[]{:S(2)}) %copy-start) | copy-done | bytes 4194328
  45.0 1.0 shard_map.156
  46.1 16.2 %all_to_all.24 = bf16[16,128,128]{2,1,0:T(8,128)(2,1)S(1)} all-to-all(bf16[16,128,128]{2,1,0:T(8,128)(2,1)S(1)} %shard_map.156), channel_id=1, replica_groups=mesh['ptg'=8,'img'=16] {'img'}, dimensions={0} | all-to-all | bytes 1048576 | tf_op jit(solution)/shard_map/all_to_all | solution.py:303
  62.3 1.6 %copy-done.8 = bf16[1024,1024]{1,0:T(8,128)(2,1)S(1)} copy-done((bf16[1024,1024]{1,0:T(8,128)(2,1)S(1)}, bf16[1024,1024]{1,0:T(8,128)(2,1)}, u32[]{:S(2)}) %copy-start.8) | copy-done | bytes 2097176
  63.9 1.6 %copy-done.9 = bf16[1024,1024]{1,0:T(8,128)(2,1)S(1)} copy-done((bf16[1024,1024]{1,0:T(8,128)(2,1)S(1)}, bf16[1024,1024]{1,0:T(8,128)(2,1)}, u32[]{:S(2)}) %copy-start.9) | copy-done | bytes 2097176
  65.5 4.6 %shard_map.157 = bf16[2048,128]{1,0:T(8,128)(2,1)S(1)} custom-call(s32[1]{0:T(128)} %bitcast.3.me_ref, bf16[2048,128]{1,0:T(8,128)(2,1)S(1)} %bitcast.25, bf16[2048,128]{1,0:T(8,128)(2,1)S(1)} %copy-done.3, bf16[1024,1024]{1,0:T(8,128)(2,1)S(1)} %copy-done.4, bf16[1024,1024]{1,0:T(8,128)(2,1)S(1)} %copy-done.5, bf16[1024,1024]{1,0:T(8,128)(2,1)S(1)} %copy-done.6, ...), custom_call_target="tpu_custom_call" | custom-call | flops 2147483648 | bytes 16777216 | tf_op jit(solution)/shard_map/pallas_call | solution.py:221
  70.1 15.0 %all_to_all.25.x_ref = bf16[16,128,128]{2,1,0:T(8,128)(2,1)S(1)} all-to-all(bf16[16,128,128]{2,1,0:T(8,128)(2,1)S(1)} %bitcast.26), channel_id=1, replica_groups=mesh['ptg'=8,'img'=16] {'img'}, dimensions={0} | all-to-all | bytes 1048576 | tf_op jit(solution)/shard_map/all_to_all | solution.py:317
  85.0 2.3 %shard_map.158 = bf16[8,128,256]{2,1,0:T(8,128)(2,1)} custom-call(bf16[16,128,128]{2,1,0:T(8,128)(2,1)S(1)} %all_to_all.25.x_ref, f32[128,2048]{1,0:T(8,128)S(1)} %fusion.beam_ref, bf16[2,1024,1024]{2,1,0:T(8,128)(2,1)S(1)} %copy-done.1), custom_call_target="tpu_custom_call" | custom-call | flops 536870912 | bytes 4194304 | tf_op jit(solution)/shard_map/pallas_call | solution.py:221
  87.3 6.8 %all-to-all-start.3 = ((bf16[8,128,256]{2,1,0:T(8,128)(2,1)}), bf16[8,128,256]{2,1,0:T(8,128)(2,1)S(1)}, u32[]{:S(2)}, u32[]{:S(2)}) async-start(bf16[8,128,256]{2,1,0:T(8,128)(2,1)} %shard_map.158), calls=%async_computation.3 | async-start | bytes 1048576 | tf_op jit(solution)/shard_map/all_to_all | solution.py:330
  94.2 9.4 %all-to-all-done.3.terms_ref = bf16[8,128,256]{2,1,0:T(8,128)(2,1)S(1)} async-done(((bf16[8,128,256]{2,1,0:T(8,128)(2,1)}), bf16[8,128,256]{2,1,0:T(8,128)(2,1)S(1)}, u32[]{:S(2)}, u32[]{:S(2)}) %all-to-all-start.3) | async-done | bytes 524320 | tf_op jit(solution)/shard_map/all_to_all | solution.py:330
  103.6 1.0 shard_map.159
  104.7 1.3 %collective-permute-done.5 = bf16[2,128,256]{2,1,0:T(8,128)(2,1)S(1)} collective-permute-done((bf16[2,128,256]{2,1,0:T(8,128)(2,1)S(1)}, bf16[2,128,256]{2,1,0:T(8,128)(2,1)S(1)}, u32[]{:S(2)}, u32[]{:S(2)}) %collective-permute-start.5) | collective-permute-done | bytes 131104 | tf_op jit(solution)/shard_map/ppermute | solution.py:340
  106.0 1.6 %collective-permute-start.6 = (bf16[256,256]{1,0:T(8,128)(2,1)S(1)}, bf16[256,256]{1,0:T(8,128)(2,1)S(1)}, u32[]{:S(2)}, u32[]{:S(2)}) collective-permute-start(bf16[256,256]{1,0:T(8,128)(2,1)S(1)} %pad_maximum_fusion), channel_id=1, source_target_pairs={{0,4},{1,12},{2,20},{3,28},{4,36},{5,44},{6,52},{7,60},{8,68},{9,7... | collective-permute-start | bytes 393224 | tf_op jit(solution)/shard_map/ppermute | solution.py:351
  107.6 5.8 %collective-permute-start.7 = (bf16[256,256]{1,0:T(8,128)(2,1)S(1)}, bf16[256,256]{1,0:T(8,128)(2,1)S(1)}, u32[]{:S(2)}, u32[]{:S(2)}) collective-permute-start(bf16[256,256]{1,0:T(8,128)(2,1)S(1)} %pad_maximum_fusion.1), channel_id=1, source_target_pairs={{0,0},{1,8},{2,16},{3,24},{4,32},{5,40},{6,48},{7,56},{8,64},{9,72... | collective-permute-start | bytes 393224 | tf_op jit(solution)/shard_map/ppermute | solution.py:351
  113.4 3.2 %collective-permute-done.6 = bf16[256,256]{1,0:T(8,128)(2,1)S(1)} collective-permute-done((bf16[256,256]{1,0:T(8,128)(2,1)S(1)}, bf16[256,256]{1,0:T(8,128)(2,1)S(1)}, u32[]{:S(2)}, u32[]{:S(2)}) %collective-permute-start.6) | collective-permute-done | bytes 131104 | tf_op jit(solution)/shard_map/ppermute | solution.py:351
  116.7 5.9 %collective-permute-done.7 = bf16[256,256]{1,0:T(8,128)(2,1)S(1)} collective-permute-done((bf16[256,256]{1,0:T(8,128)(2,1)S(1)}, bf16[256,256]{1,0:T(8,128)(2,1)S(1)}, u32[]{:S(2)}, u32[]{:S(2)}) %collective-permute-start.7) | collective-permute-done | bytes 131104 | tf_op jit(solution)/shard_map/ppermute | solution.py:351
  122.7 0.9 maximum_select_fusion
  (48 shorter events, 2.6 us)
Async XLA Ops:
  0.0 9.9 %copy-start.17 = (bf16[1,128,256]{2,1,0:T(8,128)(2,1)S(1)}, bf16[1,128,256]{2,1,0:T(8,128)(2,1)}, u32[]{:S(2)}) copy-start(bf16[1,128,256]{2,1,0:T(8,128)(2,1)} %constant.98) | copy-start | bytes 196612
  0.0 9.9 %copy-start.18 = (bf16[1,128,256]{2,1,0:T(8,128)(2,1)S(1)}, bf16[1,128,256]{2,1,0:T(8,128)(2,1)}, u32[]{:S(2)}) copy-start(bf16[1,128,256]{2,1,0:T(8,128)(2,1)} %constant.99) | copy-start | bytes 196612
  0.0 9.9 %copy-start.10 = (s32[1,2048,128]{2,1,0:T(8,128)S(1)}, s32[1,2048,128]{2,1,0:T(8,128)}, u32[]{:S(2)}) copy-start(s32[1,2048,128]{2,1,0:T(8,128)} %param.18) | copy-start | bytes 3145732
  0.0 9.9 %copy-start.16 = (bf16[16,128]{1,0:T(8,128)(2,1)S(1)}, bf16[16,128]{1,0:T(8,128)(2,1)}, u32[]{:S(2)}) copy-start(bf16[16,128]{1,0:T(8,128)(2,1)} %constant.84.clone.first_ref) | copy-start | bytes 12292
  0.0 42.8 %all-to-all-start = ((bf16[16,128,512]{2,1,0:T(8,128)(2,1)}), bf16[16,128,512]{2,1,0:T(8,128)(2,1)S(1)}, u32[]{:S(2)}, u32[]{:S(2)}) async-start(bf16[16,128,512]{2,1,0:T(8,128)(2,1)} %bitcast.28), calls=%async_computation | async-start | bytes 4194304 | tf_op jit(solution)/shard_map/all_to_all | solution.py:247
  6.7 32.3 %copy-start.13 = (bf16[256,256]{1,0:T(8,128)(2,1)S(1)}, bf16[256,256]{1,0:T(8,128)(2,1)}, u32[]{:S(2)}) copy-start(bf16[256,256]{1,0:T(8,128)(2,1)} %constant.86.clone.direct_ref) | copy-start | bytes 393220
  8.0 9.6 %collective-permute-start.2 = (s32[8]{0:T(128)}, s32[8]{0:T(128)S(1)}, u32[]{:S(2)}, u32[]{:S(2)}) collective-permute-start(s32[8]{0:T(128)} %compare_select_fusion), channel_id=1, source_target_pairs={{0,16},{16,0},{32,48},{48,32},{64,80},{80,64},{96,112},{112,96},{1... | collective-permute-start | bytes 104 | tf_op jit(solution)/shard_map/ppermute | solution.py:252
  11.1 0.8 copy-start.11
  11.9 27.1 %collective-permute-start = (bf16[1024,128]{1,0:T(8,128)(2,1)}, bf16[1024,128]{1,0:T(8,128)(2,1)S(1)}, u32[]{:S(2)}, u32[]{:S(2)}) collective-permute-start(bf16[1024,128]{1,0:T(8,128)(2,1)} %get-tuple-element.14), channel_id=1, source_target_pairs={{0,15},{1,14},{2,13},{3,12},{4,11},{5,10},{6,9},{7,8},{8,7},{9,6},... | collective-permute-start | bytes 786440 | tf_op jit(solution)/shard_map/ppermute | solution.py:267
  14.4 21.8 %collective-permute-start.1 = (bf16[16,128]{1,0:T(8,128)(2,1)S(1)}, bf16[16,128]{1,0:T(8,128)(2,1)S(1)}, u32[]{:S(2)}, u32[]{:S(2)}) collective-permute-start(bf16[16,128]{1,0:T(8,128)(2,1)S(1)} %get-tuple-element.15), channel_id=1, source_target_pairs={{8,0},{9,7},{10,6},{11,5},{12,4},{13,3},{14,2},{15,1},{24,16},{25,... | collective-permute-start | bytes 12296 | tf_op jit(solution)/shard_map/ppermute | solution.py:268
  15.7 23.3 %copy-start.12 = (bf16[2048,128]{1,0:T(8,128)(2,1)S(1)}, bf16[2048,128]{1,0:T(8,128)(2,1)}, u32[]{:S(2)}) copy-start(bf16[2048,128]{1,0:T(8,128)(2,1)} %copy-done.11) | copy-start | bytes 1572868
  17.6 5.2 %collective-permute-start.3 = (s32[8]{0:T(128)S(1)}, s32[8]{0:T(128)S(1)}, u32[]{:S(2)}, u32[]{:S(2)}) collective-permute-start(s32[8]{0:T(128)S(1)} %fusion.3), channel_id=1, source_target_pairs={{0,32},{16,48},{32,0},{48,16},{64,96},{80,112},{96,64},{112,80},{1... | collective-permute-start | bytes 104 | tf_op jit(solution)/shard_map/ppermute | solution.py:252
  22.8 3.5 %collective-permute-start.4 = (s32[8]{0:T(128)S(1)}, s32[8]{0:T(128)S(1)}, u32[]{:S(2)}, u32[]{:S(2)}) collective-permute-start(s32[8]{0:T(128)S(1)} %fusion.4), channel_id=1, source_target_pairs={{0,64},{16,80},{32,96},{48,112},{64,0},{80,16},{96,32},{112,48},{1... | collective-permute-start | bytes 104 | tf_op jit(solution)/shard_map/ppermute | solution.py:252
  39.0 0.9 copy-start.14
  39.9 0.8 copy-start.15
  42.0 0.8 copy-start.2
  42.8 2.2 %copy-start = (bf16[2,1024,1024]{2,1,0:T(8,128)(2,1)S(1)}, bf16[2,1024,1024]{2,1,0:T(8,128)(2,1)}, u32[]{:S(2)}) copy-start(bf16[2,1024,1024]{2,1,0:T(8,128)(2,1)} %constant.88.clone.table_ref) | copy-start | bytes 12582916
  45.0 17.2 %copy-start.3 = (bf16[2048,128]{1,0:T(8,128)(2,1)S(1)}, bf16[2048,128]{1,0:T(8,128)(2,1)}, u32[]{:S(2)}) copy-start(bf16[2048,128]{1,0:T(8,128)(2,1)} %copy-done.2) | copy-start | bytes 1572868
  45.0 17.2 %copy-start.4 = (bf16[1024,1024]{1,0:T(8,128)(2,1)S(1)}, bf16[1024,1024]{1,0:T(8,128)(2,1)}, u32[]{:S(2)}) copy-start(bf16[1024,1024]{1,0:T(8,128)(2,1)} %constant.89.clone.c0) | copy-start | bytes 6291460
  45.0 17.2 %copy-start.5 = (bf16[1024,1024]{1,0:T(8,128)(2,1)S(1)}, bf16[1024,1024]{1,0:T(8,128)(2,1)}, u32[]{:S(2)}) copy-start(bf16[1024,1024]{1,0:T(8,128)(2,1)} %constant.90.clone.s0) | copy-start | bytes 6291460
  45.0 17.2 %copy-start.6 = (bf16[1024,1024]{1,0:T(8,128)(2,1)S(1)}, bf16[1024,1024]{1,0:T(8,128)(2,1)}, u32[]{:S(2)}) copy-start(bf16[1024,1024]{1,0:T(8,128)(2,1)} %constant.91.clone.c1) | copy-start | bytes 6291460
  45.0 17.2 %copy-start.7 = (bf16[1024,1024]{1,0:T(8,128)(2,1)S(1)}, bf16[1024,1024]{1,0:T(8,128)(2,1)}, u32[]{:S(2)}) copy-start(bf16[1024,1024]{1,0:T(8,128)(2,1)} %constant.92.clone.s1) | copy-start | bytes 6291460
  62.3 1.6 %copy-start.8 = (bf16[1024,1024]{1,0:T(8,128)(2,1)S(1)}, bf16[1024,1024]{1,0:T(8,128)(2,1)}, u32[]{:S(2)}) copy-start(bf16[1024,1024]{1,0:T(8,128)(2,1)} %constant.93.clone.c1t) | copy-start | bytes 6291460
  63.9 1.6 %copy-start.9 = (bf16[1024,1024]{1,0:T(8,128)(2,1)S(1)}, bf16[1024,1024]{1,0:T(8,128)(2,1)}, u32[]{:S(2)}) copy-start(bf16[1024,1024]{1,0:T(8,128)(2,1)} %constant.94.clone.s1t) | copy-start | bytes 6291460
  65.5 19.6 %copy-start.1 = (bf16[2,1024,1024]{2,1,0:T(8,128)(2,1)S(1)}, bf16[2,1024,1024]{2,1,0:T(8,128)(2,1)}, u32[]{:S(2)}) copy-start(bf16[2,1024,1024]{2,1,0:T(8,128)(2,1)} %constant.88.clone.table_ref) | copy-start | bytes 12582916
  87.3 16.2 %all-to-all-start.3 = ((bf16[8,128,256]{2,1,0:T(8,128)(2,1)}), bf16[8,128,256]{2,1,0:T(8,128)(2,1)S(1)}, u32[]{:S(2)}, u32[]{:S(2)}) async-start(bf16[8,128,256]{2,1,0:T(8,128)(2,1)} %shard_map.158), calls=%async_computation.3 | async-start | bytes 1048576 | tf_op jit(solution)/shard_map/all_to_all | solution.py:330
  104.6 1.4 %collective-permute-start.5 = (bf16[2,128,256]{2,1,0:T(8,128)(2,1)S(1)}, bf16[2,128,256]{2,1,0:T(8,128)(2,1)S(1)}, u32[]{:S(2)}, u32[]{:S(2)}) collective-permute-start(bf16[2,128,256]{2,1,0:T(8,128)(2,1)S(1)} %get-tuple-element.20), channel_id=1, source_target_pairs={{0,1},{1,0},{2,3},{3,2},{4,5},{5,4},{6,7},{7,6},{8,9},{9,8},{10,11... | collective-permute-start | bytes 393224 | tf_op jit(solution)/shard_map/ppermute | solution.py:340
  106.0 10.7 %collective-permute-start.6 = (bf16[256,256]{1,0:T(8,128)(2,1)S(1)}, bf16[256,256]{1,0:T(8,128)(2,1)S(1)}, u32[]{:S(2)}, u32[]{:S(2)}) collective-permute-start(bf16[256,256]{1,0:T(8,128)(2,1)S(1)} %pad_maximum_fusion), channel_id=1, source_target_pairs={{0,4},{1,12},{2,20},{3,28},{4,36},{5,44},{6,52},{7,60},{8,68},{9,7... | collective-permute-start | bytes 393224 | tf_op jit(solution)/shard_map/ppermute | solution.py:351
  107.6 15.0 %collective-permute-start.7 = (bf16[256,256]{1,0:T(8,128)(2,1)S(1)}, bf16[256,256]{1,0:T(8,128)(2,1)S(1)}, u32[]{:S(2)}, u32[]{:S(2)}) collective-permute-start(bf16[256,256]{1,0:T(8,128)(2,1)S(1)} %pad_maximum_fusion.1), channel_id=1, source_target_pairs={{0,0},{1,8},{2,16},{3,24},{4,32},{5,40},{6,48},{7,56},{8,64},{9,72... | collective-permute-start | bytes 393224 | tf_op jit(solution)/shard_map/ppermute | solution.py:351

commit v4 on v3

--- a/solution.py
+++ b/solution.py
@@ -7,12 +7,13 @@
 from jax import lax
 from jax.experimental import pallas as pl
 from jax.experimental.pallas import tpu as pltpu
-from jax.sharding import PartitionSpec as P
+from jax.sharding import Mesh, PartitionSpec as P
 
 F32, BF16 = jnp.float32, jnp.bfloat16
 NT = (((1,), (1,)), ((), ()))
 NN = (((1,), (0,)), ((), ()))
 VMEM = pl.BlockSpec(memory_space=pltpu.VMEM)
+HBM = pl.BlockSpec(memory_space=pltpu.HBM)
 SMEM = pl.BlockSpec(memory_space=pltpu.SMEM)
 
 
@@ -135,34 +136,74 @@
         out_ref[pl.ds(points // 2 + 128 * b, 128)] = taken[128:].astype(BF16)
 
 
-def row_kernel(start_ref, tiles_ref, beam_ref, table_ref, out_ref):
-    tiles, rows, wide = tiles_ref.shape
-    points = beam_ref.shape[1]
-    start = start_ref[0]
-    per_lap = points // wide
-    lane = lax.broadcasted_iota(jnp.int32, (rows, wide), 1)
+class Stream:
+    def __init__(self, pieces, sems, ahead=6):
+        self.copies = [
+            pltpu.make_async_copy(source, target, sems.at[n])
+            for n, (source, target) in enumerate(pieces)
+        ]
+        self.ahead, self.taken = ahead, 0
+        for copy in self.copies[:ahead]:
+            copy.start()
+
+    def take(self):
+        self.copies[self.taken].wait()
+        if self.taken + self.ahead < len(self.copies):
+            self.copies[self.taken + self.ahead].start()
+        self.taken += 1
+
+
+def pick_kernel(points, place_ref, starts_ref, tiles_ref, out_ref):
+    laps, parts, rows, wide = tiles_ref.shape
+    lane = lax.broadcasted_iota(jnp.int32, (rows, wide), 1) + place_ref[0] * wide
+    for part in range(parts):
+        held = [tiles_ref[lap, part].astype(F32) for lap in range(laps)]
+        for p in range(out_ref.shape[0]):
+            start = starts_ref[p]
+            window = jnp.zeros((rows, wide), F32)
+            for lap in range(laps):
+                column = lane + lap * points
+                inside = (column >= start) & (column < start + points)
+                window = jnp.where(inside, held[lap], window)
+            out_ref[p, part] = window.astype(BF16)
+
+
+def row_kernel(window_ref, beam_ref, source_ref, out_ref, table_ref, sems):
+    shares, parts, rows, wide = window_ref.shape
+    blocks = out_ref.shape[0] // 2
+    places = [(odd, pl.ds(256 * part, 256)) for odd in (0, 1) for part in range(blocks // 2)]
+    stream = Stream(
+        [(source_ref.at[odd, :, lanes], table_ref.at[odd, :, lanes]) for odd, lanes in places],
+        sems,
+    )
     beamed = []
-    for block in range(per_lap):
-        window = jnp.zeros((rows, wide), F32)
-        for lap in range(tiles // per_lap):
-            column = lane + (lap * points + block * wide)
-            inside = (column >= start) & (column < start + points)
-            window = jnp.where(inside, tiles_ref[lap * per_lap + block].astype(F32), window)
-        beamed.append(window * beam_ref[:, pl.ds(block * wide, wide)])
-    left = jnp.concatenate(beamed[: per_lap // 2], 1)
-    right = jnp.concatenate(beamed[per_lap // 2 :], 1)
-    blocks = out_ref.shape[0] // 2
+    for part in range(parts):
+        window = jnp.concatenate([window_ref[q, part] for q in range(shares)], 0)
+        beamed.append(window.astype(F32) * beam_ref[:, pl.ds(part * wide, wide)])
+    left = jnp.concatenate(beamed[: parts // 2], 1)
+    right = jnp.concatenate(beamed[parts // 2 :], 1)
     for odd in (0, 1):
         folded = (left - right if odd else left + right).astype(BF16)
         for part in range(blocks // 2):
+            stream.take()
             spectrum = dot(folded, table_ref[odd, :, pl.ds(256 * part, 256)]).astype(BF16)
             out_ref[odd * blocks + 2 * part] = spectrum[:, :128]
             out_ref[odd * blocks + 2 * part + 1] = spectrum[:, 128:]
 
 
-def column_kernel(me_ref, x_ref, weight_ref, c0, s0, c1, s1, c1t, s1t, out_ref, upper, lower):
+def column_kernel(me_ref, x_ref, weight_ref, source_ref, out_ref, upper, lower, table_ref, sems):
+    c0, s0, c1, s1, c1t, s1t = (table_ref.at[t] for t in range(6))
     points = x_ref.shape[0]
     half = points // 2
+    places = [
+        (t, pl.ds(256 * m, 256))
+        for pair in (0, 2, 4)
+        for m in range(half // 256)
+        for t in (pair, pair + 1)
+    ]
+    stream = Stream(
+        [(source_ref.at[t, rows], table_ref.at[t, rows]) for t, rows in places], sems
+    )
     scale = 1.0 / float(points * points)
     lane = lax.broadcasted_iota(jnp.int32, (256, 128), 1)
     sign = jnp.where(lane < 64, -1.0, 1.0)
@@ -172,8 +213,10 @@
         folded = (first - second if odd else first + second).astype(BF16)
         for m in range(half // 256):
             rows = pl.ds(256 * m, 256)
-            by_cos = dot((c1 if odd else c0)[rows], folded)
-            by_sin = dot((s1 if odd else s0)[rows], folded)
+            stream.take()
+            stream.take()
+            by_cos = dot((c1 if odd else c0)[rows, :], folded)
+            by_sin = dot((s1 if odd else s0)[rows, :], folded)
             weight = weight_ref[pl.ds(odd * half + 256 * m, 256)].astype(F32) * scale
             up = weight * (by_cos + jnp.where(packed, 0.0, sign * pltpu.roll(by_sin, 64, 1)))
             down = jnp.where(packed, weight * by_sin, -sign * pltpu.roll(up, 64, 1))
@@ -181,20 +224,28 @@
             lower[odd, rows] = down.astype(BF16)
     for m in range(half // 256):
         rows = pl.ds(256 * m, 256)
-        even = dot(c0[rows], upper[0]) + dot(s0[rows], lower[0])
-        odd = dot(c1t[rows], upper[1]) + dot(s1t[rows], lower[1])
+        stream.take()
+        stream.take()
+        even = dot(c0[rows, :], upper[0]) + dot(s0[rows, :], lower[0])
+        odd = dot(c1t[rows, :], upper[1]) + dot(s1t[rows, :], lower[1])
         out_ref[rows] = (even + odd).astype(BF16)
         out_ref[pl.ds(half + 256 * m, 256)] = (even - odd).astype(BF16)
 
 
-def pixel_kernel(x_ref, beam_ref, table_ref, out_ref):
+def pixel_kernel(x_ref, beam_ref, source_ref, out_ref, table_ref, sems):
     blocks, rows, _ = x_ref.shape
     half = beam_ref.shape[1] // 2
     share = out_ref.shape[2]
+    places = [(odd, pl.ds(share * part, share)) for part in range(half // share) for odd in (0, 1)]
+    stream = Stream(
+        [(source_ref.at[odd, lanes], table_ref.at[odd, lanes]) for odd, lanes in places], sems
+    )
     even = jnp.concatenate([x_ref[b] for b in range(blocks // 2)], 1)
     odd = jnp.concatenate([x_ref[b] for b in range(blocks // 2, blocks)], 1)
     for part in range(half // share):
         lanes = pl.ds(share * part, share)
+        stream.take()
+        stream.take()
         by_even = dot(even, table_ref[0, lanes, :], NT)
         by_odd = dot(odd, table_ref[1, lanes, :], NT)
         out_ref[part] = (beam_ref[:, lanes] * (by_even + by_odd)).astype(BF16)
@@ -233,23 +284,32 @@
     return jax.ShapeDtypeStruct(dims, dtype)
 
 
+IMG = ("s", "b")
+
+
 def shards(image, beam, counts, offsets):
     points = counts.shape[1]
-    devices = lax.axis_size("img")
+    laps, parts = lax.axis_size("s"), lax.axis_size("b")
+    devices = laps * parts
     pointings = lax.axis_size("ptg")
     rows = points // devices
     tile = image.shape[1]
-    me = lax.axis_index("img").astype(jnp.int32)
+    me = lax.axis_index(IMG).astype(jnp.int32)
     ptg = lax.axis_index("ptg").astype(jnp.int32)
     start = offsets[0]
     place = me.reshape(1)
 
-    tiles = lax.all_to_all(image, "img", split_axis=0, concat_axis=0, tiled=True)
-    tiles = tiles.reshape(devices, rows, tile)
-
     starts = jnp.where(jnp.arange(pointings) == ptg, start, 0)
-    for bit in (1, 2, 4):
-        starts = starts + lax.ppermute(starts, "ptg", [(p, p ^ bit) for p in range(pointings)])
+    near = [
+        lax.ppermute(starts, "ptg", [(p, p ^ bit) for p in range(pointings)]) for bit in (1, 2, 3)
+    ]
+    starts = starts + near[0] + near[1] + near[2]
+    starts = starts + lax.ppermute(starts, "ptg", [(p, p ^ 4) for p in range(pointings)])
+
+    share_rows = rows // pointings
+    shares = image.reshape(laps, parts, pointings, share_rows, tile)
+    shares = lax.dynamic_index_in_dim(shares, ptg, 2, keepdims=False)
+    shares = lax.all_to_all(shares, "s", split_axis=0, concat_axis=0, tiled=True)
 
     choice = bf16(lane_choice(counts.shape[2]))
     choice = jnp.where(me < devices // 2, choice[0], choice[1])
@@ -264,10 +324,10 @@
         bf16(first_lane),
         flops=points * 128 * 512,
     )
-    got = lax.ppermute(send, "img", [(i, devices - 1 - i) for i in range(devices)])
+    got = lax.ppermute(send, IMG, [(i, devices - 1 - i) for i in range(devices)])
     edge = lax.ppermute(
         edge,
-        "img",
+        IMG,
         [(i, (devices - i) % (devices // 2)) for i in range(devices // 2, devices)],
     )
     direct, negated = row_choice()
@@ -288,43 +348,64 @@
 
     twice = jnp.concatenate([beam[0], beam[0]], 1)
     turned = lax.dynamic_slice_in_dim(twice, (points - start % points) % points, points, 1)
+    picked = call(
+        functools.partial(pick_kernel, points),
+        shape(pointings, parts, share_rows, tile),
+        [SMEM, SMEM, VMEM],
+        lax.axis_index("b").astype(jnp.int32).reshape(1),
+        starts,
+        shares,
+        moved=1 << 20,
+    )
+    window = lax.all_to_all(
+        picked.reshape(pointings * parts, share_rows, tile),
+        ("ptg", "b"),
+        split_axis=0,
+        concat_axis=0,
+        tiled=True,
+    ).reshape(pointings, parts, share_rows, tile)
+    window, weight, turned = lax.optimization_barrier((window, weight, turned))
     row_table = bf16(row_tables(points, devices))
-    tiles, weight, starts = lax.optimization_barrier((tiles, weight, starts))
+    table_scratch = lambda tables, pieces: [
+        pltpu.VMEM((tables, points // 2, points // 2), BF16),
+        pltpu.SemaphoreType.DMA((pieces,)),
+    ]
     spectrum = call(
         row_kernel,
         shape(devices, rows, 128),
-        [SMEM] + [VMEM] * 3,
-        start.reshape(1),
-        tiles,
+        [VMEM, VMEM, HBM],
+        window,
         turned,
         row_table,
+        scratch=table_scratch(2, 8),
         flops=rows * points * points,
     )
-    col = lax.all_to_all(spectrum, "img", split_axis=0, concat_axis=0, tiled=True)
+    col = lax.all_to_all(spectrum, IMG, split_axis=0, concat_axis=0, tiled=True)
     back = call(
         column_kernel,
         shape(points, 128),
-        [SMEM] + [VMEM] * 8,
+        [SMEM, VMEM, VMEM, HBM],
         place,
         col.reshape(points, 128),
         weight,
-        *[bf16(t) for t in column_tables(points)],
-        scratch=[pltpu.VMEM((2, points // 2, 128), BF16)] * 2,
+        bf16(np.stack(column_tables(points))),
+        scratch=[pltpu.VMEM((2, points // 2, 128), BF16)] * 2 + table_scratch(6, 24),
         flops=8 * points * points * 128 // 2,
         moved=16 << 20,
-        limit=24,
+        limit=28,
     )
     lines = lax.all_to_all(
-        back.reshape(devices, rows, 128), "img", split_axis=0, concat_axis=0, tiled=True
+        back.reshape(devices, rows, 128), IMG, split_axis=0, concat_axis=0, tiled=True
     )
     share = points // pointings
     contribution = call(
         pixel_kernel,
         shape(pointings, rows, share),
-        [VMEM] * 3,
+        [VMEM, VMEM, HBM],
         lines,
         turned,
         row_table,
+        scratch=table_scratch(2, 8),
         flops=rows * points * points,
     )
     terms = lax.all_to_all(contribution, "ptg", split_axis=0, concat_axis=0, tiled=True)
@@ -337,8 +418,8 @@
         terms,
         moved=1 << 20,
     )
-    other = lax.ppermute(theirs, "img", [(i, i ^ 1) for i in range(devices)])
-    per_lap = points // tile
+    other = lax.ppermute(theirs, IMG, [(i, i ^ 1) for i in range(devices)])
+    per_lap = parts
     halves = tile // share
     received = []
     for turn in range(2):
@@ -348,7 +429,7 @@
                 lap = 2 * (i % 2) + (turn ^ (q % 2))
                 pairs.append((q * devices + i, (i // 2) * devices + per_lap * lap + q // halves))
         block = jnp.concatenate([mine[turn], other[turn]], 0)
-        received.append(lax.ppermute(block, ("ptg", "img"), pairs))
+        received.append(lax.ppermute(block, ("ptg", *IMG), pairs))
     lap = me // per_lap
     out = jnp.where(
         lap % 2 == 1,
@@ -360,10 +441,12 @@
 
 
 def solution(mesh):
+    pointings, devices = mesh.devices.shape
+    split = Mesh(mesh.devices.reshape(pointings, 4, devices // 4), ("ptg", *IMG))
     return jax.shard_map(
         shards,
-        mesh=mesh,
-        in_specs=(P(None, "img"), P("ptg", "img", None), P("ptg", None, "img"), P("ptg")),
-        out_specs=P("ptg", "img"),
+        mesh=split,
+        in_specs=(P(None, IMG), P("ptg", IMG, None), P("ptg", None, IMG), P("ptg")),
+        out_specs=P("ptg", IMG),
         check_vma=False,
     )

time: 124 us -> 134 us (1.081)
  Pallas kernels: 11.5 us -> 20 us
  local copies, waits for them, and re-layouts: 8.72 us -> 11.6 us
  blocking collectives: 31.1 us -> 28.9 us
  waiting for transfers between devices: 36.2 us -> 34.4 us
  starting transfers between devices: 31.6 us -> 33.4 us
    pallas_call x6 -> x7, Pallas kernels: 11.5 us -> 20 us  [call(): pl.pallas_call(kernel, out_shape=outs, in_specs=specs, out_specs=jax.tree...]
    all_to_all x1 -> x2, starting transfers between devices: 6.67 us -> 14.2 us  [the longest x1 7.66 us: shards(): lax.all_to_all(picked.reshape(pointings * parts, share_rows, tile), ('ptg...]
    ppermute x3, waiting for transfers between devices: 3.73 us -> 0.01 us  [shards(): lax.ppermute(starts, 'ptg', [(p, p ^ bit) for p in range(pointings)])]
    ppermute x5 -> x6, starting transfers between devices: 11.2 us -> 8.66 us  [the longest x2 4.05 us: shards(): received.append(lax.ppermute(block, ('ptg', *IMG), pairs))]
    all_to_all x2, blocking collectives: 31.1 us -> 28.9 us  [the longest x1 15 us: shards(): lax.all_to_all(back.reshape(devices, rows, 128), IMG, split_axis=0, conca...]
    unnamed x38 -> x28, local copies, waits for them, and re-layouts: 8.66 us -> 10.8 us
    ppermute x3, starting transfers between devices: 6.92 us -> 4.98 us  [shards(): lax.ppermute(starts, 'ptg', [(p, p ^ bit) for p in range(pointings)])]
    all_to_all x1 -> x2, waiting for transfers between devices: 0.01 us -> 1.65 us  [the longest x1 1.64 us: shards(): lax.all_to_all(shares, 's', split_axis=0, concat_axis=0, tiled=True)]
  transfers between devices with their start and end apart: 10 -> 12, of which waited for: 8 -> 8; matrix products, arithmetic and copies ran while one was open for 2% -> 3% of each run, Pallas kernels for 2% -> 2%
where the time goes in v4:
time: 134 us; the launch traced here: 133 us
  waiting for transfers between devices  34.4 us (26%)
  starting transfers between devices  33.4 us (25%)
  blocking collectives  28.9 us (22%)
  Pallas kernels  20 us (15%)
  local copies, waits for them, and re-layouts  11.6 us (9%)
  other arithmetic  3.85 us (3%)
    pallas_call x7, Pallas kernels, call(): pl.pallas_call(kernel, out_shape=outs, in_specs=specs, out_specs=jax.tree...  20 us
    all_to_all x1, blocking collectives, shards(): lax.all_to_all(back.reshape(devices, rows, 128), IMG, split_axis=0, conca...  15 us
    all_to_all x1, blocking collectives, shards(): col = lax.all_to_all(spectrum, IMG, split_axis=0, concat_axis=0, tiled=True)  14 us
    ppermute x2, waiting for transfers between devices, shards(): received.append(lax.ppermute(block, ('ptg', *IMG), pairs))  12 us
    unnamed x28, local copies, waits for them, and re-layouts  10.8 us
    all_to_all x1, waiting for transfers between devices, shards(): lax.all_to_all(contribution, 'ptg', split_axis=0, concat_axis=0, tiled=True)  9.35 us
    all_to_all x1, starting transfers between devices, shards(): lax.all_to_all(picked.reshape(pointings * parts, share_rows, tile), ('ptg...  7.66 us
    all_to_all x1, starting transfers between devices, shards(): lax.all_to_all(shares, 's', split_axis=0, concat_axis=0, tiled=True)  6.53 us
  transfers between devices with their start and end apart: 12, of which 8 were waited for; matrix products, arithmetic and copies ran while one was open for 3% of the time, Pallas kernels for 2%

profile of v4, /device:TPU:14, one launch (start us, length us, event | category | flops | bytes accessed | tf_op | source)
XLA Modules:
  0.0 133.4 jit_solution(15820061506795950588)
XLA Ops:
  0.8 4.0 %collective-permute-start.1 = (s32[8]{0:T(128)S(1)}, s32[8]{0:T(128)S(1)}, u32[]{:S(2)}, u32[]{:S(2)}) collective-permute-start(s32[8]{0:T(128)S(1)} %compare_select_fusion), channel_id=1, source_target_pairs={{0,32},{16,48},{32,0},{48,16},{64,96},{80,112},{96,64},{112,80},{1... | collective-permute-start | bytes 104 | tf_op jit(solution)/shard_map/ppermute | solution.py:304
  6.5 6.5 %all-to-all-start = ((bf16[4,4,16,512]{3,2,1,0:T(8,128)(2,1)}), bf16[4,4,16,512]{3,2,1,0:T(8,128)(2,1)S(1)}, u32[]{:S(2)}, u32[]{:S(2)}) async-start(bf16[4,4,16,512]{3,2,1,0:T(8,128)(2,1)} %dynamic-slice_bitcast_fusion), calls=%async_computation | async-start | bytes 524288 | tf_op jit(solution)/shard_map/all_to_all | solution.py:312
  13.1 1.4 %collective-permute-start.3 = (s32[8]{0:T(128)S(1)}, s32[8]{0:T(128)S(1)}, u32[]{:S(2)}, u32[]{:S(2)}) collective-permute-start(s32[8]{0:T(128)S(1)} %add_add_fusion), channel_id=1, source_target_pairs={{0,64},{16,80},{32,96},{48,112},{64,0},{80,16},{96,32},{112,48},{1... | collective-permute-start | bytes 104 | tf_op jit(solution)/shard_map/ppermute | solution.py:307
  14.5 3.0 %collective-permute-done.3 = s32[8]{0:T(128)S(1)} collective-permute-done((s32[8]{0:T(128)S(1)}, s32[8]{0:T(128)S(1)}, u32[]{:S(2)}, u32[]{:S(2)}) %collective-permute-start.3) | collective-permute-done | bytes 64 | tf_op jit(solution)/shard_map/ppermute | solution.py:307
  17.5 1.6 %all-to-all-done.tiles_ref = bf16[4,4,16,512]{3,2,1,0:T(8,128)(2,1)S(1)} async-done(((bf16[4,4,16,512]{3,2,1,0:T(8,128)(2,1)}), bf16[4,4,16,512]{3,2,1,0:T(8,128)(2,1)S(1)}, u32[]{:S(2)}, u32[]{:S(2)}) %all-to-all-start) | async-done | bytes 262176 | tf_op jit(solution)/shard_map/all_to_all | solution.py:312
  19.2 2.0 %shard_map.109 = bf16[8,4,16,512]{3,2,1,0:T(8,128)(2,1)} custom-call(s32[1]{0:T(128)} %bitcast.4.place_ref, s32[8]{0:T(128)S(1)} %add.42.starts_ref, bf16[4,4,16,512]{3,2,1,0:T(8,128)(2,1)S(1)} %all-to-all-done.tiles_ref), custom_call_target="tpu_custom_call" | custom-call | bytes 1048576 | tf_op jit(solution)/shard_map/pallas_call | solution.py:272
  21.2 7.7 %all-to-all-start.1 = ((bf16[32,16,512]{2,1,0:T(8,128)(2,1)}), bf16[32,16,512]{2,1,0:T(8,128)(2,1)}, u32[]{:S(2)}, u32[]{:S(2)}) async-start(bf16[32,16,512]{2,1,0:T(8,128)(2,1)} %bitcast.7), calls=%async_computation.1 | async-start | bytes 1048576 | tf_op jit(solution)/shard_map/all_to_all | solution.py:360
  28.8 0.9 select_bitcast_fusion.choice_ref
  29.7 1.2 shard_map.110
  30.9 0.8 copy-done.8
  31.7 1.8 %collective-permute-start.4 = (bf16[1024,128]{1,0:T(8,128)(2,1)}, bf16[1024,128]{1,0:T(8,128)(2,1)S(1)}, u32[]{:S(2)}, u32[]{:S(2)}) collective-permute-start(bf16[1024,128]{1,0:T(8,128)(2,1)} %get-tuple-element.14), channel_id=1, source_target_pairs={{0,15},{1,14},{2,13},{3,12},{4,11},{5,10},{6,9},{7,8},{8,7},{9,6},... | collective-permute-start | bytes 786440 | tf_op jit(solution)/shard_map/ppermute | solution.py:327
  33.6 1.3 collective-permute-start.5
  34.9 1.9 %fusion.beam_ref = f32[128,2048]{1,0:T(8,128)S(1)} fusion(s32[]{:T(128)S(6)} %select_n.72, f32[128,2048]{1,0:T(8,128)} %bitcast.35), kind=kLoop, calls=%fused_computation.2 | loop fusion | flops 262144 | bytes 2097156 | tf_op jit(solution)/shard_map/concatenate | solution.py:349
  36.8 6.3 %collective-permute-done.5.edge_ref = bf16[16,128]{1,0:T(8,128)(2,1)S(1)} collective-permute-done((bf16[16,128]{1,0:T(8,128)(2,1)S(1)}, bf16[16,128]{1,0:T(8,128)(2,1)S(1)}, u32[]{:S(2)}, u32[]{:S(2)}) %collective-permute-start.5) | collective-permute-done | bytes 4128 | tf_op jit(solution)/shard_map/ppermute | solution.py:328
  43.1 0.8 collective-permute-done.4.got_ref
  43.9 0.9 copy-done.11
  45.6 1.3 %shard_map.111.weight_ref = bf16[2048,128]{1,0:T(8,128)(2,1)S(1)} custom-call(s32[1]{0:T(128)} %bitcast.3.me_ref, bf16[2048,128]{1,0:T(8,128)(2,1)S(1)} %copy-done.9, bf16[1024,128]{1,0:T(8,128)(2,1)S(1)} %collective-permute-done.4.got_ref, bf16[16,128]{1,0:T(8,128)(2,1)S(1)} %collective-permute-done.5.edge_ref, bf16[128,128]{1,0:T(8,128)(2,1)S(1)} %copy-done.12, ...), custom_call_target="tpu_custom_call" | custom-call | flops 268435456 | bytes 4194304 | tf_op jit(solution)/shard_map/pallas_call | solution.py:272
  47.7 2.2 %copy-done.1 = bf16[2,1024,1024]{2,1,0:T(8,128)(2,1)S(1)} copy-done((bf16[2,1024,1024]{2,1,0:T(8,128)(2,1)S(1)}, bf16[2,1024,1024]{2,1,0:T(8,128)(2,1)}, u32[]{:S(2)}) %copy-start.1) | copy-done | bytes 4194328
  49.9 4.2 %shard_map.112 = bf16[16,128,128]{2,1,0:T(8,128)(2,1)S(1)} custom-call(bf16[8,4,16,512]{3,2,1,0:T(8,128)(2,1)} %bitcast.8.window_ref, f32[128,2048]{1,0:T(8,128)S(1)} %fusion.beam_ref, bf16[2,1024,1024]{2,1,0:T(8,128)(2,1)S(1)} %copy-done.1), custom_call_target="tpu_custom_call" | custom-call | flops 536870912 | bytes 4194304 | tf_op jit(solution)/shard_map/pallas_call | solution.py:272
  54.1 14.0 %all_to_all.25 = bf16[16,128,128]{2,1,0:T(8,128)(2,1)S(1)} all-to-all(bf16[16,128,128]{2,1,0:T(8,128)(2,1)S(1)} %shard_map.112), channel_id=1, replica_groups=mesh['ptg'=8,'s'=4,'b'=4] {'s','b'}, dimensions={0} | all-to-all | bytes 1048576 | tf_op jit(solution)/shard_map/all_to_all | solution.py:383
  68.1 4.6 %copy-done.3 = bf16[6,1024,1024]{2,1,0:T(8,128)(2,1)S(1)} copy-done((bf16[6,1024,1024]{2,1,0:T(8,128)(2,1)S(1)}, bf16[6,1024,1024]{2,1,0:T(8,128)(2,1)}, u32[]{:S(2)}) %copy-start.3) | copy-done | bytes 12582936
  72.6 8.0 %shard_map.113 = bf16[2048,128]{1,0:T(8,128)(2,1)S(1)} custom-call(s32[1]{0:T(128)} %bitcast.3.me_ref, bf16[2048,128]{1,0:T(8,128)(2,1)S(1)} %bitcast.32, bf16[2048,128]{1,0:T(8,128)(2,1)S(1)} %copy-done.6, bf16[6,1024,1024]{2,1,0:T(8,128)(2,1)S(1)} %copy-done.3), custom_call_target="tpu_custom_call" | custom-call | flops 2147483648 | bytes 16777216 | tf_op jit(solution)/shard_map/pallas_call | solution.py:272
  80.6 15.0 %all_to_all.26.x_ref = bf16[16,128,128]{2,1,0:T(8,128)(2,1)S(1)} all-to-all(bf16[16,128,128]{2,1,0:T(8,128)(2,1)S(1)} %bitcast.33), channel_id=1, replica_groups=mesh['ptg'=8,'s'=4,'b'=4] {'s','b'}, dimensions={0} | all-to-all | bytes 1048576 | tf_op jit(solution)/shard_map/all_to_all | solution.py:397
  95.6 2.3 %shard_map.114 = bf16[8,128,256]{2,1,0:T(8,128)(2,1)S(1)} custom-call(bf16[16,128,128]{2,1,0:T(8,128)(2,1)S(1)} %all_to_all.26.x_ref, f32[128,2048]{1,0:T(8,128)S(1)} %fusion.beam_ref, bf16[2,1024,1024]{2,1,0:T(8,128)(2,1)S(1)} %copy-done.2), custom_call_target="tpu_custom_call" | custom-call | flops 536870912 | bytes 4194304 | tf_op jit(solution)/shard_map/pallas_call | solution.py:272
  98.7 5.6 %all-to-all-start.4 = ((bf16[8,128,256]{2,1,0:T(8,128)(2,1)}), bf16[8,128,256]{2,1,0:T(8,128)(2,1)S(1)}, u32[]{:S(2)}, u32[]{:S(2)}) async-start(bf16[8,128,256]{2,1,0:T(8,128)(2,1)} %copy-done.4), calls=%async_computation.4 | async-start | bytes 1048576 | tf_op jit(solution)/shard_map/all_to_all | solution.py:411
  104.4 9.4 %all-to-all-done.4.terms_ref = bf16[8,128,256]{2,1,0:T(8,128)(2,1)S(1)} async-done(((bf16[8,128,256]{2,1,0:T(8,128)(2,1)}), bf16[8,128,256]{2,1,0:T(8,128)(2,1)S(1)}, u32[]{:S(2)}, u32[]{:S(2)}) %all-to-all-start.4) | async-done | bytes 524320 | tf_op jit(solution)/shard_map/all_to_all | solution.py:411
  113.8 1.0 shard_map.115
  114.9 1.3 collective-permute-done.6
  116.2 4.0 %collective-permute-start.8 = (bf16[256,256]{1,0:T(8,128)(2,1)S(1)}, bf16[256,256]{1,0:T(8,128)(2,1)S(1)}, u32[]{:S(2)}, u32[]{:S(2)}) collective-permute-start(bf16[256,256]{1,0:T(8,128)(2,1)S(1)} %pad_maximum_fusion.1), channel_id=1, source_target_pairs={{0,0},{1,8},{2,16},{3,24},{4,32},{5,40},{6,48},{7,56},{8,64},{9,72... | collective-permute-start | bytes 393224 | tf_op jit(solution)/shard_map/ppermute | solution.py:432
  120.3 8.5 %collective-permute-done.8 = bf16[256,256]{1,0:T(8,128)(2,1)S(1)} collective-permute-done((bf16[256,256]{1,0:T(8,128)(2,1)S(1)}, bf16[256,256]{1,0:T(8,128)(2,1)S(1)}, u32[]{:S(2)}, u32[]{:S(2)}) %collective-permute-start.8) | collective-permute-done | bytes 131104 | tf_op jit(solution)/shard_map/ppermute | solution.py:432
  128.8 3.5 %collective-permute-done.7 = bf16[256,256]{1,0:T(8,128)(2,1)S(1)} collective-permute-done((bf16[256,256]{1,0:T(8,128)(2,1)S(1)}, bf16[256,256]{1,0:T(8,128)(2,1)S(1)}, u32[]{:S(2)}, u32[]{:S(2)}) %collective-permute-start.7) | collective-permute-done | bytes 131104 | tf_op jit(solution)/shard_map/ppermute | solution.py:432
  132.5 0.9 maximum_select_fusion
  (43 shorter events, 4.6 us)
Async XLA Ops:
  0.0 5.8 %copy-start = (bf16[2048,512]{1,0:T(8,128)(2,1)S(1)}, bf16[2048,512]{1,0:T(8,128)(2,1)}, u32[]{:S(2)}) copy-start(bf16[2048,512]{1,0:T(8,128)(2,1)} %param.11) | copy-start | bytes 6291460
  0.0 29.7 %copy-start.13 = (bf16[16,128]{1,0:T(8,128)(2,1)S(1)}, bf16[16,128]{1,0:T(8,128)(2,1)}, u32[]{:S(2)}) copy-start(bf16[16,128]{1,0:T(8,128)(2,1)} %constant.83.clone.first_ref) | copy-start | bytes 12292
  0.0 29.7 %copy-start.7 = (s32[1,2048,128]{2,1,0:T(8,128)S(1)}, s32[1,2048,128]{2,1,0:T(8,128)}, u32[]{:S(2)}) copy-start(s32[1,2048,128]{2,1,0:T(8,128)} %param.13) | copy-start | bytes 3145732
  0.8 12.2 %collective-permute-start.1 = (s32[8]{0:T(128)S(1)}, s32[8]{0:T(128)S(1)}, u32[]{:S(2)}, u32[]{:S(2)}) collective-permute-start(s32[8]{0:T(128)S(1)} %compare_select_fusion), channel_id=1, source_target_pairs={{0,32},{16,48},{32,0},{48,16},{64,96},{80,112},{96,64},{112,80},{1... | collective-permute-start | bytes 104 | tf_op jit(solution)/shard_map/ppermute | solution.py:304
  4.8 8.3 %collective-permute-start.2 = (s32[8]{0:T(128)S(1)}, s32[8]{0:T(128)S(1)}, u32[]{:S(2)}, u32[]{:S(2)}) collective-permute-start(s32[8]{0:T(128)S(1)} %compare_select_fusion), channel_id=1, source_target_pairs={{0,48},{16,32},{32,16},{48,0},{64,112},{80,96},{96,80},{112,64},{1... | collective-permute-start | bytes 104 | tf_op jit(solution)/shard_map/ppermute | solution.py:304
  5.5 7.6 %collective-permute-start = (s32[8]{0:T(128)S(1)}, s32[8]{0:T(128)S(1)}, u32[]{:S(2)}, u32[]{:S(2)}) collective-permute-start(s32[8]{0:T(128)S(1)} %compare_select_fusion), channel_id=1, source_target_pairs={{0,16},{16,0},{32,48},{48,32},{64,80},{80,64},{96,112},{112,96},{1... | collective-permute-start | bytes 104 | tf_op jit(solution)/shard_map/ppermute | solution.py:304
  6.5 12.7 %all-to-all-start = ((bf16[4,4,16,512]{3,2,1,0:T(8,128)(2,1)}), bf16[4,4,16,512]{3,2,1,0:T(8,128)(2,1)S(1)}, u32[]{:S(2)}, u32[]{:S(2)}) async-start(bf16[4,4,16,512]{3,2,1,0:T(8,128)(2,1)} %dynamic-slice_bitcast_fusion), calls=%async_computation | async-start | bytes 524288 | tf_op jit(solution)/shard_map/all_to_all | solution.py:312
  13.1 4.5 %collective-permute-start.3 = (s32[8]{0:T(128)S(1)}, s32[8]{0:T(128)S(1)}, u32[]{:S(2)}, u32[]{:S(2)}) collective-permute-start(s32[8]{0:T(128)S(1)} %add_add_fusion), channel_id=1, source_target_pairs={{0,64},{16,80},{32,96},{48,112},{64,0},{80,16},{96,32},{112,48},{1... | collective-permute-start | bytes 104 | tf_op jit(solution)/shard_map/ppermute | solution.py:307
  21.2 22.7 %copy-start.10 = (bf16[256,256]{1,0:T(8,128)(2,1)S(1)}, bf16[256,256]{1,0:T(8,128)(2,1)}, u32[]{:S(2)}) copy-start(bf16[256,256]{1,0:T(8,128)(2,1)} %constant.86.clone.negated_ref) | copy-start | bytes 393220
  21.2 26.6 %all-to-all-start.1 = ((bf16[32,16,512]{2,1,0:T(8,128)(2,1)}), bf16[32,16,512]{2,1,0:T(8,128)(2,1)}, u32[]{:S(2)}, u32[]{:S(2)}) async-start(bf16[32,16,512]{2,1,0:T(8,128)(2,1)} %bitcast.7), calls=%async_computation.1 | async-start | bytes 1048576 | tf_op jit(solution)/shard_map/all_to_all | solution.py:360
  30.9 0.8 copy-start.8
  31.7 12.1 %collective-permute-start.4 = (bf16[1024,128]{1,0:T(8,128)(2,1)}, bf16[1024,128]{1,0:T(8,128)(2,1)S(1)}, u32[]{:S(2)}, u32[]{:S(2)}) collective-permute-start(bf16[1024,128]{1,0:T(8,128)(2,1)} %get-tuple-element.14), channel_id=1, source_target_pairs={{0,15},{1,14},{2,13},{3,12},{4,11},{5,10},{6,9},{7,8},{8,7},{9,6},... | collective-permute-start | bytes 786440 | tf_op jit(solution)/shard_map/ppermute | solution.py:327
  33.6 9.5 %collective-permute-start.5 = (bf16[16,128]{1,0:T(8,128)(2,1)S(1)}, bf16[16,128]{1,0:T(8,128)(2,1)S(1)}, u32[]{:S(2)}, u32[]{:S(2)}) collective-permute-start(bf16[16,128]{1,0:T(8,128)(2,1)S(1)} %get-tuple-element.15), channel_id=1, source_target_pairs={{8,0},{9,7},{10,6},{11,5},{12,4},{13,3},{14,2},{15,1},{24,16},{25,... | collective-permute-start | bytes 12296 | tf_op jit(solution)/shard_map/ppermute | solution.py:328
  34.9 9.0 %copy-start.9 = (bf16[2048,128]{1,0:T(8,128)(2,1)S(1)}, bf16[2048,128]{1,0:T(8,128)(2,1)}, u32[]{:S(2)}) copy-start(bf16[2048,128]{1,0:T(8,128)(2,1)} %copy-done.8) | copy-start | bytes 1572868
  43.9 0.9 copy-start.11
  44.8 0.8 copy-start.12
  46.9 0.8 copy-start.5
  47.7 2.2 %copy-start.1 = (bf16[2,1024,1024]{2,1,0:T(8,128)(2,1)S(1)}, bf16[2,1024,1024]{2,1,0:T(8,128)(2,1)}, u32[]{:S(2)}) copy-start(bf16[2,1024,1024]{2,1,0:T(8,128)(2,1)} %constant.87.clone.source_ref) | copy-start | bytes 12582916
  49.9 18.1 %copy-start.6 = (bf16[2048,128]{1,0:T(8,128)(2,1)S(1)}, bf16[2048,128]{1,0:T(8,128)(2,1)}, u32[]{:S(2)}) copy-start(bf16[2048,128]{1,0:T(8,128)(2,1)} %copy-done.5) | copy-start | bytes 1572868
  68.1 4.6 %copy-start.3 = (bf16[6,1024,1024]{2,1,0:T(8,128)(2,1)S(1)}, bf16[6,1024,1024]{2,1,0:T(8,128)(2,1)}, u32[]{:S(2)}) copy-start(bf16[6,1024,1024]{2,1,0:T(8,128)(2,1)} %constant.88.clone.source_ref) | copy-start | bytes 37748740
  72.6 23.0 %copy-start.2 = (bf16[2,1024,1024]{2,1,0:T(8,128)(2,1)S(1)}, bf16[2,1024,1024]{2,1,0:T(8,128)(2,1)}, u32[]{:S(2)}) copy-start(bf16[2,1024,1024]{2,1,0:T(8,128)(2,1)} %constant.87.clone.source_ref) | copy-start | bytes 12582916
  97.9 0.8 copy-start.4
  98.7 15.0 %all-to-all-start.4 = ((bf16[8,128,256]{2,1,0:T(8,128)(2,1)}), bf16[8,128,256]{2,1,0:T(8,128)(2,1)S(1)}, u32[]{:S(2)}, u32[]{:S(2)}) async-start(bf16[8,128,256]{2,1,0:T(8,128)(2,1)} %copy-done.4), calls=%async_computation.4 | async-start | bytes 1048576 | tf_op jit(solution)/shard_map/all_to_all | solution.py:411
  114.8 1.4 %collective-permute-start.6 = (bf16[2,128,256]{2,1,0:T(8,128)(2,1)S(1)}, bf16[2,128,256]{2,1,0:T(8,128)(2,1)S(1)}, u32[]{:S(2)}, u32[]{:S(2)}) collective-permute-start(bf16[2,128,256]{2,1,0:T(8,128)(2,1)S(1)} %get-tuple-element.20), channel_id=1, source_target_pairs={{0,1},{1,0},{2,3},{3,2},{4,5},{5,4},{6,7},{7,6},{8,9},{9,8},{10,11... | collective-permute-start | bytes 393224 | tf_op jit(solution)/shard_map/ppermute | solution.py:421
  116.2 12.6 %collective-permute-start.8 = (bf16[256,256]{1,0:T(8,128)(2,1)S(1)}, bf16[256,256]{1,0:T(8,128)(2,1)S(1)}, u32[]{:S(2)}, u32[]{:S(2)}) collective-permute-start(bf16[256,256]{1,0:T(8,128)(2,1)S(1)} %pad_maximum_fusion.1), channel_id=1, source_target_pairs={{0,0},{1,8},{2,16},{3,24},{4,32},{5,40},{6,48},{7,56},{8,64},{9,72... | collective-permute-start | bytes 393224 | tf_op jit(solution)/shard_map/ppermute | solution.py:432
  120.2 12.1 %collective-permute-start.7 = (bf16[256,256]{1,0:T(8,128)(2,1)S(1)}, bf16[256,256]{1,0:T(8,128)(2,1)S(1)}, u32[]{:S(2)}, u32[]{:S(2)}) collective-permute-start(bf16[256,256]{1,0:T(8,128)(2,1)S(1)} %pad_maximum_fusion), channel_id=1, source_target_pairs={{0,4},{1,12},{2,20},{3,28},{4,36},{5,44},{6,52},{7,60},{8,68},{9,7... | collective-permute-start | bytes 393224 | tf_op jit(solution)/shard_map/ppermute | solution.py:432

commit v5 on v4

--- a/solution.py
+++ b/solution.py
@@ -61,35 +61,27 @@
     return jnp.asarray(np.asarray(table, np.float32).astype(jnp.bfloat16))
 
 
-def lane_choice(lanes):
-    half = lanes // 2
-    k = np.arange(half)
-    chosen = np.zeros((2, lanes, 2, 2, half), np.float32)
-    for copy in (0, 1):
-        chosen[0, 2 * k, 0, copy, k] = 1
-        chosen[0, 2 * k + 1, 1, copy, k] = 1
-        chosen[1, lanes - 1 - 2 * k, 0, copy, k] = 1
-        chosen[1, lanes - 2 * k[1:], 1, copy, k[1:]] = 1
-    return chosen.reshape(2, lanes, 4 * half)
-
-
-def row_choice():
-    k = np.arange(128)
-    direct, negated = np.zeros((256, 256), np.float32), np.zeros((256, 256), np.float32)
-    direct[k, 2 * k] = 1
-    direct[128 + k, 2 * k + 1] = 1
-    negated[k[1:], 256 - 2 * k[1:]] = 1
-    negated[128 + k, 255 - 2 * k] = 1
-    return direct, negated
-
-
-def choose_kernel(counts_ref, choice_ref, first_ref, own_ref, send_ref, edge_ref):
+def ones_where(condition):
+    return jnp.where(condition, 1.0, 0.0).astype(BF16)
+
+
+def grid(rows, lanes):
+    index = lambda axis: lax.broadcasted_iota(jnp.int32, (rows, lanes), axis)
+    return index(0), index(1)
+
+
+def choose_kernel(me_ref, counts_ref, own_ref, send_ref, edge_ref):
     points = counts_ref.shape[0]
+    source, target = grid(128, 256)
+    k, sent = target % 64, target // 128
+    choice = ones_where(source == jnp.where(me_ref[0] < 8, 2 * k, 127 - 2 * k) + sent)
+    unit_row, unit_lane = grid(16, 128)
+    first = ones_where((unit_row == 0) & (unit_lane == 0))
     lane = lax.broadcasted_iota(jnp.int32, (256, 128), 1)
     for b in range(points // 512):
         low = counts_ref[pl.ds(256 * b, 256)].astype(F32).astype(BF16)
         high = counts_ref[pl.ds(256 * b + points // 2, 256)].astype(F32).astype(BF16)
-        got_low, got_high = dot(low, choice_ref[...]), dot(high, choice_ref[...])
+        got_low, got_high = dot(low, choice), dot(high, choice)
         own_ref[pl.ds(256 * b, 256)] = got_low[:, :128].astype(BF16)
         own_ref[pl.ds(256 * b + points // 2, 256)] = got_high[:, :128].astype(BF16)
         send_ref[pl.ds(256 * b, 256)] = jnp.where(
@@ -98,15 +90,21 @@
     edges = []
     for b in range(points // 128):
         block = counts_ref[pl.ds(128 * b, 128)].astype(F32).astype(BF16)
-        edges.append(dot(first_ref[...], block, NT)[:1])
+        edges.append(dot(first, block, NT)[:1])
     edge_ref[...] = jnp.concatenate(edges, 0).astype(BF16)
 
 
-def weight_kernel(me_ref, own_ref, got_ref, edge_ref, eye_ref, direct_ref, negated_ref, out_ref, plus, minus):
+def weight_kernel(me_ref, own_ref, got_ref, edge_ref, out_ref, plus, minus):
     points = own_ref.shape[0]
+    target, source = grid(256, 256)
+    k, odd = target % 128, target // 128
+    direct = ones_where(source == 2 * k + odd)
+    negated = ones_where(source == 256 - 2 * k - odd)
+    row, column = grid(128, 128)
+    eye = ones_where(row == column)
     me = me_ref[0]
     low, zero = me < 8, me == 0
-    edge = dot(eye_ref[...], edge_ref[...], NT)
+    edge = dot(eye, edge_ref[...], NT)
     lane = lax.broadcasted_iota(jnp.int32, (128, 128), 1)
     for b in range(points // 128):
         rows = pl.ds(128 * b, 128)
@@ -128,8 +126,8 @@
     wide = lax.broadcasted_iota(jnp.int32, (256, 128), 1)
     scale = jnp.where(zero & (wide % 64 == 0), 0.5, 1.0)
     for b in range(blocks):
-        taken = dot(direct_ref[...], plus[pl.ds(256 * b, 256)])
-        taken += dot(negated_ref[...], minus[pl.ds(256 * (blocks - 1 - b), 256)].astype(BF16))
+        taken = dot(direct, plus[pl.ds(256 * b, 256)])
+        taken += dot(negated, minus[pl.ds(256 * (blocks - 1 - b), 256)].astype(BF16))
         wrapped = minus[pl.ds(256 * ((blocks - b) % blocks), 1)]
         taken = scale * (taken + jnp.where(row == 0, wrapped, 0.0))
         out_ref[pl.ds(128 * b, 128)] = taken[:128].astype(BF16)
@@ -171,11 +169,7 @@
 def row_kernel(window_ref, beam_ref, source_ref, out_ref, table_ref, sems):
     shares, parts, rows, wide = window_ref.shape
     blocks = out_ref.shape[0] // 2
-    places = [(odd, pl.ds(256 * part, 256)) for odd in (0, 1) for part in range(blocks // 2)]
-    stream = Stream(
-        [(source_ref.at[odd, :, lanes], table_ref.at[odd, :, lanes]) for odd, lanes in places],
-        sems,
-    )
+    stream = Stream([(source_ref.at[n], table_ref.at[n]) for n in range(blocks)], sems)
     beamed = []
     for part in range(parts):
         window = jnp.concatenate([window_ref[q, part] for q in range(shares)], 0)
@@ -186,7 +180,7 @@
         folded = (left - right if odd else left + right).astype(BF16)
         for part in range(blocks // 2):
             stream.take()
-            spectrum = dot(folded, table_ref[odd, :, pl.ds(256 * part, 256)]).astype(BF16)
+            spectrum = dot(folded, table_ref[odd * blocks // 2 + part]).astype(BF16)
             out_ref[odd * blocks + 2 * part] = spectrum[:, :128]
             out_ref[odd * blocks + 2 * part + 1] = spectrum[:, 128:]
 
@@ -232,20 +226,14 @@
         out_ref[pl.ds(half + 256 * m, 256)] = (even - odd).astype(BF16)
 
 
-def pixel_kernel(x_ref, beam_ref, source_ref, out_ref, table_ref, sems):
+def pixel_kernel(x_ref, beam_ref, table_ref, out_ref):
     blocks, rows, _ = x_ref.shape
     half = beam_ref.shape[1] // 2
     share = out_ref.shape[2]
-    places = [(odd, pl.ds(share * part, share)) for part in range(half // share) for odd in (0, 1)]
-    stream = Stream(
-        [(source_ref.at[odd, lanes], table_ref.at[odd, lanes]) for odd, lanes in places], sems
-    )
     even = jnp.concatenate([x_ref[b] for b in range(blocks // 2)], 1)
     odd = jnp.concatenate([x_ref[b] for b in range(blocks // 2, blocks)], 1)
     for part in range(half // share):
         lanes = pl.ds(share * part, share)
-        stream.take()
-        stream.take()
         by_even = dot(even, table_ref[0, lanes, :], NT)
         by_odd = dot(odd, table_ref[1, lanes, :], NT)
         out_ref[part] = (beam_ref[:, lanes] * (by_even + by_odd)).astype(BF16)
@@ -300,48 +288,38 @@
     place = me.reshape(1)
 
     starts = jnp.where(jnp.arange(pointings) == ptg, start, 0)
+    share_rows = rows // pointings
+    shares = image.reshape(laps, parts, pointings, share_rows, tile)
+    shares = lax.dynamic_index_in_dim(shares, ptg, 2, keepdims=False)
+    own, send, edge = call(
+        choose_kernel,
+        (shape(points, 128), shape(points // 2, 128), shape(points // 128, 128)),
+        [SMEM, VMEM],
+        place,
+        counts[0],
+        flops=points * 128 * 512,
+    )
+    shares, send, edge, starts = lax.optimization_barrier((shares, send, edge, starts))
+    shares = lax.all_to_all(shares, "s", split_axis=0, concat_axis=0, tiled=True)
     near = [
         lax.ppermute(starts, "ptg", [(p, p ^ bit) for p in range(pointings)]) for bit in (1, 2, 3)
     ]
     starts = starts + near[0] + near[1] + near[2]
     starts = starts + lax.ppermute(starts, "ptg", [(p, p ^ 4) for p in range(pointings)])
-
-    share_rows = rows // pointings
-    shares = image.reshape(laps, parts, pointings, share_rows, tile)
-    shares = lax.dynamic_index_in_dim(shares, ptg, 2, keepdims=False)
-    shares = lax.all_to_all(shares, "s", split_axis=0, concat_axis=0, tiled=True)
-
-    choice = bf16(lane_choice(counts.shape[2]))
-    choice = jnp.where(me < devices // 2, choice[0], choice[1])
-    first_lane = np.zeros((16, 128), np.float32)
-    first_lane[0, 0] = 1
-    own, send, edge = call(
-        choose_kernel,
-        (shape(points, 128), shape(points // 2, 128), shape(points // 128, 128)),
-        [VMEM] * 3,
-        counts[0],
-        choice,
-        bf16(first_lane),
-        flops=points * 128 * 512,
-    )
     got = lax.ppermute(send, IMG, [(i, devices - 1 - i) for i in range(devices)])
     edge = lax.ppermute(
         edge,
         IMG,
         [(i, (devices - i) % (devices // 2)) for i in range(devices // 2, devices)],
     )
-    direct, negated = row_choice()
     weight = call(
         weight_kernel,
         shape(points, 128),
-        [SMEM] + [VMEM] * 6,
+        [SMEM] + [VMEM] * 3,
         place,
         own,
         got,
         edge,
-        bf16(np.eye(128)),
-        bf16(direct),
-        bf16(negated),
         scratch=[pltpu.VMEM((points, 128), BF16), pltpu.VMEM((points, 128), F32)],
         flops=points * 128 * 1024,
     )
@@ -365,20 +343,19 @@
         tiled=True,
     ).reshape(pointings, parts, share_rows, tile)
     window, weight, turned = lax.optimization_barrier((window, weight, turned))
-    row_table = bf16(row_tables(points, devices))
-    table_scratch = lambda tables, pieces: [
-        pltpu.VMEM((tables, points // 2, points // 2), BF16),
-        pltpu.SemaphoreType.DMA((pieces,)),
-    ]
+    row_table = row_tables(points, devices)
+    pieces = row_table.reshape(2, points // 2, -1, 256).transpose(0, 2, 1, 3)
+    pieces = bf16(pieces.reshape(-1, points // 2, 256))
     spectrum = call(
         row_kernel,
         shape(devices, rows, 128),
         [VMEM, VMEM, HBM],
         window,
         turned,
-        row_table,
-        scratch=table_scratch(2, 8),
+        pieces,
+        scratch=[pltpu.VMEM(pieces.shape, BF16), pltpu.SemaphoreType.DMA((pieces.shape[0],))],
         flops=rows * points * points,
+        limit=60,
     )
     col = lax.all_to_all(spectrum, IMG, split_axis=0, concat_axis=0, tiled=True)
     back = call(
@@ -389,10 +366,11 @@
         col.reshape(points, 128),
         weight,
         bf16(np.stack(column_tables(points))),
-        scratch=[pltpu.VMEM((2, points // 2, 128), BF16)] * 2 + table_scratch(6, 24),
+        scratch=[pltpu.VMEM((2, points // 2, 128), BF16)] * 2
+        + [pltpu.VMEM((6, points // 2, points // 2), BF16), pltpu.SemaphoreType.DMA((24,))],
         flops=8 * points * points * 128 // 2,
         moved=16 << 20,
-        limit=28,
+        limit=60,
     )
     lines = lax.all_to_all(
         back.reshape(devices, rows, 128), IMG, split_axis=0, concat_axis=0, tiled=True
@@ -401,11 +379,10 @@
     contribution = call(
         pixel_kernel,
         shape(pointings, rows, share),
-        [VMEM, VMEM, HBM],
+        [VMEM] * 3,
         lines,
         turned,
-        row_table,
-        scratch=table_scratch(2, 8),
+        bf16(row_table),
         flops=rows * points * points,
     )
     terms = lax.all_to_all(contribution, "ptg", split_axis=0, concat_axis=0, tiled=True)

time: 134 us -> 134 us (level)
  local copies, waits for them, and re-layouts: 11.6 us -> 5.78 us
  Pallas kernels: 20 us -> 23.2 us
  blocking collectives: 28.9 us -> 31.5 us
    unnamed x28 -> x10, local copies, waits for them, and re-layouts: 10.8 us -> 5 us
    pallas_call x7, Pallas kernels: 20 us -> 23.2 us  [call(): pl.pallas_call(kernel, out_shape=outs, in_specs=specs, out_specs=jax.tree...]
    all_to_all x1, blocking collectives: 14 us -> 15.6 us  [shards(): col = lax.all_to_all(spectrum, IMG, split_axis=0, concat_axis=0, tiled=True)]
  transfers between devices with their start and end apart: 12 -> 12, of which waited for: 8 -> 9; matrix products, arithmetic and copies ran while one was open for 3% -> 2% of each run, Pallas kernels for 2% -> 1%
where the time goes in v5:
time: 134 us; the launch traced here: 133 us
  waiting for transfers between devices  34.1 us (25%)
  starting transfers between devices  33.2 us (25%)
  blocking collectives  31.5 us (24%)
  Pallas kernels  23.2 us (17%)
  local copies, waits for them, and re-layouts  5.78 us (4%)
  other arithmetic  3.94 us (3%)
    pallas_call x7, Pallas kernels, call(): pl.pallas_call(kernel, out_shape=outs, in_specs=specs, out_specs=jax.tree...  23.2 us
    all_to_all x1, blocking collectives, shards(): lax.all_to_all(back.reshape(devices, rows, 128), IMG, split_axis=0, conca...  15.9 us
    all_to_all x1, blocking collectives, shards(): col = lax.all_to_all(spectrum, IMG, split_axis=0, concat_axis=0, tiled=True)  15.6 us
    ppermute x2, waiting for transfers between devices, shards(): received.append(lax.ppermute(block, ('ptg', *IMG), pairs))  12 us
    all_to_all x1, waiting for transfers between devices, shards(): lax.all_to_all(contribution, 'ptg', split_axis=0, concat_axis=0, tiled=True)  9.35 us
    all_to_all x1, starting transfers between devices, shards(): lax.all_to_all(picked.reshape(pointings * parts, share_rows, tile), ('ptg...  7 us
    all_to_all x1, starting transfers between devices, shards(): lax.all_to_all(shares, 's', split_axis=0, concat_axis=0, tiled=True)  6.53 us
    all_to_all x1, starting transfers between devices, shards(): lax.all_to_all(contribution, 'ptg', split_axis=0, concat_axis=0, tiled=True)  5.97 us
  transfers between devices with their start and end apart: 12, of which 9 were waited for; matrix products, arithmetic and copies ran while one was open for 2% of the time, Pallas kernels for 1%

profile of v5, /device:TPU:14, one launch (start us, length us, event | category | flops | bytes accessed | tf_op | source)
XLA Modules:
  0.0 132.8 jit_solution(10473543034440019912)
XLA Ops:
  0.8 0.8 copy-done
  1.6 0.7 dynamic-slice_bitcast_fusion
  2.3 1.2 copy-done.4
  4.2 4.1 %collective-permute-start.2 = (s32[8]{0:T(128)S(1)}, s32[8]{0:T(128)S(1)}, u32[]{:S(2)}, u32[]{:S(2)}) collective-permute-start(s32[8]{0:T(128)S(1)} %compare_select_fusion), channel_id=1, source_target_pairs={{0,48},{16,32},{32,16},{48,0},{64,112},{80,96},{96,80},{112,64},{1... | collective-permute-start | bytes 104 | tf_op jit(solution)/shard_map/ppermute | solution.py:305
  8.3 0.9 collective-permute-start
  9.2 6.5 %all-to-all-start = ((bf16[4,4,16,512]{3,2,1,0:T(8,128)(2,1)}), bf16[4,4,16,512]{3,2,1,0:T(8,128)(2,1)S(1)}, u32[]{:S(2)}, u32[]{:S(2)}) async-start(bf16[4,4,16,512]{3,2,1,0:T(8,128)(2,1)} %dynamic-slice_bitcast_fusion), calls=%async_computation | async-start | bytes 524288 | tf_op jit(solution)/shard_map/all_to_all | solution.py:303
  15.8 1.4 %collective-permute-start.3 = (s32[8]{0:T(128)S(1)}, s32[8]{0:T(128)S(1)}, u32[]{:S(2)}, u32[]{:S(2)}) collective-permute-start(s32[8]{0:T(128)S(1)} %add_add_fusion), channel_id=1, source_target_pairs={{0,64},{16,80},{32,96},{48,112},{64,0},{80,16},{96,32},{112,48},{1... | collective-permute-start | bytes 104 | tf_op jit(solution)/shard_map/ppermute | solution.py:308
  17.2 3.0 %collective-permute-done.3 = s32[8]{0:T(128)S(1)} collective-permute-done((s32[8]{0:T(128)S(1)}, s32[8]{0:T(128)S(1)}, u32[]{:S(2)}, u32[]{:S(2)}) %collective-permute-start.3) | collective-permute-done | bytes 64 | tf_op jit(solution)/shard_map/ppermute | solution.py:308
  20.2 1.6 %all-to-all-done.tiles_ref = bf16[4,4,16,512]{3,2,1,0:T(8,128)(2,1)S(1)} async-done(((bf16[4,4,16,512]{3,2,1,0:T(8,128)(2,1)}), bf16[4,4,16,512]{3,2,1,0:T(8,128)(2,1)S(1)}, u32[]{:S(2)}, u32[]{:S(2)}) %all-to-all-start) | async-done | bytes 262176 | tf_op jit(solution)/shard_map/all_to_all | solution.py:303
  21.9 2.0 %shard_map.74 = bf16[8,4,16,512]{3,2,1,0:T(8,128)(2,1)} custom-call(s32[1]{0:T(128)} %bitcast.7.place_ref, s32[8]{0:T(128)S(1)} %add.43.starts_ref, bf16[4,4,16,512]{3,2,1,0:T(8,128)(2,1)S(1)} %all-to-all-done.tiles_ref), custom_call_target="tpu_custom_call" | custom-call | bytes 1048576 | tf_op jit(solution)/shard_map/pallas_call | solution.py:260
  23.8 7.0 %all-to-all-start.1 = ((bf16[32,16,512]{2,1,0:T(8,128)(2,1)}), bf16[32,16,512]{2,1,0:T(8,128)(2,1)}, u32[]{:S(2)}, u32[]{:S(2)}) async-start(bf16[32,16,512]{2,1,0:T(8,128)(2,1)} %bitcast.8), calls=%async_computation.1 | async-start | bytes 1048576 | tf_op jit(solution)/shard_map/all_to_all | solution.py:338
  30.9 1.9 %collective-permute-start.4 = (bf16[1024,128]{1,0:T(8,128)(2,1)S(1)}, bf16[1024,128]{1,0:T(8,128)(2,1)S(1)}, u32[]{:S(2)}, u32[]{:S(2)}) collective-permute-start(bf16[1024,128]{1,0:T(8,128)(2,1)S(1)} %get-tuple-element.22), channel_id=1, source_target_pairs={{0,15},{1,14},{2,13},{3,12},{4,11},{5,10},{6,9},{7,8},{8,7},{9,6},... | collective-permute-start | bytes 786440 | tf_op jit(solution)/shard_map/ppermute | solution.py:309
  32.7 1.3 collective-permute-start.5
  34.1 2.8 %fusion.beam_ref = f32[128,2048]{1,0:T(8,128)} fusion(s32[]{:T(128)S(6)} %select_n.59, f32[128,2048]{1,0:T(8,128)} %bitcast.32), kind=kLoop, calls=%fused_computation.2 | loop fusion | flops 262144 | bytes 2097156 | tf_op jit(solution)/shard_map/concatenate | solution.py:327
  36.9 5.4 %collective-permute-done.5.edge_ref = bf16[16,128]{1,0:T(8,128)(2,1)S(1)} collective-permute-done((bf16[16,128]{1,0:T(8,128)(2,1)S(1)}, bf16[16,128]{1,0:T(8,128)(2,1)S(1)}, u32[]{:S(2)}, u32[]{:S(2)}) %collective-permute-start.5) | collective-permute-done | bytes 4128 | tf_op jit(solution)/shard_map/ppermute | solution.py:310
  42.3 1.0 collective-permute-done.4.got_ref
  43.3 1.4 %shard_map.75.weight_ref = bf16[2048,128]{1,0:T(8,128)(2,1)S(1)} custom-call(s32[1]{0:T(128)} %bitcast.4.me_ref, bf16[2048,128]{1,0:T(8,128)(2,1)S(1)} %get-tuple-element.21.own_ref, bf16[1024,128]{1,0:T(8,128)(2,1)S(1)} %collective-permute-done.4.got_ref, bf16[16,128]{1,0:T(8,128)(2,1)S(1)} %collective-permute-done.5.edge_ref), custom_call_target="tpu_custom_call" | custom-call | flops 268435456 | bytes 4194304 | tf_op jit(solution)/shard_map/pallas_call | solution.py:260
  44.7 0.8 copy-done.3
  45.8 5.6 %shard_map.76 = bf16[16,128,128]{2,1,0:T(8,128)(2,1)} custom-call(bf16[8,4,16,512]{3,2,1,0:T(8,128)(2,1)} %bitcast.9.window_ref, f32[128,2048]{1,0:T(8,128)} %fusion.beam_ref, bf16[8,1024,256]{2,1,0:T(8,128)(2,1)} %constant.73.clone.source_ref), custom_call_target="tpu_custom_call" | custom-call | flops 536870912 | bytes 4194304 | tf_op jit(solution)/shard_map/pallas_call | solution.py:260
  51.4 15.6 %all_to_all.25 = bf16[16,128,128]{2,1,0:T(8,128)(2,1)} all-to-all(bf16[16,128,128]{2,1,0:T(8,128)(2,1)} %shard_map.76), channel_id=1, replica_groups=mesh['ptg'=8,'s'=4,'b'=4] {'s','b'}, dimensions={0} | all-to-all | bytes 1048576 | tf_op jit(solution)/shard_map/all_to_all | solution.py:360
  67.1 10.3 %shard_map.77 = bf16[2048,128]{1,0:T(8,128)(2,1)} custom-call(s32[1]{0:T(128)} %bitcast.4.me_ref, bf16[2048,128]{1,0:T(8,128)(2,1)} %bitcast.30, bf16[2048,128]{1,0:T(8,128)(2,1)} %copy-done.3, bf16[6,1024,1024]{2,1,0:T(8,128)(2,1)} %constant.74.clone.source_ref), custom_call_target="tpu_custom_call" | custom-call | flops 2147483648 | bytes 16777216 | tf_op jit(solution)/shard_map/pallas_call | solution.py:260
  77.4 15.9 %all_to_all.26.x_ref = bf16[16,128,128]{2,1,0:T(8,128)(2,1)S(1)} all-to-all(bf16[16,128,128]{2,1,0:T(8,128)(2,1)} %bitcast.31), channel_id=1, replica_groups=mesh['ptg'=8,'s'=4,'b'=4] {'s','b'}, dimensions={0} | all-to-all | bytes 1048576 | tf_op jit(solution)/shard_map/all_to_all | solution.py:375
  93.3 2.2 %copy-done.2 = bf16[2,1024,1024]{2,1,0:T(8,128)(2,1)S(1)} copy-done((bf16[2,1024,1024]{2,1,0:T(8,128)(2,1)S(1)}, bf16[2,1024,1024]{2,1,0:T(8,128)(2,1)}, u32[]{:S(2)}) %copy-start.2) | copy-done | bytes 4194328
  95.5 2.3 %shard_map.78 = bf16[8,128,256]{2,1,0:T(8,128)(2,1)} custom-call(bf16[16,128,128]{2,1,0:T(8,128)(2,1)S(1)} %all_to_all.26.x_ref, f32[128,2048]{1,0:T(8,128)S(1)} %copy-done.1, bf16[2,1024,1024]{2,1,0:T(8,128)(2,1)S(1)} %copy-done.2), custom_call_target="tpu_custom_call" | custom-call | flops 536870912 | bytes 4194304 | tf_op jit(solution)/shard_map/pallas_call | solution.py:260
  97.8 6.0 %all-to-all-start.4 = ((bf16[8,128,256]{2,1,0:T(8,128)(2,1)}), bf16[8,128,256]{2,1,0:T(8,128)(2,1)S(1)}, u32[]{:S(2)}, u32[]{:S(2)}) async-start(bf16[8,128,256]{2,1,0:T(8,128)(2,1)} %shard_map.78), calls=%async_computation.4 | async-start | bytes 1048576 | tf_op jit(solution)/shard_map/all_to_all | solution.py:388
  103.8 9.4 %all-to-all-done.4.terms_ref = bf16[8,128,256]{2,1,0:T(8,128)(2,1)S(1)} async-done(((bf16[8,128,256]{2,1,0:T(8,128)(2,1)}), bf16[8,128,256]{2,1,0:T(8,128)(2,1)S(1)}, u32[]{:S(2)}, u32[]{:S(2)}) %all-to-all-start.4) | async-done | bytes 524320 | tf_op jit(solution)/shard_map/all_to_all | solution.py:388
  113.2 1.0 shard_map.79
  114.3 1.3 collective-permute-done.6
  115.6 4.0 %collective-permute-start.8 = (bf16[256,256]{1,0:T(8,128)(2,1)S(1)}, bf16[256,256]{1,0:T(8,128)(2,1)S(1)}, u32[]{:S(2)}, u32[]{:S(2)}) collective-permute-start(bf16[256,256]{1,0:T(8,128)(2,1)S(1)} %pad_maximum_fusion.1), channel_id=1, source_target_pairs={{0,0},{1,8},{2,16},{3,24},{4,32},{5,40},{6,48},{7,56},{8,64},{9,72... | collective-permute-start | bytes 393224 | tf_op jit(solution)/shard_map/ppermute | solution.py:409
  119.7 8.5 %collective-permute-done.8 = bf16[256,256]{1,0:T(8,128)(2,1)S(1)} collective-permute-done((bf16[256,256]{1,0:T(8,128)(2,1)S(1)}, bf16[256,256]{1,0:T(8,128)(2,1)S(1)}, u32[]{:S(2)}, u32[]{:S(2)}) %collective-permute-start.8) | collective-permute-done | bytes 131104 | tf_op jit(solution)/shard_map/ppermute | solution.py:409
  128.2 3.5 %collective-permute-done.7 = bf16[256,256]{1,0:T(8,128)(2,1)S(1)} collective-permute-done((bf16[256,256]{1,0:T(8,128)(2,1)S(1)}, bf16[256,256]{1,0:T(8,128)(2,1)S(1)}, u32[]{:S(2)}, u32[]{:S(2)}) %collective-permute-start.7) | collective-permute-done | bytes 131104 | tf_op jit(solution)/shard_map/ppermute | solution.py:409
  131.9 0.9 maximum_select_fusion
  (24 shorter events, 1.4 us)
Async XLA Ops:
  0.0 1.6 %copy-start = (bf16[2048,512]{1,0:T(8,128)(2,1)S(1)}, bf16[2048,512]{1,0:T(8,128)(2,1)}, u32[]{:S(2)}) copy-start(bf16[2048,512]{1,0:T(8,128)(2,1)} %param.7) | copy-start | bytes 6291460
  2.3 1.2 copy-start.4
  4.2 11.5 %collective-permute-start.2 = (s32[8]{0:T(128)S(1)}, s32[8]{0:T(128)S(1)}, u32[]{:S(2)}, u32[]{:S(2)}) collective-permute-start(s32[8]{0:T(128)S(1)} %compare_select_fusion), channel_id=1, source_target_pairs={{0,48},{16,32},{32,16},{48,0},{64,112},{80,96},{96,80},{112,64},{1... | collective-permute-start | bytes 104 | tf_op jit(solution)/shard_map/ppermute | solution.py:305
  8.3 7.5 %collective-permute-start.1 = (s32[8]{0:T(128)S(1)}, s32[8]{0:T(128)S(1)}, u32[]{:S(2)}, u32[]{:S(2)}) collective-permute-start(s32[8]{0:T(128)S(1)} %compare_select_fusion), channel_id=1, source_target_pairs={{0,32},{16,48},{32,0},{48,16},{64,96},{80,112},{96,64},{112,80},{1... | collective-permute-start | bytes 104 | tf_op jit(solution)/shard_map/ppermute | solution.py:305
  8.3 7.5 %collective-permute-start = (s32[8]{0:T(128)S(1)}, s32[8]{0:T(128)S(1)}, u32[]{:S(2)}, u32[]{:S(2)}) collective-permute-start(s32[8]{0:T(128)S(1)} %compare_select_fusion), channel_id=1, source_target_pairs={{0,16},{16,0},{32,48},{48,32},{64,80},{80,64},{96,112},{112,96},{1... | collective-permute-start | bytes 104 | tf_op jit(solution)/shard_map/ppermute | solution.py:305
  9.2 12.7 %all-to-all-start = ((bf16[4,4,16,512]{3,2,1,0:T(8,128)(2,1)}), bf16[4,4,16,512]{3,2,1,0:T(8,128)(2,1)S(1)}, u32[]{:S(2)}, u32[]{:S(2)}) async-start(bf16[4,4,16,512]{3,2,1,0:T(8,128)(2,1)} %dynamic-slice_bitcast_fusion), calls=%async_computation | async-start | bytes 524288 | tf_op jit(solution)/shard_map/all_to_all | solution.py:303
  15.8 4.5 %collective-permute-start.3 = (s32[8]{0:T(128)S(1)}, s32[8]{0:T(128)S(1)}, u32[]{:S(2)}, u32[]{:S(2)}) collective-permute-start(s32[8]{0:T(128)S(1)} %add_add_fusion), channel_id=1, source_target_pairs={{0,64},{16,80},{32,96},{48,112},{64,0},{80,16},{96,32},{112,48},{1... | collective-permute-start | bytes 104 | tf_op jit(solution)/shard_map/ppermute | solution.py:308
  23.8 22.0 %all-to-all-start.1 = ((bf16[32,16,512]{2,1,0:T(8,128)(2,1)}), bf16[32,16,512]{2,1,0:T(8,128)(2,1)}, u32[]{:S(2)}, u32[]{:S(2)}) async-start(bf16[32,16,512]{2,1,0:T(8,128)(2,1)} %bitcast.8), calls=%async_computation.1 | async-start | bytes 1048576 | tf_op jit(solution)/shard_map/all_to_all | solution.py:338
  30.9 12.5 %collective-permute-start.4 = (bf16[1024,128]{1,0:T(8,128)(2,1)S(1)}, bf16[1024,128]{1,0:T(8,128)(2,1)S(1)}, u32[]{:S(2)}, u32[]{:S(2)}) collective-permute-start(bf16[1024,128]{1,0:T(8,128)(2,1)S(1)} %get-tuple-element.22), channel_id=1, source_target_pairs={{0,15},{1,14},{2,13},{3,12},{4,11},{5,10},{6,9},{7,8},{8,7},{9,6},... | collective-permute-start | bytes 786440 | tf_op jit(solution)/shard_map/ppermute | solution.py:309
  32.7 9.6 %collective-permute-start.5 = (bf16[16,128]{1,0:T(8,128)(2,1)S(1)}, bf16[16,128]{1,0:T(8,128)(2,1)S(1)}, u32[]{:S(2)}, u32[]{:S(2)}) collective-permute-start(bf16[16,128]{1,0:T(8,128)(2,1)S(1)} %get-tuple-element.23), channel_id=1, source_target_pairs={{8,0},{9,7},{10,6},{11,5},{12,4},{13,3},{14,2},{15,1},{24,16},{25,... | collective-permute-start | bytes 12296 | tf_op jit(solution)/shard_map/ppermute | solution.py:310
  44.7 0.8 copy-start.3
  67.1 26.2 %copy-start.1 = (f32[128,2048]{1,0:T(8,128)S(1)}, f32[128,2048]{1,0:T(8,128)}, u32[]{:S(2)}) copy-start(f32[128,2048]{1,0:T(8,128)} %fusion.beam_ref) | copy-start | bytes 3145732
  93.3 2.2 %copy-start.2 = (bf16[2,1024,1024]{2,1,0:T(8,128)(2,1)S(1)}, bf16[2,1024,1024]{2,1,0:T(8,128)(2,1)}, u32[]{:S(2)}) copy-start(bf16[2,1024,1024]{2,1,0:T(8,128)(2,1)} %constant.75.clone.table_ref) | copy-start | bytes 12582916
  97.8 15.4 %all-to-all-start.4 = ((bf16[8,128,256]{2,1,0:T(8,128)(2,1)}), bf16[8,128,256]{2,1,0:T(8,128)(2,1)S(1)}, u32[]{:S(2)}, u32[]{:S(2)}) async-start(bf16[8,128,256]{2,1,0:T(8,128)(2,1)} %shard_map.78), calls=%async_computation.4 | async-start | bytes 1048576 | tf_op jit(solution)/shard_map/all_to_all | solution.py:388
  114.2 1.4 %collective-permute-start.6 = (bf16[2,128,256]{2,1,0:T(8,128)(2,1)S(1)}, bf16[2,128,256]{2,1,0:T(8,128)(2,1)S(1)}, u32[]{:S(2)}, u32[]{:S(2)}) collective-permute-start(bf16[2,128,256]{2,1,0:T(8,128)(2,1)S(1)} %get-tuple-element.28), channel_id=1, source_target_pairs={{0,1},{1,0},{2,3},{3,2},{4,5},{5,4},{6,7},{7,6},{8,9},{9,8},{10,11... | collective-permute-start | bytes 393224 | tf_op jit(solution)/shard_map/ppermute | solution.py:398
  115.6 12.6 %collective-permute-start.8 = (bf16[256,256]{1,0:T(8,128)(2,1)S(1)}, bf16[256,256]{1,0:T(8,128)(2,1)S(1)}, u32[]{:S(2)}, u32[]{:S(2)}) collective-permute-start(bf16[256,256]{1,0:T(8,128)(2,1)S(1)} %pad_maximum_fusion.1), channel_id=1, source_target_pairs={{0,0},{1,8},{2,16},{3,24},{4,32},{5,40},{6,48},{7,56},{8,64},{9,72... | collective-permute-start | bytes 393224 | tf_op jit(solution)/shard_map/ppermute | solution.py:409
  119.6 12.1 %collective-permute-start.7 = (bf16[256,256]{1,0:T(8,128)(2,1)S(1)}, bf16[256,256]{1,0:T(8,128)(2,1)S(1)}, u32[]{:S(2)}, u32[]{:S(2)}) collective-permute-start(bf16[256,256]{1,0:T(8,128)(2,1)S(1)} %pad_maximum_fusion), channel_id=1, source_target_pairs={{0,4},{1,12},{2,20},{3,28},{4,36},{5,44},{6,52},{7,60},{8,68},{9,7... | collective-permute-start | bytes 393224 | tf_op jit(solution)/shard_map/ppermute | solution.py:409

commit v6 on v5

--- a/solution.py
+++ b/solution.py
@@ -13,7 +13,6 @@
 NT = (((1,), (1,)), ((), ()))
 NN = (((1,), (0,)), ((), ()))
 VMEM = pl.BlockSpec(memory_space=pltpu.VMEM)
-HBM = pl.BlockSpec(memory_space=pltpu.HBM)
 SMEM = pl.BlockSpec(memory_space=pltpu.SMEM)
 
 
@@ -21,40 +20,35 @@
     return lax.dot_general(a, b, dims, preferred_element_type=F32)
 
 
-def row_tables(points, devices):
+def row_table(points, devices):
     half, lanes = points // 2, points // devices
     index = np.arange(half)
     turn = 2.0 * np.pi / points * np.arange(points)
     cos_of, sin_of = np.cos(turn), -np.sin(turn)
-    made = []
-    for odd in (0, 1):
-        blocks = np.arange(devices // 2)
-        if odd:
-            blocks = blocks[::-1]
-        freq = lanes * blocks[:, None] + 2 * np.arange(lanes // 2)[None, :] + odd
-        phase = index[:, None, None] * freq[None] % points
-        imag = sin_of[phase]
-        if not odd:
-            imag[:, 0, 0] = cos_of[index * half % points]
-        made.append(np.concatenate([cos_of[phase], imag], axis=2).reshape(half, half))
-    return np.stack(made)
-
-
-def column_tables(points):
-    half = points // 2
-    index = np.arange(half)
-    turn = 2.0 * np.pi / points * np.arange(points)
-    cos_of, sin_of = np.cos(turn), -np.sin(turn)
-    even = index[:, None] * (2 * index[None, :]) % points
-    odd = index[:, None] * (2 * index[None, :] + 1) % points
-    return [
-        cos_of[even].T,
-        sin_of[even].T,
-        cos_of[odd].T,
-        sin_of[odd].T,
-        cos_of[odd],
-        sin_of[odd],
-    ]
+    freq = lanes * np.arange(devices // 2)[:, None] + 2 * np.arange(lanes // 2)[None, :]
+    phase = index[:, None, None] * freq[None] % points
+    imag = sin_of[phase]
+    imag[:, 0, 0] = cos_of[index * half % points]
+    return np.concatenate([cos_of[phase], imag], axis=2).reshape(half, half)
+
+
+def row_turn(points):
+    angle = 2.0 * np.pi / points * np.arange(points // 2)
+    return np.stack([np.cos(angle), np.sin(angle)] * 4).astype(np.float32)
+
+
+def column_table(points):
+    quarter = points // 4
+    index = np.arange(quarter)
+    angle = 2.0 * np.pi / quarter * (index[:, None] * index[None, :] % quarter)
+    return np.concatenate([np.cos(angle), -np.sin(angle)])
+
+
+def column_turn(points):
+    angle = 2.0 * np.pi / points * np.arange(points // 4)[:, None] * np.arange(4)[None, :]
+    made = np.zeros((points // 4, 128), np.float32)
+    made[:, :4], made[:, 4:8] = np.cos(angle), np.sin(angle)
+    return made
 
 
 def bf16(table):
@@ -97,9 +91,9 @@
 def weight_kernel(me_ref, own_ref, got_ref, edge_ref, out_ref, plus, minus):
     points = own_ref.shape[0]
     target, source = grid(256, 256)
-    k, odd = target % 128, target // 128
-    direct = ones_where(source == 2 * k + odd)
-    negated = ones_where(source == 256 - 2 * k - odd)
+    index = 4 * (target % 64) + target // 64
+    direct = ones_where(source == index)
+    negated = ones_where(source == 256 - index)
     row, column = grid(128, 128)
     eye = ones_where(row == column)
     me = me_ref[0]
@@ -130,25 +124,8 @@
         taken += dot(negated, minus[pl.ds(256 * (blocks - 1 - b), 256)].astype(BF16))
         wrapped = minus[pl.ds(256 * ((blocks - b) % blocks), 1)]
         taken = scale * (taken + jnp.where(row == 0, wrapped, 0.0))
-        out_ref[pl.ds(128 * b, 128)] = taken[:128].astype(BF16)
-        out_ref[pl.ds(points // 2 + 128 * b, 128)] = taken[128:].astype(BF16)
-
-
-class Stream:
-    def __init__(self, pieces, sems, ahead=6):
-        self.copies = [
-            pltpu.make_async_copy(source, target, sems.at[n])
-            for n, (source, target) in enumerate(pieces)
-        ]
-        self.ahead, self.taken = ahead, 0
-        for copy in self.copies[:ahead]:
-            copy.start()
-
-    def take(self):
-        self.copies[self.taken].wait()
-        if self.taken + self.ahead < len(self.copies):
-            self.copies[self.taken + self.ahead].start()
-        self.taken += 1
+        for r in range(4):
+            out_ref[pl.ds(r * points // 4 + 64 * b, 64)] = taken[64 * r : 64 * r + 64].astype(BF16)
 
 
 def pick_kernel(points, place_ref, starts_ref, tiles_ref, out_ref):
@@ -166,76 +143,116 @@
             out_ref[p, part] = window.astype(BF16)
 
 
-def row_kernel(window_ref, beam_ref, source_ref, out_ref, table_ref, sems):
-    shares, parts, rows, wide = window_ref.shape
-    blocks = out_ref.shape[0] // 2
-    stream = Stream([(source_ref.at[n], table_ref.at[n]) for n in range(blocks)], sems)
+def row_kernel(window_ref, beam_ref, table_ref, turn_ref, out_ref):
+    shares, parts, _, wide = window_ref.shape
+    rows = out_ref.shape[1]
     beamed = []
     for part in range(parts):
         window = jnp.concatenate([window_ref[q, part] for q in range(shares)], 0)
         beamed.append(window.astype(F32) * beam_ref[:, pl.ds(part * wide, wide)])
     left = jnp.concatenate(beamed[: parts // 2], 1)
     right = jnp.concatenate(beamed[parts // 2 :], 1)
-    for odd in (0, 1):
-        folded = (left - right if odd else left + right).astype(BF16)
-        for part in range(blocks // 2):
-            stream.take()
-            spectrum = dot(folded, table_ref[odd * blocks // 2 + part]).astype(BF16)
-            out_ref[odd * blocks + 2 * part] = spectrum[:, :128]
-            out_ref[odd * blocks + 2 * part + 1] = spectrum[:, 128:]
-
-
-def column_kernel(me_ref, x_ref, weight_ref, source_ref, out_ref, upper, lower, table_ref, sems):
-    c0, s0, c1, s1, c1t, s1t = (table_ref.at[t] for t in range(6))
+    minus = left - right
+    folded = [left + right, minus * turn_ref[0:1], minus * turn_ref[1:2]]
+    folded = jnp.concatenate([t.astype(BF16) for t in folded], 0)
+    last = out_ref.shape[0] - 1
+    lane = lax.broadcasted_iota(jnp.int32, (rows, 128), 1)
+    for part in range(table_ref.shape[1] // 256):
+        got = dot(folded, table_ref[:, pl.ds(256 * part, 256)])
+        for n in (0, 1):
+            block = 2 * part + n
+            even, by_cos, by_sin = (
+                got[rows * t : rows * (t + 1), 128 * n : 128 * (n + 1)] for t in range(3)
+            )
+            if block == 0:
+                by_cos = jnp.where(lane == 64, 0.0, by_cos)
+                by_sin = jnp.where(lane == 64, 0.0, by_sin)
+            moved = pltpu.roll(by_sin, 64, 1)
+            out_ref[block] = even.astype(BF16)
+            out_ref[last - block] = jnp.where(lane < 64, by_cos + moved, by_cos - moved).astype(BF16)
+
+
+def column_kernel(me_ref, x_ref, weight_ref, table_ref, turn_ref, out_ref, both):
     points = x_ref.shape[0]
-    half = points // 2
-    places = [
-        (t, pl.ds(256 * m, 256))
-        for pair in (0, 2, 4)
-        for m in range(half // 256)
-        for t in (pair, pair + 1)
-    ]
-    stream = Stream(
-        [(source_ref.at[t, rows], table_ref.at[t, rows]) for t, rows in places], sems
-    )
+    quarter = points // 4
     scale = 1.0 / float(points * points)
     lane = lax.broadcasted_iota(jnp.int32, (256, 128), 1)
     sign = jnp.where(lane < 64, -1.0, 1.0)
     packed = (me_ref[0] == 0) & (lane % 64 == 0)
-    first, second = x_ref[:half].astype(F32), x_ref[half:].astype(F32)
-    for odd in (0, 1):
-        folded = (first - second if odd else first + second).astype(BF16)
-        for m in range(half // 256):
-            rows = pl.ds(256 * m, 256)
-            stream.take()
-            stream.take()
-            by_cos = dot((c1 if odd else c0)[rows, :], folded)
-            by_sin = dot((s1 if odd else s0)[rows, :], folded)
-            weight = weight_ref[pl.ds(odd * half + 256 * m, 256)].astype(F32) * scale
+    turns = lambda r, rows: (
+        jnp.broadcast_to(turn_ref[rows, r : r + 1], (256, 128)),
+        jnp.broadcast_to(turn_ref[rows, 4 + r : 5 + r], (256, 128)),
+    )
+    for m in range(quarter // 256):
+        rows = pl.ds(256 * m, 256)
+        x = [x_ref[pl.ds(quarter * t + 256 * m, 256)].astype(F32) for t in range(4)]
+        even, p, odd, q = x[0] + x[2], x[0] - x[2], x[1] + x[3], x[1] - x[3]
+        c1, s1 = turns(1, rows)
+        c2, s2 = turns(2, rows)
+        c3, s3 = turns(3, rows)
+        pairs = [
+            (even + odd, jnp.zeros_like(even)),
+            (p * c1 - q * s1, -(p * s1 + q * c1)),
+            ((even - odd) * c2, -(even - odd) * s2),
+            (p * c3 + q * s3, q * c3 - p * s3),
+        ]
+        for r in range(4):
+            both[4 + r, rows, 0:128] = pairs[r][0].astype(BF16)
+            both[4 + r, rows, 128:256] = pairs[r][1].astype(BF16)
+    for r in range(4):
+        for m in range(quarter // 256):
+            rows, below = pl.ds(256 * m, 256), pl.ds(quarter + 256 * m, 256)
+            wide = both[4 + r] if r else both[4, :, 0:128]
+            by_c, by_s = dot(table_ref[rows], wide), dot(table_ref[below], wide)
+            by_cos, by_sin = by_c[:, :128], by_s[:, :128]
+            if r:
+                by_cos, by_sin = by_cos - by_s[:, 128:], by_sin + by_c[:, 128:]
+            weight = weight_ref[pl.ds(r * quarter + 256 * m, 256)].astype(F32) * scale
             up = weight * (by_cos + jnp.where(packed, 0.0, sign * pltpu.roll(by_sin, 64, 1)))
             down = jnp.where(packed, weight * by_sin, -sign * pltpu.roll(up, 64, 1))
-            upper[odd, rows] = up.astype(BF16)
-            lower[odd, rows] = down.astype(BF16)
-    for m in range(half // 256):
-        rows = pl.ds(256 * m, 256)
-        stream.take()
-        stream.take()
-        even = dot(c0[rows, :], upper[0]) + dot(s0[rows, :], lower[0])
-        odd = dot(c1t[rows, :], upper[1]) + dot(s1t[rows, :], lower[1])
-        out_ref[rows] = (even + odd).astype(BF16)
-        out_ref[pl.ds(half + 256 * m, 256)] = (even - odd).astype(BF16)
-
-
-def pixel_kernel(x_ref, beam_ref, table_ref, out_ref):
+            both[r, rows, 0:128] = up.astype(BF16)
+            both[r, rows, 128:256] = down.astype(BF16)
+    for m in range(quarter // 256):
+        rows, below = pl.ds(256 * m, 256), pl.ds(quarter + 256 * m, 256)
+        parts = []
+        for r in range(4):
+            by_c, by_s = dot(table_ref[rows], both[r]), dot(table_ref[below], both[r])
+            parts.append((by_c[:, :128] + by_s[:, 128:], by_c[:, 128:] - by_s[:, :128]))
+        c1, s1 = turns(1, rows)
+        c2, s2 = turns(2, rows)
+        c3, s3 = turns(3, rows)
+        (g0, _), (g1, h1), (g2, h2), (g3, h3) = parts
+        middle = c2 * g2 - s2 * h2
+        p = c1 * g1 - s1 * h1 + c3 * g3 - s3 * h3
+        q = s3 * g3 + c3 * h3 - s1 * g1 - c1 * h1
+        plus, minus = g0 + middle, g0 - middle
+        for t, value in enumerate((plus + p, minus + q, plus - p, minus - q)):
+            out_ref[pl.ds(quarter * t + 256 * m, 256)] = value.astype(BF16)
+
+
+def pixel_kernel(x_ref, beam_ref, table_ref, turn_ref, out_ref):
     blocks, rows, _ = x_ref.shape
     half = beam_ref.shape[1] // 2
     share = out_ref.shape[2]
-    even = jnp.concatenate([x_ref[b] for b in range(blocks // 2)], 1)
-    odd = jnp.concatenate([x_ref[b] for b in range(blocks // 2, blocks)], 1)
+    lane = lax.broadcasted_iota(jnp.int32, (rows, 128), 1)
+    even = [x_ref[b] for b in range(blocks // 2)]
+    straight, crossed = [], []
+    for b in range(blocks // 2):
+        odd = x_ref[blocks - 1 - b].astype(F32)
+        moved = pltpu.roll(odd, 64, 1)
+        turned = jnp.where(lane < 64, -moved, moved)
+        if b == 0:
+            odd = jnp.where(lane == 64, 0.0, odd)
+            turned = jnp.where(lane == 64, 0.0, turned)
+        straight.append(odd.astype(BF16))
+        crossed.append(turned.astype(BF16))
+    wide = [jnp.concatenate(part, 1) for part in (even, straight, crossed)]
+    wide = jnp.concatenate(wide, 0)
     for part in range(half // share):
         lanes = pl.ds(share * part, share)
-        by_even = dot(even, table_ref[0, lanes, :], NT)
-        by_odd = dot(odd, table_ref[1, lanes, :], NT)
+        got = dot(wide, table_ref[lanes, :], NT)
+        by_even = got[:rows]
+        by_odd = turn_ref[0:1, lanes] * got[rows : 2 * rows] + turn_ref[1:2, lanes] * got[2 * rows :]
         out_ref[part] = (beam_ref[:, lanes] * (by_even + by_odd)).astype(BF16)
         late = pl.ds(half + share * part, share)
         out_ref[part + half // share] = (beam_ref[:, late] * (by_even - by_odd)).astype(BF16)
@@ -326,6 +343,7 @@
 
     twice = jnp.concatenate([beam[0], beam[0]], 1)
     turned = lax.dynamic_slice_in_dim(twice, (points - start % points) % points, points, 1)
+    shares, got, edge = lax.optimization_barrier((shares, got, edge))
     picked = call(
         functools.partial(pick_kernel, points),
         shape(pointings, parts, share_rows, tile),
@@ -343,34 +361,29 @@
         tiled=True,
     ).reshape(pointings, parts, share_rows, tile)
     window, weight, turned = lax.optimization_barrier((window, weight, turned))
-    row_table = row_tables(points, devices)
-    pieces = row_table.reshape(2, points // 2, -1, 256).transpose(0, 2, 1, 3)
-    pieces = bf16(pieces.reshape(-1, points // 2, 256))
+    across, turn = bf16(row_table(points, devices)), jnp.asarray(row_turn(points))
     spectrum = call(
         row_kernel,
         shape(devices, rows, 128),
-        [VMEM, VMEM, HBM],
+        [VMEM] * 4,
         window,
         turned,
-        pieces,
-        scratch=[pltpu.VMEM(pieces.shape, BF16), pltpu.SemaphoreType.DMA((pieces.shape[0],))],
+        across,
+        turn,
         flops=rows * points * points,
-        limit=60,
     )
     col = lax.all_to_all(spectrum, IMG, split_axis=0, concat_axis=0, tiled=True)
     back = call(
         column_kernel,
         shape(points, 128),
-        [SMEM, VMEM, VMEM, HBM],
+        [SMEM] + [VMEM] * 4,
         place,
         col.reshape(points, 128),
         weight,
-        bf16(np.stack(column_tables(points))),
-        scratch=[pltpu.VMEM((2, points // 2, 128), BF16)] * 2
-        + [pltpu.VMEM((6, points // 2, points // 2), BF16), pltpu.SemaphoreType.DMA((24,))],
-        flops=8 * points * points * 128 // 2,
-        moved=16 << 20,
-        limit=60,
+        bf16(column_table(points)),
+        jnp.asarray(column_turn(points)),
+        scratch=[pltpu.VMEM((8, points // 4, 256), BF16)],
+        flops=4 * points * points * 128,
     )
     lines = lax.all_to_all(
         back.reshape(devices, rows, 128), IMG, split_axis=0, concat_axis=0, tiled=True
@@ -379,10 +392,11 @@
     contribution = call(
         pixel_kernel,
         shape(pointings, rows, share),
-        [VMEM] * 3,
+        [VMEM] * 4,
         lines,
         turned,
-        bf16(row_table),
+        across,
+        turn,
         flops=rows * points * points,
     )
     terms = lax.all_to_all(contribution, "ptg", split_axis=0, concat_axis=0, tiled=True)

time: 134 us -> 118 us (0.88)
  Pallas kernels: 23.2 us -> 11 us
  blocking collectives: 31.5 us -> 29.2 us
  local copies, waits for them, and re-layouts: 5.78 us -> 7.88 us
  starting transfers between devices: 33.2 us -> 31.2 us
    pallas_call x7, Pallas kernels: 23.2 us -> 11 us  [call(): pl.pallas_call(kernel, out_shape=outs, in_specs=specs, out_specs=jax.tree...]
    all_to_all x1, waiting for transfers between devices: 0.32 us -> 4.63 us  [shards(): lax.all_to_all(picked.reshape(pointings * parts, share_rows, tile), ('ptg...]
    unnamed x10 -> x24, local copies, waits for them, and re-layouts: 5 us -> 7.1 us
    all_to_all x1, waiting for transfers between devices: 1.64 us -> 0.01 us  [shards(): lax.all_to_all(shares, 's', split_axis=0, concat_axis=0, tiled=True)]
    all_to_all x1, starting transfers between devices: 5.97 us -> 4.56 us  [shards(): lax.all_to_all(contribution, 'ptg', split_axis=0, concat_axis=0, tiled=True)]
    all_to_all x1, blocking collectives: 15.6 us -> 14.3 us  [shards(): col = lax.all_to_all(spectrum, IMG, split_axis=0, concat_axis=0, tiled=True)]
  transfers between devices with their start and end apart: 12 -> 12, of which waited for: 9 -> 7; matrix products, arithmetic and copies ran while one was open for 2% -> 2% of each run, Pallas kernels for 1% -> 1%
where the time goes in v6:
time: 118 us; the launch traced here: 117 us
  waiting for transfers between devices  34 us (29%)
  starting transfers between devices  31.2 us (26%)
  blocking collectives  29.2 us (25%)
  Pallas kernels  11 us (9%)
  local copies, waits for them, and re-layouts  7.88 us (7%)
  other arithmetic  2.93 us (2%)
    all_to_all x1, blocking collectives, shards(): lax.all_to_all(back.reshape(devices, rows, 128), IMG, split_axis=0, conca...  15 us
    all_to_all x1, blocking collectives, shards(): col = lax.all_to_all(spectrum, IMG, split_axis=0, concat_axis=0, tiled=True)  14.3 us
    ppermute x2, waiting for transfers between devices, shards(): received.append(lax.ppermute(block, ('ptg', *IMG), pairs))  11.7 us
    pallas_call x7, Pallas kernels, call(): pl.pallas_call(kernel, out_shape=outs, in_specs=specs, out_specs=jax.tree...  11 us
    all_to_all x1, waiting for transfers between devices, shards(): lax.all_to_all(contribution, 'ptg', split_axis=0, concat_axis=0, tiled=True)  9.66 us
    all_to_all x1, starting transfers between devices, shards(): lax.all_to_all(picked.reshape(pointings * parts, share_rows, tile), ('ptg...  7.22 us
    unnamed x24, local copies, waits for them, and re-layouts  7.1 us
    all_to_all x1, starting transfers between devices, shards(): lax.all_to_all(shares, 's', split_axis=0, concat_axis=0, tiled=True)  5.79 us
  transfers between devices with their start and end apart: 12, of which 7 were waited for; matrix products, arithmetic and copies ran while one was open for 2% of the time, Pallas kernels for 1%

profile of v6, /device:TPU:14, one launch (start us, length us, event | category | flops | bytes accessed | tf_op | source)
XLA Modules:
  0.0 117.3 jit_solution(10463411336657438191)
XLA Ops:
  2.3 1.2 %copy-done.4 = s32[1,2048,128]{2,1,0:T(8,128)S(1)} copy-done((s32[1,2048,128]{2,1,0:T(8,128)S(1)}, s32[1,2048,128]{2,1,0:T(8,128)}, u32[]{:S(2)}) %copy-start.4) | copy-done | bytes 1048600
  4.2 0.8 copy-done.5
  5.1 1.6 %collective-permute-start.4 = (bf16[1024,128]{1,0:T(8,128)(2,1)S(1)}, bf16[1024,128]{1,0:T(8,128)(2,1)S(1)}, u32[]{:S(2)}, u32[]{:S(2)}) collective-permute-start(bf16[1024,128]{1,0:T(8,128)(2,1)S(1)} %get-tuple-element.22), channel_id=1, source_target_pairs={{0,15},{1,14},{2,13},{3,12},{4,11},{5,10},{6,9},{7,8},{8,7},{9,6},... | collective-permute-start | bytes 786440 | tf_op jit(solution)/shard_map/ppermute | solution.py:326
  6.7 4.0 %collective-permute-start.2 = (s32[8]{0:T(128)S(1)}, s32[8]{0:T(128)S(1)}, u32[]{:S(2)}, u32[]{:S(2)}) collective-permute-start(s32[8]{0:T(128)S(1)} %compare_select_fusion), channel_id=1, source_target_pairs={{0,48},{16,32},{32,16},{48,0},{64,112},{80,96},{96,80},{112,64},{1... | collective-permute-start | bytes 104 | tf_op jit(solution)/shard_map/ppermute | solution.py:322
  10.7 0.9 collective-permute-start
  11.6 5.8 %all-to-all-start = ((bf16[4,4,16,512]{3,2,1,0:T(8,128)(2,1)}), bf16[4,4,16,512]{3,2,1,0:T(8,128)(2,1)S(1)}, u32[]{:S(2)}, u32[]{:S(2)}) async-start(bf16[4,4,16,512]{3,2,1,0:T(8,128)(2,1)} %dynamic-slice_bitcast_fusion), calls=%async_computation | async-start | bytes 524288 | tf_op jit(solution)/shard_map/all_to_all | solution.py:320
  17.4 1.3 %collective-permute-start.5 = (bf16[16,128]{1,0:T(8,128)(2,1)S(1)}, bf16[16,128]{1,0:T(8,128)(2,1)S(1)}, u32[]{:S(2)}, u32[]{:S(2)}) collective-permute-start(bf16[16,128]{1,0:T(8,128)(2,1)S(1)} %get-tuple-element.23), channel_id=1, source_target_pairs={{8,0},{9,7},{10,6},{11,5},{12,4},{13,3},{14,2},{15,1},{24,16},{25,... | collective-permute-start | bytes 12296 | tf_op jit(solution)/shard_map/ppermute | solution.py:327
  18.7 1.4 %collective-permute-start.3 = (s32[8]{0:T(128)S(1)}, s32[8]{0:T(128)S(1)}, u32[]{:S(2)}, u32[]{:S(2)}) collective-permute-start(s32[8]{0:T(128)S(1)} %add_add_fusion), channel_id=1, source_target_pairs={{0,64},{16,80},{32,96},{48,112},{64,0},{80,16},{96,32},{112,48},{1... | collective-permute-start | bytes 104 | tf_op jit(solution)/shard_map/ppermute | solution.py:325
  20.2 2.3 %collective-permute-done.3 = s32[8]{0:T(128)S(1)} collective-permute-done((s32[8]{0:T(128)S(1)}, s32[8]{0:T(128)S(1)}, u32[]{:S(2)}, u32[]{:S(2)}) %collective-permute-start.3) | collective-permute-done | bytes 64 | tf_op jit(solution)/shard_map/ppermute | solution.py:325
  22.5 4.3 %collective-permute-done.5.edge_ref = bf16[16,128]{1,0:T(8,128)(2,1)S(1)} collective-permute-done((bf16[16,128]{1,0:T(8,128)(2,1)S(1)}, bf16[16,128]{1,0:T(8,128)(2,1)S(1)}, u32[]{:S(2)}, u32[]{:S(2)}) %collective-permute-start.5) | collective-permute-done | bytes 4128 | tf_op jit(solution)/shard_map/ppermute | solution.py:327
  26.8 2.0 %shard_map.83 = bf16[8,4,16,512]{3,2,1,0:T(8,128)(2,1)} custom-call(s32[1]{0:T(128)} %bitcast.7.place_ref, s32[8]{0:T(128)S(1)} %add.43.starts_ref, bf16[4,4,16,512]{3,2,1,0:T(8,128)(2,1)S(1)} %all-to-all-done.tiles_ref), custom_call_target="tpu_custom_call" | custom-call | bytes 1048576 | tf_op jit(solution)/shard_map/pallas_call | solution.py:277
  28.8 7.2 %all-to-all-start.1 = ((bf16[32,16,512]{2,1,0:T(8,128)(2,1)}), bf16[32,16,512]{2,1,0:T(8,128)(2,1)}, u32[]{:S(2)}, u32[]{:S(2)}) async-start(bf16[32,16,512]{2,1,0:T(8,128)(2,1)} %bitcast.8), calls=%async_computation.1 | async-start | bytes 1048576 | tf_op jit(solution)/shard_map/all_to_all | solution.py:356
  36.0 1.8 %fusion.beam_ref = f32[128,2048]{1,0:T(8,128)S(1)} fusion(s32[]{:T(128)S(6)} %select_n.59, f32[128,2048]{1,0:T(8,128)} %bitcast.32), kind=kLoop, calls=%fused_computation.2 | loop fusion | flops 262144 | bytes 2097156 | tf_op jit(solution)/shard_map/concatenate | solution.py:344
  37.9 1.0 copy-done.6
  38.9 1.4 %shard_map.84.weight_ref = bf16[2048,128]{1,0:T(8,128)(2,1)S(1)} custom-call(s32[1]{0:T(128)} %bitcast.4.me_ref, bf16[2048,128]{1,0:T(8,128)(2,1)S(1)} %copy-done.6, bf16[1024,128]{1,0:T(8,128)(2,1)S(1)} %collective-permute-done.4.got_ref, bf16[16,128]{1,0:T(8,128)(2,1)S(1)} %collective-permute-done.5.edge_ref), custom_call_target="tpu_custom_call" | custom-call | flops 268435456 | bytes 4194304 | tf_op jit(solution)/shard_map/pallas_call | solution.py:277
  40.3 0.8 copy-done.7
  41.1 4.6 %all-to-all-done.1 = bf16[32,16,512]{2,1,0:T(8,128)(2,1)} async-done(((bf16[32,16,512]{2,1,0:T(8,128)(2,1)}), bf16[32,16,512]{2,1,0:T(8,128)(2,1)}, u32[]{:S(2)}, u32[]{:S(2)}) %all-to-all-start.1) | async-done | bytes 524320 | tf_op jit(solution)/shard_map/all_to_all | solution.py:356
  45.8 1.6 %copy-done.1 = bf16[1024,1024]{1,0:T(8,128)(2,1)S(1)} copy-done((bf16[1024,1024]{1,0:T(8,128)(2,1)S(1)}, bf16[1024,1024]{1,0:T(8,128)(2,1)}, u32[]{:S(2)}) %copy-start.1) | copy-done | bytes 2097176
  47.3 2.3 %shard_map.85 = bf16[16,128,128]{2,1,0:T(8,128)(2,1)S(1)} custom-call(bf16[8,4,16,512]{3,2,1,0:T(8,128)(2,1)} %bitcast.9.window_ref, f32[128,2048]{1,0:T(8,128)S(1)} %fusion.beam_ref, bf16[1024,1024]{1,0:T(8,128)(2,1)S(1)} %copy-done.1, f32[8,1024]{1,0:T(8,128)S(1)} %copy-done.9), custom_call_target="tpu_custom_call" | custom-call | flops 536870912 | bytes 4194304 | tf_op jit(solution)/shard_map/pallas_call | solution.py:277
  49.6 14.3 %all_to_all.25 = bf16[16,128,128]{2,1,0:T(8,128)(2,1)S(1)} all-to-all(bf16[16,128,128]{2,1,0:T(8,128)(2,1)S(1)} %shard_map.85), channel_id=1, replica_groups=mesh['ptg'=8,'s'=4,'b'=4] {'s','b'}, dimensions={0} | all-to-all | bytes 1048576 | tf_op jit(solution)/shard_map/all_to_all | solution.py:375
  63.9 2.7 %shard_map.86 = bf16[2048,128]{1,0:T(8,128)(2,1)S(1)} custom-call(s32[1]{0:T(128)} %bitcast.4.me_ref, bf16[2048,128]{1,0:T(8,128)(2,1)S(1)} %bitcast.30, bf16[2048,128]{1,0:T(8,128)(2,1)S(1)} %copy-done.8, bf16[1024,512]{1,0:T(8,128)(2,1)S(1)} %copy-done.10, f32[512,128]{1,0:T(8,128)S(1)} %copy-done.11), custom_call_target="tpu_custom_call" | custom-call | flops 2147483648 | bytes 4194304 | tf_op jit(solution)/shard_map/pallas_call | solution.py:277
  66.6 15.0 %all_to_all.26.x_ref = bf16[16,128,128]{2,1,0:T(8,128)(2,1)S(1)} all-to-all(bf16[16,128,128]{2,1,0:T(8,128)(2,1)S(1)} %bitcast.31), channel_id=1, replica_groups=mesh['ptg'=8,'s'=4,'b'=4] {'s','b'}, dimensions={0} | all-to-all | bytes 1048576 | tf_op jit(solution)/shard_map/all_to_all | solution.py:388
  81.6 1.1 shard_map.87
  82.7 0.8 copy-done.3
  83.5 4.6 %all-to-all-start.4 = ((bf16[8,128,256]{2,1,0:T(8,128)(2,1)}), bf16[8,128,256]{2,1,0:T(8,128)(2,1)S(1)}, u32[]{:S(2)}, u32[]{:S(2)}) async-start(bf16[8,128,256]{2,1,0:T(8,128)(2,1)} %copy-done.3), calls=%async_computation.4 | async-start | bytes 1048576 | tf_op jit(solution)/shard_map/all_to_all | solution.py:402
  88.1 9.7 %all-to-all-done.4.terms_ref = bf16[8,128,256]{2,1,0:T(8,128)(2,1)S(1)} async-done(((bf16[8,128,256]{2,1,0:T(8,128)(2,1)}), bf16[8,128,256]{2,1,0:T(8,128)(2,1)S(1)}, u32[]{:S(2)}, u32[]{:S(2)}) %all-to-all-start.4) | async-done | bytes 524320 | tf_op jit(solution)/shard_map/all_to_all | solution.py:402
  97.8 1.0 shard_map.88
  98.9 1.3 %collective-permute-done.6 = bf16[2,128,256]{2,1,0:T(8,128)(2,1)S(1)} collective-permute-done((bf16[2,128,256]{2,1,0:T(8,128)(2,1)S(1)}, bf16[2,128,256]{2,1,0:T(8,128)(2,1)S(1)}, u32[]{:S(2)}, u32[]{:S(2)}) %collective-permute-start.6) | collective-permute-done | bytes 131104 | tf_op jit(solution)/shard_map/ppermute | solution.py:412
  100.2 4.2 %collective-permute-start.8 = (bf16[256,256]{1,0:T(8,128)(2,1)S(1)}, bf16[256,256]{1,0:T(8,128)(2,1)S(1)}, u32[]{:S(2)}, u32[]{:S(2)}) collective-permute-start(bf16[256,256]{1,0:T(8,128)(2,1)S(1)} %pad_maximum_fusion.1), channel_id=1, source_target_pairs={{0,0},{1,8},{2,16},{3,24},{4,32},{5,40},{6,48},{7,56},{8,64},{9,72... | collective-permute-start | bytes 393224 | tf_op jit(solution)/shard_map/ppermute | solution.py:423
  104.5 8.2 %collective-permute-done.8 = bf16[256,256]{1,0:T(8,128)(2,1)S(1)} collective-permute-done((bf16[256,256]{1,0:T(8,128)(2,1)S(1)}, bf16[256,256]{1,0:T(8,128)(2,1)S(1)}, u32[]{:S(2)}, u32[]{:S(2)}) %collective-permute-start.8) | collective-permute-done | bytes 131104 | tf_op jit(solution)/shard_map/ppermute | solution.py:423
  112.7 3.5 %collective-permute-done.7 = bf16[256,256]{1,0:T(8,128)(2,1)S(1)} collective-permute-done((bf16[256,256]{1,0:T(8,128)(2,1)S(1)}, bf16[256,256]{1,0:T(8,128)(2,1)S(1)}, u32[]{:S(2)}, u32[]{:S(2)}) %collective-permute-start.7) | collective-permute-done | bytes 131104 | tf_op jit(solution)/shard_map/ppermute | solution.py:423
  116.4 0.9 maximum_select_fusion
  (38 shorter events, 2.6 us)
Async XLA Ops:
  0.0 1.6 %copy-start = (bf16[2048,512]{1,0:T(8,128)(2,1)S(1)}, bf16[2048,512]{1,0:T(8,128)(2,1)}, u32[]{:S(2)}) copy-start(bf16[2048,512]{1,0:T(8,128)(2,1)} %param.8) | copy-start | bytes 6291460
  2.3 1.2 %copy-start.4 = (s32[1,2048,128]{2,1,0:T(8,128)S(1)}, s32[1,2048,128]{2,1,0:T(8,128)}, u32[]{:S(2)}) copy-start(s32[1,2048,128]{2,1,0:T(8,128)} %param.10) | copy-start | bytes 3145732
  4.2 0.8 copy-start.5
  5.1 21.7 %collective-permute-start.4 = (bf16[1024,128]{1,0:T(8,128)(2,1)S(1)}, bf16[1024,128]{1,0:T(8,128)(2,1)S(1)}, u32[]{:S(2)}, u32[]{:S(2)}) collective-permute-start(bf16[1024,128]{1,0:T(8,128)(2,1)S(1)} %get-tuple-element.22), channel_id=1, source_target_pairs={{0,15},{1,14},{2,13},{3,12},{4,11},{5,10},{6,9},{7,8},{8,7},{9,6},... | collective-permute-start | bytes 786440 | tf_op jit(solution)/shard_map/ppermute | solution.py:326
  6.7 12.0 %collective-permute-start.2 = (s32[8]{0:T(128)S(1)}, s32[8]{0:T(128)S(1)}, u32[]{:S(2)}, u32[]{:S(2)}) collective-permute-start(s32[8]{0:T(128)S(1)} %compare_select_fusion), channel_id=1, source_target_pairs={{0,48},{16,32},{32,16},{48,0},{64,112},{80,96},{96,80},{112,64},{1... | collective-permute-start | bytes 104 | tf_op jit(solution)/shard_map/ppermute | solution.py:322
  10.7 8.0 %collective-permute-start.1 = (s32[8]{0:T(128)S(1)}, s32[8]{0:T(128)S(1)}, u32[]{:S(2)}, u32[]{:S(2)}) collective-permute-start(s32[8]{0:T(128)S(1)} %compare_select_fusion), channel_id=1, source_target_pairs={{0,32},{16,48},{32,0},{48,16},{64,96},{80,112},{96,64},{112,80},{1... | collective-permute-start | bytes 104 | tf_op jit(solution)/shard_map/ppermute | solution.py:322
  10.7 8.0 %collective-permute-start = (s32[8]{0:T(128)S(1)}, s32[8]{0:T(128)S(1)}, u32[]{:S(2)}, u32[]{:S(2)}) collective-permute-start(s32[8]{0:T(128)S(1)} %compare_select_fusion), channel_id=1, source_target_pairs={{0,16},{16,0},{32,48},{48,32},{64,80},{80,64},{96,112},{112,96},{1... | collective-permute-start | bytes 104 | tf_op jit(solution)/shard_map/ppermute | solution.py:322
  11.6 15.2 %all-to-all-start = ((bf16[4,4,16,512]{3,2,1,0:T(8,128)(2,1)}), bf16[4,4,16,512]{3,2,1,0:T(8,128)(2,1)S(1)}, u32[]{:S(2)}, u32[]{:S(2)}) async-start(bf16[4,4,16,512]{3,2,1,0:T(8,128)(2,1)} %dynamic-slice_bitcast_fusion), calls=%async_computation | async-start | bytes 524288 | tf_op jit(solution)/shard_map/all_to_all | solution.py:320
  17.4 9.4 %collective-permute-start.5 = (bf16[16,128]{1,0:T(8,128)(2,1)S(1)}, bf16[16,128]{1,0:T(8,128)(2,1)S(1)}, u32[]{:S(2)}, u32[]{:S(2)}) collective-permute-start(bf16[16,128]{1,0:T(8,128)(2,1)S(1)} %get-tuple-element.23), channel_id=1, source_target_pairs={{8,0},{9,7},{10,6},{11,5},{12,4},{13,3},{14,2},{15,1},{24,16},{25,... | collective-permute-start | bytes 12296 | tf_op jit(solution)/shard_map/ppermute | solution.py:327
  18.7 3.8 %collective-permute-start.3 = (s32[8]{0:T(128)S(1)}, s32[8]{0:T(128)S(1)}, u32[]{:S(2)}, u32[]{:S(2)}) collective-permute-start(s32[8]{0:T(128)S(1)} %add_add_fusion), channel_id=1, source_target_pairs={{0,64},{16,80},{32,96},{48,112},{64,0},{80,16},{96,32},{112,48},{1... | collective-permute-start | bytes 104 | tf_op jit(solution)/shard_map/ppermute | solution.py:325
  28.8 17.0 %copy-start.9 = (f32[8,1024]{1,0:T(8,128)S(1)}, f32[8,1024]{1,0:T(8,128)}, u32[]{:S(2)}) copy-start(f32[8,1024]{1,0:T(8,128)} %constant.76.clone.turn_ref) | copy-start | bytes 98308
  28.8 17.0 %all-to-all-start.1 = ((bf16[32,16,512]{2,1,0:T(8,128)(2,1)}), bf16[32,16,512]{2,1,0:T(8,128)(2,1)}, u32[]{:S(2)}, u32[]{:S(2)}) async-start(bf16[32,16,512]{2,1,0:T(8,128)(2,1)} %bitcast.8), calls=%async_computation.1 | async-start | bytes 1048576 | tf_op jit(solution)/shard_map/all_to_all | solution.py:356
  37.9 1.0 copy-start.6
  40.3 0.8 copy-start.7
  45.8 1.6 %copy-start.1 = (bf16[1024,1024]{1,0:T(8,128)(2,1)S(1)}, bf16[1024,1024]{1,0:T(8,128)(2,1)}, u32[]{:S(2)}) copy-start(bf16[1024,1024]{1,0:T(8,128)(2,1)} %constant.75.clone.table_ref) | copy-start | bytes 6291460
  47.3 16.6 %copy-start.8 = (bf16[2048,128]{1,0:T(8,128)(2,1)S(1)}, bf16[2048,128]{1,0:T(8,128)(2,1)}, u32[]{:S(2)}) copy-start(bf16[2048,128]{1,0:T(8,128)(2,1)} %copy-done.7) | copy-start | bytes 1572868
  47.3 16.6 %copy-start.10 = (bf16[1024,512]{1,0:T(8,128)(2,1)S(1)}, bf16[1024,512]{1,0:T(8,128)(2,1)}, u32[]{:S(2)}) copy-start(bf16[1024,512]{1,0:T(8,128)(2,1)} %constant.77.clone.table_ref) | copy-start | bytes 3145732
  47.3 16.6 %copy-start.11 = (f32[512,128]{1,0:T(8,128)S(1)}, f32[512,128]{1,0:T(8,128)}, u32[]{:S(2)}) copy-start(f32[512,128]{1,0:T(8,128)} %constant.78.clone.turn_ref) | copy-start | bytes 786436
  63.9 17.6 %copy-start.2 = (bf16[1024,1024]{1,0:T(8,128)(2,1)S(1)}, bf16[1024,1024]{1,0:T(8,128)(2,1)}, u32[]{:S(2)}) copy-start(bf16[1024,1024]{1,0:T(8,128)(2,1)} %constant.75.clone.table_ref) | copy-start | bytes 6291460
  82.7 0.8 copy-start.3
  83.5 14.3 %all-to-all-start.4 = ((bf16[8,128,256]{2,1,0:T(8,128)(2,1)}), bf16[8,128,256]{2,1,0:T(8,128)(2,1)S(1)}, u32[]{:S(2)}, u32[]{:S(2)}) async-start(bf16[8,128,256]{2,1,0:T(8,128)(2,1)} %copy-done.3), calls=%async_computation.4 | async-start | bytes 1048576 | tf_op jit(solution)/shard_map/all_to_all | solution.py:402
  98.8 1.4 %collective-permute-start.6 = (bf16[2,128,256]{2,1,0:T(8,128)(2,1)S(1)}, bf16[2,128,256]{2,1,0:T(8,128)(2,1)S(1)}, u32[]{:S(2)}, u32[]{:S(2)}) collective-permute-start(bf16[2,128,256]{2,1,0:T(8,128)(2,1)S(1)} %get-tuple-element.30), channel_id=1, source_target_pairs={{0,1},{1,0},{2,3},{3,2},{4,5},{5,4},{6,7},{7,6},{8,9},{9,8},{10,11... | collective-permute-start | bytes 393224 | tf_op jit(solution)/shard_map/ppermute | solution.py:412
  100.2 12.5 %collective-permute-start.8 = (bf16[256,256]{1,0:T(8,128)(2,1)S(1)}, bf16[256,256]{1,0:T(8,128)(2,1)S(1)}, u32[]{:S(2)}, u32[]{:S(2)}) collective-permute-start(bf16[256,256]{1,0:T(8,128)(2,1)S(1)} %pad_maximum_fusion.1), channel_id=1, source_target_pairs={{0,0},{1,8},{2,16},{3,24},{4,32},{5,40},{6,48},{7,56},{8,64},{9,72... | collective-permute-start | bytes 393224 | tf_op jit(solution)/shard_map/ppermute | solution.py:423
  104.4 11.8 %collective-permute-start.7 = (bf16[256,256]{1,0:T(8,128)(2,1)S(1)}, bf16[256,256]{1,0:T(8,128)(2,1)S(1)}, u32[]{:S(2)}, u32[]{:S(2)}) collective-permute-start(bf16[256,256]{1,0:T(8,128)(2,1)S(1)} %pad_maximum_fusion), channel_id=1, source_target_pairs={{0,4},{1,12},{2,20},{3,28},{4,36},{5,44},{6,52},{7,60},{8,68},{9,7... | collective-permute-start | bytes 393224 | tf_op jit(solution)/shard_map/ppermute | solution.py:423

commit v7 on v6

--- a/solution.py
+++ b/solution.py
@@ -64,7 +64,7 @@
     return index(0), index(1)
 
 
-def choose_kernel(me_ref, counts_ref, own_ref, send_ref, edge_ref):
+def choose_kernel(me_ref, counts_ref, _, own_ref, send_ref, edge_ref):
     points = counts_ref.shape[0]
     source, target = grid(128, 256)
     k, sent = target % 64, target // 128
@@ -308,21 +308,41 @@
     share_rows = rows // pointings
     shares = image.reshape(laps, parts, pointings, share_rows, tile)
     shares = lax.dynamic_index_in_dim(shares, ptg, 2, keepdims=False)
+    across, turn = bf16(row_table(points, devices)), jnp.asarray(row_turn(points))
     own, send, edge = call(
         choose_kernel,
         (shape(points, 128), shape(points // 2, 128), shape(points // 128, 128)),
-        [SMEM, VMEM],
+        [SMEM, VMEM, VMEM],
         place,
         counts[0],
+        across,
         flops=points * 128 * 512,
     )
-    shares, send, edge, starts = lax.optimization_barrier((shares, send, edge, starts))
     shares = lax.all_to_all(shares, "s", split_axis=0, concat_axis=0, tiled=True)
     near = [
         lax.ppermute(starts, "ptg", [(p, p ^ bit) for p in range(pointings)]) for bit in (1, 2, 3)
     ]
     starts = starts + near[0] + near[1] + near[2]
     starts = starts + lax.ppermute(starts, "ptg", [(p, p ^ 4) for p in range(pointings)])
+    twice = jnp.concatenate([beam[0], beam[0]], 1)
+    turned = lax.dynamic_slice_in_dim(twice, (points - start % points) % points, points, 1)
+    picked = call(
+        functools.partial(pick_kernel, points),
+        shape(pointings, parts, share_rows, tile),
+        [SMEM, SMEM, VMEM],
+        lax.axis_index("b").astype(jnp.int32).reshape(1),
+        starts,
+        shares,
+        moved=1 << 20,
+    )
+    window = lax.all_to_all(
+        picked.reshape(pointings * parts, share_rows, tile),
+        ("ptg", "b"),
+        split_axis=0,
+        concat_axis=0,
+        tiled=True,
+    ).reshape(pointings, parts, share_rows, tile)
+    window, turned, own, send, edge = lax.optimization_barrier((window, turned, own, send, edge))
     got = lax.ppermute(send, IMG, [(i, devices - 1 - i) for i in range(devices)])
     edge = lax.ppermute(
         edge,
@@ -341,27 +361,6 @@
         flops=points * 128 * 1024,
     )
 
-    twice = jnp.concatenate([beam[0], beam[0]], 1)
-    turned = lax.dynamic_slice_in_dim(twice, (points - start % points) % points, points, 1)
-    shares, got, edge = lax.optimization_barrier((shares, got, edge))
-    picked = call(
-        functools.partial(pick_kernel, points),
-        shape(pointings, parts, share_rows, tile),
-        [SMEM, SMEM, VMEM],
-        lax.axis_index("b").astype(jnp.int32).reshape(1),
-        starts,
-        shares,
-        moved=1 << 20,
-    )
-    window = lax.all_to_all(
-        picked.reshape(pointings * parts, share_rows, tile),
-        ("ptg", "b"),
-        split_axis=0,
-        concat_axis=0,
-        tiled=True,
-    ).reshape(pointings, parts, share_rows, tile)
-    window, weight, turned = lax.optimization_barrier((window, weight, turned))
-    across, turn = bf16(row_table(points, devices)), jnp.asarray(row_turn(points))
     spectrum = call(
         row_kernel,
         shape(devices, rows, 128),

time: 118 us -> 126 us (1.068)
  blocking collectives: 29.2 us -> 14.8 us
  starting transfers between devices: 31.2 us -> 42.2 us
  waiting for transfers between devices: 34 us -> 41.8 us
  local copies, waits for them, and re-layouts: 7.88 us -> 11.4 us
    all_to_all x1 -> x0, blocking collectives: 14.3 us -> none  [shards(): col = lax.all_to_all(spectrum, IMG, split_axis=0, concat_axis=0, tiled=True)]
    all_to_all x0 -> x1, starting transfers between devices: none -> 5.82 us  [shards(): col = lax.all_to_all(spectrum, IMG, split_axis=0, concat_axis=0, tiled=True)]
    ppermute x1, waiting for transfers between devices: 4.28 us -> 8.27 us  [shards(): lax.ppermute(edge, IMG, [(i, (devices - i) % (devices // 2)) for i in ran...]
    unnamed x24 -> x30, local copies, waits for them, and re-layouts: 7.1 us -> 10.7 us
    ppermute x2, starting transfers between devices: 4.27 us -> 7.35 us  [shards(): received.append(lax.ppermute(block, ('ptg', *IMG), pairs))]
    ppermute x1, waiting for transfers between devices: 0.01 us -> 2.75 us  [shards(): lax.ppermute(send, IMG, [(i, devices - 1 - i) for i in range(devices)])]
    ppermute x2, waiting for transfers between devices: 11.7 us -> 9.12 us  [shards(): received.append(lax.ppermute(block, ('ptg', *IMG), pairs))]
    all_to_all x1, waiting for transfers between devices: 0.01 us -> 1.64 us  [shards(): lax.all_to_all(shares, 's', split_axis=0, concat_axis=0, tiled=True)]
  transfers between devices with their start and end apart: 12 -> 13, of which waited for: 7 -> 9; matrix products, arithmetic and copies ran while one was open for 2% -> 1% of each run, Pallas kernels for 1% -> 2%
where the time goes in v7:
time: 126 us; the launch traced here: 125 us
  starting transfers between devices  42.2 us (33%)
  waiting for transfers between devices  41.8 us (33%)
  blocking collectives  14.8 us (12%)
  Pallas kernels  12 us (10%)
  local copies, waits for them, and re-layouts  11.4 us (9%)
  other arithmetic  1.72 us (1%)
    all_to_all x1, blocking collectives, shards(): lax.all_to_all(back.reshape(devices, rows, 128), IMG, split_axis=0, conca...  14.8 us
    pallas_call x7, Pallas kernels, call(): pl.pallas_call(kernel, out_shape=outs, in_specs=specs, out_specs=jax.tree...  12 us
    unnamed x30, local copies, waits for them, and re-layouts  10.7 us
    all_to_all x1, waiting for transfers between devices, shards(): lax.all_to_all(contribution, 'ptg', split_axis=0, concat_axis=0, tiled=True)  9.63 us
    ppermute x2, waiting for transfers between devices, shards(): received.append(lax.ppermute(block, ('ptg', *IMG), pairs))  9.12 us
    ppermute x1, waiting for transfers between devices, shards(): lax.ppermute(edge, IMG, [(i, (devices - i) % (devices // 2)) for i in ran...  8.27 us
    ppermute x2, starting transfers between devices, shards(): received.append(lax.ppermute(block, ('ptg', *IMG), pairs))  7.35 us
    all_to_all x1, starting transfers between devices, shards(): lax.all_to_all(picked.reshape(pointings * parts, share_rows, tile), ('ptg...  7.08 us
  transfers between devices with their start and end apart: 13, of which 9 were waited for; matrix products, arithmetic and copies ran while one was open for 1% of the time, Pallas kernels for 2%

profile of v7, /device:TPU:14, one launch (start us, length us, event | category | flops | bytes accessed | tf_op | source)
XLA Modules:
  0.0 124.9 jit_solution(1998598907974064082)
XLA Ops:
  0.8 2.0 %collective-permute-start = (s32[8]{0:T(128)S(1)}, s32[8]{0:T(128)S(1)}, u32[]{:S(2)}, u32[]{:S(2)}) collective-permute-start(s32[8]{0:T(128)S(1)} %compare_select_fusion), channel_id=1, source_target_pairs={{0,16},{16,0},{32,48},{48,32},{64,80},{80,64},{96,112},{112,96},{1... | collective-permute-start | bytes 104 | tf_op jit(solution)/shard_map/ppermute | solution.py:323
  2.8 3.6 %collective-permute-start.1 = (s32[8]{0:T(128)S(1)}, s32[8]{0:T(128)S(1)}, u32[]{:S(2)}, u32[]{:S(2)}) collective-permute-start(s32[8]{0:T(128)S(1)} %compare_select_fusion), channel_id=1, source_target_pairs={{0,32},{16,48},{32,0},{48,16},{64,96},{80,112},{96,64},{112,80},{1... | collective-permute-start | bytes 104 | tf_op jit(solution)/shard_map/ppermute | solution.py:323
  7.1 6.5 %all-to-all-start = ((bf16[4,4,16,512]{3,2,1,0:T(8,128)(2,1)}), bf16[4,4,16,512]{3,2,1,0:T(8,128)(2,1)S(1)}, u32[]{:S(2)}, u32[]{:S(2)}) async-start(bf16[4,4,16,512]{3,2,1,0:T(8,128)(2,1)} %dynamic-slice_bitcast_fusion), calls=%async_computation | async-start | bytes 524288 | tf_op jit(solution)/shard_map/all_to_all | solution.py:321
  13.7 1.4 %collective-permute-start.3 = (s32[8]{0:T(128)S(1)}, s32[8]{0:T(128)S(1)}, u32[]{:S(2)}, u32[]{:S(2)}) collective-permute-start(s32[8]{0:T(128)S(1)} %add_add_fusion), channel_id=1, source_target_pairs={{0,64},{16,80},{32,96},{48,112},{64,0},{80,16},{96,32},{112,48},{1... | collective-permute-start | bytes 104 | tf_op jit(solution)/shard_map/ppermute | solution.py:326
  15.1 3.0 %collective-permute-done.3 = s32[8]{0:T(128)S(1)} collective-permute-done((s32[8]{0:T(128)S(1)}, s32[8]{0:T(128)S(1)}, u32[]{:S(2)}, u32[]{:S(2)}) %collective-permute-start.3) | collective-permute-done | bytes 64 | tf_op jit(solution)/shard_map/ppermute | solution.py:326
  18.1 1.6 %all-to-all-done.tiles_ref = bf16[4,4,16,512]{3,2,1,0:T(8,128)(2,1)S(1)} async-done(((bf16[4,4,16,512]{3,2,1,0:T(8,128)(2,1)}), bf16[4,4,16,512]{3,2,1,0:T(8,128)(2,1)S(1)}, u32[]{:S(2)}, u32[]{:S(2)}) %all-to-all-start) | async-done | bytes 262176 | tf_op jit(solution)/shard_map/all_to_all | solution.py:321
  19.8 2.0 %shard_map.82 = bf16[8,4,16,512]{3,2,1,0:T(8,128)(2,1)} custom-call(s32[1]{0:T(128)} %bitcast.4.place_ref, s32[8]{0:T(128)S(1)} %add.42.starts_ref, bf16[4,4,16,512]{3,2,1,0:T(8,128)(2,1)S(1)} %all-to-all-done.tiles_ref), custom_call_target="tpu_custom_call" | custom-call | bytes 1048576 | tf_op jit(solution)/shard_map/pallas_call | solution.py:277
  21.8 7.1 %all-to-all-start.1 = ((bf16[32,16,512]{2,1,0:T(8,128)(2,1)}), bf16[32,16,512]{2,1,0:T(8,128)(2,1)}, u32[]{:S(2)}, u32[]{:S(2)}) async-start(bf16[32,16,512]{2,1,0:T(8,128)(2,1)} %bitcast.7), calls=%async_computation.1 | async-start | bytes 1048576 | tf_op jit(solution)/shard_map/all_to_all | solution.py:338
  28.9 1.6 %copy-done.1 = bf16[1024,1024]{1,0:T(8,128)(2,1)S(1)} copy-done((bf16[1024,1024]{1,0:T(8,128)(2,1)S(1)}, bf16[1024,1024]{1,0:T(8,128)(2,1)}, u32[]{:S(2)}) %copy-start.1) | copy-done | bytes 2097176
  32.6 6.0 %all-to-all-done.1 = bf16[32,16,512]{2,1,0:T(8,128)(2,1)} async-done(((bf16[32,16,512]{2,1,0:T(8,128)(2,1)}), bf16[32,16,512]{2,1,0:T(8,128)(2,1)}, u32[]{:S(2)}, u32[]{:S(2)}) %all-to-all-start.1) | async-done | bytes 524320 | tf_op jit(solution)/shard_map/all_to_all | solution.py:338
  38.6 1.6 %copy-done.2 = bf16[1024,1024]{1,0:T(8,128)(2,1)S(1)} copy-done((bf16[1024,1024]{1,0:T(8,128)(2,1)S(1)}, bf16[1024,1024]{1,0:T(8,128)(2,1)}, u32[]{:S(2)}) %copy-start.2) | copy-done | bytes 2097176
  40.2 2.2 %shard_map.84 = bf16[16,128,128]{2,1,0:T(8,128)(2,1)S(1)} custom-call(bf16[8,4,16,512]{3,2,1,0:T(8,128)(2,1)} %bitcast.8.window_ref, f32[128,2048]{1,0:T(8,128)S(1)} %fusion.beam_ref, bf16[1024,1024]{1,0:T(8,128)(2,1)S(1)} %copy-done.2, f32[8,1024]{1,0:T(8,128)S(1)} %copy-done.11), custom_call_target="tpu_custom_call" | custom-call | flops 536870912 | bytes 4194304 | tf_op jit(solution)/shard_map/pallas_call | solution.py:277
  43.2 5.8 %all-to-all-start.2 = ((bf16[16,128,128]{2,1,0:T(8,128)(2,1)}), bf16[16,128,128]{2,1,0:T(8,128)(2,1)}, u32[]{:S(2)}, u32[]{:S(2)}) async-start(bf16[16,128,128]{2,1,0:T(8,128)(2,1)} %copy-done.5), calls=%async_computation.2 | async-start | bytes 1048576 | tf_op jit(solution)/shard_map/all_to_all | solution.py:374
  49.0 2.7 %collective-permute-start.4 = (bf16[1024,128]{1,0:T(8,128)(2,1)S(1)}, bf16[1024,128]{1,0:T(8,128)(2,1)S(1)}, u32[]{:S(2)}, u32[]{:S(2)}) collective-permute-start(bf16[1024,128]{1,0:T(8,128)(2,1)S(1)} %get-tuple-element.21), channel_id=1, source_target_pairs={{0,15},{1,14},{2,13},{3,12},{4,11},{5,10},{6,9},{7,8},{8,7},{9,6},... | collective-permute-start | bytes 786440 | tf_op jit(solution)/shard_map/ppermute | solution.py:346
  51.7 1.3 %collective-permute-start.5 = (bf16[16,128]{1,0:T(8,128)(2,1)S(1)}, bf16[16,128]{1,0:T(8,128)(2,1)S(1)}, u32[]{:S(2)}, u32[]{:S(2)}) collective-permute-start(bf16[16,128]{1,0:T(8,128)(2,1)S(1)} %get-tuple-element.22), channel_id=1, source_target_pairs={{8,0},{9,7},{10,6},{11,5},{12,4},{13,3},{14,2},{15,1},{24,16},{25,... | collective-permute-start | bytes 12296 | tf_op jit(solution)/shard_map/ppermute | solution.py:347
  53.0 8.3 %collective-permute-done.5.edge_ref = bf16[16,128]{1,0:T(8,128)(2,1)S(1)} collective-permute-done((bf16[16,128]{1,0:T(8,128)(2,1)S(1)}, bf16[16,128]{1,0:T(8,128)(2,1)S(1)}, u32[]{:S(2)}, u32[]{:S(2)}) %collective-permute-start.5) | collective-permute-done | bytes 4128 | tf_op jit(solution)/shard_map/ppermute | solution.py:347
  61.3 2.7 %collective-permute-done.4.got_ref = bf16[1024,128]{1,0:T(8,128)(2,1)S(1)} collective-permute-done((bf16[1024,128]{1,0:T(8,128)(2,1)S(1)}, bf16[1024,128]{1,0:T(8,128)(2,1)S(1)}, u32[]{:S(2)}, u32[]{:S(2)}) %collective-permute-start.4) | collective-permute-done | bytes 262176 | tf_op jit(solution)/shard_map/ppermute | solution.py:346
  64.0 1.0 copy-done.8
  65.1 1.4 %shard_map.85.weight_ref = bf16[2048,128]{1,0:T(8,128)(2,1)S(1)} custom-call(s32[1]{0:T(128)} %bitcast.3.me_ref, bf16[2048,128]{1,0:T(8,128)(2,1)S(1)} %copy-done.8, bf16[1024,128]{1,0:T(8,128)(2,1)S(1)} %collective-permute-done.4.got_ref, bf16[16,128]{1,0:T(8,128)(2,1)S(1)} %collective-permute-done.5.edge_ref), custom_call_target="tpu_custom_call" | custom-call | flops 268435456 | bytes 4194304 | tf_op jit(solution)/shard_map/pallas_call | solution.py:277
  67.3 1.0 copy-done.10
  68.3 1.2 copy-done.12
  70.5 3.7 %shard_map.86 = bf16[2048,128]{1,0:T(8,128)(2,1)S(1)} custom-call(s32[1]{0:T(128)} %bitcast.3.me_ref, bf16[2048,128]{1,0:T(8,128)(2,1)} %bitcast.11.x_ref, bf16[2048,128]{1,0:T(8,128)(2,1)S(1)} %copy-done.10, bf16[1024,512]{1,0:T(8,128)(2,1)S(1)} %copy-done.12, f32[512,128]{1,0:T(8,128)S(1)} %copy-done.13), custom_call_target="tpu_custom_call" | custom-call | flops 2147483648 | bytes 4194304 | tf_op jit(solution)/shard_map/pallas_call | solution.py:277
  74.2 14.8 %all_to_all.25.x_ref = bf16[16,128,128]{2,1,0:T(8,128)(2,1)S(1)} all-to-all(bf16[16,128,128]{2,1,0:T(8,128)(2,1)S(1)} %bitcast.31), channel_id=1, replica_groups=mesh['ptg'=8,'s'=4,'b'=4] {'s','b'}, dimensions={0} | all-to-all | bytes 1048576 | tf_op jit(solution)/shard_map/all_to_all | solution.py:387
  89.0 1.1 shard_map.87
  90.9 4.3 %all-to-all-start.4 = ((bf16[8,128,256]{2,1,0:T(8,128)(2,1)}), bf16[8,128,256]{2,1,0:T(8,128)(2,1)S(1)}, u32[]{:S(2)}, u32[]{:S(2)}) async-start(bf16[8,128,256]{2,1,0:T(8,128)(2,1)} %copy-done.4), calls=%async_computation.4 | async-start | bytes 1048576 | tf_op jit(solution)/shard_map/all_to_all | solution.py:401
  95.3 9.6 %all-to-all-done.4.terms_ref = bf16[8,128,256]{2,1,0:T(8,128)(2,1)S(1)} async-done(((bf16[8,128,256]{2,1,0:T(8,128)(2,1)}), bf16[8,128,256]{2,1,0:T(8,128)(2,1)S(1)}, u32[]{:S(2)}, u32[]{:S(2)}) %all-to-all-start.4) | async-done | bytes 524320 | tf_op jit(solution)/shard_map/all_to_all | solution.py:401
  104.9 1.0 shard_map.88
  106.0 1.3 %collective-permute-done.6 = bf16[2,128,256]{2,1,0:T(8,128)(2,1)S(1)} collective-permute-done((bf16[2,128,256]{2,1,0:T(8,128)(2,1)S(1)}, bf16[2,128,256]{2,1,0:T(8,128)(2,1)S(1)}, u32[]{:S(2)}, u32[]{:S(2)}) %collective-permute-start.6) | collective-permute-done | bytes 131104 | tf_op jit(solution)/shard_map/ppermute | solution.py:411
  107.4 1.6 %collective-permute-start.7 = (bf16[256,256]{1,0:T(8,128)(2,1)S(1)}, bf16[256,256]{1,0:T(8,128)(2,1)S(1)}, u32[]{:S(2)}, u32[]{:S(2)}) collective-permute-start(bf16[256,256]{1,0:T(8,128)(2,1)S(1)} %pad_maximum_fusion), channel_id=1, source_target_pairs={{0,4},{1,12},{2,20},{3,28},{4,36},{5,44},{6,52},{7,60},{8,68},{9,7... | collective-permute-start | bytes 393224 | tf_op jit(solution)/shard_map/ppermute | solution.py:422
  109.0 5.8 %collective-permute-start.8 = (bf16[256,256]{1,0:T(8,128)(2,1)S(1)}, bf16[256,256]{1,0:T(8,128)(2,1)S(1)}, u32[]{:S(2)}, u32[]{:S(2)}) collective-permute-start(bf16[256,256]{1,0:T(8,128)(2,1)S(1)} %pad_maximum_fusion.1), channel_id=1, source_target_pairs={{0,0},{1,8},{2,16},{3,24},{4,32},{5,40},{6,48},{7,56},{8,64},{9,72... | collective-permute-start | bytes 393224 | tf_op jit(solution)/shard_map/ppermute | solution.py:422
  114.8 3.3 %collective-permute-done.7 = bf16[256,256]{1,0:T(8,128)(2,1)S(1)} collective-permute-done((bf16[256,256]{1,0:T(8,128)(2,1)S(1)}, bf16[256,256]{1,0:T(8,128)(2,1)S(1)}, u32[]{:S(2)}, u32[]{:S(2)}) %collective-permute-start.7) | collective-permute-done | bytes 131104 | tf_op jit(solution)/shard_map/ppermute | solution.py:422
  118.0 5.9 %collective-permute-done.8 = bf16[256,256]{1,0:T(8,128)(2,1)S(1)} collective-permute-done((bf16[256,256]{1,0:T(8,128)(2,1)S(1)}, bf16[256,256]{1,0:T(8,128)(2,1)S(1)}, u32[]{:S(2)}, u32[]{:S(2)}) %collective-permute-start.8) | collective-permute-done | bytes 131104 | tf_op jit(solution)/shard_map/ppermute | solution.py:422
  (45 shorter events, 7.4 us)
Async XLA Ops:
  0.0 6.4 %copy-start = (bf16[2048,512]{1,0:T(8,128)(2,1)S(1)}, bf16[2048,512]{1,0:T(8,128)(2,1)}, u32[]{:S(2)}) copy-start(bf16[2048,512]{1,0:T(8,128)(2,1)} %param.8) | copy-start | bytes 6291460
  0.0 28.9 %copy-start.6 = (s32[1,2048,128]{2,1,0:T(8,128)S(1)}, s32[1,2048,128]{2,1,0:T(8,128)}, u32[]{:S(2)}) copy-start(s32[1,2048,128]{2,1,0:T(8,128)} %param.10) | copy-start | bytes 3145732
  0.8 12.8 %collective-permute-start = (s32[8]{0:T(128)S(1)}, s32[8]{0:T(128)S(1)}, u32[]{:S(2)}, u32[]{:S(2)}) collective-permute-start(s32[8]{0:T(128)S(1)} %compare_select_fusion), channel_id=1, source_target_pairs={{0,16},{16,0},{32,48},{48,32},{64,80},{80,64},{96,112},{112,96},{1... | collective-permute-start | bytes 104 | tf_op jit(solution)/shard_map/ppermute | solution.py:323
  2.8 10.8 %collective-permute-start.1 = (s32[8]{0:T(128)S(1)}, s32[8]{0:T(128)S(1)}, u32[]{:S(2)}, u32[]{:S(2)}) collective-permute-start(s32[8]{0:T(128)S(1)} %compare_select_fusion), channel_id=1, source_target_pairs={{0,32},{16,48},{32,0},{48,16},{64,96},{80,112},{96,64},{112,80},{1... | collective-permute-start | bytes 104 | tf_op jit(solution)/shard_map/ppermute | solution.py:323
  6.4 7.3 %collective-permute-start.2 = (s32[8]{0:T(128)S(1)}, s32[8]{0:T(128)S(1)}, u32[]{:S(2)}, u32[]{:S(2)}) collective-permute-start(s32[8]{0:T(128)S(1)} %compare_select_fusion), channel_id=1, source_target_pairs={{0,48},{16,32},{32,16},{48,0},{64,112},{80,96},{96,80},{112,64},{1... | collective-permute-start | bytes 104 | tf_op jit(solution)/shard_map/ppermute | solution.py:323
  7.1 12.7 %all-to-all-start = ((bf16[4,4,16,512]{3,2,1,0:T(8,128)(2,1)}), bf16[4,4,16,512]{3,2,1,0:T(8,128)(2,1)S(1)}, u32[]{:S(2)}, u32[]{:S(2)}) async-start(bf16[4,4,16,512]{3,2,1,0:T(8,128)(2,1)} %dynamic-slice_bitcast_fusion), calls=%async_computation | async-start | bytes 524288 | tf_op jit(solution)/shard_map/all_to_all | solution.py:321
  13.7 4.5 %collective-permute-start.3 = (s32[8]{0:T(128)S(1)}, s32[8]{0:T(128)S(1)}, u32[]{:S(2)}, u32[]{:S(2)}) collective-permute-start(s32[8]{0:T(128)S(1)} %add_add_fusion), channel_id=1, source_target_pairs={{0,64},{16,80},{32,96},{48,112},{64,0},{80,16},{96,32},{112,48},{1... | collective-permute-start | bytes 104 | tf_op jit(solution)/shard_map/ppermute | solution.py:326
  21.8 16.8 %all-to-all-start.1 = ((bf16[32,16,512]{2,1,0:T(8,128)(2,1)}), bf16[32,16,512]{2,1,0:T(8,128)(2,1)}, u32[]{:S(2)}, u32[]{:S(2)}) async-start(bf16[32,16,512]{2,1,0:T(8,128)(2,1)} %bitcast.7), calls=%async_computation.1 | async-start | bytes 1048576 | tf_op jit(solution)/shard_map/all_to_all | solution.py:338
  28.9 1.6 %copy-start.1 = (bf16[1024,1024]{1,0:T(8,128)(2,1)S(1)}, bf16[1024,1024]{1,0:T(8,128)(2,1)}, u32[]{:S(2)}) copy-start(bf16[1024,1024]{1,0:T(8,128)(2,1)} %constant.75.clone._.table_ref) | copy-start | bytes 6291460
  30.5 1.5 %copy-start.14 = (f32[1,128,2048]{2,1,0:T(8,128)S(1)}, f32[1,128,2048]{2,1,0:T(8,128)}, u32[]{:S(2)}) copy-start(f32[1,128,2048]{2,1,0:T(8,128)} %param.9) | copy-start | bytes 3145732
  30.5 8.1 %copy-start.11 = (f32[8,1024]{1,0:T(8,128)S(1)}, f32[8,1024]{1,0:T(8,128)}, u32[]{:S(2)}) copy-start(f32[8,1024]{1,0:T(8,128)} %constant.76.clone.turn_ref) | copy-start | bytes 98308
  31.2 0.8 copy-start.7
  38.6 1.6 %copy-start.2 = (bf16[1024,1024]{1,0:T(8,128)(2,1)S(1)}, bf16[1024,1024]{1,0:T(8,128)(2,1)}, u32[]{:S(2)}) copy-start(bf16[1024,1024]{1,0:T(8,128)(2,1)} %constant.75.clone._.table_ref) | copy-start | bytes 6291460
  42.4 0.8 copy-start.5
  43.2 24.1 %all-to-all-start.2 = ((bf16[16,128,128]{2,1,0:T(8,128)(2,1)}), bf16[16,128,128]{2,1,0:T(8,128)(2,1)}, u32[]{:S(2)}, u32[]{:S(2)}) async-start(bf16[16,128,128]{2,1,0:T(8,128)(2,1)} %copy-done.5), calls=%async_computation.2 | async-start | bytes 1048576 | tf_op jit(solution)/shard_map/all_to_all | solution.py:374
  49.0 15.0 %collective-permute-start.4 = (bf16[1024,128]{1,0:T(8,128)(2,1)S(1)}, bf16[1024,128]{1,0:T(8,128)(2,1)S(1)}, u32[]{:S(2)}, u32[]{:S(2)}) collective-permute-start(bf16[1024,128]{1,0:T(8,128)(2,1)S(1)} %get-tuple-element.21), channel_id=1, source_target_pairs={{0,15},{1,14},{2,13},{3,12},{4,11},{5,10},{6,9},{7,8},{8,7},{9,6},... | collective-permute-start | bytes 786440 | tf_op jit(solution)/shard_map/ppermute | solution.py:346
  51.7 9.6 %collective-permute-start.5 = (bf16[16,128]{1,0:T(8,128)(2,1)S(1)}, bf16[16,128]{1,0:T(8,128)(2,1)S(1)}, u32[]{:S(2)}, u32[]{:S(2)}) collective-permute-start(bf16[16,128]{1,0:T(8,128)(2,1)S(1)} %get-tuple-element.22), channel_id=1, source_target_pairs={{8,0},{9,7},{10,6},{11,5},{12,4},{13,3},{14,2},{15,1},{24,16},{25,... | collective-permute-start | bytes 12296 | tf_op jit(solution)/shard_map/ppermute | solution.py:347
  64.0 1.0 copy-start.8
  66.5 0.8 copy-start.9
  67.3 1.0 copy-start.10
  68.3 1.2 copy-start.12
  69.5 0.9 copy-start.13
  70.5 18.5 %copy-start.3 = (bf16[1024,1024]{1,0:T(8,128)(2,1)S(1)}, bf16[1024,1024]{1,0:T(8,128)(2,1)}, u32[]{:S(2)}) copy-start(bf16[1024,1024]{1,0:T(8,128)(2,1)} %constant.75.clone._.table_ref) | copy-start | bytes 6291460
  90.1 0.8 copy-start.4
  90.9 14.0 %all-to-all-start.4 = ((bf16[8,128,256]{2,1,0:T(8,128)(2,1)}), bf16[8,128,256]{2,1,0:T(8,128)(2,1)S(1)}, u32[]{:S(2)}, u32[]{:S(2)}) async-start(bf16[8,128,256]{2,1,0:T(8,128)(2,1)} %copy-done.4), calls=%async_computation.4 | async-start | bytes 1048576 | tf_op jit(solution)/shard_map/all_to_all | solution.py:401
  105.9 1.4 %collective-permute-start.6 = (bf16[2,128,256]{2,1,0:T(8,128)(2,1)S(1)}, bf16[2,128,256]{2,1,0:T(8,128)(2,1)S(1)}, u32[]{:S(2)}, u32[]{:S(2)}) collective-permute-start(bf16[2,128,256]{2,1,0:T(8,128)(2,1)S(1)} %get-tuple-element.24), channel_id=1, source_target_pairs={{0,1},{1,0},{2,3},{3,2},{4,5},{5,4},{6,7},{7,6},{8,9},{9,8},{10,11... | collective-permute-start | bytes 393224 | tf_op jit(solution)/shard_map/ppermute | solution.py:411
  107.4 10.7 %collective-permute-start.7 = (bf16[256,256]{1,0:T(8,128)(2,1)S(1)}, bf16[256,256]{1,0:T(8,128)(2,1)S(1)}, u32[]{:S(2)}, u32[]{:S(2)}) collective-permute-start(bf16[256,256]{1,0:T(8,128)(2,1)S(1)} %pad_maximum_fusion), channel_id=1, source_target_pairs={{0,4},{1,12},{2,20},{3,28},{4,36},{5,44},{6,52},{7,60},{8,68},{9,7... | collective-permute-start | bytes 393224 | tf_op jit(solution)/shard_map/ppermute | solution.py:422
  109.0 14.9 %collective-permute-start.8 = (bf16[256,256]{1,0:T(8,128)(2,1)S(1)}, bf16[256,256]{1,0:T(8,128)(2,1)S(1)}, u32[]{:S(2)}, u32[]{:S(2)}) collective-permute-start(bf16[256,256]{1,0:T(8,128)(2,1)S(1)} %pad_maximum_fusion.1), channel_id=1, source_target_pairs={{0,0},{1,8},{2,16},{3,24},{4,32},{5,40},{6,48},{7,56},{8,64},{9,72... | collective-permute-start | bytes 393224 | tf_op jit(solution)/shard_map/ppermute | solution.py:422

commit v8 on v7

--- a/solution.py
+++ b/solution.py
@@ -324,6 +324,12 @@
     ]
     starts = starts + near[0] + near[1] + near[2]
     starts = starts + lax.ppermute(starts, "ptg", [(p, p ^ 4) for p in range(pointings)])
+    got = lax.ppermute(send, IMG, [(i, devices - 1 - i) for i in range(devices)])
+    edge = lax.ppermute(
+        edge,
+        IMG,
+        [(i, (devices - i) % (devices // 2)) for i in range(devices // 2, devices)],
+    )
     twice = jnp.concatenate([beam[0], beam[0]], 1)
     turned = lax.dynamic_slice_in_dim(twice, (points - start % points) % points, points, 1)
     picked = call(
@@ -335,6 +341,7 @@
         shares,
         moved=1 << 20,
     )
+    picked, got, edge = lax.optimization_barrier((picked, got, edge))
     window = lax.all_to_all(
         picked.reshape(pointings * parts, share_rows, tile),
         ("ptg", "b"),
@@ -342,13 +349,6 @@
         concat_axis=0,
         tiled=True,
     ).reshape(pointings, parts, share_rows, tile)
-    window, turned, own, send, edge = lax.optimization_barrier((window, turned, own, send, edge))
-    got = lax.ppermute(send, IMG, [(i, devices - 1 - i) for i in range(devices)])
-    edge = lax.ppermute(
-        edge,
-        IMG,
-        [(i, (devices - i) % (devices // 2)) for i in range(devices // 2, devices)],
-    )
     weight = call(
         weight_kernel,
         shape(points, 128),
@@ -360,7 +360,7 @@
         scratch=[pltpu.VMEM((points, 128), BF16), pltpu.VMEM((points, 128), F32)],
         flops=points * 128 * 1024,
     )
-
+    window, weight, turned = lax.optimization_barrier((window, weight, turned))
     spectrum = call(
         row_kernel,
         shape(devices, rows, 128),

time: 126 us -> 119 us (0.944)
  blocking collectives: 14.8 us -> 30.6 us
  starting transfers between devices: 42.2 us -> 31.5 us
  waiting for transfers between devices: 41.8 us -> 32 us
  local copies, waits for them, and re-layouts: 11.4 us -> 8.68 us
    all_to_all x0 -> x1, blocking collectives: none -> 15.6 us  [shards(): col = lax.all_to_all(spectrum, IMG, split_axis=0, concat_axis=0, tiled=True)]
    ppermute x1, waiting for transfers between devices: 8.27 us -> 0.16 us  [shards(): lax.ppermute(edge, IMG, [(i, (devices - i) % (devices // 2)) for i in ran...]
    all_to_all x1 -> x0, starting transfers between devices: 5.82 us -> none  [shards(): col = lax.all_to_all(spectrum, IMG, split_axis=0, concat_axis=0, tiled=True)]
    ppermute x2, starting transfers between devices: 7.35 us -> 4.27 us  [shards(): received.append(lax.ppermute(block, ('ptg', *IMG), pairs))]
    unnamed x30 -> x26, local copies, waits for them, and re-layouts: 10.7 us -> 7.9 us
    ppermute x1, waiting for transfers between devices: 2.75 us -> 0.01 us  [shards(): lax.ppermute(send, IMG, [(i, devices - 1 - i) for i in range(devices)])]
    ppermute x2, waiting for transfers between devices: 9.12 us -> 11.7 us  [shards(): received.append(lax.ppermute(block, ('ptg', *IMG), pairs))]
    ppermute x1, starting transfers between devices: 2.73 us -> 1.09 us  [shards(): lax.ppermute(send, IMG, [(i, devices - 1 - i) for i in range(devices)])]
  transfers between devices with their start and end apart: 13 -> 12, of which waited for: 9 -> 8; matrix products, arithmetic and copies ran while one was open for 1% -> 2% of each run, Pallas kernels for 2% -> 3%
where the time goes in v8:
time: 119 us; the launch traced here: 118 us
  waiting for transfers between devices  32 us (27%)
  starting transfers between devices  31.5 us (26%)
  blocking collectives  30.6 us (26%)
  Pallas kernels  11 us (9%)
  local copies, waits for them, and re-layouts  8.68 us (7%)
  other arithmetic  2.94 us (2%)
    all_to_all x1, blocking collectives, shards(): col = lax.all_to_all(spectrum, IMG, split_axis=0, concat_axis=0, tiled=True)  15.6 us
    all_to_all x1, blocking collectives, shards(): lax.all_to_all(back.reshape(devices, rows, 128), IMG, split_axis=0, conca...  15 us
    ppermute x2, waiting for transfers between devices, shards(): received.append(lax.ppermute(block, ('ptg', *IMG), pairs))  11.7 us
    pallas_call x7, Pallas kernels, call(): pl.pallas_call(kernel, out_shape=outs, in_specs=specs, out_specs=jax.tree...  11 us
    all_to_all x1, waiting for transfers between devices, shards(): lax.all_to_all(contribution, 'ptg', split_axis=0, concat_axis=0, tiled=True)  9.66 us
    unnamed x26, local copies, waits for them, and re-layouts  7.9 us
    all_to_all x1, starting transfers between devices, shards(): lax.all_to_all(picked.reshape(pointings * parts, share_rows, tile), ('ptg...  7.4 us
    all_to_all x1, starting transfers between devices, shards(): lax.all_to_all(shares, 's', split_axis=0, concat_axis=0, tiled=True)  5.79 us
  transfers between devices with their start and end apart: 12, of which 8 were waited for; matrix products, arithmetic and copies ran while one was open for 2% of the time, Pallas kernels for 3%

profile of v8, /device:TPU:14, one launch (start us, length us, event | category | flops | bytes accessed | tf_op | source)
XLA Modules:
  0.0 117.8 jit_solution(7886836941693279298)
XLA Ops:
  0.8 4.0 %collective-permute-start.1 = (s32[8]{0:T(128)S(1)}, s32[8]{0:T(128)S(1)}, u32[]{:S(2)}, u32[]{:S(2)}) collective-permute-start(s32[8]{0:T(128)S(1)} %compare_select_fusion), channel_id=1, source_target_pairs={{0,32},{16,48},{32,0},{48,16},{64,96},{80,112},{96,64},{112,80},{1... | collective-permute-start | bytes 104 | tf_op jit(solution)/shard_map/ppermute | solution.py:323
  5.8 1.6 %copy-done.1 = bf16[1024,1024]{1,0:T(8,128)(2,1)S(1)} copy-done((bf16[1024,1024]{1,0:T(8,128)(2,1)S(1)}, bf16[1024,1024]{1,0:T(8,128)(2,1)}, u32[]{:S(2)}) %copy-start.1) | copy-done | bytes 2097176
  7.4 1.2 %copy-done.5 = s32[1,2048,128]{2,1,0:T(8,128)S(1)} copy-done((s32[1,2048,128]{2,1,0:T(8,128)S(1)}, s32[1,2048,128]{2,1,0:T(8,128)}, u32[]{:S(2)}) %copy-start.5) | copy-done | bytes 1048600
  9.3 0.8 copy-done.6
  10.1 1.1 collective-permute-start.4
  11.2 0.7 dynamic-slice_bitcast_fusion
  11.9 5.8 %all-to-all-start = ((bf16[4,4,16,512]{3,2,1,0:T(8,128)(2,1)}), bf16[4,4,16,512]{3,2,1,0:T(8,128)(2,1)S(1)}, u32[]{:S(2)}, u32[]{:S(2)}) async-start(bf16[4,4,16,512]{3,2,1,0:T(8,128)(2,1)} %dynamic-slice_bitcast_fusion), calls=%async_computation | async-start | bytes 524288 | tf_op jit(solution)/shard_map/all_to_all | solution.py:321
  17.7 1.3 %collective-permute-start.5 = (bf16[16,128]{1,0:T(8,128)(2,1)S(1)}, bf16[16,128]{1,0:T(8,128)(2,1)S(1)}, u32[]{:S(2)}, u32[]{:S(2)}) collective-permute-start(bf16[16,128]{1,0:T(8,128)(2,1)S(1)} %get-tuple-element.17), channel_id=1, source_target_pairs={{8,0},{9,7},{10,6},{11,5},{12,4},{13,3},{14,2},{15,1},{24,16},{25,... | collective-permute-start | bytes 12296 | tf_op jit(solution)/shard_map/ppermute | solution.py:328
  19.0 1.4 %collective-permute-start.3 = (s32[8]{0:T(128)S(1)}, s32[8]{0:T(128)S(1)}, u32[]{:S(2)}, u32[]{:S(2)}) collective-permute-start(s32[8]{0:T(128)S(1)} %add_add_fusion), channel_id=1, source_target_pairs={{0,64},{16,80},{32,96},{48,112},{64,0},{80,16},{96,32},{112,48},{1... | collective-permute-start | bytes 104 | tf_op jit(solution)/shard_map/ppermute | solution.py:326
  20.5 4.4 %collective-permute-done.3 = s32[8]{0:T(128)S(1)} collective-permute-done((s32[8]{0:T(128)S(1)}, s32[8]{0:T(128)S(1)}, u32[]{:S(2)}, u32[]{:S(2)}) %collective-permute-start.3) | collective-permute-done | bytes 64 | tf_op jit(solution)/shard_map/ppermute | solution.py:326
  25.0 2.0 %shard_map.82 = bf16[8,4,16,512]{3,2,1,0:T(8,128)(2,1)} custom-call(s32[1]{0:T(128)} %bitcast.4.place_ref, s32[8]{0:T(128)S(1)} %add.42.starts_ref, bf16[4,4,16,512]{3,2,1,0:T(8,128)(2,1)S(1)} %all-to-all-done.tiles_ref), custom_call_target="tpu_custom_call" | custom-call | bytes 1048576 | tf_op jit(solution)/shard_map/pallas_call | solution.py:277
  27.1 7.4 %all-to-all-start.1 = ((bf16[32,16,512]{2,1,0:T(8,128)(2,1)}), bf16[32,16,512]{2,1,0:T(8,128)(2,1)}, u32[]{:S(2)}, u32[]{:S(2)}) async-start(bf16[32,16,512]{2,1,0:T(8,128)(2,1)} %bitcast.8), calls=%async_computation.1 | async-start | bytes 1048576 | tf_op jit(solution)/shard_map/all_to_all | solution.py:345
  34.6 1.8 %fusion.beam_ref = f32[128,2048]{1,0:T(8,128)S(1)} fusion(s32[]{:T(128)S(6)} %select_n.59, f32[128,2048]{1,0:T(8,128)} %bitcast.33), kind=kLoop, calls=%fused_computation.2 | loop fusion | flops 262144 | bytes 2097156 | tf_op jit(solution)/shard_map/concatenate | solution.py:333
  36.4 1.0 copy-done.7
  37.4 1.4 %shard_map.84.weight_ref = bf16[2048,128]{1,0:T(8,128)(2,1)S(1)} custom-call(s32[1]{0:T(128)} %bitcast.3.me_ref, bf16[2048,128]{1,0:T(8,128)(2,1)S(1)} %copy-done.7, bf16[1024,128]{1,0:T(8,128)(2,1)S(1)} %collective-permute-done.4.got_ref, bf16[16,128]{1,0:T(8,128)(2,1)S(1)} %collective-permute-done.5.edge_ref), custom_call_target="tpu_custom_call" | custom-call | flops 268435456 | bytes 4194304 | tf_op jit(solution)/shard_map/pallas_call | solution.py:277
  38.8 0.8 copy-done.8
  39.6 4.6 %all-to-all-done.1 = bf16[32,16,512]{2,1,0:T(8,128)(2,1)} async-done(((bf16[32,16,512]{2,1,0:T(8,128)(2,1)}), bf16[32,16,512]{2,1,0:T(8,128)(2,1)}, u32[]{:S(2)}, u32[]{:S(2)}) %all-to-all-start.1) | async-done | bytes 524320 | tf_op jit(solution)/shard_map/all_to_all | solution.py:345
  44.3 1.6 %copy-done.2 = bf16[1024,1024]{1,0:T(8,128)(2,1)S(1)} copy-done((bf16[1024,1024]{1,0:T(8,128)(2,1)S(1)}, bf16[1024,1024]{1,0:T(8,128)(2,1)}, u32[]{:S(2)}) %copy-start.2) | copy-done | bytes 2097176
  45.9 2.3 %shard_map.85 = bf16[16,128,128]{2,1,0:T(8,128)(2,1)S(1)} custom-call(bf16[8,4,16,512]{3,2,1,0:T(8,128)(2,1)} %bitcast.9.window_ref, f32[128,2048]{1,0:T(8,128)S(1)} %fusion.beam_ref, bf16[1024,1024]{1,0:T(8,128)(2,1)S(1)} %copy-done.2, f32[8,1024]{1,0:T(8,128)S(1)} %copy-done.10), custom_call_target="tpu_custom_call" | custom-call | flops 536870912 | bytes 4194304 | tf_op jit(solution)/shard_map/pallas_call | solution.py:277
  48.2 15.6 %all_to_all.25 = bf16[16,128,128]{2,1,0:T(8,128)(2,1)S(1)} all-to-all(bf16[16,128,128]{2,1,0:T(8,128)(2,1)S(1)} %shard_map.85), channel_id=1, replica_groups=mesh['ptg'=8,'s'=4,'b'=4] {'s','b'}, dimensions={0} | all-to-all | bytes 1048576 | tf_op jit(solution)/shard_map/all_to_all | solution.py:374
  63.8 2.7 %shard_map.86 = bf16[2048,128]{1,0:T(8,128)(2,1)S(1)} custom-call(s32[1]{0:T(128)} %bitcast.3.me_ref, bf16[2048,128]{1,0:T(8,128)(2,1)S(1)} %bitcast.31, bf16[2048,128]{1,0:T(8,128)(2,1)S(1)} %copy-done.9, bf16[1024,512]{1,0:T(8,128)(2,1)S(1)} %copy-done.11, f32[512,128]{1,0:T(8,128)S(1)} %copy-done.12), custom_call_target="tpu_custom_call" | custom-call | flops 2147483648 | bytes 4194304 | tf_op jit(solution)/shard_map/pallas_call | solution.py:277
  66.4 15.0 %all_to_all.26.x_ref = bf16[16,128,128]{2,1,0:T(8,128)(2,1)S(1)} all-to-all(bf16[16,128,128]{2,1,0:T(8,128)(2,1)S(1)} %bitcast.32), channel_id=1, replica_groups=mesh['ptg'=8,'s'=4,'b'=4] {'s','b'}, dimensions={0} | all-to-all | bytes 1048576 | tf_op jit(solution)/shard_map/all_to_all | solution.py:387
  81.4 1.1 shard_map.87
  82.5 0.8 copy-done.4
  83.3 5.2 %all-to-all-start.4 = ((bf16[8,128,256]{2,1,0:T(8,128)(2,1)}), bf16[8,128,256]{2,1,0:T(8,128)(2,1)S(1)}, u32[]{:S(2)}, u32[]{:S(2)}) async-start(bf16[8,128,256]{2,1,0:T(8,128)(2,1)} %copy-done.4), calls=%async_computation.4 | async-start | bytes 1048576 | tf_op jit(solution)/shard_map/all_to_all | solution.py:401
  88.6 9.7 %all-to-all-done.4.terms_ref = bf16[8,128,256]{2,1,0:T(8,128)(2,1)S(1)} async-done(((bf16[8,128,256]{2,1,0:T(8,128)(2,1)}), bf16[8,128,256]{2,1,0:T(8,128)(2,1)S(1)}, u32[]{:S(2)}, u32[]{:S(2)}) %all-to-all-start.4) | async-done | bytes 524320 | tf_op jit(solution)/shard_map/all_to_all | solution.py:401
  98.2 1.0 shard_map.88
  99.3 1.3 %collective-permute-done.6 = bf16[2,128,256]{2,1,0:T(8,128)(2,1)S(1)} collective-permute-done((bf16[2,128,256]{2,1,0:T(8,128)(2,1)S(1)}, bf16[2,128,256]{2,1,0:T(8,128)(2,1)S(1)}, u32[]{:S(2)}, u32[]{:S(2)}) %collective-permute-start.6) | collective-permute-done | bytes 131104 | tf_op jit(solution)/shard_map/ppermute | solution.py:411
  100.7 4.2 %collective-permute-start.8 = (bf16[256,256]{1,0:T(8,128)(2,1)S(1)}, bf16[256,256]{1,0:T(8,128)(2,1)S(1)}, u32[]{:S(2)}, u32[]{:S(2)}) collective-permute-start(bf16[256,256]{1,0:T(8,128)(2,1)S(1)} %pad_maximum_fusion.1), channel_id=1, source_target_pairs={{0,0},{1,8},{2,16},{3,24},{4,32},{5,40},{6,48},{7,56},{8,64},{9,72... | collective-permute-start | bytes 393224 | tf_op jit(solution)/shard_map/ppermute | solution.py:422
  105.0 8.2 %collective-permute-done.8 = bf16[256,256]{1,0:T(8,128)(2,1)S(1)} collective-permute-done((bf16[256,256]{1,0:T(8,128)(2,1)S(1)}, bf16[256,256]{1,0:T(8,128)(2,1)S(1)}, u32[]{:S(2)}, u32[]{:S(2)}) %collective-permute-start.8) | collective-permute-done | bytes 131104 | tf_op jit(solution)/shard_map/ppermute | solution.py:422
  113.2 3.5 %collective-permute-done.7 = bf16[256,256]{1,0:T(8,128)(2,1)S(1)} collective-permute-done((bf16[256,256]{1,0:T(8,128)(2,1)S(1)}, bf16[256,256]{1,0:T(8,128)(2,1)S(1)}, u32[]{:S(2)}, u32[]{:S(2)}) %collective-permute-start.7) | collective-permute-done | bytes 131104 | tf_op jit(solution)/shard_map/ppermute | solution.py:422
  116.9 0.9 maximum_select_fusion
  (40 shorter events, 2.4 us)
Async XLA Ops:
  0.0 11.2 %copy-start = (bf16[2048,512]{1,0:T(8,128)(2,1)S(1)}, bf16[2048,512]{1,0:T(8,128)(2,1)}, u32[]{:S(2)}) copy-start(bf16[2048,512]{1,0:T(8,128)(2,1)} %param.8) | copy-start | bytes 6291460
  0.8 18.2 %collective-permute-start.1 = (s32[8]{0:T(128)S(1)}, s32[8]{0:T(128)S(1)}, u32[]{:S(2)}, u32[]{:S(2)}) collective-permute-start(s32[8]{0:T(128)S(1)} %compare_select_fusion), channel_id=1, source_target_pairs={{0,32},{16,48},{32,0},{48,16},{64,96},{80,112},{96,64},{112,80},{1... | collective-permute-start | bytes 104 | tf_op jit(solution)/shard_map/ppermute | solution.py:323
  4.8 14.2 %collective-permute-start.2 = (s32[8]{0:T(128)S(1)}, s32[8]{0:T(128)S(1)}, u32[]{:S(2)}, u32[]{:S(2)}) collective-permute-start(s32[8]{0:T(128)S(1)} %compare_select_fusion), channel_id=1, source_target_pairs={{0,48},{16,32},{32,16},{48,0},{64,112},{80,96},{96,80},{112,64},{1... | collective-permute-start | bytes 104 | tf_op jit(solution)/shard_map/ppermute | solution.py:323
  5.5 13.5 %collective-permute-start = (s32[8]{0:T(128)S(1)}, s32[8]{0:T(128)S(1)}, u32[]{:S(2)}, u32[]{:S(2)}) collective-permute-start(s32[8]{0:T(128)S(1)} %compare_select_fusion), channel_id=1, source_target_pairs={{0,16},{16,0},{32,48},{48,32},{64,80},{80,64},{96,112},{112,96},{1... | collective-permute-start | bytes 104 | tf_op jit(solution)/shard_map/ppermute | solution.py:323
  5.8 1.6 %copy-start.1 = (bf16[1024,1024]{1,0:T(8,128)(2,1)S(1)}, bf16[1024,1024]{1,0:T(8,128)(2,1)}, u32[]{:S(2)}) copy-start(bf16[1024,1024]{1,0:T(8,128)(2,1)} %constant.75.clone._.table_ref) | copy-start | bytes 6291460
  7.4 1.2 %copy-start.5 = (s32[1,2048,128]{2,1,0:T(8,128)S(1)}, s32[1,2048,128]{2,1,0:T(8,128)}, u32[]{:S(2)}) copy-start(s32[1,2048,128]{2,1,0:T(8,128)} %param.10) | copy-start | bytes 3145732
  9.3 0.8 copy-start.6
  10.1 17.0 %collective-permute-start.4 = (bf16[1024,128]{1,0:T(8,128)(2,1)S(1)}, bf16[1024,128]{1,0:T(8,128)(2,1)S(1)}, u32[]{:S(2)}, u32[]{:S(2)}) collective-permute-start(bf16[1024,128]{1,0:T(8,128)(2,1)S(1)} %get-tuple-element.16), channel_id=1, source_target_pairs={{0,15},{1,14},{2,13},{3,12},{4,11},{5,10},{6,9},{7,8},{8,7},{9,6},... | collective-permute-start | bytes 786440 | tf_op jit(solution)/shard_map/ppermute | solution.py:327
  11.9 13.1 %all-to-all-start = ((bf16[4,4,16,512]{3,2,1,0:T(8,128)(2,1)}), bf16[4,4,16,512]{3,2,1,0:T(8,128)(2,1)S(1)}, u32[]{:S(2)}, u32[]{:S(2)}) async-start(bf16[4,4,16,512]{3,2,1,0:T(8,128)(2,1)} %dynamic-slice_bitcast_fusion), calls=%async_computation | async-start | bytes 524288 | tf_op jit(solution)/shard_map/all_to_all | solution.py:321
  17.7 9.4 %collective-permute-start.5 = (bf16[16,128]{1,0:T(8,128)(2,1)S(1)}, bf16[16,128]{1,0:T(8,128)(2,1)S(1)}, u32[]{:S(2)}, u32[]{:S(2)}) collective-permute-start(bf16[16,128]{1,0:T(8,128)(2,1)S(1)} %get-tuple-element.17), channel_id=1, source_target_pairs={{8,0},{9,7},{10,6},{11,5},{12,4},{13,3},{14,2},{15,1},{24,16},{25,... | collective-permute-start | bytes 12296 | tf_op jit(solution)/shard_map/ppermute | solution.py:328
  19.0 5.8 %collective-permute-start.3 = (s32[8]{0:T(128)S(1)}, s32[8]{0:T(128)S(1)}, u32[]{:S(2)}, u32[]{:S(2)}) collective-permute-start(s32[8]{0:T(128)S(1)} %add_add_fusion), channel_id=1, source_target_pairs={{0,64},{16,80},{32,96},{48,112},{64,0},{80,16},{96,32},{112,48},{1... | collective-permute-start | bytes 104 | tf_op jit(solution)/shard_map/ppermute | solution.py:326
  27.1 17.2 %copy-start.10 = (f32[8,1024]{1,0:T(8,128)S(1)}, f32[8,1024]{1,0:T(8,128)}, u32[]{:S(2)}) copy-start(f32[8,1024]{1,0:T(8,128)} %constant.76.clone.turn_ref) | copy-start | bytes 98308
  27.1 17.2 %all-to-all-start.1 = ((bf16[32,16,512]{2,1,0:T(8,128)(2,1)}), bf16[32,16,512]{2,1,0:T(8,128)(2,1)}, u32[]{:S(2)}, u32[]{:S(2)}) async-start(bf16[32,16,512]{2,1,0:T(8,128)(2,1)} %bitcast.8), calls=%async_computation.1 | async-start | bytes 1048576 | tf_op jit(solution)/shard_map/all_to_all | solution.py:345
  36.4 1.0 copy-start.7
  38.8 0.8 copy-start.8
  44.3 1.6 %copy-start.2 = (bf16[1024,1024]{1,0:T(8,128)(2,1)S(1)}, bf16[1024,1024]{1,0:T(8,128)(2,1)}, u32[]{:S(2)}) copy-start(bf16[1024,1024]{1,0:T(8,128)(2,1)} %constant.75.clone._.table_ref) | copy-start | bytes 6291460
  45.9 17.9 %copy-start.9 = (bf16[2048,128]{1,0:T(8,128)(2,1)S(1)}, bf16[2048,128]{1,0:T(8,128)(2,1)}, u32[]{:S(2)}) copy-start(bf16[2048,128]{1,0:T(8,128)(2,1)} %copy-done.8) | copy-start | bytes 1572868
  45.9 17.9 %copy-start.11 = (bf16[1024,512]{1,0:T(8,128)(2,1)S(1)}, bf16[1024,512]{1,0:T(8,128)(2,1)}, u32[]{:S(2)}) copy-start(bf16[1024,512]{1,0:T(8,128)(2,1)} %constant.77.clone.table_ref) | copy-start | bytes 3145732
  45.9 17.9 %copy-start.12 = (f32[512,128]{1,0:T(8,128)S(1)}, f32[512,128]{1,0:T(8,128)}, u32[]{:S(2)}) copy-start(f32[512,128]{1,0:T(8,128)} %constant.78.clone.turn_ref) | copy-start | bytes 786436
  63.8 17.6 %copy-start.3 = (bf16[1024,1024]{1,0:T(8,128)(2,1)S(1)}, bf16[1024,1024]{1,0:T(8,128)(2,1)}, u32[]{:S(2)}) copy-start(bf16[1024,1024]{1,0:T(8,128)(2,1)} %constant.75.clone._.table_ref) | copy-start | bytes 6291460
  82.5 0.8 copy-start.4
  83.3 14.9 %all-to-all-start.4 = ((bf16[8,128,256]{2,1,0:T(8,128)(2,1)}), bf16[8,128,256]{2,1,0:T(8,128)(2,1)S(1)}, u32[]{:S(2)}, u32[]{:S(2)}) async-start(bf16[8,128,256]{2,1,0:T(8,128)(2,1)} %copy-done.4), calls=%async_computation.4 | async-start | bytes 1048576 | tf_op jit(solution)/shard_map/all_to_all | solution.py:401
  99.2 1.4 %collective-permute-start.6 = (bf16[2,128,256]{2,1,0:T(8,128)(2,1)S(1)}, bf16[2,128,256]{2,1,0:T(8,128)(2,1)S(1)}, u32[]{:S(2)}, u32[]{:S(2)}) collective-permute-start(bf16[2,128,256]{2,1,0:T(8,128)(2,1)S(1)} %get-tuple-element.26), channel_id=1, source_target_pairs={{0,1},{1,0},{2,3},{3,2},{4,5},{5,4},{6,7},{7,6},{8,9},{9,8},{10,11... | collective-permute-start | bytes 393224 | tf_op jit(solution)/shard_map/ppermute | solution.py:411
  100.7 12.5 %collective-permute-start.8 = (bf16[256,256]{1,0:T(8,128)(2,1)S(1)}, bf16[256,256]{1,0:T(8,128)(2,1)S(1)}, u32[]{:S(2)}, u32[]{:S(2)}) collective-permute-start(bf16[256,256]{1,0:T(8,128)(2,1)S(1)} %pad_maximum_fusion.1), channel_id=1, source_target_pairs={{0,0},{1,8},{2,16},{3,24},{4,32},{5,40},{6,48},{7,56},{8,64},{9,72... | collective-permute-start | bytes 393224 | tf_op jit(solution)/shard_map/ppermute | solution.py:422
  104.9 11.8 %collective-permute-start.7 = (bf16[256,256]{1,0:T(8,128)(2,1)S(1)}, bf16[256,256]{1,0:T(8,128)(2,1)S(1)}, u32[]{:S(2)}, u32[]{:S(2)}) collective-permute-start(bf16[256,256]{1,0:T(8,128)(2,1)S(1)} %pad_maximum_fusion), channel_id=1, source_target_pairs={{0,4},{1,12},{2,20},{3,28},{4,36},{5,44},{6,52},{7,60},{8,68},{9,7... | collective-permute-start | bytes 393224 | tf_op jit(solution)/shard_map/ppermute | solution.py:422

commit v9 on v0

v9 whole, which is shorter than its diff:
```python
import functools

import numpy as np

import jax
import jax.numpy as jnp
from jax import lax
from jax.experimental import pallas as pl
from jax.experimental.pallas import tpu as pltpu
from jax.sharding import Mesh, PartitionSpec as P

F32, BF16 = jnp.float32, jnp.bfloat16
NT = (((1,), (1,)), ((), ()))
NN = (((1,), (0,)), ((), ()))
VMEM = pl.BlockSpec(memory_space=pltpu.VMEM)
SMEM = pl.BlockSpec(memory_space=pltpu.SMEM)


def dot(a, b, dims=NN):
    return lax.dot_general(a, b, dims, preferred_element_type=F32)


def half_table(points, devices):
    half, lanes = points // 2, points // devices
    index = np.arange(half)
    turn = 2.0 * np.pi / points * np.arange(points)
    cos_of, sin_of = np.cos(turn), -np.sin(turn)
    freq = lanes * np.arange(devices // 2)[:, None] + 2 * np.arange(lanes // 2)[None, :]
    phase = index[:, None, None] * freq[None] % points
    imag = sin_of[phase]
    imag[:, 0, 0] = cos_of[index * half % points]
    return np.concatenate([cos_of[phase], imag], axis=2).reshape(half, half)


def half_turn(points):
    angle = 2.0 * np.pi / points * np.arange(points // 2)
    made = np.zeros((points // 2, 128), np.float32)
    made[:, 0], made[:, 1] = np.cos(angle), np.sin(angle)
    return made


def quarter_table(points):
    quarter = points // 4
    index = np.arange(quarter)
    angle = 2.0 * np.pi / quarter * (index[:, None] * index[None, :] % quarter)
    return np.concatenate([np.cos(angle), -np.sin(angle)], 1)


def quarter_turn(points):
    angle = 2.0 * np.pi / points * np.arange(4)[:, None] * np.arange(points // 4)[None, :]
    return np.concatenate([np.cos(angle), np.sin(angle)]).astype(np.float32)


def bf16(table):
    return jnp.asarray(np.asarray(table, np.float32).astype(jnp.bfloat16))


def ones_where(condition):
    return jnp.where(condition, 1.0, 0.0).astype(BF16)


def grid(rows, lanes):
    index = lambda axis: lax.broadcasted_iota(jnp.int32, (rows, lanes), axis)
    return index(0), index(1)


def swap_rows(t):
    half = t.shape[0] // 2
    return jnp.concatenate([t[half:], t[:half]], 0)


def choose_kernel(counts_ref, out_ref):
    blocks = out_ref.shape[0]
    target, source = grid(128, 128)
    k, odd = target % 64, target // 64
    direct = ones_where(source == 2 * k + odd)
    negated = ones_where(source == 128 - 2 * k - odd)
    row, _ = grid(128, 128)
    for i in range(blocks // 2):
        part = lambda b: counts_ref[pl.ds(128 * b, 128)].astype(F32)
        kept = dot(direct, part(i).astype(BF16))
        mirrored = dot(negated, part(blocks - 1 - i).astype(BF16))
        wrapped = counts_ref[pl.ds(128 * (blocks - i if i else blocks // 2), 8)].astype(F32)[:1]
        mirrored = mirrored + jnp.where(row == 0, wrapped, 0.0)
        for side, m in ((0, i), (1, blocks - 1 - i)):
            out_ref[m, 0:64] = kept[64 * side : 64 * side + 64].astype(BF16)
            out_ref[m, 64:128] = mirrored[64 * side : 64 * side + 64].astype(BF16)


def weight_kernel(me_ref, got_ref, out_ref):
    zero = me_ref[0] == 0
    source, target = grid(512, 512)
    index = 4 * (target % 128) + target // 128
    direct, negated = ones_where(source == index), ones_where(source == 512 - index)
    row, lane = grid(64, 128)
    only = zero & (row == 0)
    wide_row, _ = grid(64, 512)
    group = lambda g: jnp.concatenate([got_ref[4 * g + n] for n in range(4)], 1)
    for g in range(4):
        here = dot(group(g), direct)
        there = dot(group(3 - g)[64:], negated)
        corner = jnp.where(lane == 0, got_ref[4 * ((4 - g) % 4), 64:128].astype(F32), 0.0)
        first = there[:, :128] + corner
        there = jnp.concatenate([first, there[:, 128:]], 1)
        above = here[:64] + jnp.where(zero & (wide_row == 0), 0.0, there)
        below = jnp.where(zero & (wide_row == 0), here[64:], above)
        for r in range(4):
            lanes = pl.ds(512 * r + 128 * g, 128)
            out_ref[0:64, lanes] = above[:, 128 * r : 128 * r + 128].astype(BF16)
            out_ref[64:128, lanes] = below[:, 128 * r : 128 * r + 128].astype(BF16)


def beam_kernel(start_ref, beam_ref, out_ref):
    rows, points = beam_ref.shape
    turned = pltpu.roll(beam_ref[...], lax.rem(start_ref[0], points), 1).astype(BF16)
    for s in range(4):
        for b in range(4):
            out_ref[4 * s + b] = turned[:, 512 * b + 128 * s : 512 * b + 128 * s + 128]


def pick_kernel(points, place_ref, starts_ref, tiles_ref, out_ref):
    laps, rows, wide = tiles_ref.shape
    lane = lax.broadcasted_iota(jnp.int32, (rows, wide), 1) + place_ref[0] * wide
    held = [tiles_ref[lap].astype(F32) for lap in range(laps)]
    for p in range(out_ref.shape[0]):
        ahead = lane - starts_ref[p]
        window = held[0]
        for lap in range(1, laps):
            column = ahead + lap * points
            window = jnp.where((column >= 0) & (column < points), held[lap], window)
        out_ref[p] = window.astype(BF16)


def half_kernel(window_ref, beam_ref, table_ref, turn_ref, out_ref):
    points = beam_ref.shape[0]
    half = points // 2
    blocks = out_ref.shape[0]
    beamed = window_ref[...].astype(F32) * beam_ref[...].astype(F32)
    left, right = beamed[:half], beamed[half:]
    minus = left - right
    cos_of = jnp.broadcast_to(turn_ref[:, 0:1], (half, 128))
    sin_of = jnp.broadcast_to(turn_ref[:, 1:2], (half, 128))
    folded = [left + right, minus * cos_of, minus * sin_of]
    folded = jnp.concatenate([t.astype(BF16) for t in folded], 1)
    row, _ = grid(128, 128)
    for part in range(half // 256):
        got = dot(table_ref[pl.ds(256 * part, 256), :], folded)
        for n in (0, 1):
            block = 2 * part + n
            even, by_cos, by_sin = (
                got[128 * n : 128 * (n + 1), 128 * t : 128 * (t + 1)] for t in range(3)
            )
            if block == 0:
                by_cos = jnp.where(row == 64, 0.0, by_cos)
                by_sin = jnp.where(row == 64, 0.0, by_sin)
            moved = swap_rows(by_sin)
            odd = jnp.where(row < 64, by_cos + moved, by_cos - moved)
            out_ref[block] = even.astype(BF16)
            out_ref[blocks - 1 - block] = odd.astype(BF16)


def middle_kernel(me_ref, x_ref, weight_ref, table_ref, turn_ref, out_ref, both):
    quarter = table_ref.shape[0]
    scale = 1.0 / float(16 * quarter * quarter)
    row, _ = grid(128, 256)
    sign = jnp.where(row < 64, -1.0, 1.0)
    packed = (me_ref[0] == 0) & (row % 64 == 0)
    x = []
    for t in range(4):
        x.append(jnp.concatenate([x_ref[4 * s + t] for s in range(4)], 1).astype(F32))
    even, p, odd, q = x[0] + x[2], x[0] - x[2], x[1] + x[3], x[1] - x[3]
    c1, c2, c3 = (turn_ref[r : r + 1] for r in (1, 2, 3))
    s1, s2, s3 = (turn_ref[4 + r : 5 + r] for r in (1, 2, 3))
    pairs = [
        (even + odd, None),
        (p * c1 - q * s1, -(p * s1 + q * c1)),
        ((even - odd) * c2, -(even - odd) * s2),
        (p * c3 + q * s3, q * c3 - p * s3),
    ]
    for r in range(4):
        g = pairs[r][0].astype(BF16)
        wide = jnp.concatenate([g, pairs[r][1].astype(BF16)], 0) if r else g
        for m in range(quarter // 256):
            lanes, beside = pl.ds(256 * m, 256), pl.ds(quarter + 256 * m, 256)
            by_c, by_s = dot(wide, table_ref[:, lanes]), dot(wide, table_ref[:, beside])
            by_cos, by_sin = by_c[:128], by_s[:128]
            if r:
                by_cos, by_sin = by_cos - by_s[128:], by_sin + by_c[128:]
            weight = weight_ref[:, pl.ds(r * quarter + 256 * m, 256)].astype(F32) * scale
            up = weight * (by_cos + jnp.where(packed, 0.0, sign * swap_rows(by_sin)))
            down = jnp.where(packed, weight * by_sin, -sign * swap_rows(up))
            both[r, 0:128, lanes] = up.astype(BF16)
            both[r, 128:256, lanes] = down.astype(BF16)
    for m in range(quarter // 256):
        lanes, beside = pl.ds(256 * m, 256), pl.ds(quarter + 256 * m, 256)
        parts = []
        for r in range(4):
            by_c, by_s = dot(both[r], table_ref[:, lanes]), dot(both[r], table_ref[:, beside])
            parts.append((by_c[:128] + by_s[128:], by_c[128:] - by_s[:128]))
        c1, c2, c3 = (turn_ref[r : r + 1, lanes] for r in (1, 2, 3))
        s1, s2, s3 = (turn_ref[4 + r : 5 + r, lanes] for r in (1, 2, 3))
        (g0, _), (g1, h1), (g2, h2), (g3, h3) = parts
        middle = c2 * g2 - s2 * h2
        p = c1 * g1 - s1 * h1 + c3 * g3 - s3 * h3
        q = s3 * g3 + c3 * h3 - s1 * g1 - c1 * h1
        plus, minus = g0 + middle, g0 - middle
        for t, value in enumerate((plus + p, minus + q, plus - p, minus - q)):
            for n in (0, 1):
                out_ref[4 * (2 * m + n) + t] = value[:, 128 * n : 128 * n + 128].astype(BF16)


def pixel_kernel(x_ref, beam_ref, table_ref, turn_ref, out_ref):
    blocks = x_ref.shape[0]
    half = beam_ref.shape[0] // 2
    share = out_ref.shape[1]
    row, _ = grid(128, 128)
    wide = []
    for b in range(blocks // 2):
        odd = x_ref[blocks - 1 - b].astype(F32)
        moved = swap_rows(odd)
        crossed = jnp.where(row < 64, -moved, moved)
        if b == 0:
            odd = jnp.where(row == 64, 0.0, odd)
            crossed = jnp.where(row == 64, 0.0, crossed)
        wide.append(jnp.concatenate([x_ref[b], odd.astype(BF16), crossed.astype(BF16)], 1))
    wide = jnp.concatenate(wide, 0)
    for part in range(half // share):
        rows, late = pl.ds(share * part, share), pl.ds(half + share * part, share)
        got = dot(table_ref[rows, :], wide)
        cos_of = jnp.broadcast_to(turn_ref[rows, 0:1], (share, 128))
        sin_of = jnp.broadcast_to(turn_ref[rows, 1:2], (share, 128))
        by_even = got[:, :128]
        by_odd = cos_of * got[:, 128:256] + sin_of * got[:, 256:]
        out_ref[part] = (beam_ref[rows, :].astype(F32) * (by_even + by_odd)).astype(BF16)
        out_ref[part + half // share] = (
            beam_ref[late, :].astype(F32) * (by_even - by_odd)
        ).astype(BF16)


def sum_kernel(points, place_ref, starts_ref, terms_ref, out_ref):
    pointings, rows, wide = terms_ref.shape
    lane = lax.broadcasted_iota(jnp.int32, (rows, wide), 1) + place_ref[0] * wide
    totals = [jnp.zeros((rows, wide), F32) for _ in range(out_ref.shape[0])]
    for p in range(pointings):
        term = terms_ref[p].astype(F32)
        ahead = lane - starts_ref[p]
        for lap in range(len(totals)):
            column = ahead + lap * points
            inside = (column >= 0) & (column < points)
            totals[lap] += jnp.where(inside, term, 0.0)
    for lap, total in enumerate(totals):
        out_ref[lap] = total.astype(BF16)


def call(kernel, outs, specs, *args, scratch=(), flops=0, moved=4 << 20, limit=16):
    return pl.pallas_call(
        kernel,
        out_shape=outs,
        in_specs=specs,
        out_specs=jax.tree.map(lambda _: VMEM, outs),
        scratch_shapes=list(scratch),
        compiler_params=pltpu.CompilerParams(vmem_limit_bytes=limit << 20),
        cost_estimate=pl.CostEstimate(flops=flops, bytes_accessed=moved, transcendentals=0),
    )(*args)


def shape(*dims, dtype=BF16):
    return jax.ShapeDtypeStruct(dims, dtype)


IMG = ("s", "b")


def swap(x, axes):
    return lax.all_to_all(x, axes, split_axis=0, concat_axis=0, tiled=True)


def shards(image, beam, counts, offsets):
    points = counts.shape[1]
    laps, parts = lax.axis_size("s"), lax.axis_size("b")
    devices = laps * parts
    pointings = lax.axis_size("ptg")
    rows = points // devices
    share = points // pointings
    tile = image.shape[1]
    lap, part = lax.axis_index("s").astype(jnp.int32), lax.axis_index("b").astype(jnp.int32)
    me = lax.axis_index(IMG).astype(jnp.int32).reshape(1)
    ptg = lax.axis_index("ptg").astype(jnp.int32)
    place = (laps * part + lap).reshape(1)

    starts = jnp.where(jnp.arange(pointings) == ptg, offsets[0], 0)
    near = [
        lax.ppermute(starts, "ptg", [(p, p ^ bit) for p in range(pointings)]) for bit in (1, 2, 3)
    ]
    starts = starts + near[0] + near[1] + near[2]
    starts = starts + lax.ppermute(starts, "ptg", [(p, p ^ 4) for p in range(pointings)])

    tiles = lax.dynamic_slice_in_dim(image, ptg * share, share, 0)
    tiles = tiles.reshape(share, laps, tile // laps).transpose(1, 0, 2)
    tiles = swap(tiles, "s")

    turned = call(
        beam_kernel, shape(devices, rows, 128), [SMEM, VMEM], offsets, beam[0], moved=2 << 20
    )
    turned = swap(turned, IMG).reshape(points, 128)
    chosen = call(
        choose_kernel,
        shape(devices, 128, counts.shape[2]),
        [VMEM],
        counts[0],
        flops=points * 128 * 256,
    )
    chosen = swap(chosen, IMG)

    picked = call(
        functools.partial(pick_kernel, points),
        shape(pointings, share, 128),
        [SMEM, SMEM, VMEM],
        place,
        starts,
        tiles,
        moved=1 << 20,
    )
    window = swap(picked, "ptg").reshape(points, 128)
    weight = call(
        weight_kernel,
        shape(128, points),
        [SMEM, VMEM],
        me,
        chosen,
        scratch=[],
        flops=points * 128 * 1024,
    )
    window, turned, weight = lax.optimization_barrier((window, turned, weight))
    table, turn = half_table(points, devices), jnp.asarray(half_turn(points))
    spectrum = call(
        half_kernel,
        shape(devices, 128, 128),
        [VMEM] * 4,
        window,
        turned,
        bf16(table.T),
        turn,
        flops=points * points * 128,
    )
    lines = call(
        middle_kernel,
        shape(devices, 128, 128),
        [SMEM] + [VMEM] * 4,
        me,
        swap(spectrum, IMG),
        weight,
        bf16(quarter_table(points)),
        jnp.asarray(quarter_turn(points)),
        scratch=[pltpu.VMEM((4, 256, points // 4), BF16)],
        flops=4 * points * points * 128,
    )
    contribution = call(
        pixel_kernel,
        shape(pointings, share, 128),
        [VMEM] * 4,
        swap(lines, IMG),
        turned,
        bf16(table),
        turn,
        flops=points * points * 128,
    )
    sums = call(
        functools.partial(sum_kernel, points),
        shape(laps, share, 128),
        [SMEM, SMEM, VMEM],
        place,
        starts,
        swap(contribution, "ptg"),
        moved=1 << 20,
    )
    sums = swap(sums, "s")
    return sums.transpose(1, 0, 2).reshape(share, tile).astype(F32)


def solution(mesh):
    pointings, devices = mesh.devices.shape
    split = Mesh(mesh.devices.reshape(pointings, 4, devices // 4), ("ptg", *IMG))
    return jax.shard_map(
        shards,
        mesh=split,
        in_specs=(P(None, IMG), P("ptg", IMG, None), P("ptg", None, IMG), P("ptg")),
        out_specs=P("ptg", IMG),
        check_vma=False,
    )
```

time: 1030 us -> 136 us (0.13)
  the two profiles are of different devices: /device:TPU:14 before, /device:TPU:0 now
where the time goes in v9:
time: 136 us; the launch traced here: 135 us
  blocking collectives  57.6 us (42%)
  waiting for transfers between devices  30.5 us (22%)
  starting transfers between devices  24 us (18%)
  Pallas kernels  11.3 us (8%)
  local copies, waits for them, and re-layouts  10.9 us (8%)
    all_to_all x4, blocking collectives, swap(): return lax.all_to_all(x, axes, split_axis=0, concat_axis=0, tiled=True)  57.6 us
    all_to_all x4, waiting for transfers between devices, swap(): return lax.all_to_all(x, axes, split_axis=0, concat_axis=0, tiled=True)  23.9 us
    all_to_all x4, starting transfers between devices, swap(): return lax.all_to_all(x, axes, split_axis=0, concat_axis=0, tiled=True)  18.3 us
    pallas_call x8, Pallas kernels, call(): pl.pallas_call(kernel, out_shape=outs, in_specs=specs, out_specs=jax.tree...  11.3 us
    unnamed x25, local copies, waits for them, and re-layouts  7.88 us
    ppermute x3, starting transfers between devices, shards(): lax.ppermute(starts, 'ptg', [(p, p ^ bit) for p in range(pointings)])  4.98 us
    ppermute x3, waiting for transfers between devices, shards(): lax.ppermute(starts, 'ptg', [(p, p ^ bit) for p in range(pointings)])  3.73 us
    ppermute x1, waiting for transfers between devices, shards(): lax.ppermute(starts, 'ptg', [(p, p ^ 4) for p in range(pointings)])  2.86 us
  transfers between devices with their start and end apart: 8, of which 6 were waited for; matrix products, arithmetic and copies ran while one was open for 0% of the time, Pallas kernels for 3%

profile of v9, /device:TPU:0, one launch (start us, length us, event | category | flops | bytes accessed | tf_op | source)
XLA Modules:
  0.0 135.2 jit_solution(6551384776779604423)
XLA Ops:
  0.0 1.6 %copy-done = bf16[2048,512]{1,0:T(8,128)(2,1)S(1)} copy-done((bf16[2048,512]{1,0:T(8,128)(2,1)S(1)}, bf16[2048,512]{1,0:T(8,128)(2,1)}, u32[]{:S(2)}) %copy-start) | copy-done | bytes 2097176
  1.6 0.8 copy.14
  2.5 1.8 %copy.11 = bf16[256,4,128]{2,0,1:T(8,128)(2,1)} copy(bf16[256,4,128]{0,2,1:T(8,128)(2,1)} %bitcast.20) | data formatting | bytes 524288 | tf_op jit(solution)/shard_map/reshape | solution.py:299
  4.2 7.0 %all-to-all-start = ((bf16[4,256,128]{2,1,0:T(8,128)(2,1)}), bf16[4,256,128]{2,1,0:T(8,128)(2,1)S(1)}, u32[]{:S(2)}, u32[]{:S(2)}) async-start(bf16[4,256,128]{2,1,0:T(8,128)(2,1)} %bitcast.19), calls=%async_computation | async-start | bytes 524288 | tf_op jit(solution)/shard_map/all_to_all | solution.py:275
  11.9 1.2 shard_map.92
  13.1 6.5 %all-to-all-done.tiles_ref = bf16[4,256,128]{2,1,0:T(8,128)(2,1)S(1)} async-done(((bf16[4,256,128]{2,1,0:T(8,128)(2,1)}), bf16[4,256,128]{2,1,0:T(8,128)(2,1)S(1)}, u32[]{:S(2)}, u32[]{:S(2)}) %all-to-all-start) | async-done | bytes 262176 | tf_op jit(solution)/shard_map/all_to_all | solution.py:275
  19.6 3.6 %all-to-all-start.2 = ((bf16[16,128,128]{2,1,0:T(8,128)(2,1)}), bf16[16,128,128]{2,1,0:T(8,128)(2,1)S(1)}, u32[]{:S(2)}, u32[]{:S(2)}) async-start(bf16[16,128,128]{2,1,0:T(8,128)(2,1)} %shard_map.92), calls=%async_computation.2 | async-start | bytes 1048576 | tf_op jit(solution)/shard_map/all_to_all | solution.py:275
  23.2 1.2 copy-done.6
  24.4 1.1 shard_map.93
  25.6 10.0 %all-to-all-done.2 = bf16[16,128,128]{2,1,0:T(8,128)(2,1)S(1)} async-done(((bf16[16,128,128]{2,1,0:T(8,128)(2,1)}), bf16[16,128,128]{2,1,0:T(8,128)(2,1)S(1)}, u32[]{:S(2)}, u32[]{:S(2)}) %all-to-all-start.2) | async-done | bytes 524320 | tf_op jit(solution)/shard_map/all_to_all | solution.py:275
  35.5 3.6 %all-to-all-start.3 = ((bf16[16,128,128]{2,1,0:T(8,128)(2,1)}), bf16[16,128,128]{2,1,0:T(8,128)(2,1)S(1)}, u32[]{:S(2)}, u32[]{:S(2)}) async-start(bf16[16,128,128]{2,1,0:T(8,128)(2,1)} %shard_map.93), calls=%async_computation.3 | async-start | bytes 1048576 | tf_op jit(solution)/shard_map/all_to_all | solution.py:275
  39.1 4.0 %collective-permute-start.1 = (s32[8]{0:T(128)S(1)}, s32[8]{0:T(128)S(1)}, u32[]{:S(2)}, u32[]{:S(2)}) collective-permute-start(s32[8]{0:T(128)S(1)} %compare_select_fusion), channel_id=1, source_target_pairs={{0,32},{16,48},{32,0},{48,16},{64,96},{80,112},{96,64},{112,80},{1... | collective-permute-start | bytes 104 | tf_op jit(solution)/shard_map/ppermute | solution.py:293
  44.6 3.2 %collective-permute-done.2 = s32[8]{0:T(128)S(1)} collective-permute-done((s32[8]{0:T(128)S(1)}, s32[8]{0:T(128)S(1)}, u32[]{:S(2)}, u32[]{:S(2)}) %collective-permute-start.2) | collective-permute-done | bytes 64 | tf_op jit(solution)/shard_map/ppermute | solution.py:293
  47.8 0.8 collective-permute-start.3
  48.6 2.9 %collective-permute-done.3 = s32[8]{0:T(128)S(1)} collective-permute-done((s32[8]{0:T(128)S(1)}, s32[8]{0:T(128)S(1)}, u32[]{:S(2)}, u32[]{:S(2)}) %collective-permute-start.3) | collective-permute-done | bytes 64 | tf_op jit(solution)/shard_map/ppermute | solution.py:296
  51.5 0.7 shard_map.91
  52.2 0.8 copy-done.3
  53.0 4.1 %all-to-all-start.1 = ((bf16[8,256,128]{2,1,0:T(8,128)(2,1)}), bf16[8,256,128]{2,1,0:T(8,128)(2,1)}, u32[]{:S(2)}, u32[]{:S(2)}) async-start(bf16[8,256,128]{2,1,0:T(8,128)(2,1)} %copy-done.3), calls=%async_computation.1 | async-start | bytes 1048576 | tf_op jit(solution)/shard_map/all_to_all | solution.py:275
  57.2 0.9 shard_map.94.weight_ref
  58.1 0.8 copy-done.8
  58.9 7.4 %all-to-all-done.1 = bf16[8,256,128]{2,1,0:T(8,128)(2,1)} async-done(((bf16[8,256,128]{2,1,0:T(8,128)(2,1)}), bf16[8,256,128]{2,1,0:T(8,128)(2,1)}, u32[]{:S(2)}, u32[]{:S(2)}) %all-to-all-start.1) | async-done | bytes 524320 | tf_op jit(solution)/shard_map/all_to_all | solution.py:275
  66.3 1.6 %copy-done.2 = bf16[1024,1024]{1,0:T(8,128)(2,1)S(1)} copy-done((bf16[1024,1024]{1,0:T(8,128)(2,1)S(1)}, bf16[1024,1024]{1,0:T(8,128)(2,1)}, u32[]{:S(2)}) %copy-start.2) | copy-done | bytes 2097176
  67.9 1.0 copy-done.4
  68.9 2.6 %shard_map.95 = bf16[16,128,128]{2,1,0:T(8,128)(2,1)S(1)} custom-call(bf16[2048,128]{1,0:T(8,128)(2,1)} %bitcast.5.window_ref, bf16[2048,128]{1,0:T(8,128)(2,1)S(1)} %bitcast.14, bf16[1024,1024]{1,0:T(8,128)(2,1)S(1)} %copy-done.2, f32[1024,128]{1,0:T(8,128)S(1)} %copy-done.4), custom_call_target="tpu_custom_call" | custom-call | flops 536870912 | bytes 4194304 | tf_op jit(solution)/shard_map/pallas_call | solution.py:256
  71.5 18.5 %all_to_all.40.x_ref = bf16[16,128,128]{2,1,0:T(8,128)(2,1)S(1)} all-to-all(bf16[16,128,128]{2,1,0:T(8,128)(2,1)S(1)} %shard_map.95), channel_id=1, replica_groups=mesh['ptg'=8,'s'=4,'b'=4] {'s','b'}, dimensions={0} | all-to-all | bytes 1048576 | tf_op jit(solution)/shard_map/all_to_all | solution.py:275
  90.1 2.6 %shard_map.96 = bf16[16,128,128]{2,1,0:T(8,128)(2,1)S(1)} custom-call(s32[1]{0:T(128)} %bitcast.2.me_ref, bf16[16,128,128]{2,1,0:T(8,128)(2,1)S(1)} %all_to_all.40.x_ref, bf16[128,2048]{1,0:T(8,128)(2,1)S(1)} %copy-done.9, bf16[512,1024]{1,0:T(8,128)(2,1)S(1)} %copy-done.10, f32[8,512]{1,0:T(8,128)S(1)} %copy-done.11), custom_call_target="tpu_custom_call" | custom-call | flops 2147483648 | bytes 4194304 | tf_op jit(solution)/shard_map/pallas_call | solution.py:256
  92.7 15.0 %all_to_all.41.x_ref = bf16[16,128,128]{2,1,0:T(8,128)(2,1)S(1)} all-to-all(bf16[16,128,128]{2,1,0:T(8,128)(2,1)S(1)} %shard_map.96), channel_id=1, replica_groups=mesh['ptg'=8,'s'=4,'b'=4] {'s','b'}, dimensions={0} | all-to-all | bytes 1048576 | tf_op jit(solution)/shard_map/all_to_all | solution.py:275
  107.7 1.3 shard_map.97
  109.0 12.4 %all_to_all.42.terms_ref = bf16[8,256,128]{2,1,0:T(8,128)(2,1)S(1)} all-to-all(bf16[8,256,128]{2,1,0:T(8,128)(2,1)S(1)} %shard_map.97), channel_id=1, replica_groups=mesh['ptg'=8,'s'=4,'b'=4] {'ptg'}, dimensions={0} | all-to-all | bytes 1048576 | tf_op jit(solution)/shard_map/all_to_all | solution.py:275
  121.4 0.9 shard_map.98
  122.2 11.8 %all_to_all.43 = bf16[4,256,128]{2,1,0:T(8,128)(2,1)S(1)} all-to-all(bf16[4,256,128]{2,1,0:T(8,128)(2,1)S(1)} %shard_map.98), channel_id=1, replica_groups=mesh['ptg'=8,'s'=4,'b'=4] {'s'}, dimensions={0} | all-to-all | bytes 524288 | tf_op jit(solution)/shard_map/all_to_all | solution.py:275
  134.2 1.0 copy.13
  (29 shorter events, 1.8 us)
Async XLA Ops:
  0.0 1.6 %copy-start = (bf16[2048,512]{1,0:T(8,128)(2,1)S(1)}, bf16[2048,512]{1,0:T(8,128)(2,1)}, u32[]{:S(2)}) copy-start(bf16[2048,512]{1,0:T(8,128)(2,1)} %param.9) | copy-start | bytes 6291460
  0.0 11.9 %copy-start.7 = (f32[1,128,2048]{2,1,0:T(8,128)S(1)}, f32[1,128,2048]{2,1,0:T(8,128)}, u32[]{:S(2)}) copy-start(f32[1,128,2048]{2,1,0:T(8,128)} %param.10) | copy-start | bytes 3145732
  4.2 15.4 %all-to-all-start = ((bf16[4,256,128]{2,1,0:T(8,128)(2,1)}), bf16[4,256,128]{2,1,0:T(8,128)(2,1)S(1)}, u32[]{:S(2)}, u32[]{:S(2)}) async-start(bf16[4,256,128]{2,1,0:T(8,128)(2,1)} %bitcast.19), calls=%async_computation | async-start | bytes 524288 | tf_op jit(solution)/shard_map/all_to_all | solution.py:275
  19.6 15.9 %all-to-all-start.2 = ((bf16[16,128,128]{2,1,0:T(8,128)(2,1)}), bf16[16,128,128]{2,1,0:T(8,128)(2,1)S(1)}, u32[]{:S(2)}, u32[]{:S(2)}) async-start(bf16[16,128,128]{2,1,0:T(8,128)(2,1)} %shard_map.92), calls=%async_computation.2 | async-start | bytes 1048576 | tf_op jit(solution)/shard_map/all_to_all | solution.py:275
  23.2 1.2 copy-start.6
  35.5 17.5 %all-to-all-start.3 = ((bf16[16,128,128]{2,1,0:T(8,128)(2,1)}), bf16[16,128,128]{2,1,0:T(8,128)(2,1)S(1)}, u32[]{:S(2)}, u32[]{:S(2)}) async-start(bf16[16,128,128]{2,1,0:T(8,128)(2,1)} %shard_map.93), calls=%async_computation.3 | async-start | bytes 1048576 | tf_op jit(solution)/shard_map/all_to_all | solution.py:275
  39.1 5.5 %collective-permute-start.1 = (s32[8]{0:T(128)S(1)}, s32[8]{0:T(128)S(1)}, u32[]{:S(2)}, u32[]{:S(2)}) collective-permute-start(s32[8]{0:T(128)S(1)} %compare_select_fusion), channel_id=1, source_target_pairs={{0,32},{16,48},{32,0},{48,16},{64,96},{80,112},{96,64},{112,80},{1... | collective-permute-start | bytes 104 | tf_op jit(solution)/shard_map/ppermute | solution.py:293
  43.1 4.8 %collective-permute-start.2 = (s32[8]{0:T(128)S(1)}, s32[8]{0:T(128)S(1)}, u32[]{:S(2)}, u32[]{:S(2)}) collective-permute-start(s32[8]{0:T(128)S(1)} %compare_select_fusion), channel_id=1, source_target_pairs={{0,48},{16,32},{32,16},{48,0},{64,112},{80,96},{96,80},{112,64},{1... | collective-permute-start | bytes 104 | tf_op jit(solution)/shard_map/ppermute | solution.py:293
  43.8 4.0 %collective-permute-start = (s32[8]{0:T(128)S(1)}, s32[8]{0:T(128)S(1)}, u32[]{:S(2)}, u32[]{:S(2)}) collective-permute-start(s32[8]{0:T(128)S(1)} %compare_select_fusion), channel_id=1, source_target_pairs={{0,16},{16,0},{32,48},{48,32},{64,80},{80,64},{96,112},{112,96},{1... | collective-permute-start | bytes 104 | tf_op jit(solution)/shard_map/ppermute | solution.py:293
  47.8 3.6 %collective-permute-start.3 = (s32[8]{0:T(128)S(1)}, s32[8]{0:T(128)S(1)}, u32[]{:S(2)}, u32[]{:S(2)}) collective-permute-start(s32[8]{0:T(128)S(1)} %add_add_fusion), channel_id=1, source_target_pairs={{0,64},{16,80},{32,96},{48,112},{64,0},{80,16},{96,32},{112,48},{1... | collective-permute-start | bytes 104 | tf_op jit(solution)/shard_map/ppermute | solution.py:296
  52.2 0.8 copy-start.3
  53.0 13.3 %all-to-all-start.1 = ((bf16[8,256,128]{2,1,0:T(8,128)(2,1)}), bf16[8,256,128]{2,1,0:T(8,128)(2,1)}, u32[]{:S(2)}, u32[]{:S(2)}) async-start(bf16[8,256,128]{2,1,0:T(8,128)(2,1)} %copy-done.3), calls=%async_computation.1 | async-start | bytes 1048576 | tf_op jit(solution)/shard_map/all_to_all | solution.py:275
  58.1 0.8 copy-start.8
  66.3 1.6 %copy-start.2 = (bf16[1024,1024]{1,0:T(8,128)(2,1)S(1)}, bf16[1024,1024]{1,0:T(8,128)(2,1)}, u32[]{:S(2)}) copy-start(bf16[1024,1024]{1,0:T(8,128)(2,1)} %constant.32.clone.table_ref) | copy-start | bytes 6291460
  67.9 1.0 copy-start.4
  68.9 21.1 %copy-start.9 = (bf16[128,2048]{1,0:T(8,128)(2,1)S(1)}, bf16[128,2048]{1,0:T(8,128)(2,1)}, u32[]{:S(2)}) copy-start(bf16[128,2048]{1,0:T(8,128)(2,1)} %copy-done.8) | copy-start | bytes 1572868
  68.9 21.1 %copy-start.10 = (bf16[512,1024]{1,0:T(8,128)(2,1)S(1)}, bf16[512,1024]{1,0:T(8,128)(2,1)}, u32[]{:S(2)}) copy-start(bf16[512,1024]{1,0:T(8,128)(2,1)} %constant.33.clone.table_ref) | copy-start | bytes 3145732
  68.9 21.1 %copy-start.11 = (f32[8,512]{1,0:T(8,128)S(1)}, f32[8,512]{1,0:T(8,128)}, u32[]{:S(2)}) copy-start(f32[8,512]{1,0:T(8,128)} %constant.34.clone.turn_ref) | copy-start | bytes 49156
  90.0 17.7 %copy-start.1 = (bf16[1024,1024]{1,0:T(8,128)(2,1)S(1)}, bf16[1024,1024]{1,0:T(8,128)(2,1)}, u32[]{:S(2)}) copy-start(bf16[1024,1024]{1,0:T(8,128)(2,1)} %constant.35.clone.table_ref) | copy-start | bytes 6291460
  90.1 17.6 %copy-start.5 = (f32[1024,128]{1,0:T(8,128)S(1)}, f32[1024,128]{1,0:T(8,128)}, u32[]{:S(2)}) copy-start(f32[1024,128]{1,0:T(8,128)} %constant.31.clone.turn_ref) | copy-start | bytes 1572868

commit v10 on v6

--- a/solution.py
+++ b/solution.py
@@ -64,11 +64,11 @@
     return index(0), index(1)
 
 
-def choose_kernel(me_ref, counts_ref, own_ref, send_ref, edge_ref):
+def choose_kernel(me_ref, counts_ref, send_ref, edge_ref):
     points = counts_ref.shape[0]
-    source, target = grid(128, 256)
-    k, sent = target % 64, target // 128
-    choice = ones_where(source == jnp.where(me_ref[0] < 8, 2 * k, 127 - 2 * k) + sent)
+    source, target = grid(128, 128)
+    k = target % 64
+    choice = ones_where(source == jnp.where(me_ref[0] < 8, 2 * k + 1, 128 - 2 * k))
     unit_row, unit_lane = grid(16, 128)
     first = ones_where((unit_row == 0) & (unit_lane == 0))
     lane = lax.broadcasted_iota(jnp.int32, (256, 128), 1)
@@ -76,11 +76,7 @@
         low = counts_ref[pl.ds(256 * b, 256)].astype(F32).astype(BF16)
         high = counts_ref[pl.ds(256 * b + points // 2, 256)].astype(F32).astype(BF16)
         got_low, got_high = dot(low, choice), dot(high, choice)
-        own_ref[pl.ds(256 * b, 256)] = got_low[:, :128].astype(BF16)
-        own_ref[pl.ds(256 * b + points // 2, 256)] = got_high[:, :128].astype(BF16)
-        send_ref[pl.ds(256 * b, 256)] = jnp.where(
-            lane < 64, got_low[:, 128:], got_high[:, 128:]
-        ).astype(BF16)
+        send_ref[pl.ds(256 * b, 256)] = jnp.where(lane < 64, got_low, got_high).astype(BF16)
     edges = []
     for b in range(points // 128):
         block = counts_ref[pl.ds(128 * b, 128)].astype(F32).astype(BF16)
@@ -88,8 +84,8 @@
     edge_ref[...] = jnp.concatenate(edges, 0).astype(BF16)
 
 
-def weight_kernel(me_ref, own_ref, got_ref, edge_ref, out_ref, plus, minus):
-    points = own_ref.shape[0]
+def weight_kernel(me_ref, counts_ref, got_ref, edge_ref, out_ref, plus, minus):
+    points = counts_ref.shape[0]
     target, source = grid(256, 256)
     index = 4 * (target % 64) + target // 64
     direct = ones_where(source == index)
@@ -98,11 +94,14 @@
     eye = ones_where(row == column)
     me = me_ref[0]
     low, zero = me < 8, me == 0
+    held, kept = grid(128, 128)
+    kept = kept % 64
+    choice = ones_where(held == jnp.where(low, 2 * kept, 127 - 2 * kept))
     edge = dot(eye, edge_ref[...], NT)
     lane = lax.broadcasted_iota(jnp.int32, (128, 128), 1)
     for b in range(points // 128):
         rows = pl.ds(128 * b, 128)
-        own = own_ref[rows].astype(F32)
+        own = dot(counts_ref[rows].astype(F32).astype(BF16), choice)
         packed = got_ref[pl.ds(128 * b % (points // 2), 128)].astype(F32)
         moved = pltpu.roll(packed, 64, 1)
         in_left = 128 * b < points // 2
@@ -128,18 +127,35 @@
             out_ref[pl.ds(r * points // 4 + 64 * b, 64)] = taken[64 * r : 64 * r + 64].astype(BF16)
 
 
+def cut_kernel(ptg_ref, image_ref, out_ref, sems):
+    blocks, share, _ = out_ref.shape
+    rows = image_ref.shape[0] // blocks
+    copies = []
+    for n in range(blocks):
+        first = pl.multiple_of(rows * n + share * ptg_ref[0], share)
+        copies.append(
+            pltpu.make_async_copy(image_ref.at[pl.ds(first, share)], out_ref.at[n], sems.at[n])
+        )
+    for copy in copies:
+        copy.start()
+    for copy in copies:
+        copy.wait()
+
+
 def pick_kernel(points, place_ref, starts_ref, tiles_ref, out_ref):
     laps, parts, rows, wide = tiles_ref.shape
     lane = lax.broadcasted_iota(jnp.int32, (rows, wide), 1) + place_ref[0] * wide
-    for part in range(parts):
-        held = [tiles_ref[lap, part].astype(F32) for lap in range(laps)]
-        for p in range(out_ref.shape[0]):
-            start = starts_ref[p]
-            window = jnp.zeros((rows, wide), F32)
-            for lap in range(laps):
-                column = lane + lap * points
-                inside = (column >= start) & (column < start + points)
-                window = jnp.where(inside, held[lap], window)
+    held = [[tiles_ref[lap, part].astype(F32) for part in range(parts)] for lap in range(laps)]
+    for p in range(out_ref.shape[0]):
+        ahead = lane - starts_ref[p]
+        inside = []
+        for lap in range(1, laps):
+            column = ahead + lap * points
+            inside.append((column >= 0) & (column < points))
+        for part in range(parts):
+            window = held[0][part]
+            for lap in range(1, laps):
+                window = jnp.where(inside[lap - 1], held[lap][part], window)
             out_ref[p, part] = window.astype(BF16)
 
 
@@ -306,17 +322,25 @@
 
     starts = jnp.where(jnp.arange(pointings) == ptg, start, 0)
     share_rows = rows // pointings
-    shares = image.reshape(laps, parts, pointings, share_rows, tile)
-    shares = lax.dynamic_index_in_dim(shares, ptg, 2, keepdims=False)
-    own, send, edge = call(
+    shares = call(
+        cut_kernel,
+        shape(devices, share_rows, tile),
+        [SMEM, pl.BlockSpec(memory_space=pl.ANY)],
+        ptg.reshape(1),
+        image,
+        scratch=[pltpu.SemaphoreType.DMA((devices,))],
+        moved=1 << 19,
+        limit=60,
+    ).reshape(laps, parts, share_rows, tile)
+    send, edge = call(
         choose_kernel,
-        (shape(points, 128), shape(points // 2, 128), shape(points // 128, 128)),
+        (shape(points // 2, 128), shape(points // 128, 128)),
         [SMEM, VMEM],
         place,
         counts[0],
         flops=points * 128 * 512,
     )
-    shares, send, edge, starts = lax.optimization_barrier((shares, send, edge, starts))
+    shares, send = lax.optimization_barrier((shares, send))
     shares = lax.all_to_all(shares, "s", split_axis=0, concat_axis=0, tiled=True)
     near = [
         lax.ppermute(starts, "ptg", [(p, p ^ bit) for p in range(pointings)]) for bit in (1, 2, 3)
@@ -334,7 +358,7 @@
         shape(points, 128),
         [SMEM] + [VMEM] * 3,
         place,
-        own,
+        counts[0],
         got,
         edge,
         scratch=[pltpu.VMEM((points, 128), BF16), pltpu.VMEM((points, 128), F32)],
@@ -343,7 +367,7 @@
 
     twice = jnp.concatenate([beam[0], beam[0]], 1)
     turned = lax.dynamic_slice_in_dim(twice, (points - start % points) % points, points, 1)
-    shares, got, edge = lax.optimization_barrier((shares, got, edge))
+    shares, got = lax.optimization_barrier((shares, got))
     picked = call(
         functools.partial(pick_kernel, points),
         shape(pointings, parts, share_rows, tile),
@@ -360,7 +384,10 @@
         concat_axis=0,
         tiled=True,
     ).reshape(pointings, parts, share_rows, tile)
-    window, weight, turned = lax.optimization_barrier((window, weight, turned))
+    seat = jnp.stack([ptg, me % 2])
+    window, weight, turned, seat, starts = lax.optimization_barrier(
+        (window, weight, turned, seat, starts)
+    )
     across, turn = bf16(row_table(points, devices)), jnp.asarray(row_turn(points))
     spectrum = call(
         row_kernel,
@@ -404,7 +431,7 @@
         functools.partial(sum_kernel, points),
         (shape(2, rows, share), shape(2, rows, share)),
         [SMEM, SMEM, VMEM],
-        jnp.stack([ptg, me % 2]),
+        seat,
         starts,
         terms,
         moved=1 << 20,

time: 118 us -> 115 us (0.975)
  blocking collectives: 29.2 us -> 43.8 us
  waiting for transfers between devices: 34 us -> 25.2 us
  local copies, waits for them, and re-layouts: 7.88 us -> 2.11 us
  starting transfers between devices: 31.2 us -> 26.6 us
  Pallas kernels: 11 us -> 12.2 us
    all_to_all x0 -> x1, blocking collectives: none -> 15 us  [shards(): lax.all_to_all(contribution, 'ptg', split_axis=0, concat_axis=0, tiled=True)]
    all_to_all x1 -> x0, waiting for transfers between devices: 9.66 us -> none  [shards(): lax.all_to_all(contribution, 'ptg', split_axis=0, concat_axis=0, tiled=True)]
    unnamed x24 -> x16, local copies, waits for them, and re-layouts: 7.1 us -> 2.05 us
    all_to_all x1, waiting for transfers between devices: 4.63 us -> 0.01 us  [shards(): lax.all_to_all(picked.reshape(pointings * parts, share_rows, tile), ('ptg...]
    all_to_all x1 -> x0, starting transfers between devices: 4.56 us -> none  [shards(): lax.all_to_all(contribution, 'ptg', split_axis=0, concat_axis=0, tiled=True)]
    ppermute x1, waiting for transfers between devices: 4.28 us -> 6.6 us  [shards(): lax.ppermute(edge, IMG, [(i, (devices - i) % (devices // 2)) for i in ran...]
    all_to_all x1, waiting for transfers between devices: 0.01 us -> 1.61 us  [shards(): lax.all_to_all(shares, 's', split_axis=0, concat_axis=0, tiled=True)]
    ppermute x1, waiting for transfers between devices: 2.35 us -> 3.57 us  [shards(): lax.ppermute(starts, 'ptg', [(p, p ^ 4) for p in range(pointings)])]
  transfers between devices with their start and end apart: 12 -> 11, of which waited for: 7 -> 6; matrix products, arithmetic and copies ran while one was open for 2% -> 2% of each run, Pallas kernels for 1% -> 1%
where the time goes in v10:
time: 115 us; the launch traced here: 114 us
  blocking collectives  43.8 us (38%)
  starting transfers between devices  26.6 us (23%)
  waiting for transfers between devices  25.2 us (22%)
  Pallas kernels  12.2 us (11%)
  other arithmetic  2.93 us (3%)
  local copies, waits for them, and re-layouts  2.11 us (2%)
    all_to_all x1, blocking collectives, shards(): lax.all_to_all(contribution, 'ptg', split_axis=0, concat_axis=0, tiled=True)  15 us
    all_to_all x1, blocking collectives, shards(): lax.all_to_all(back.reshape(devices, rows, 128), IMG, split_axis=0, conca...  15 us
    all_to_all x1, blocking collectives, shards(): col = lax.all_to_all(spectrum, IMG, split_axis=0, concat_axis=0, tiled=True)  13.8 us
    pallas_call x8, Pallas kernels, call(): pl.pallas_call(kernel, out_shape=outs, in_specs=specs, out_specs=jax.tree...  12.2 us
    ppermute x2, waiting for transfers between devices, shards(): received.append(lax.ppermute(block, ('ptg', *IMG), pairs))  12.1 us
    all_to_all x1, starting transfers between devices, shards(): lax.all_to_all(picked.reshape(pointings * parts, share_rows, tile), ('ptg...  7.28 us
    ppermute x1, waiting for transfers between devices, shards(): lax.ppermute(edge, IMG, [(i, (devices - i) % (devices // 2)) for i in ran...  6.6 us
    all_to_all x1, starting transfers between devices, shards(): lax.all_to_all(shares, 's', split_axis=0, concat_axis=0, tiled=True)  5.83 us
  transfers between devices with their start and end apart: 11, of which 6 were waited for; matrix products, arithmetic and copies ran while one was open for 2% of the time, Pallas kernels for 1%

profile of v10, /device:TPU:14, one launch (start us, length us, event | category | flops | bytes accessed | tf_op | source)
XLA Modules:
  0.0 113.9 jit_solution(7045960405836422470)
XLA Ops:
  0.0 1.8 %shard_map.82 = bf16[16,16,512]{2,1,0:T(8,128)(2,1)} custom-call(s32[1]{0:T(128)} %bitcast.2.ptg_ref, bf16[2048,512]{1,0:T(8,128)(2,1)} %image_ref.1), custom_call_target="tpu_custom_call" | custom-call | bytes 524288 | tf_op jit(solution)/shard_map/pallas_call | solution.py:293
  1.8 0.5 shard_map.83
  2.3 1.7 %collective-permute-start.4 = (bf16[1024,128]{1,0:T(8,128)(2,1)S(1)}, bf16[1024,128]{1,0:T(8,128)(2,1)S(1)}, u32[]{:S(2)}, u32[]{:S(2)}) collective-permute-start(bf16[1024,128]{1,0:T(8,128)(2,1)S(1)} %get-tuple-element.19), channel_id=1, source_target_pairs={{0,15},{1,14},{2,13},{3,12},{4,11},{5,10},{6,9},{7,8},{8,7},{9,6},... | collective-permute-start | bytes 786440 | tf_op jit(solution)/shard_map/ppermute | solution.py:350
  4.7 4.0 %collective-permute-start.1 = (s32[8]{0:T(128)S(1)}, s32[8]{0:T(128)S(1)}, u32[]{:S(2)}, u32[]{:S(2)}) collective-permute-start(s32[8]{0:T(128)S(1)} %compare_select_fusion), channel_id=1, source_target_pairs={{0,32},{16,48},{32,0},{48,16},{64,96},{80,112},{96,64},{112,80},{1... | collective-permute-start | bytes 104 | tf_op jit(solution)/shard_map/ppermute | solution.py:346
  8.6 0.7 collective-permute-start.2
  9.3 0.3 collective-permute-start
  9.7 5.8 %all-to-all-start = ((bf16[4,4,16,512]{3,2,1,0:T(8,128)(2,1)}), bf16[4,4,16,512]{3,2,1,0:T(8,128)(2,1)S(1)}, u32[]{:S(2)}, u32[]{:S(2)}) async-start(bf16[4,4,16,512]{3,2,1,0:T(8,128)(2,1)} %bitcast.30), calls=%async_computation | async-start | bytes 524288 | tf_op jit(solution)/shard_map/all_to_all | solution.py:344
  15.5 1.4 %collective-permute-start.3 = (s32[8]{0:T(128)S(1)}, s32[8]{0:T(128)S(1)}, u32[]{:S(2)}, u32[]{:S(2)}) collective-permute-start(s32[8]{0:T(128)S(1)} %add_add_fusion), channel_id=1, source_target_pairs={{0,64},{16,80},{32,96},{48,112},{64,0},{80,16},{96,32},{112,48},{1... | collective-permute-start | bytes 104 | tf_op jit(solution)/shard_map/ppermute | solution.py:349
  16.9 3.6 %collective-permute-done.3 = s32[8]{0:T(128)S(1)} collective-permute-done((s32[8]{0:T(128)S(1)}, s32[8]{0:T(128)S(1)}, u32[]{:S(2)}, u32[]{:S(2)}) %collective-permute-start.3) | collective-permute-done | bytes 64 | tf_op jit(solution)/shard_map/ppermute | solution.py:349
  20.5 1.6 %all-to-all-done.tiles_ref = bf16[4,4,16,512]{3,2,1,0:T(8,128)(2,1)S(1)} async-done(((bf16[4,4,16,512]{3,2,1,0:T(8,128)(2,1)}), bf16[4,4,16,512]{3,2,1,0:T(8,128)(2,1)S(1)}, u32[]{:S(2)}, u32[]{:S(2)}) %all-to-all-start) | async-done | bytes 262176 | tf_op jit(solution)/shard_map/all_to_all | solution.py:344
  22.1 1.5 %shard_map.84 = bf16[8,4,16,512]{3,2,1,0:T(8,128)(2,1)} custom-call(s32[1]{0:T(128)} %bitcast.place_ref, s32[8]{0:T(128)S(1)} %add.37.starts_ref, bf16[4,4,16,512]{3,2,1,0:T(8,128)(2,1)S(1)} %all-to-all-done.tiles_ref), custom_call_target="tpu_custom_call" | custom-call | bytes 1048576 | tf_op jit(solution)/shard_map/pallas_call | solution.py:293
  23.7 7.3 %all-to-all-start.1 = ((bf16[32,16,512]{2,1,0:T(8,128)(2,1)}), bf16[32,16,512]{2,1,0:T(8,128)(2,1)}, u32[]{:S(2)}, u32[]{:S(2)}) async-start(bf16[32,16,512]{2,1,0:T(8,128)(2,1)} %bitcast.6), calls=%async_computation.1 | async-start | bytes 1048576 | tf_op jit(solution)/shard_map/all_to_all | solution.py:380
  31.0 1.4 %collective-permute-start.5 = (bf16[16,128]{1,0:T(8,128)(2,1)S(1)}, bf16[16,128]{1,0:T(8,128)(2,1)S(1)}, u32[]{:S(2)}, u32[]{:S(2)}) collective-permute-start(bf16[16,128]{1,0:T(8,128)(2,1)S(1)} %get-tuple-element.21), channel_id=1, source_target_pairs={{8,0},{9,7},{10,6},{11,5},{12,4},{13,3},{14,2},{15,1},{24,16},{25,... | collective-permute-start | bytes 12296 | tf_op jit(solution)/shard_map/ppermute | solution.py:351
  32.5 1.8 %fusion.beam_ref = f32[128,2048]{1,0:T(8,128)S(1)} fusion(s32[]{:T(128)S(6)} %select_n.53, f32[128,2048]{1,0:T(8,128)} %bitcast.29), kind=kLoop, calls=%fused_computation.2 | loop fusion | flops 262144 | bytes 2097156 | tf_op jit(solution)/shard_map/concatenate | solution.py:368
  34.4 6.6 %collective-permute-done.5.edge_ref = bf16[16,128]{1,0:T(8,128)(2,1)S(1)} collective-permute-done((bf16[16,128]{1,0:T(8,128)(2,1)S(1)}, bf16[16,128]{1,0:T(8,128)(2,1)S(1)}, u32[]{:S(2)}, u32[]{:S(2)}) %collective-permute-start.5) | collective-permute-done | bytes 4128 | tf_op jit(solution)/shard_map/ppermute | solution.py:351
  41.0 1.2 %copy-done.2 = s32[1,2048,128]{2,1,0:T(8,128)S(1)} copy-done((s32[1,2048,128]{2,1,0:T(8,128)S(1)}, s32[1,2048,128]{2,1,0:T(8,128)}, u32[]{:S(2)}) %copy-start.2) | copy-done | bytes 1048600
  42.2 1.4 %shard_map.85.weight_ref = bf16[2048,128]{1,0:T(8,128)(2,1)S(1)} custom-call(s32[1]{0:T(128)} %bitcast.4.me_ref, s32[2048,128]{1,0:T(8,128)S(1)} %bitcast.26, bf16[1024,128]{1,0:T(8,128)(2,1)S(1)} %collective-permute-done.4.got_ref, bf16[16,128]{1,0:T(8,128)(2,1)S(1)} %collective-permute-done.5.edge_ref), custom_call_target="tpu_custom_call" | custom-call | flops 268435456 | bytes 4194304 | tf_op jit(solution)/shard_map/pallas_call | solution.py:293
  43.6 0.8 copy-done.3
  44.5 2.3 %shard_map.86 = bf16[16,128,128]{2,1,0:T(8,128)(2,1)S(1)} custom-call(bf16[8,4,16,512]{3,2,1,0:T(8,128)(2,1)} %bitcast.7.window_ref, f32[128,2048]{1,0:T(8,128)S(1)} %fusion.beam_ref, bf16[1024,1024]{1,0:T(8,128)(2,1)S(1)} %copy-done, f32[8,1024]{1,0:T(8,128)S(1)} %copy-done.5), custom_call_target="tpu_custom_call" | custom-call | flops 536870912 | bytes 4194304 | tf_op jit(solution)/shard_map/pallas_call | solution.py:293
  46.8 13.8 %all_to_all.25 = bf16[16,128,128]{2,1,0:T(8,128)(2,1)S(1)} all-to-all(bf16[16,128,128]{2,1,0:T(8,128)(2,1)S(1)} %shard_map.86), channel_id=1, replica_groups=mesh['ptg'=8,'s'=4,'b'=4] {'s','b'}, dimensions={0} | all-to-all | bytes 1048576 | tf_op jit(solution)/shard_map/all_to_all | solution.py:402
  60.6 2.6 %shard_map.87 = bf16[2048,128]{1,0:T(8,128)(2,1)S(1)} custom-call(s32[1]{0:T(128)} %bitcast.4.me_ref, bf16[2048,128]{1,0:T(8,128)(2,1)S(1)} %bitcast.27, bf16[2048,128]{1,0:T(8,128)(2,1)S(1)} %copy-done.4, bf16[1024,512]{1,0:T(8,128)(2,1)S(1)} %copy-done.6, f32[512,128]{1,0:T(8,128)S(1)} %copy-done.7), custom_call_target="tpu_custom_call" | custom-call | flops 2147483648 | bytes 4194304 | tf_op jit(solution)/shard_map/pallas_call | solution.py:293
  63.2 15.0 %all_to_all.26.x_ref = bf16[16,128,128]{2,1,0:T(8,128)(2,1)S(1)} all-to-all(bf16[16,128,128]{2,1,0:T(8,128)(2,1)S(1)} %bitcast.28), channel_id=1, replica_groups=mesh['ptg'=8,'s'=4,'b'=4] {'s','b'}, dimensions={0} | all-to-all | bytes 1048576 | tf_op jit(solution)/shard_map/all_to_all | solution.py:415
  78.1 1.1 shard_map.88
  79.3 15.0 %all_to_all.27.terms_ref = bf16[8,128,256]{2,1,0:T(8,128)(2,1)S(1)} all-to-all(bf16[8,128,256]{2,1,0:T(8,128)(2,1)S(1)} %shard_map.88), channel_id=1, replica_groups=mesh['ptg'=8,'s'=4,'b'=4] {'ptg'}, dimensions={0} | all-to-all | bytes 1048576 | tf_op jit(solution)/shard_map/all_to_all | solution.py:429
  94.3 1.0 shard_map.89
  95.2 0.1 collective-permute-start.6
  95.4 1.3 %collective-permute-done.6 = bf16[2,128,256]{2,1,0:T(8,128)(2,1)S(1)} collective-permute-done((bf16[2,128,256]{2,1,0:T(8,128)(2,1)S(1)}, bf16[2,128,256]{2,1,0:T(8,128)(2,1)S(1)}, u32[]{:S(2)}, u32[]{:S(2)}) %collective-permute-start.6) | collective-permute-done | bytes 131104 | tf_op jit(solution)/shard_map/ppermute | solution.py:439
  96.7 3.8 %collective-permute-start.8 = (bf16[256,256]{1,0:T(8,128)(2,1)S(1)}, bf16[256,256]{1,0:T(8,128)(2,1)S(1)}, u32[]{:S(2)}, u32[]{:S(2)}) collective-permute-start(bf16[256,256]{1,0:T(8,128)(2,1)S(1)} %pad_maximum_fusion.1), channel_id=1, source_target_pairs={{0,0},{1,8},{2,16},{3,24},{4,32},{5,40},{6,48},{7,56},{8,64},{9,72... | collective-permute-start | bytes 393224 | tf_op jit(solution)/shard_map/ppermute | solution.py:450
  100.7 8.6 %collective-permute-done.8 = bf16[256,256]{1,0:T(8,128)(2,1)S(1)} collective-permute-done((bf16[256,256]{1,0:T(8,128)(2,1)S(1)}, bf16[256,256]{1,0:T(8,128)(2,1)S(1)}, u32[]{:S(2)}, u32[]{:S(2)}) %collective-permute-start.8) | collective-permute-done | bytes 131104 | tf_op jit(solution)/shard_map/ppermute | solution.py:450
  109.3 3.5 %collective-permute-done.7 = bf16[256,256]{1,0:T(8,128)(2,1)S(1)} collective-permute-done((bf16[256,256]{1,0:T(8,128)(2,1)S(1)}, bf16[256,256]{1,0:T(8,128)(2,1)S(1)}, u32[]{:S(2)}, u32[]{:S(2)}) %collective-permute-start.7) | collective-permute-done | bytes 131104 | tf_op jit(solution)/shard_map/ppermute | solution.py:450
  112.8 0.1 fusion.1
  113.0 0.9 maximum_select_fusion
  (29 shorter events, 0.3 us)
Async XLA Ops:
  0.0 1.8 %copy-start.1 = (s32[1,2048,128]{2,1,0:T(8,128)S(1)}, s32[1,2048,128]{2,1,0:T(8,128)}, u32[]{:S(2)}) copy-start(s32[1,2048,128]{2,1,0:T(8,128)} %param.10) | copy-start | bytes 3145732
  2.3 19.8 %collective-permute-start.4 = (bf16[1024,128]{1,0:T(8,128)(2,1)S(1)}, bf16[1024,128]{1,0:T(8,128)(2,1)S(1)}, u32[]{:S(2)}, u32[]{:S(2)}) collective-permute-start(bf16[1024,128]{1,0:T(8,128)(2,1)S(1)} %get-tuple-element.19), channel_id=1, source_target_pairs={{0,15},{1,14},{2,13},{3,12},{4,11},{5,10},{6,9},{7,8},{8,7},{9,6},... | collective-permute-start | bytes 786440 | tf_op jit(solution)/shard_map/ppermute | solution.py:350
  4.7 10.8 %collective-permute-start.1 = (s32[8]{0:T(128)S(1)}, s32[8]{0:T(128)S(1)}, u32[]{:S(2)}, u32[]{:S(2)}) collective-permute-start(s32[8]{0:T(128)S(1)} %compare_select_fusion), channel_id=1, source_target_pairs={{0,32},{16,48},{32,0},{48,16},{64,96},{80,112},{96,64},{112,80},{1... | collective-permute-start | bytes 104 | tf_op jit(solution)/shard_map/ppermute | solution.py:346
  8.6 6.8 %collective-permute-start.2 = (s32[8]{0:T(128)S(1)}, s32[8]{0:T(128)S(1)}, u32[]{:S(2)}, u32[]{:S(2)}) collective-permute-start(s32[8]{0:T(128)S(1)} %compare_select_fusion), channel_id=1, source_target_pairs={{0,48},{16,32},{32,16},{48,0},{64,112},{80,96},{96,80},{112,64},{1... | collective-permute-start | bytes 104 | tf_op jit(solution)/shard_map/ppermute | solution.py:346
  9.3 6.1 %collective-permute-start = (s32[8]{0:T(128)S(1)}, s32[8]{0:T(128)S(1)}, u32[]{:S(2)}, u32[]{:S(2)}) collective-permute-start(s32[8]{0:T(128)S(1)} %compare_select_fusion), channel_id=1, source_target_pairs={{0,16},{16,0},{32,48},{48,32},{64,80},{80,64},{96,112},{112,96},{1... | collective-permute-start | bytes 104 | tf_op jit(solution)/shard_map/ppermute | solution.py:346
  9.7 12.5 %all-to-all-start = ((bf16[4,4,16,512]{3,2,1,0:T(8,128)(2,1)}), bf16[4,4,16,512]{3,2,1,0:T(8,128)(2,1)S(1)}, u32[]{:S(2)}, u32[]{:S(2)}) async-start(bf16[4,4,16,512]{3,2,1,0:T(8,128)(2,1)} %bitcast.30), calls=%async_computation | async-start | bytes 524288 | tf_op jit(solution)/shard_map/all_to_all | solution.py:344
  15.5 5.0 %collective-permute-start.3 = (s32[8]{0:T(128)S(1)}, s32[8]{0:T(128)S(1)}, u32[]{:S(2)}, u32[]{:S(2)}) collective-permute-start(s32[8]{0:T(128)S(1)} %add_add_fusion), channel_id=1, source_target_pairs={{0,64},{16,80},{32,96},{48,112},{64,0},{80,16},{96,32},{112,48},{1... | collective-permute-start | bytes 104 | tf_op jit(solution)/shard_map/ppermute | solution.py:349
  23.7 20.7 %all-to-all-start.1 = ((bf16[32,16,512]{2,1,0:T(8,128)(2,1)}), bf16[32,16,512]{2,1,0:T(8,128)(2,1)}, u32[]{:S(2)}, u32[]{:S(2)}) async-start(bf16[32,16,512]{2,1,0:T(8,128)(2,1)} %bitcast.6), calls=%async_computation.1 | async-start | bytes 1048576 | tf_op jit(solution)/shard_map/all_to_all | solution.py:380
  31.0 13.5 %copy-start = (bf16[1024,1024]{1,0:T(8,128)(2,1)S(1)}, bf16[1024,1024]{1,0:T(8,128)(2,1)}, u32[]{:S(2)}) copy-start(bf16[1024,1024]{1,0:T(8,128)(2,1)} %constant.70.clone.table_ref) | copy-start | bytes 6291460
  31.0 13.4 %copy-start.5 = (f32[8,1024]{1,0:T(8,128)S(1)}, f32[8,1024]{1,0:T(8,128)}, u32[]{:S(2)}) copy-start(f32[8,1024]{1,0:T(8,128)} %constant.71.clone.turn_ref) | copy-start | bytes 98308
  31.0 10.0 %collective-permute-start.5 = (bf16[16,128]{1,0:T(8,128)(2,1)S(1)}, bf16[16,128]{1,0:T(8,128)(2,1)S(1)}, u32[]{:S(2)}, u32[]{:S(2)}) collective-permute-start(bf16[16,128]{1,0:T(8,128)(2,1)S(1)} %get-tuple-element.21), channel_id=1, source_target_pairs={{8,0},{9,7},{10,6},{11,5},{12,4},{13,3},{14,2},{15,1},{24,16},{25,... | collective-permute-start | bytes 12296 | tf_op jit(solution)/shard_map/ppermute | solution.py:351
  41.0 1.2 %copy-start.2 = (s32[1,2048,128]{2,1,0:T(8,128)S(1)}, s32[1,2048,128]{2,1,0:T(8,128)}, u32[]{:S(2)}) copy-start(s32[1,2048,128]{2,1,0:T(8,128)} %param.10) | copy-start | bytes 3145732
  43.6 0.8 copy-start.3
  44.4 16.2 %copy-start.4 = (bf16[2048,128]{1,0:T(8,128)(2,1)S(1)}, bf16[2048,128]{1,0:T(8,128)(2,1)}, u32[]{:S(2)}) copy-start(bf16[2048,128]{1,0:T(8,128)(2,1)} %copy-done.3) | copy-start | bytes 1572868
  44.4 16.2 %copy-start.6 = (bf16[1024,512]{1,0:T(8,128)(2,1)S(1)}, bf16[1024,512]{1,0:T(8,128)(2,1)}, u32[]{:S(2)}) copy-start(bf16[1024,512]{1,0:T(8,128)(2,1)} %constant.72.clone.table_ref) | copy-start | bytes 3145732
  44.5 16.2 %copy-start.7 = (f32[512,128]{1,0:T(8,128)S(1)}, f32[512,128]{1,0:T(8,128)}, u32[]{:S(2)}) copy-start(f32[512,128]{1,0:T(8,128)} %constant.73.clone.turn_ref) | copy-start | bytes 786436
  95.2 1.4 %collective-permute-start.6 = (bf16[2,128,256]{2,1,0:T(8,128)(2,1)S(1)}, bf16[2,128,256]{2,1,0:T(8,128)(2,1)S(1)}, u32[]{:S(2)}, u32[]{:S(2)}) collective-permute-start(bf16[2,128,256]{2,1,0:T(8,128)(2,1)S(1)} %get-tuple-element.28), channel_id=1, source_target_pairs={{0,1},{1,0},{2,3},{3,2},{4,5},{5,4},{6,7},{7,6},{8,9},{9,8},{10,11... | collective-permute-start | bytes 393224 | tf_op jit(solution)/shard_map/ppermute | solution.py:439
  96.7 12.6 %collective-permute-start.8 = (bf16[256,256]{1,0:T(8,128)(2,1)S(1)}, bf16[256,256]{1,0:T(8,128)(2,1)S(1)}, u32[]{:S(2)}, u32[]{:S(2)}) collective-permute-start(bf16[256,256]{1,0:T(8,128)(2,1)S(1)} %pad_maximum_fusion.1), channel_id=1, source_target_pairs={{0,0},{1,8},{2,16},{3,24},{4,32},{5,40},{6,48},{7,56},{8,64},{9,72... | collective-permute-start | bytes 393224 | tf_op jit(solution)/shard_map/ppermute | solution.py:450
  100.6 12.2 %collective-permute-start.7 = (bf16[256,256]{1,0:T(8,128)(2,1)S(1)}, bf16[256,256]{1,0:T(8,128)(2,1)S(1)}, u32[]{:S(2)}, u32[]{:S(2)}) collective-permute-start(bf16[256,256]{1,0:T(8,128)(2,1)S(1)} %pad_maximum_fusion), channel_id=1, source_target_pairs={{0,4},{1,12},{2,20},{3,28},{4,36},{5,44},{6,52},{7,60},{8,68},{9,7... | collective-permute-start | bytes 393224 | tf_op jit(solution)/shard_map/ppermute | solution.py:450

commit v11 on v10

--- a/solution.py
+++ b/solution.py
@@ -367,7 +367,7 @@
 
     twice = jnp.concatenate([beam[0], beam[0]], 1)
     turned = lax.dynamic_slice_in_dim(twice, (points - start % points) % points, points, 1)
-    shares, got = lax.optimization_barrier((shares, got))
+    shares, got, edge = lax.optimization_barrier((shares, got, edge))
     picked = call(
         functools.partial(pick_kernel, points),
         shape(pointings, parts, share_rows, tile),

time: 115 us -> 113 us (0.983)
    all_to_all x1, waiting for transfers between devices: 0.01 us -> 4.21 us  [shards(): lax.all_to_all(picked.reshape(pointings * parts, share_rows, tile), ('ptg...]
    ppermute x1, waiting for transfers between devices: 6.6 us -> 4.36 us  [shards(): lax.ppermute(edge, IMG, [(i, (devices - i) % (devices // 2)) for i in ran...]
    all_to_all x1, waiting for transfers between devices: 1.61 us -> 0.01 us  [shards(): lax.all_to_all(shares, 's', split_axis=0, concat_axis=0, tiled=True)]
    all_to_all x1, blocking collectives: 15 us -> 13.5 us  [shards(): lax.all_to_all(contribution, 'ptg', split_axis=0, concat_axis=0, tiled=True)]
    ppermute x1, waiting for transfers between devices: 3.57 us -> 2.27 us  [shards(): lax.ppermute(starts, 'ptg', [(p, p ^ 4) for p in range(pointings)])]
where the time goes in v11:
time: 113 us; the launch traced here: 112 us
  blocking collectives  42.7 us (38%)
  starting transfers between devices  26.7 us (24%)
  waiting for transfers between devices  24.3 us (22%)
  Pallas kernels  12.2 us (11%)
  other arithmetic  3.06 us (3%)
  local copies, waits for them, and re-layouts  2.1 us (2%)
    all_to_all x1, blocking collectives, shards(): lax.all_to_all(back.reshape(devices, rows, 128), IMG, split_axis=0, conca...  15 us
    all_to_all x1, blocking collectives, shards(): col = lax.all_to_all(spectrum, IMG, split_axis=0, concat_axis=0, tiled=True)  14.3 us
    all_to_all x1, blocking collectives, shards(): lax.all_to_all(contribution, 'ptg', split_axis=0, concat_axis=0, tiled=True)  13.5 us
    pallas_call x8, Pallas kernels, call(): pl.pallas_call(kernel, out_shape=outs, in_specs=specs, out_specs=jax.tree...  12.2 us
    ppermute x2, waiting for transfers between devices, shards(): received.append(lax.ppermute(block, ('ptg', *IMG), pairs))  12.1 us
    all_to_all x1, starting transfers between devices, shards(): lax.all_to_all(picked.reshape(pointings * parts, share_rows, tile), ('ptg...  7.49 us
    all_to_all x1, starting transfers between devices, shards(): lax.all_to_all(shares, 's', split_axis=0, concat_axis=0, tiled=True)  5.83 us
    ppermute x3, starting transfers between devices, shards(): lax.ppermute(starts, 'ptg', [(p, p ^ bit) for p in range(pointings)])  4.97 us
  transfers between devices with their start and end apart: 11, of which 6 were waited for; matrix products, arithmetic and copies ran while one was open for 2% of the time, Pallas kernels for 1%

profile of v11, /device:TPU:14, one launch (start us, length us, event | category | flops | bytes accessed | tf_op | source)
XLA Modules:
  0.0 112.1 jit_solution(7357034050007443627)
XLA Ops:
  0.0 1.8 %shard_map.82 = bf16[16,16,512]{2,1,0:T(8,128)(2,1)} custom-call(s32[1]{0:T(128)} %bitcast.2.ptg_ref, bf16[2048,512]{1,0:T(8,128)(2,1)} %image_ref.1), custom_call_target="tpu_custom_call" | custom-call | bytes 524288 | tf_op jit(solution)/shard_map/pallas_call | solution.py:293
  1.8 0.5 shard_map.83
  2.3 1.7 %collective-permute-start.4 = (bf16[1024,128]{1,0:T(8,128)(2,1)S(1)}, bf16[1024,128]{1,0:T(8,128)(2,1)S(1)}, u32[]{:S(2)}, u32[]{:S(2)}) collective-permute-start(bf16[1024,128]{1,0:T(8,128)(2,1)S(1)} %get-tuple-element.19), channel_id=1, source_target_pairs={{0,15},{1,14},{2,13},{3,12},{4,11},{5,10},{6,9},{7,8},{8,7},{9,6},... | collective-permute-start | bytes 786440 | tf_op jit(solution)/shard_map/ppermute | solution.py:350
  4.7 4.0 %collective-permute-start.1 = (s32[8]{0:T(128)S(1)}, s32[8]{0:T(128)S(1)}, u32[]{:S(2)}, u32[]{:S(2)}) collective-permute-start(s32[8]{0:T(128)S(1)} %compare_select_fusion), channel_id=1, source_target_pairs={{0,32},{16,48},{32,0},{48,16},{64,96},{80,112},{96,64},{112,80},{1... | collective-permute-start | bytes 104 | tf_op jit(solution)/shard_map/ppermute | solution.py:346
  8.6 0.7 collective-permute-start.2
  9.3 0.3 collective-permute-start
  9.7 5.8 %all-to-all-start = ((bf16[4,4,16,512]{3,2,1,0:T(8,128)(2,1)}), bf16[4,4,16,512]{3,2,1,0:T(8,128)(2,1)S(1)}, u32[]{:S(2)}, u32[]{:S(2)}) async-start(bf16[4,4,16,512]{3,2,1,0:T(8,128)(2,1)} %bitcast.30), calls=%async_computation | async-start | bytes 524288 | tf_op jit(solution)/shard_map/all_to_all | solution.py:344
  15.5 1.3 %collective-permute-start.5 = (bf16[16,128]{1,0:T(8,128)(2,1)S(1)}, bf16[16,128]{1,0:T(8,128)(2,1)S(1)}, u32[]{:S(2)}, u32[]{:S(2)}) collective-permute-start(bf16[16,128]{1,0:T(8,128)(2,1)S(1)} %get-tuple-element.20), channel_id=1, source_target_pairs={{8,0},{9,7},{10,6},{11,5},{12,4},{13,3},{14,2},{15,1},{24,16},{25,... | collective-permute-start | bytes 12296 | tf_op jit(solution)/shard_map/ppermute | solution.py:351
  16.8 1.4 %collective-permute-start.3 = (s32[8]{0:T(128)S(1)}, s32[8]{0:T(128)S(1)}, u32[]{:S(2)}, u32[]{:S(2)}) collective-permute-start(s32[8]{0:T(128)S(1)} %add_add_fusion), channel_id=1, source_target_pairs={{0,64},{16,80},{32,96},{48,112},{64,0},{80,16},{96,32},{112,48},{1... | collective-permute-start | bytes 104 | tf_op jit(solution)/shard_map/ppermute | solution.py:349
  18.2 2.3 %collective-permute-done.3 = s32[8]{0:T(128)S(1)} collective-permute-done((s32[8]{0:T(128)S(1)}, s32[8]{0:T(128)S(1)}, u32[]{:S(2)}, u32[]{:S(2)}) %collective-permute-start.3) | collective-permute-done | bytes 64 | tf_op jit(solution)/shard_map/ppermute | solution.py:349
  20.5 4.4 %collective-permute-done.5.edge_ref = bf16[16,128]{1,0:T(8,128)(2,1)S(1)} collective-permute-done((bf16[16,128]{1,0:T(8,128)(2,1)S(1)}, bf16[16,128]{1,0:T(8,128)(2,1)S(1)}, u32[]{:S(2)}, u32[]{:S(2)}) %collective-permute-start.5) | collective-permute-done | bytes 4128 | tf_op jit(solution)/shard_map/ppermute | solution.py:351
  24.9 1.5 %shard_map.84 = bf16[8,4,16,512]{3,2,1,0:T(8,128)(2,1)} custom-call(s32[1]{0:T(128)} %bitcast.place_ref, s32[8]{0:T(128)S(1)} %add.37.starts_ref, bf16[4,4,16,512]{3,2,1,0:T(8,128)(2,1)S(1)} %all-to-all-done.tiles_ref), custom_call_target="tpu_custom_call" | custom-call | bytes 1048576 | tf_op jit(solution)/shard_map/pallas_call | solution.py:293
  26.4 7.5 %all-to-all-start.1 = ((bf16[32,16,512]{2,1,0:T(8,128)(2,1)}), bf16[32,16,512]{2,1,0:T(8,128)(2,1)}, u32[]{:S(2)}, u32[]{:S(2)}) async-start(bf16[32,16,512]{2,1,0:T(8,128)(2,1)} %bitcast.6), calls=%async_computation.1 | async-start | bytes 1048576 | tf_op jit(solution)/shard_map/all_to_all | solution.py:380
  34.1 1.9 %fusion.beam_ref = f32[128,2048]{1,0:T(8,128)S(1)} fusion(s32[]{:T(128)S(6)} %select_n.53, f32[128,2048]{1,0:T(8,128)} %bitcast.29), kind=kLoop, calls=%fused_computation.2 | loop fusion | flops 262144 | bytes 2097156 | tf_op jit(solution)/shard_map/concatenate | solution.py:368
  36.0 1.2 %copy-done.2 = s32[1,2048,128]{2,1,0:T(8,128)S(1)} copy-done((s32[1,2048,128]{2,1,0:T(8,128)S(1)}, s32[1,2048,128]{2,1,0:T(8,128)}, u32[]{:S(2)}) %copy-start.2) | copy-done | bytes 1048600
  37.3 1.4 %shard_map.85.weight_ref = bf16[2048,128]{1,0:T(8,128)(2,1)S(1)} custom-call(s32[1]{0:T(128)} %bitcast.4.me_ref, s32[2048,128]{1,0:T(8,128)S(1)} %bitcast.26, bf16[1024,128]{1,0:T(8,128)(2,1)S(1)} %collective-permute-done.4.got_ref, bf16[16,128]{1,0:T(8,128)(2,1)S(1)} %collective-permute-done.5.edge_ref), custom_call_target="tpu_custom_call" | custom-call | flops 268435456 | bytes 4194304 | tf_op jit(solution)/shard_map/pallas_call | solution.py:293
  38.7 0.8 copy-done.3
  39.5 4.2 %all-to-all-done.1 = bf16[32,16,512]{2,1,0:T(8,128)(2,1)} async-done(((bf16[32,16,512]{2,1,0:T(8,128)(2,1)}), bf16[32,16,512]{2,1,0:T(8,128)(2,1)}, u32[]{:S(2)}, u32[]{:S(2)}) %all-to-all-start.1) | async-done | bytes 524320 | tf_op jit(solution)/shard_map/all_to_all | solution.py:380
  43.7 2.3 %shard_map.86 = bf16[16,128,128]{2,1,0:T(8,128)(2,1)S(1)} custom-call(bf16[8,4,16,512]{3,2,1,0:T(8,128)(2,1)} %bitcast.7.window_ref, f32[128,2048]{1,0:T(8,128)S(1)} %fusion.beam_ref, bf16[1024,1024]{1,0:T(8,128)(2,1)S(1)} %copy-done, f32[8,1024]{1,0:T(8,128)S(1)} %copy-done.5), custom_call_target="tpu_custom_call" | custom-call | flops 536870912 | bytes 4194304 | tf_op jit(solution)/shard_map/pallas_call | solution.py:293
  46.0 14.3 %all_to_all.25 = bf16[16,128,128]{2,1,0:T(8,128)(2,1)S(1)} all-to-all(bf16[16,128,128]{2,1,0:T(8,128)(2,1)S(1)} %shard_map.86), channel_id=1, replica_groups=mesh['ptg'=8,'s'=4,'b'=4] {'s','b'}, dimensions={0} | all-to-all | bytes 1048576 | tf_op jit(solution)/shard_map/all_to_all | solution.py:402
  60.3 2.6 %shard_map.87 = bf16[2048,128]{1,0:T(8,128)(2,1)S(1)} custom-call(s32[1]{0:T(128)} %bitcast.4.me_ref, bf16[2048,128]{1,0:T(8,128)(2,1)S(1)} %bitcast.27, bf16[2048,128]{1,0:T(8,128)(2,1)S(1)} %copy-done.4, bf16[1024,512]{1,0:T(8,128)(2,1)S(1)} %copy-done.6, f32[512,128]{1,0:T(8,128)S(1)} %copy-done.7), custom_call_target="tpu_custom_call" | custom-call | flops 2147483648 | bytes 4194304 | tf_op jit(solution)/shard_map/pallas_call | solution.py:293
  62.9 15.0 %all_to_all.26.x_ref = bf16[16,128,128]{2,1,0:T(8,128)(2,1)S(1)} all-to-all(bf16[16,128,128]{2,1,0:T(8,128)(2,1)S(1)} %bitcast.28), channel_id=1, replica_groups=mesh['ptg'=8,'s'=4,'b'=4] {'s','b'}, dimensions={0} | all-to-all | bytes 1048576 | tf_op jit(solution)/shard_map/all_to_all | solution.py:415
  77.8 1.1 shard_map.88
  79.0 13.5 %all_to_all.27.terms_ref = bf16[8,128,256]{2,1,0:T(8,128)(2,1)S(1)} all-to-all(bf16[8,128,256]{2,1,0:T(8,128)(2,1)S(1)} %shard_map.88), channel_id=1, replica_groups=mesh['ptg'=8,'s'=4,'b'=4] {'ptg'}, dimensions={0} | all-to-all | bytes 1048576 | tf_op jit(solution)/shard_map/all_to_all | solution.py:429
  92.5 1.0 shard_map.89
  93.5 0.1 collective-permute-start.6
  93.6 1.3 %collective-permute-done.6 = bf16[2,128,256]{2,1,0:T(8,128)(2,1)S(1)} collective-permute-done((bf16[2,128,256]{2,1,0:T(8,128)(2,1)S(1)}, bf16[2,128,256]{2,1,0:T(8,128)(2,1)S(1)}, u32[]{:S(2)}, u32[]{:S(2)}) %collective-permute-start.6) | collective-permute-done | bytes 131104 | tf_op jit(solution)/shard_map/ppermute | solution.py:439
  94.9 3.8 %collective-permute-start.8 = (bf16[256,256]{1,0:T(8,128)(2,1)S(1)}, bf16[256,256]{1,0:T(8,128)(2,1)S(1)}, u32[]{:S(2)}, u32[]{:S(2)}) collective-permute-start(bf16[256,256]{1,0:T(8,128)(2,1)S(1)} %pad_maximum_fusion.1), channel_id=1, source_target_pairs={{0,0},{1,8},{2,16},{3,24},{4,32},{5,40},{6,48},{7,56},{8,64},{9,72... | collective-permute-start | bytes 393224 | tf_op jit(solution)/shard_map/ppermute | solution.py:450
  98.9 8.6 %collective-permute-done.8 = bf16[256,256]{1,0:T(8,128)(2,1)S(1)} collective-permute-done((bf16[256,256]{1,0:T(8,128)(2,1)S(1)}, bf16[256,256]{1,0:T(8,128)(2,1)S(1)}, u32[]{:S(2)}, u32[]{:S(2)}) %collective-permute-start.8) | collective-permute-done | bytes 131104 | tf_op jit(solution)/shard_map/ppermute | solution.py:450
  107.5 3.5 %collective-permute-done.7 = bf16[256,256]{1,0:T(8,128)(2,1)S(1)} collective-permute-done((bf16[256,256]{1,0:T(8,128)(2,1)S(1)}, bf16[256,256]{1,0:T(8,128)(2,1)S(1)}, u32[]{:S(2)}, u32[]{:S(2)}) %collective-permute-start.7) | collective-permute-done | bytes 131104 | tf_op jit(solution)/shard_map/ppermute | solution.py:450
  111.0 0.1 fusion.1
  111.2 0.9 maximum_select_fusion
  (29 shorter events, 0.3 us)
Async XLA Ops:
  0.0 1.8 %copy-start.1 = (s32[1,2048,128]{2,1,0:T(8,128)S(1)}, s32[1,2048,128]{2,1,0:T(8,128)}, u32[]{:S(2)}) copy-start(s32[1,2048,128]{2,1,0:T(8,128)} %param.10) | copy-start | bytes 3145732
  2.3 22.6 %collective-permute-start.4 = (bf16[1024,128]{1,0:T(8,128)(2,1)S(1)}, bf16[1024,128]{1,0:T(8,128)(2,1)S(1)}, u32[]{:S(2)}, u32[]{:S(2)}) collective-permute-start(bf16[1024,128]{1,0:T(8,128)(2,1)S(1)} %get-tuple-element.19), channel_id=1, source_target_pairs={{0,15},{1,14},{2,13},{3,12},{4,11},{5,10},{6,9},{7,8},{8,7},{9,6},... | collective-permute-start | bytes 786440 | tf_op jit(solution)/shard_map/ppermute | solution.py:350
  4.7 12.1 %collective-permute-start.1 = (s32[8]{0:T(128)S(1)}, s32[8]{0:T(128)S(1)}, u32[]{:S(2)}, u32[]{:S(2)}) collective-permute-start(s32[8]{0:T(128)S(1)} %compare_select_fusion), channel_id=1, source_target_pairs={{0,32},{16,48},{32,0},{48,16},{64,96},{80,112},{96,64},{112,80},{1... | collective-permute-start | bytes 104 | tf_op jit(solution)/shard_map/ppermute | solution.py:346
  8.6 8.1 %collective-permute-start.2 = (s32[8]{0:T(128)S(1)}, s32[8]{0:T(128)S(1)}, u32[]{:S(2)}, u32[]{:S(2)}) collective-permute-start(s32[8]{0:T(128)S(1)} %compare_select_fusion), channel_id=1, source_target_pairs={{0,48},{16,32},{32,16},{48,0},{64,112},{80,96},{96,80},{112,64},{1... | collective-permute-start | bytes 104 | tf_op jit(solution)/shard_map/ppermute | solution.py:346
  9.3 7.4 %collective-permute-start = (s32[8]{0:T(128)S(1)}, s32[8]{0:T(128)S(1)}, u32[]{:S(2)}, u32[]{:S(2)}) collective-permute-start(s32[8]{0:T(128)S(1)} %compare_select_fusion), channel_id=1, source_target_pairs={{0,16},{16,0},{32,48},{48,32},{64,80},{80,64},{96,112},{112,96},{1... | collective-permute-start | bytes 104 | tf_op jit(solution)/shard_map/ppermute | solution.py:346
  9.7 15.2 %all-to-all-start = ((bf16[4,4,16,512]{3,2,1,0:T(8,128)(2,1)}), bf16[4,4,16,512]{3,2,1,0:T(8,128)(2,1)S(1)}, u32[]{:S(2)}, u32[]{:S(2)}) async-start(bf16[4,4,16,512]{3,2,1,0:T(8,128)(2,1)} %bitcast.30), calls=%async_computation | async-start | bytes 524288 | tf_op jit(solution)/shard_map/all_to_all | solution.py:344
  15.5 9.4 %collective-permute-start.5 = (bf16[16,128]{1,0:T(8,128)(2,1)S(1)}, bf16[16,128]{1,0:T(8,128)(2,1)S(1)}, u32[]{:S(2)}, u32[]{:S(2)}) collective-permute-start(bf16[16,128]{1,0:T(8,128)(2,1)S(1)} %get-tuple-element.20), channel_id=1, source_target_pairs={{8,0},{9,7},{10,6},{11,5},{12,4},{13,3},{14,2},{15,1},{24,16},{25,... | collective-permute-start | bytes 12296 | tf_op jit(solution)/shard_map/ppermute | solution.py:351
  16.8 3.7 %collective-permute-start.3 = (s32[8]{0:T(128)S(1)}, s32[8]{0:T(128)S(1)}, u32[]{:S(2)}, u32[]{:S(2)}) collective-permute-start(s32[8]{0:T(128)S(1)} %add_add_fusion), channel_id=1, source_target_pairs={{0,64},{16,80},{32,96},{48,112},{64,0},{80,16},{96,32},{112,48},{1... | collective-permute-start | bytes 104 | tf_op jit(solution)/shard_map/ppermute | solution.py:349
  26.4 17.3 %all-to-all-start.1 = ((bf16[32,16,512]{2,1,0:T(8,128)(2,1)}), bf16[32,16,512]{2,1,0:T(8,128)(2,1)}, u32[]{:S(2)}, u32[]{:S(2)}) async-start(bf16[32,16,512]{2,1,0:T(8,128)(2,1)} %bitcast.6), calls=%async_computation.1 | async-start | bytes 1048576 | tf_op jit(solution)/shard_map/all_to_all | solution.py:380
  33.9 9.8 %copy-start = (bf16[1024,1024]{1,0:T(8,128)(2,1)S(1)}, bf16[1024,1024]{1,0:T(8,128)(2,1)}, u32[]{:S(2)}) copy-start(bf16[1024,1024]{1,0:T(8,128)(2,1)} %constant.70.clone.table_ref) | copy-start | bytes 6291460
  34.0 9.7 %copy-start.5 = (f32[8,1024]{1,0:T(8,128)S(1)}, f32[8,1024]{1,0:T(8,128)}, u32[]{:S(2)}) copy-start(f32[8,1024]{1,0:T(8,128)} %constant.71.clone.turn_ref) | copy-start | bytes 98308
  36.0 1.2 %copy-start.2 = (s32[1,2048,128]{2,1,0:T(8,128)S(1)}, s32[1,2048,128]{2,1,0:T(8,128)}, u32[]{:S(2)}) copy-start(s32[1,2048,128]{2,1,0:T(8,128)} %param.10) | copy-start | bytes 3145732
  38.7 0.8 copy-start.3
  43.7 16.6 %copy-start.4 = (bf16[2048,128]{1,0:T(8,128)(2,1)S(1)}, bf16[2048,128]{1,0:T(8,128)(2,1)}, u32[]{:S(2)}) copy-start(bf16[2048,128]{1,0:T(8,128)(2,1)} %copy-done.3) | copy-start | bytes 1572868
  43.7 16.6 %copy-start.6 = (bf16[1024,512]{1,0:T(8,128)(2,1)S(1)}, bf16[1024,512]{1,0:T(8,128)(2,1)}, u32[]{:S(2)}) copy-start(bf16[1024,512]{1,0:T(8,128)(2,1)} %constant.72.clone.table_ref) | copy-start | bytes 3145732
  43.7 16.6 %copy-start.7 = (f32[512,128]{1,0:T(8,128)S(1)}, f32[512,128]{1,0:T(8,128)}, u32[]{:S(2)}) copy-start(f32[512,128]{1,0:T(8,128)} %constant.73.clone.turn_ref) | copy-start | bytes 786436
  93.5 1.4 %collective-permute-start.6 = (bf16[2,128,256]{2,1,0:T(8,128)(2,1)S(1)}, bf16[2,128,256]{2,1,0:T(8,128)(2,1)S(1)}, u32[]{:S(2)}, u32[]{:S(2)}) collective-permute-start(bf16[2,128,256]{2,1,0:T(8,128)(2,1)S(1)} %get-tuple-element.28), channel_id=1, source_target_pairs={{0,1},{1,0},{2,3},{3,2},{4,5},{5,4},{6,7},{7,6},{8,9},{9,8},{10,11... | collective-permute-start | bytes 393224 | tf_op jit(solution)/shard_map/ppermute | solution.py:439
  94.9 12.6 %collective-permute-start.8 = (bf16[256,256]{1,0:T(8,128)(2,1)S(1)}, bf16[256,256]{1,0:T(8,128)(2,1)S(1)}, u32[]{:S(2)}, u32[]{:S(2)}) collective-permute-start(bf16[256,256]{1,0:T(8,128)(2,1)S(1)} %pad_maximum_fusion.1), channel_id=1, source_target_pairs={{0,0},{1,8},{2,16},{3,24},{4,32},{5,40},{6,48},{7,56},{8,64},{9,72... | collective-permute-start | bytes 393224 | tf_op jit(solution)/shard_map/ppermute | solution.py:450
  98.8 12.2 %collective-permute-start.7 = (bf16[256,256]{1,0:T(8,128)(2,1)S(1)}, bf16[256,256]{1,0:T(8,128)(2,1)S(1)}, u32[]{:S(2)}, u32[]{:S(2)}) collective-permute-start(bf16[256,256]{1,0:T(8,128)(2,1)S(1)} %pad_maximum_fusion), channel_id=1, source_target_pairs={{0,4},{1,12},{2,20},{3,28},{4,36},{5,44},{6,52},{7,60},{8,68},{9,7... | collective-permute-start | bytes 393224 | tf_op jit(solution)/shard_map/ppermute | solution.py:450

commit v12 on v11

--- a/solution.py
+++ b/solution.py
@@ -367,7 +367,6 @@
 
     twice = jnp.concatenate([beam[0], beam[0]], 1)
     turned = lax.dynamic_slice_in_dim(twice, (points - start % points) % points, points, 1)
-    shares, got, edge = lax.optimization_barrier((shares, got, edge))
     picked = call(
         functools.partial(pick_kernel, points),
         shape(pointings, parts, share_rows, tile),
@@ -377,6 +376,7 @@
         shares,
         moved=1 << 20,
     )
+    picked, got, edge = lax.optimization_barrier((picked, got, edge))
     window = lax.all_to_all(
         picked.reshape(pointings * parts, share_rows, tile),
         ("ptg", "b"),

time: 113 us -> 112 us (level)
  waiting for transfers between devices: 24.3 us -> 22.7 us
    ppermute x1, waiting for transfers between devices: 4.36 us -> 1.2 us  [shards(): lax.ppermute(edge, IMG, [(i, (devices - i) % (devices // 2)) for i in ran...]
    all_to_all x1, waiting for transfers between devices: 0.01 us -> 1.61 us  [shards(): lax.all_to_all(shares, 's', split_axis=0, concat_axis=0, tiled=True)]
  transfers between devices with their start and end apart: 11 -> 11, of which waited for: 6 -> 7; matrix products, arithmetic and copies ran while one was open for 2% -> 2% of each run, Pallas kernels for 1% -> 3%
where the time goes in v12:
time: 112 us; the launch traced here: 111 us
  blocking collectives  43.6 us (39%)
  starting transfers between devices  26.7 us (24%)
  waiting for transfers between devices  22.7 us (20%)
  Pallas kernels  12.2 us (11%)
  other arithmetic  3.05 us (3%)
  local copies, waits for them, and re-layouts  2.1 us (2%)
    all_to_all x1, blocking collectives, shards(): lax.all_to_all(back.reshape(devices, rows, 128), IMG, split_axis=0, conca...  15 us
    all_to_all x1, blocking collectives, shards(): col = lax.all_to_all(spectrum, IMG, split_axis=0, concat_axis=0, tiled=True)  14.8 us
    all_to_all x1, blocking collectives, shards(): lax.all_to_all(contribution, 'ptg', split_axis=0, concat_axis=0, tiled=True)  13.9 us
    pallas_call x8, Pallas kernels, call(): pl.pallas_call(kernel, out_shape=outs, in_specs=specs, out_specs=jax.tree...  12.2 us
    ppermute x2, waiting for transfers between devices, shards(): received.append(lax.ppermute(block, ('ptg', *IMG), pairs))  12.1 us
    all_to_all x1, starting transfers between devices, shards(): lax.all_to_all(picked.reshape(pointings * parts, share_rows, tile), ('ptg...  7.5 us
    all_to_all x1, starting transfers between devices, shards(): lax.all_to_all(shares, 's', split_axis=0, concat_axis=0, tiled=True)  5.83 us
    ppermute x3, starting transfers between devices, shards(): lax.ppermute(starts, 'ptg', [(p, p ^ bit) for p in range(pointings)])  4.97 us
  transfers between devices with their start and end apart: 11, of which 7 were waited for; matrix products, arithmetic and copies ran while one was open for 2% of the time, Pallas kernels for 3%

profile of v12, /device:TPU:14, one launch (start us, length us, event | category | flops | bytes accessed | tf_op | source)
XLA Modules:
  0.0 111.4 jit_solution(5927119210718790757)
XLA Ops:
  0.0 1.8 %shard_map.82 = bf16[16,16,512]{2,1,0:T(8,128)(2,1)} custom-call(s32[1]{0:T(128)} %bitcast.2.ptg_ref, bf16[2048,512]{1,0:T(8,128)(2,1)} %image_ref.1), custom_call_target="tpu_custom_call" | custom-call | bytes 524288 | tf_op jit(solution)/shard_map/pallas_call | solution.py:293
  1.8 0.5 shard_map.83
  2.3 1.7 %collective-permute-start.4 = (bf16[1024,128]{1,0:T(8,128)(2,1)S(1)}, bf16[1024,128]{1,0:T(8,128)(2,1)S(1)}, u32[]{:S(2)}, u32[]{:S(2)}) collective-permute-start(bf16[1024,128]{1,0:T(8,128)(2,1)S(1)} %get-tuple-element.19), channel_id=1, source_target_pairs={{0,15},{1,14},{2,13},{3,12},{4,11},{5,10},{6,9},{7,8},{8,7},{9,6},... | collective-permute-start | bytes 786440 | tf_op jit(solution)/shard_map/ppermute | solution.py:350
  4.7 4.0 %collective-permute-start.1 = (s32[8]{0:T(128)S(1)}, s32[8]{0:T(128)S(1)}, u32[]{:S(2)}, u32[]{:S(2)}) collective-permute-start(s32[8]{0:T(128)S(1)} %compare_select_fusion), channel_id=1, source_target_pairs={{0,32},{16,48},{32,0},{48,16},{64,96},{80,112},{96,64},{112,80},{1... | collective-permute-start | bytes 104 | tf_op jit(solution)/shard_map/ppermute | solution.py:346
  8.6 0.7 collective-permute-start.2
  9.3 0.3 collective-permute-start
  9.7 5.8 %all-to-all-start = ((bf16[4,4,16,512]{3,2,1,0:T(8,128)(2,1)}), bf16[4,4,16,512]{3,2,1,0:T(8,128)(2,1)S(1)}, u32[]{:S(2)}, u32[]{:S(2)}) async-start(bf16[4,4,16,512]{3,2,1,0:T(8,128)(2,1)} %bitcast.30), calls=%async_computation | async-start | bytes 524288 | tf_op jit(solution)/shard_map/all_to_all | solution.py:344
  15.5 1.3 %collective-permute-start.5 = (bf16[16,128]{1,0:T(8,128)(2,1)S(1)}, bf16[16,128]{1,0:T(8,128)(2,1)S(1)}, u32[]{:S(2)}, u32[]{:S(2)}) collective-permute-start(bf16[16,128]{1,0:T(8,128)(2,1)S(1)} %get-tuple-element.20), channel_id=1, source_target_pairs={{8,0},{9,7},{10,6},{11,5},{12,4},{13,3},{14,2},{15,1},{24,16},{25,... | collective-permute-start | bytes 12296 | tf_op jit(solution)/shard_map/ppermute | solution.py:351
  16.8 1.4 %collective-permute-start.3 = (s32[8]{0:T(128)S(1)}, s32[8]{0:T(128)S(1)}, u32[]{:S(2)}, u32[]{:S(2)}) collective-permute-start(s32[8]{0:T(128)S(1)} %add_add_fusion), channel_id=1, source_target_pairs={{0,64},{16,80},{32,96},{48,112},{64,0},{80,16},{96,32},{112,48},{1... | collective-permute-start | bytes 104 | tf_op jit(solution)/shard_map/ppermute | solution.py:349
  18.2 2.3 %collective-permute-done.3 = s32[8]{0:T(128)S(1)} collective-permute-done((s32[8]{0:T(128)S(1)}, s32[8]{0:T(128)S(1)}, u32[]{:S(2)}, u32[]{:S(2)}) %collective-permute-start.3) | collective-permute-done | bytes 64 | tf_op jit(solution)/shard_map/ppermute | solution.py:349
  20.5 1.6 %all-to-all-done.tiles_ref = bf16[4,4,16,512]{3,2,1,0:T(8,128)(2,1)S(1)} async-done(((bf16[4,4,16,512]{3,2,1,0:T(8,128)(2,1)}), bf16[4,4,16,512]{3,2,1,0:T(8,128)(2,1)S(1)}, u32[]{:S(2)}, u32[]{:S(2)}) %all-to-all-start) | async-done | bytes 262176 | tf_op jit(solution)/shard_map/all_to_all | solution.py:344
  22.1 1.5 %shard_map.84 = bf16[8,4,16,512]{3,2,1,0:T(8,128)(2,1)} custom-call(s32[1]{0:T(128)} %bitcast.place_ref, s32[8]{0:T(128)S(1)} %add.37.starts_ref, bf16[4,4,16,512]{3,2,1,0:T(8,128)(2,1)S(1)} %all-to-all-done.tiles_ref), custom_call_target="tpu_custom_call" | custom-call | bytes 1048576 | tf_op jit(solution)/shard_map/pallas_call | solution.py:293
  23.7 1.2 %collective-permute-done.5.edge_ref = bf16[16,128]{1,0:T(8,128)(2,1)S(1)} collective-permute-done((bf16[16,128]{1,0:T(8,128)(2,1)S(1)}, bf16[16,128]{1,0:T(8,128)(2,1)S(1)}, u32[]{:S(2)}, u32[]{:S(2)}) %collective-permute-start.5) | collective-permute-done | bytes 4128 | tf_op jit(solution)/shard_map/ppermute | solution.py:351
  24.9 7.5 %all-to-all-start.1 = ((bf16[32,16,512]{2,1,0:T(8,128)(2,1)}), bf16[32,16,512]{2,1,0:T(8,128)(2,1)}, u32[]{:S(2)}, u32[]{:S(2)}) async-start(bf16[32,16,512]{2,1,0:T(8,128)(2,1)} %bitcast.6), calls=%async_computation.1 | async-start | bytes 1048576 | tf_op jit(solution)/shard_map/all_to_all | solution.py:380
  32.5 1.9 %fusion.beam_ref = f32[128,2048]{1,0:T(8,128)S(1)} fusion(s32[]{:T(128)S(6)} %select_n.53, f32[128,2048]{1,0:T(8,128)} %bitcast.29), kind=kLoop, calls=%fused_computation.2 | loop fusion | flops 262144 | bytes 2097156 | tf_op jit(solution)/shard_map/concatenate | solution.py:368
  34.5 1.2 %copy-done.2 = s32[1,2048,128]{2,1,0:T(8,128)S(1)} copy-done((s32[1,2048,128]{2,1,0:T(8,128)S(1)}, s32[1,2048,128]{2,1,0:T(8,128)}, u32[]{:S(2)}) %copy-start.2) | copy-done | bytes 1048600
  35.7 1.4 %shard_map.85.weight_ref = bf16[2048,128]{1,0:T(8,128)(2,1)S(1)} custom-call(s32[1]{0:T(128)} %bitcast.4.me_ref, s32[2048,128]{1,0:T(8,128)S(1)} %bitcast.26, bf16[1024,128]{1,0:T(8,128)(2,1)S(1)} %collective-permute-done.4.got_ref, bf16[16,128]{1,0:T(8,128)(2,1)S(1)} %collective-permute-done.5.edge_ref), custom_call_target="tpu_custom_call" | custom-call | flops 268435456 | bytes 4194304 | tf_op jit(solution)/shard_map/pallas_call | solution.py:293
  37.1 0.8 copy-done.3
  37.9 4.2 %all-to-all-done.1 = bf16[32,16,512]{2,1,0:T(8,128)(2,1)} async-done(((bf16[32,16,512]{2,1,0:T(8,128)(2,1)}), bf16[32,16,512]{2,1,0:T(8,128)(2,1)}, u32[]{:S(2)}, u32[]{:S(2)}) %all-to-all-start.1) | async-done | bytes 524320 | tf_op jit(solution)/shard_map/all_to_all | solution.py:380
  42.2 2.3 %shard_map.86 = bf16[16,128,128]{2,1,0:T(8,128)(2,1)S(1)} custom-call(bf16[8,4,16,512]{3,2,1,0:T(8,128)(2,1)} %bitcast.7.window_ref, f32[128,2048]{1,0:T(8,128)S(1)} %fusion.beam_ref, bf16[1024,1024]{1,0:T(8,128)(2,1)S(1)} %copy-done, f32[8,1024]{1,0:T(8,128)S(1)} %copy-done.5), custom_call_target="tpu_custom_call" | custom-call | flops 536870912 | bytes 4194304 | tf_op jit(solution)/shard_map/pallas_call | solution.py:293
  44.5 14.8 %all_to_all.25 = bf16[16,128,128]{2,1,0:T(8,128)(2,1)S(1)} all-to-all(bf16[16,128,128]{2,1,0:T(8,128)(2,1)S(1)} %shard_map.86), channel_id=1, replica_groups=mesh['ptg'=8,'s'=4,'b'=4] {'s','b'}, dimensions={0} | all-to-all | bytes 1048576 | tf_op jit(solution)/shard_map/all_to_all | solution.py:402
  59.3 2.6 %shard_map.87 = bf16[2048,128]{1,0:T(8,128)(2,1)S(1)} custom-call(s32[1]{0:T(128)} %bitcast.4.me_ref, bf16[2048,128]{1,0:T(8,128)(2,1)S(1)} %bitcast.27, bf16[2048,128]{1,0:T(8,128)(2,1)S(1)} %copy-done.4, bf16[1024,512]{1,0:T(8,128)(2,1)S(1)} %copy-done.6, f32[512,128]{1,0:T(8,128)S(1)} %copy-done.7), custom_call_target="tpu_custom_call" | custom-call | flops 2147483648 | bytes 4194304 | tf_op jit(solution)/shard_map/pallas_call | solution.py:293
  61.9 15.0 %all_to_all.26.x_ref = bf16[16,128,128]{2,1,0:T(8,128)(2,1)S(1)} all-to-all(bf16[16,128,128]{2,1,0:T(8,128)(2,1)S(1)} %bitcast.28), channel_id=1, replica_groups=mesh['ptg'=8,'s'=4,'b'=4] {'s','b'}, dimensions={0} | all-to-all | bytes 1048576 | tf_op jit(solution)/shard_map/all_to_all | solution.py:415
  76.8 1.1 %shard_map.88 = bf16[8,128,256]{2,1,0:T(8,128)(2,1)S(1)} custom-call(bf16[16,128,128]{2,1,0:T(8,128)(2,1)S(1)} %all_to_all.26.x_ref, f32[128,2048]{1,0:T(8,128)S(1)} %fusion.beam_ref, bf16[1024,1024]{1,0:T(8,128)(2,1)S(1)} %copy-done, f32[8,1024]{1,0:T(8,128)S(1)} %copy-done.5), custom_call_target="tpu_custom_call" | custom-call | flops 536870912 | bytes 4194304 | tf_op jit(solution)/shard_map/pallas_call | solution.py:293
  78.0 13.9 %all_to_all.27.terms_ref = bf16[8,128,256]{2,1,0:T(8,128)(2,1)S(1)} all-to-all(bf16[8,128,256]{2,1,0:T(8,128)(2,1)S(1)} %shard_map.88), channel_id=1, replica_groups=mesh['ptg'=8,'s'=4,'b'=4] {'ptg'}, dimensions={0} | all-to-all | bytes 1048576 | tf_op jit(solution)/shard_map/all_to_all | solution.py:429
  91.8 1.0 shard_map.89
  92.9 1.3 %collective-permute-done.6 = bf16[2,128,256]{2,1,0:T(8,128)(2,1)S(1)} collective-permute-done((bf16[2,128,256]{2,1,0:T(8,128)(2,1)S(1)}, bf16[2,128,256]{2,1,0:T(8,128)(2,1)S(1)}, u32[]{:S(2)}, u32[]{:S(2)}) %collective-permute-start.6) | collective-permute-done | bytes 131104 | tf_op jit(solution)/shard_map/ppermute | solution.py:439
  94.3 3.9 %collective-permute-start.8 = (bf16[256,256]{1,0:T(8,128)(2,1)S(1)}, bf16[256,256]{1,0:T(8,128)(2,1)S(1)}, u32[]{:S(2)}, u32[]{:S(2)}) collective-permute-start(bf16[256,256]{1,0:T(8,128)(2,1)S(1)} %pad_maximum_fusion.1), channel_id=1, source_target_pairs={{0,0},{1,8},{2,16},{3,24},{4,32},{5,40},{6,48},{7,56},{8,64},{9,72... | collective-permute-start | bytes 393224 | tf_op jit(solution)/shard_map/ppermute | solution.py:450
  98.3 8.5 %collective-permute-done.8 = bf16[256,256]{1,0:T(8,128)(2,1)S(1)} collective-permute-done((bf16[256,256]{1,0:T(8,128)(2,1)S(1)}, bf16[256,256]{1,0:T(8,128)(2,1)S(1)}, u32[]{:S(2)}, u32[]{:S(2)}) %collective-permute-start.8) | collective-permute-done | bytes 131104 | tf_op jit(solution)/shard_map/ppermute | solution.py:450
  106.8 3.5 %collective-permute-done.7 = bf16[256,256]{1,0:T(8,128)(2,1)S(1)} collective-permute-done((bf16[256,256]{1,0:T(8,128)(2,1)S(1)}, bf16[256,256]{1,0:T(8,128)(2,1)S(1)}, u32[]{:S(2)}, u32[]{:S(2)}) %collective-permute-start.7) | collective-permute-done | bytes 131104 | tf_op jit(solution)/shard_map/ppermute | solution.py:450
  110.4 0.1 fusion.1
  110.5 0.9 maximum_select_fusion
  (29 shorter events, 0.4 us)
Async XLA Ops:
  0.0 1.8 %copy-start.1 = (s32[1,2048,128]{2,1,0:T(8,128)S(1)}, s32[1,2048,128]{2,1,0:T(8,128)}, u32[]{:S(2)}) copy-start(s32[1,2048,128]{2,1,0:T(8,128)} %param.10) | copy-start | bytes 3145732
  2.3 22.5 %collective-permute-start.4 = (bf16[1024,128]{1,0:T(8,128)(2,1)S(1)}, bf16[1024,128]{1,0:T(8,128)(2,1)S(1)}, u32[]{:S(2)}, u32[]{:S(2)}) collective-permute-start(bf16[1024,128]{1,0:T(8,128)(2,1)S(1)} %get-tuple-element.19), channel_id=1, source_target_pairs={{0,15},{1,14},{2,13},{3,12},{4,11},{5,10},{6,9},{7,8},{8,7},{9,6},... | collective-permute-start | bytes 786440 | tf_op jit(solution)/shard_map/ppermute | solution.py:350
  4.7 12.1 %collective-permute-start.1 = (s32[8]{0:T(128)S(1)}, s32[8]{0:T(128)S(1)}, u32[]{:S(2)}, u32[]{:S(2)}) collective-permute-start(s32[8]{0:T(128)S(1)} %compare_select_fusion), channel_id=1, source_target_pairs={{0,32},{16,48},{32,0},{48,16},{64,96},{80,112},{96,64},{112,80},{1... | collective-permute-start | bytes 104 | tf_op jit(solution)/shard_map/ppermute | solution.py:346
  8.6 8.1 %collective-permute-start.2 = (s32[8]{0:T(128)S(1)}, s32[8]{0:T(128)S(1)}, u32[]{:S(2)}, u32[]{:S(2)}) collective-permute-start(s32[8]{0:T(128)S(1)} %compare_select_fusion), channel_id=1, source_target_pairs={{0,48},{16,32},{32,16},{48,0},{64,112},{80,96},{96,80},{112,64},{1... | collective-permute-start | bytes 104 | tf_op jit(solution)/shard_map/ppermute | solution.py:346
  9.3 7.4 %collective-permute-start = (s32[8]{0:T(128)S(1)}, s32[8]{0:T(128)S(1)}, u32[]{:S(2)}, u32[]{:S(2)}) collective-permute-start(s32[8]{0:T(128)S(1)} %compare_select_fusion), channel_id=1, source_target_pairs={{0,16},{16,0},{32,48},{48,32},{64,80},{80,64},{96,112},{112,96},{1... | collective-permute-start | bytes 104 | tf_op jit(solution)/shard_map/ppermute | solution.py:346
  9.7 12.5 %all-to-all-start = ((bf16[4,4,16,512]{3,2,1,0:T(8,128)(2,1)}), bf16[4,4,16,512]{3,2,1,0:T(8,128)(2,1)S(1)}, u32[]{:S(2)}, u32[]{:S(2)}) async-start(bf16[4,4,16,512]{3,2,1,0:T(8,128)(2,1)} %bitcast.30), calls=%async_computation | async-start | bytes 524288 | tf_op jit(solution)/shard_map/all_to_all | solution.py:344
  15.5 9.4 %collective-permute-start.5 = (bf16[16,128]{1,0:T(8,128)(2,1)S(1)}, bf16[16,128]{1,0:T(8,128)(2,1)S(1)}, u32[]{:S(2)}, u32[]{:S(2)}) collective-permute-start(bf16[16,128]{1,0:T(8,128)(2,1)S(1)} %get-tuple-element.20), channel_id=1, source_target_pairs={{8,0},{9,7},{10,6},{11,5},{12,4},{13,3},{14,2},{15,1},{24,16},{25,... | collective-permute-start | bytes 12296 | tf_op jit(solution)/shard_map/ppermute | solution.py:351
  16.8 3.7 %collective-permute-start.3 = (s32[8]{0:T(128)S(1)}, s32[8]{0:T(128)S(1)}, u32[]{:S(2)}, u32[]{:S(2)}) collective-permute-start(s32[8]{0:T(128)S(1)} %add_add_fusion), channel_id=1, source_target_pairs={{0,64},{16,80},{32,96},{48,112},{64,0},{80,16},{96,32},{112,48},{1... | collective-permute-start | bytes 104 | tf_op jit(solution)/shard_map/ppermute | solution.py:349
  24.9 17.3 %all-to-all-start.1 = ((bf16[32,16,512]{2,1,0:T(8,128)(2,1)}), bf16[32,16,512]{2,1,0:T(8,128)(2,1)}, u32[]{:S(2)}, u32[]{:S(2)}) async-start(bf16[32,16,512]{2,1,0:T(8,128)(2,1)} %bitcast.6), calls=%async_computation.1 | async-start | bytes 1048576 | tf_op jit(solution)/shard_map/all_to_all | solution.py:380
  32.4 9.8 %copy-start = (bf16[1024,1024]{1,0:T(8,128)(2,1)S(1)}, bf16[1024,1024]{1,0:T(8,128)(2,1)}, u32[]{:S(2)}) copy-start(bf16[1024,1024]{1,0:T(8,128)(2,1)} %constant.70.clone.table_ref) | copy-start | bytes 6291460
  32.4 9.7 %copy-start.5 = (f32[8,1024]{1,0:T(8,128)S(1)}, f32[8,1024]{1,0:T(8,128)}, u32[]{:S(2)}) copy-start(f32[8,1024]{1,0:T(8,128)} %constant.71.clone.turn_ref) | copy-start | bytes 98308
  34.5 1.2 %copy-start.2 = (s32[1,2048,128]{2,1,0:T(8,128)S(1)}, s32[1,2048,128]{2,1,0:T(8,128)}, u32[]{:S(2)}) copy-start(s32[1,2048,128]{2,1,0:T(8,128)} %param.10) | copy-start | bytes 3145732
  37.1 0.8 copy-start.3
  42.1 17.2 %copy-start.4 = (bf16[2048,128]{1,0:T(8,128)(2,1)S(1)}, bf16[2048,128]{1,0:T(8,128)(2,1)}, u32[]{:S(2)}) copy-start(bf16[2048,128]{1,0:T(8,128)(2,1)} %copy-done.3) | copy-start | bytes 1572868
  42.1 17.2 %copy-start.6 = (bf16[1024,512]{1,0:T(8,128)(2,1)S(1)}, bf16[1024,512]{1,0:T(8,128)(2,1)}, u32[]{:S(2)}) copy-start(bf16[1024,512]{1,0:T(8,128)(2,1)} %constant.72.clone.table_ref) | copy-start | bytes 3145732
  42.2 17.2 %copy-start.7 = (f32[512,128]{1,0:T(8,128)S(1)}, f32[512,128]{1,0:T(8,128)}, u32[]{:S(2)}) copy-start(f32[512,128]{1,0:T(8,128)} %constant.73.clone.turn_ref) | copy-start | bytes 786436
  92.8 1.4 %collective-permute-start.6 = (bf16[2,128,256]{2,1,0:T(8,128)(2,1)S(1)}, bf16[2,128,256]{2,1,0:T(8,128)(2,1)S(1)}, u32[]{:S(2)}, u32[]{:S(2)}) collective-permute-start(bf16[2,128,256]{2,1,0:T(8,128)(2,1)S(1)} %get-tuple-element.28), channel_id=1, source_target_pairs={{0,1},{1,0},{2,3},{3,2},{4,5},{5,4},{6,7},{7,6},{8,9},{9,8},{10,11... | collective-permute-start | bytes 393224 | tf_op jit(solution)/shard_map/ppermute | solution.py:439
  94.3 12.6 %collective-permute-start.8 = (bf16[256,256]{1,0:T(8,128)(2,1)S(1)}, bf16[256,256]{1,0:T(8,128)(2,1)S(1)}, u32[]{:S(2)}, u32[]{:S(2)}) collective-permute-start(bf16[256,256]{1,0:T(8,128)(2,1)S(1)} %pad_maximum_fusion.1), channel_id=1, source_target_pairs={{0,0},{1,8},{2,16},{3,24},{4,32},{5,40},{6,48},{7,56},{8,64},{9,72... | collective-permute-start | bytes 393224 | tf_op jit(solution)/shard_map/ppermute | solution.py:450
  98.2 12.2 %collective-permute-start.7 = (bf16[256,256]{1,0:T(8,128)(2,1)S(1)}, bf16[256,256]{1,0:T(8,128)(2,1)S(1)}, u32[]{:S(2)}, u32[]{:S(2)}) collective-permute-start(bf16[256,256]{1,0:T(8,128)(2,1)S(1)} %pad_maximum_fusion), channel_id=1, source_target_pairs={{0,4},{1,12},{2,20},{3,28},{4,36},{5,44},{6,52},{7,60},{8,68},{9,7... | collective-permute-start | bytes 393224 | tf_op jit(solution)/shard_map/ppermute | solution.py:450
